TPU v7x, 128 devices: a whole 4x4x4 slice. The times are simulated.
128 devices in a mesh: region: 64 (over y, x_hi, z, core), coord: 2 (over x_lo).
Axes of the slice: x: 4 (x_hi: 2, x_lo: 2; x = x_hi * 2 + x_lo), y: 4, z: 4, core: 2. Of those that a mesh axis runs over, the one named last changes fastest.
Arguments:
- right_side: float32 [2, 262144], P(None, ('region', 'coord')), may hold values from -6 to 6
- anchor: float32 [262144], P(('region', 'coord')), may hold values from 0.5 to 2
- blocks: float32 [2048, 2, 128, 128], P(('region', 'coord')), may hold values from 2.734375e-05 to 0.02734375
- tile_nbr: int32 [2048, 2], P(('region', 'coord')), may hold values from 0 to 31
- cut_cells: int32 [128, 128, 128], P(('region', 'coord')), may hold values from 0 to 2047
- cut_weight: float32 [128, 128, 128], P(('region', 'coord')), may hold values from 0 to 1, as said below
- pin_cell: int32 [524288], P(('region', 'coord')), may hold values from 0 to 2047
- pin_net: int32 [524288], P(('region', 'coord')), may hold values from 0 to 16383, as said below
- star_weight: float32 [16384], replicated, may hold values from 0.2 to 2
Outputs:
- positions: float32 [2, 262144], P(None, ('region', 'coord'))
- residual: float32 [2, 262144], P(None, ('region', 'coord'))
Inputs may be any that keep to these rules, and one draw needn't show every extreme that they name: cut_weight[d, p, s] equals cut_weight[p, d, s], and it is 0 where p equals d. Every net number appears exactly 32 times; net n is owned by partition n // 128, and pin_net[d * 4096 + o * 32 + s] is a net owned by partition o for every partition d, owner o and s below 32.
All inputs are finite; a program needn't handle non-finite values.
Results may differ from a plain program's by a relative error of at most 0.00021.
Values sent between devices are 32-bit elements; how exact they have to be, the bound alone decides.
No kernel may reach another device: no remote copies, remote signals or barrier semaphores. Data moves between devices by JAX's collectives and lax.ppermute only.
A program may use at most 128 MiB of HBM per device.

v0:
```python
import jax
import jax.numpy as jnp
from jax import lax
from jax.sharding import PartitionSpec as P

FANOUT = 32
ITERS = 3


exact_prec = lax.Precision.HIGHEST


def per_device(
    right_side, anchor, blocks, tile_nbr, cut_cells, cut_weight, pin_cell, pin_net, star_weight
):
    tile_count = blocks.shape[0]
    tile_width = blocks.shape[2]
    cell_count = tile_count * tile_width
    halves = lax.axis_size("coord")
    net_count = star_weight.shape[0]
    spread_map = (
        jnp.arange(halves * tile_count, dtype=jnp.int32)[:, None] == tile_nbr.reshape(-1)[None, :]
    ).astype(jnp.float32)
    send_cells = cut_cells[0]
    link_weight = cut_weight[0]
    pin_weight = star_weight[pin_net]

    def spread_back(parts):
        spread = jnp.einsum("ab,kbw->kaw", spread_map, parts, precision=exact_prec)
        return lax.psum_scatter(
            spread.reshape(parts.shape[0], halves * cell_count),
            "coord",
            scatter_dimension=1,
            tiled=True,
        )

    col_sums = jnp.sum(blocks, axis=2).reshape(1, -1, tile_width)
    degree = anchor + jnp.sum(blocks, axis=(1, 3)).reshape(-1) + spread_back(col_sums)[0]
    degree = degree + jnp.zeros((cell_count,), jnp.float32).at[send_cells.reshape(-1)].add(
        link_weight.reshape(-1)
    )
    degree = degree + jnp.zeros((cell_count,), jnp.float32).at[pin_cell].add(pin_weight)
    positions = jnp.zeros_like(right_side)
    residual = right_side

    def squares(vectors):
        return lax.psum(jnp.sum(vectors * vectors, axis=1, keepdims=True), ("region", "coord"))

    direction = right_side
    norm_now = squares(residual)
    for iteration in range(ITERS):
        totals = lax.psum(
            jnp.zeros((2, net_count), jnp.float32).at[:, pin_net].add(direction[:, pin_cell]),
            ("region", "coord"),
        )
        whole = lax.all_gather(direction, "coord", axis=1, tiled=True).reshape(
            2, halves * tile_count, tile_width
        )
        by_tile = direction.reshape(2, tile_count, tile_width)
        backward = jnp.einsum("tkij,cti->ctkj", blocks, by_tile, precision=exact_prec)
        forward = jnp.einsum("tkij,ctkj->cti", blocks, whole[:, tile_nbr], precision=exact_prec)
        local_part = forward.reshape(2, cell_count) + spread_back(
            backward.reshape(2, -1, tile_width)
        )
        outgoing = direction[:, send_cells]
        incoming = lax.all_to_all(
            outgoing, ("region", "coord"), split_axis=1, concat_axis=1, tiled=True
        )
        cut_part = (
            jnp.zeros((2, cell_count), jnp.float32)
            .at[:, send_cells.reshape(-1)]
            .add((link_weight * incoming).reshape(2, -1))
        )
        centre = totals[:, pin_net] / FANOUT
        star_part = jnp.zeros((2, cell_count), jnp.float32).at[:, pin_cell].add(pin_weight * centre)
        applied = degree * direction - local_part - cut_part - star_part
        product = lax.psum(jnp.sum(direction * applied, axis=1, keepdims=True), ("region", "coord"))
        step_size = norm_now / product
        positions = positions + step_size * direction
        residual = residual - step_size * applied
        norm_next = squares(residual)
        direction = residual + norm_next / norm_now * direction
        norm_now = norm_next
    return (positions, residual)


def solution(mesh):
    return jax.shard_map(
        per_device,
        mesh=mesh,
        in_specs=(
            P(None, ("region", "coord")),
            P(("region", "coord")),
            P(("region", "coord"), None, None, None),
            P(("region", "coord"), None),
            P(("region", "coord"), None, None),
            P(("region", "coord"), None, None),
            P(("region", "coord")),
            P(("region", "coord")),
            P(),
        ),
        out_specs=(P(None, ("region", "coord")), P(None, ("region", "coord"))),
        check_vma=False,
    )
```

profile of v0, /device:TPU:1, one launch (start us, length us, event | category | flops | bytes accessed | tf_op | source)
XLA Modules:
  0.0 1656.8 jit_solution(11445257267086849629)
XLA Ops:
  8.1 0.8 copy.202
  8.9 2.0 fusion.65
  11.0 2.0 copy.236
  13.1 0.4 copy.206
  13.4 0.4 copy-done.6
  13.9 54.4 %gather_fusion.2 = f32[16384,2]{1,0:T(8,128)} fusion(f32[2,2048]{0,1:T(8,128)S(1)} %copy.206, s32[16384]{0:T(1024)S(1)} %fusion.40), kind=kCustom, calls=%fused_computation.2 | custom fusion | bytes 327680 | tf_op jit(solution)/shard_map/gather | solution.py:65
  68.3 5.9 copy.207
  74.2 11.5 all-to-all-start
  85.9 37.9 %scatter_custom_fusion.3 = f32[2,16384]{0,1:T(8,128)} fusion(s32[4096]{0:T(1024)S(1)} %get-tuple-element.22, f32[]{:T(128)} %constant.6.clone.1, f32[2,2048]{0,1:T(8,128)S(1)} %copy.206, s32[4096]{0:T(1024)S(1)} %get-tuple-element.32), kind=kCustom, calls=%fused_computation.28 | custom fusion | flops 8192 | bytes 131076 | tf_op jit(solution)/shard_map/scatter-add | solution.py:53
  123.9 1.5 copy-done.2
  125.4 1.1 fusion.48
  126.7 1.9 copy.244
  128.7 3.3 all_gather.9
  131.9 23.0 %gather_fusion = f32[4096]{0:T(1024)S(1)} fusion(f32[16384]{0:T(1024)S(1)} %copy-done, s32[4096]{0:T(1024)S(1)} %get-tuple-element.23), kind=kCustom, calls=%fused_computation | custom fusion | bytes 49152 | tf_op jit(solution)/shard_map/gather | solution.py:26
  155.0 22.1 %scatter_custom_fusion.1 = f32[2048]{0:T(1024)S(1)} fusion(s32[4096]{0:T(1024)S(1)} %get-tuple-element.31, f32[4096]{0:T(1024)S(1)} %gather_fusion, f32[]{:T(128)} %constant.6.clone.1), kind=kCustom, calls=%fused_computation.112 | custom fusion | flops 4096 | bytes 8196 | tf_op jit(solution)/shard_map/scatter-add | solution.py:42
  177.3 0.6 gather_fusion.1
  178.0 1.6 copy.237
  179.6 89.1 %scatter_fusion = f32[2048]{0:T(1024)S(1)} fusion(f32[2048]{0:T(1024)S(1)} %fusion.55, s32[16384]{0:T(1024)S(1)} %bitcast.192, f32[16384]{0:T(1024)S(1)} %bitcast.184), kind=kCustom, calls=%fused_computation.13 | custom fusion | flops 16384 | bytes 262144 | tf_op jit(solution)/shard_map/scatter-add | solution.py:39
  268.7 39.0 %all-reduce.5.cloned.1.call-done = f32[2,16384]{0,1:T(8,128)} async-done(((f32[2,16384]{0,1:T(8,128)}), f32[2,16384]{0,1:T(8,128)}) %all-reduce.5.cloned.1.call-update) | async-done | bytes 131088 | tf_op jit(solution)/shard_map/psum | solution.py:52
  307.7 47.6 %scatter_custom_fusion.4 = f32[2,2048]{0,1:T(8,128)S(1)} fusion(s32[4096]{0:T(1024)S(1)} %get-tuple-element.31, f32[4096]{0:T(1024)S(1)} %broadcast_multiply_fusion, f32[]{:T(128)} %constant.6.clone.1, f32[2,16384]{0,1:T(8,128)} %all-reduce.5.cloned.1.call-done, s32[4096]{0:T(1024)S(1)} %get-tuple-element.23), kind=kCustom, calls=%fused_computation.49 | custom fusion | flops 16384 | bytes 180228 | tf_op jit(solution)/shard_map/scatter-add | solution.py:75
  355.3 0.3 copy.211
  355.6 1.6 copy.239
  357.3 5.0 copy.208
  362.2 87.8 %scatter_custom_fusion.2 = f32[2,2048]{0,1:T(8,128)S(1)} fusion(s32[16384]{0:T(1024)} %bitcast.193, f32[16384,2]{1,0:T(8,128)} %copy.208, f32[]{:T(128)} %constant.6.clone.1), kind=kCustom, calls=%fused_computation.67 | custom fusion | flops 32768 | bytes 16896 | tf_op jit(solution)/shard_map/scatter-add | solution.py:72
  450.4 2.0 multiply_reduce_fusion.4
  452.4 63.8 %all-reduce = (f32[2,1]{0,1:T(1,128)S(1)}, f32[2,1]{0,1:T(1,128)S(1)}) all-reduce(f32[2,1]{0,1:T(1,128)S(1)} %bitcast.214, f32[2,1]{0,1:T(1,128)S(1)} %bitcast.213), channel_id=1, replica_groups=mesh['region'=64,'coord'=2] {'region','coord'}, use_global_device_ids=true, to_apply=%region_1.0 | all-reduce | flops 4 | bytes 32 | tf_op jit(solution)/shard_map/psum | solution.py:47
  516.4 64.4 %psum.66 = f32[2,1]{0,1:T(1,128)S(1)} all-reduce(f32[2,1]{0,1:T(1,128)S(1)} %bitcast.212), channel_id=1, replica_groups=mesh['region'=64,'coord'=2] {'region','coord'}, use_global_device_ids=true, to_apply=%region_15.0 | all-reduce | flops 2 | bytes 16 | tf_op jit(solution)/shard_map/psum | solution.py:47
  580.9 0.4 copy.215
  581.3 54.4 %gather_fusion.4 = f32[16384,2]{1,0:T(8,128)} fusion(f32[2,2048]{0,1:T(8,128)S(1)} %copy.215, s32[16384]{0:T(1024)S(1)} %fusion.40), kind=kCustom, calls=%fused_computation.6 | custom fusion | bytes 327680 | tf_op jit(solution)/shard_map/gather | solution.py:65
  635.7 38.1 %scatter_custom_fusion.6 = f32[2,16384]{0,1:T(8,128)} fusion(s32[4096]{0:T(1024)} %copy-done.13, f32[]{:T(128)} %constant.6.clone.1, f32[2,2048]{0,1:T(8,128)S(1)} %copy.215, s32[4096]{0:T(1024)} %copy-done.14), kind=kCustom, calls=%fused_computation.26 | custom fusion | flops 8192 | bytes 131584 | tf_op jit(solution)/shard_map/scatter-add | solution.py:53
  673.8 1.1 fusion.46
  674.9 5.9 copy.216
  680.8 4.7 all-to-all-start.1
  685.6 0.5 all-reduce.7.cloned.1.call-update
  686.3 2.0 copy.245
  688.3 3.7 all_gather.10
  692.1 1.2 gather_fusion.3
  693.3 180.7 %all-reduce.7.cloned.1.call-done = f32[2,16384]{0,1:T(8,128)} async-done(((f32[2,16384]{0,1:T(8,128)}), f32[2,16384]{0,1:T(8,128)}) %all-reduce.7.cloned.1.call-update) | async-done | bytes 131088 | tf_op jit(solution)/shard_map/psum | solution.py:52
  874.0 47.7 %scatter_custom_fusion.7 = f32[2,2048]{0,1:T(8,128)S(1)} fusion(s32[4096]{0:T(1024)} %copy-done.12, f32[4096]{0:T(1024)S(1)} %broadcast_multiply_fusion, f32[]{:T(128)} %constant.6.clone.1, f32[2,16384]{0,1:T(8,128)} %all-reduce.7.cloned.1.call-done, s32[4096]{0:T(1024)S(1)} %get-tuple-element.23), kind=kCustom, calls=%fused_computation.47 | custom fusion | flops 16384 | bytes 8438272 | tf_op jit(solution)/shard_map/scatter-add | solution.py:75
  922.0 1.6 copy.241
  923.6 5.0 copy.217
  928.6 87.8 %scatter_custom_fusion.5 = f32[2,2048]{0,1:T(8,128)S(1)} fusion(s32[16384]{0:T(1024)} %bitcast.194, f32[16384,2]{1,0:T(8,128)} %copy.217, f32[]{:T(128)} %constant.6.clone.1), kind=kCustom, calls=%fused_computation.64 | custom fusion | flops 32768 | bytes 16896 | tf_op jit(solution)/shard_map/scatter-add | solution.py:72
  1016.8 2.0 multiply_reduce_fusion.2
  1018.8 63.9 %psum.68 = f32[2,1]{0,1:T(1,128)S(1)} all-reduce(f32[2,1]{0,1:T(1,128)S(1)} %bitcast.210), channel_id=1, replica_groups=mesh['region'=64,'coord'=2] {'region','coord'}, use_global_device_ids=true, to_apply=%region_22.0 | all-reduce | flops 2 | bytes 16 | tf_op jit(solution)/shard_map/psum | solution.py:77
  1082.9 63.7 %psum.69 = f32[2,1]{0,1:T(1,128)S(1)} all-reduce(f32[2,1]{0,1:T(1,128)S(1)} %bitcast.211), channel_id=1, replica_groups=mesh['region'=64,'coord'=2] {'region','coord'}, use_global_device_ids=true, to_apply=%region_24.0 | all-reduce | flops 2 | bytes 16 | tf_op jit(solution)/shard_map/psum | solution.py:47
  1146.6 0.4 copy.224
  1147.0 54.4 %gather_fusion.6 = f32[16384,2]{1,0:T(8,128)} fusion(f32[2,2048]{0,1:T(8,128)S(1)} %copy.224, s32[16384]{0:T(1024)S(1)} %fusion.40), kind=kCustom, calls=%fused_computation.10 | custom fusion | bytes 327680 | tf_op jit(solution)/shard_map/gather | solution.py:65
  1201.4 38.1 %scatter_custom_fusion.9 = f32[2,16384]{0,1:T(8,128)} fusion(s32[4096]{0:T(1024)} %copy-done.13, f32[]{:T(128)} %constant.6.clone.1, f32[2,2048]{0,1:T(8,128)S(1)} %copy.224, s32[4096]{0:T(1024)} %copy-done.14), kind=kCustom, calls=%fused_computation.24 | custom fusion | flops 8192 | bytes 131584 | tf_op jit(solution)/shard_map/scatter-add | solution.py:53
  1239.5 1.1 fusion.44
  1240.6 5.9 copy.225
  1246.5 4.8 all-to-all-start.2
  1251.3 0.5 all-reduce.9.cloned.1.call-update
  1252.0 2.0 copy.246
  1254.1 3.8 all_gather.11
  1257.9 0.6 gather_fusion.5
  1258.5 181.0 %all-reduce.9.cloned.1.call-done = f32[2,16384]{0,1:T(8,128)} async-done(((f32[2,16384]{0,1:T(8,128)}), f32[2,16384]{0,1:T(8,128)}) %all-reduce.9.cloned.1.call-update) | async-done | bytes 131088 | tf_op jit(solution)/shard_map/psum | solution.py:52
  1439.5 47.7 %scatter_custom_fusion.10 = f32[2,2048]{0,1:T(8,128)S(1)} fusion(s32[4096]{0:T(1024)} %copy-done.12, f32[4096]{0:T(1024)S(1)} %broadcast_multiply_fusion, f32[]{:T(128)} %constant.6.clone.1, f32[2,16384]{0,1:T(8,128)} %all-reduce.9.cloned.1.call-done, s32[4096]{0:T(1024)S(1)} %get-tuple-element.23), kind=kCustom, calls=%fused_computation.45 | custom fusion | flops 16384 | bytes 8438272 | tf_op jit(solution)/shard_map/scatter-add | solution.py:75
  1487.2 0.3 copy.229
  1487.6 1.6 copy.243
  1489.2 5.0 copy.226
  1494.2 87.8 %scatter_custom_fusion.8 = f32[2,2048]{0,1:T(8,128)S(1)} fusion(s32[16384]{0:T(1024)} %bitcast.195, f32[16384,2]{1,0:T(8,128)} %copy.226, f32[]{:T(128)} %constant.6.clone.1), kind=kCustom, calls=%fused_computation.61 | custom fusion | flops 32768 | bytes 16896 | tf_op jit(solution)/shard_map/scatter-add | solution.py:72
  1582.4 2.0 multiply_reduce_fusion
  1584.3 63.9 %psum.71 = f32[2,1]{0,1:T(1,128)S(1)} all-reduce(f32[2,1]{0,1:T(1,128)S(1)} %bitcast.209), channel_id=1, replica_groups=mesh['region'=64,'coord'=2] {'region','coord'}, use_global_device_ids=true, to_apply=%region_31.0 | all-reduce | flops 2 | bytes 16 | tf_op jit(solution)/shard_map/psum | solution.py:77
  1648.3 0.7 multiply_subtract_fusion
  (98 shorter events, 3.6 us)
Async XLA Ops:
  8.0 123.9 %copy-start = (f32[16384]{0:T(1024)S(1)}, f32[16384]{0:T(1024)}, u32[]{:S(2)}) copy-start(f32[16384]{0:T(1024)} %param.17) | copy-start | bytes 196612
  8.0 169.9 %reduce-scatter.13.cloned.1.call-start = ((), (), s32[]{:S(2)}) async-start(), calls=%async_computation.10 | async-start | bytes 3145728
  8.9 117.6 %copy-start.15 = (s32[32]{0:T(128)}, s32[32]{0:T(128)S(1)}, u32[]{:S(2)}) copy-start(s32[32]{0:T(128)S(1)} %eq.16) | copy-start | bytes 388
  11.0 2.0 copy-start.4
  13.0 0.8 copy-start.6
  68.3 17.5 %copy-start.10 = (s32[4096]{0:T(1024)S(1)}, s32[4096]{0:T(1024)}, u32[]{:S(2)}) copy-start(s32[4096]{0:T(1024)} %param.16) | copy-start | bytes 49156
  68.3 17.5 %copy-start.11 = (s32[4096]{0:T(1024)S(1)}, s32[4096]{0:T(1024)}, u32[]{:S(2)}) copy-start(s32[4096]{0:T(1024)} %param.15) | copy-start | bytes 49156
  74.2 282.9 %all-to-all-start = ((f32[2,128,128]{2,0,1:T(2,128)}), f32[2,128,128]{2,0,1:T(2,128)S(1)}, u32[]{:S(2)}, u32[]{:S(2)}) async-start(f32[2,128,128]{2,0,1:T(2,128)} %bitcast.28), calls=%async_computation | async-start | bytes 262144 | tf_op jit(solution)/shard_map/all_to_all | solution.py:66
  85.7 221.9 %all-reduce.5.cloned.1.call-start = ((), (), s32[]{:S(2)}) async-start(), calls=%async_computation.7 | async-start | bytes 16777216 | tf_op jit(solution)/shard_map/psum | solution.py:52
  85.8 38.0 %copy-start.13 = (s32[4096]{0:T(1024)}, s32[4096]{0:T(1024)S(1)}, u32[]{:S(2)}) copy-start(s32[4096]{0:T(1024)S(1)} %get-tuple-element.22) | copy-start | bytes 49156
  85.8 38.0 %copy-start.14 = (s32[4096]{0:T(1024)}, s32[4096]{0:T(1024)S(1)}, u32[]{:S(2)}) copy-start(s32[4096]{0:T(1024)S(1)} %get-tuple-element.32) | copy-start | bytes 49156
  85.8 221.8 %copy-start.12 = (s32[4096]{0:T(1024)}, s32[4096]{0:T(1024)S(1)}, u32[]{:S(2)}) copy-start(s32[4096]{0:T(1024)S(1)} %get-tuple-element.31) | copy-start | bytes 49156
  123.8 1.6 copy-start.2
  123.8 231.8 %reduce-scatter.15.cloned.1.call-start = ((), (), s32[]{:S(2)}) async-start(), calls=%async_computation.11 | async-start | bytes 3145728
  126.7 2.0 copy-start.18
  131.9 47.6 %copy-start.17 = (f32[2048]{0:T(1024)S(1)}, f32[2048]{0:T(1024)}, u32[]{:S(2)}) copy-start(f32[2048]{0:T(1024)} %param.10) | copy-start | bytes 24580
  131.9 47.7 %copy-start.3 = (f32[1,128,128]{2,1,0:T(8,128)S(1)}, f32[1,128,128]{2,1,0:T(8,128)}, u32[]{:S(2)}) copy-start(f32[1,128,128]{2,1,0:T(8,128)} %param.14) | copy-start | bytes 196612
  177.1 91.5 %copy-start.5 = (s32[16384,1]{0,1:T(1,128)}, s32[16384,1]{0,1:T(1,128)S(1)}, u32[]{:S(2)}) copy-start(s32[16384,1]{0,1:T(1,128)S(1)} %compare_select_fusion) | copy-start | bytes 196612
  268.7 748.1 %copy-start.7 = (f32[2048]{0:T(1024)}, f32[2048]{0:T(1024)S(1)}, u32[]{:S(2)}) copy-start(f32[2048]{0:T(1024)S(1)} %add.133) | copy-start | bytes 24580
  516.2 157.6 %copy-start.19 = (f32[2]{0:T(128)}, f32[2]{0:T(128)S(1)}, u32[]{:S(2)}) copy-start(f32[2]{0:T(128)S(1)} %divide_bitcast_fusion.4) | copy-start | bytes 28
  680.8 242.8 %all-to-all-start.1 = ((f32[2,128,128]{2,0,1:T(2,128)}), f32[2,128,128]{2,0,1:T(2,128)S(1)}, u32[]{:S(2)}, u32[]{:S(2)}) async-start(f32[2,128,128]{2,0,1:T(2,128)} %bitcast.49), calls=%async_computation.1 | async-start | bytes 262144 | tf_op jit(solution)/shard_map/all_to_all | solution.py:66
  685.5 0.7 copy-start.16
  685.5 188.4 %all-reduce.7.cloned.1.call-start = ((), (), s32[]{:S(2)}) async-start(), calls=%async_computation.8 | async-start | bytes 16777216 | tf_op jit(solution)/shard_map/psum | solution.py:52
  686.1 235.9 %reduce-scatter.17.cloned.1.call-start = ((), (), s32[]{:S(2)}) async-start(), calls=%async_computation.12 | async-start | bytes 3145728
  928.6 88.2 %copy-start.9 = (f32[32,2,128]{2,1,0:T(2,128)S(1)}, f32[32,2,128]{2,1,0:T(2,128)}, u32[]{:S(2)}) copy-start(f32[32,2,128]{2,1,0:T(2,128)} %gather_fusion.3) | copy-start | bytes 98308
  1082.7 156.8 %copy-start.21 = (f32[2]{0:T(128)}, f32[2]{0:T(128)S(1)}, u32[]{:S(2)}) copy-start(f32[2]{0:T(128)S(1)} %divide_bitcast_fusion.2) | copy-start | bytes 28
  1146.5 92.9 %copy-start.23 = (f32[2,1]{0,1:T(1,128)}, f32[2,1]{0,1:T(1,128)S(1)}, u32[]{:S(2)}) copy-start(f32[2,1]{0,1:T(1,128)S(1)} %psum.69) | copy-start | bytes 28
  1246.5 242.7 %all-to-all-start.2 = ((f32[2,128,128]{2,0,1:T(2,128)}), f32[2,128,128]{2,0,1:T(2,128)S(1)}, u32[]{:S(2)}, u32[]{:S(2)}) async-start(f32[2,128,128]{2,0,1:T(2,128)} %bitcast.70), calls=%async_computation.2 | async-start | bytes 262144 | tf_op jit(solution)/shard_map/all_to_all | solution.py:66
  1251.3 188.3 %all-reduce.9.cloned.1.call-start = ((), (), s32[]{:S(2)}) async-start(), calls=%async_computation.9 | async-start | bytes 16777216 | tf_op jit(solution)/shard_map/psum | solution.py:52
  1251.8 235.7 %reduce-scatter.19.cloned.1.call-start = ((), (), s32[]{:S(2)}) async-start(), calls=%async_computation.13 | async-start | bytes 3145728
  1489.2 159.8 %copy-start.1 = (f32[16384]{0:T(1024)S(1)}, f32[16384]{0:T(1024)}, u32[]{:S(2)}) copy-start(f32[16384]{0:T(1024)} %param.17) | copy-start | bytes 196612
  1494.2 88.2 %copy-start.8 = (f32[2048]{0:T(1024)S(1)}, f32[2048]{0:T(1024)}, u32[]{:S(2)}) copy-start(f32[2048]{0:T(1024)} %copy-done.7) | copy-start | bytes 24580
  1494.2 154.0 %copy-start.24 = (f32[2,1]{0,1:T(1,128)S(1)}, f32[2,1]{0,1:T(1,128)}, u32[]{:S(2)}) copy-start(f32[2,1]{0,1:T(1,128)} %copy-done.23) | copy-start | bytes 28
  1494.2 154.1 %copy-start.20 = (f32[2]{0:T(128)S(1)}, f32[2]{0:T(128)}, u32[]{:S(2)}) copy-start(f32[2]{0:T(128)} %copy-done.19) | copy-start | bytes 28
  1494.2 154.1 %copy-start.22 = (f32[2]{0:T(128)S(1)}, f32[2]{0:T(128)}, u32[]{:S(2)}) copy-start(f32[2]{0:T(128)} %copy-done.21) | copy-start | bytes 28
Sparse Core Ops, SparseCore 0:
  13.2 37.5 reduce-scatter.12
  128.8 36.0 reduce-scatter.14
  689.3 35.8 reduce-scatter.16
  1254.7 35.7 reduce-scatter.18
Sparse Core Ops, SparseCore 1:
  123.9 183.7 all-reduce.4
  691.9 182.1 all-reduce.6
  1257.6 181.9 all-reduce.8
where the time goes:
time: 1670 us; the launch traced here: 1660 us
  other arithmetic  635 us (38%)
  waiting for transfers between devices  402 us (24%)
  blocking collectives  331 us (20%)
  local copies, waits for them, and re-layouts  242 us (14%)
  starting transfers between devices  21.3 us (1%)
    psum x3, waiting for transfers between devices, per_device(): lax.psum(jnp.zeros((2, net_count), jnp.float32).at[:, pin_net].add(direct...  401 us
    scatter-add x3, other arithmetic, per_device(): cut_part = jnp.zeros((2, cell_count), jnp.float32).at[:, send_cells.resha...  264 us
    psum x3, blocking collectives, squares(): lax.psum(jnp.sum(vectors * vectors, axis=1, keepdims=True), ('region', 'c...  192 us
    gather x6, local copies, waits for them, and re-layouts, per_device(): outgoing = direction[:, send_cells]  181 us
    scatter-add x3, other arithmetic, per_device(): jnp.zeros((2, cell_count), jnp.float32).at[:, pin_cell]  143 us
    psum x2, blocking collectives, per_device(): lax.psum(jnp.sum(direction * applied, axis=1, keepdims=True), ('region',...  128 us
    scatter-add x3, other arithmetic, per_device(): jnp.zeros((2, net_count), jnp.float32).at[:, pin_net]  114 us
    scatter-add x1, other arithmetic, per_device(): jnp.zeros((cell_count,), jnp.float32).at[send_cells.reshape(-1)]  89.1 us
  transfers between devices with their start and end apart: 10, of which 3 were waited for; matrix products, arithmetic and copies ran while one was open for 24% of the time, Pallas kernels for 0%

commit v1 on v0

v1 whole, which is shorter than its diff:
```python
import functools

import jax
import jax.numpy as jnp
from jax import lax
from jax.experimental import pallas as pl
from jax.experimental.pallas import tpu as pltpu
from jax.sharding import PartitionSpec as P

FANOUT = 32
ITERS = 3
AXES = ("region", "coord")
LANES = 128
TILES = 16
F32 = jnp.float32
BF16 = jnp.bfloat16
I32 = jnp.int32
SUM_LANE = 96


def iota(shape, axis):
    return lax.broadcasted_iota(I32, shape, axis)


def split2(x):
    high = x.astype(BF16).astype(F32)
    return [high, (x - high).astype(BF16).astype(F32)]


def split3(x):
    high = x.astype(BF16).astype(F32)
    return [high] + split2(x - high)


def dot_nt(a, b):
    return lax.dot_general(a, b, (((1,), (1,)), ((), ())), preferred_element_type=F32)


def dot_nn(a, b):
    return lax.dot_general(a, b, (((1,), (0,)), ((), ())), preferred_element_type=F32)


def roll(x, shift):
    shift = shift % LANES
    return x if shift == 0 else pltpu.roll(x, shift, 1)


def total(x):
    return jnp.sum(jnp.sum(x, axis=0, keepdims=True), axis=1, keepdims=True)


def lane_value(row, lane):
    return jnp.sum(jnp.where(iota(row.shape, 1) == lane, row, 0.0), axis=1, keepdims=True)


def pick(tables, cells):
    low = cells & (LANES - 1)
    high = cells >> 7
    rows = [jnp.zeros(cells.shape, F32) for _ in tables]
    for tile in range(TILES):
        here = high == tile
        for v, table in enumerate(tables):
            wide = jnp.broadcast_to(table[tile], cells.shape)
            got = jnp.take_along_axis(wide, low, axis=1, mode="promise_in_bounds")
            rows[v] = jnp.where(here, got, rows[v])
    return rows


def one_hot(row, count):
    return jnp.where(iota((count, LANES), 0) == row, 1.0, 0.0).astype(BF16)


def add_rows(row_count, cell_row, value_rows):
    acc = None
    for j in range(0, row_count, 2):
        hots, masked = [], []
        for i in (j, j + 1):
            cells = cell_row(i)
            hots.append(one_hot(cells & (LANES - 1), LANES))
            here = iota((TILES, LANES), 0) == (cells >> 7)
            masked.append(
                jnp.concatenate([jnp.where(here, v, 0.0) for v in value_rows(i)], axis=0).astype(BF16)
            )
        part = dot_nt(jnp.concatenate(masked, axis=1), jnp.concatenate(hots, axis=1))
        acc = part if acc is None else acc + part
    return acc


def fold(acc, vectors, parts):
    size = vectors * TILES
    return sum(acc[i * size : (i + 1) * size] for i in range(parts))


def put_gathered(vectors, sums, cut_cells, pin_cell, pin_net, out_ref):
    lane = iota((32, LANES), 1)
    tail = jnp.zeros((1, LANES), F32)
    for i, s in enumerate(sums):
        tail = jnp.where(iota((1, LANES), 1) == SUM_LANE + i, s, tail)
    gx, gy = pick(vectors, pin_cell[...])
    net = (pin_net[...] & (LANES - 1)).astype(F32)
    for q in range(4):
        row = jnp.where(
            lane < 32,
            roll(gx, -32 * q),
            jnp.where(
                lane < 64,
                roll(gy, 32 - 32 * q),
                jnp.where(lane < 96, roll(net, 64 - 32 * q), tail),
            ),
        )
        out_ref[pl.ds(4 * q + 2, 32, stride=16), :] = row
        out_ref[pl.ds(4 * q + 3, 32, stride=16), :] = jnp.zeros((32, LANES), F32)
    for g in range(16):
        gx, gy = pick(vectors, cut_cells[pl.ds(8 * g, 8), :])
        out_ref[pl.ds(32 * g, 8, stride=4), :] = gx
        out_ref[pl.ds(32 * g + 1, 8, stride=4), :] = gy


def dense(rows, offset):
    lane = iota((32, LANES), 1)
    out = roll(rows[0], -offset)
    for q in range(1, 4):
        out = jnp.where(lane >= 32 * q, roll(rows[q], 32 * q - offset), out)
    return out


def first_kernel(right_ref, cut_cells, pin_cell, pin_net, send_ref, start_ref):
    tables = [
        [right_ref[v : v + 1, LANES * t : LANES * (t + 1)] for t in range(TILES)] for v in range(2)
    ]
    for v in range(2):
        for t in range(TILES):
            start_ref[TILES * v + t : TILES * v + t + 1, :] = tables[v][t]
    r = start_ref[...]
    sums = [total(r[16 * v : 16 * v + 16] * r[16 * v : 16 * v + 16]) for v in range(2)]
    put_gathered(tables, sums, cut_cells, pin_cell, pin_net, send_ref)


def degree_kernel(cut_cells, cut_weight, pin_cell, pin_net, star, anchor, out_ref, rows_ref, pins_ref):
    lane = iota((32, LANES), 1)
    net = pin_net[...] & (LANES - 1)
    for q in range(4):
        got = jnp.take_along_axis(
            star[pl.ds(q, 32, stride=4), :], roll(net, -32 * q), axis=1, mode="promise_in_bounds"
        )
        rows_ref[pl.ds(32 * q, 32), :] = got
    weight = dense([rows_ref[pl.ds(32 * q, 32), :] for q in range(4)], 0)
    for i, part in enumerate(split3(weight)):
        pins_ref[pl.ds(32 * i, 32), :] = part
    acc = add_rows(
        32,
        lambda j: pin_cell[j : j + 1, :],
        lambda j: [pins_ref[32 * i + j : 32 * i + j + 1, :] for i in range(3)],
    )
    acc = acc + add_rows(
        128,
        lambda j: cut_cells[j : j + 1, :],
        lambda j: split3(cut_weight[j : j + 1, :]),
    )
    out_ref[...] = anchor[...] + fold(acc, 1, 3)


def block_kernel(first, place, nbr_row, nbr_col, blocks, own_ref, peer_ref, local_ref, forward_ref, back_ref, near, far, got_f, got_b):
    vectors = 3 if first else 2
    me = place[0]
    pick_rows = jnp.where(iota((32, 32), 1) == nbr_col[...], 1.0, 0.0).astype(BF16)
    spread_rows = jnp.where(iota((32, 32), 0) == nbr_row[...], 1.0, 0.0).astype(BF16)
    own, peer = own_ref[...], peer_ref[...]
    upper = me == 1
    near[...] = jnp.ones(near.shape, F32)
    far[...] = jnp.ones(far.shape, F32)
    for v in range(2):
        o, p = own[16 * v : 16 * v + 16], peer[16 * v : 16 * v + 16]
        whole = jnp.concatenate([jnp.where(upper, p, o), jnp.where(upper, o, p)], axis=0)
        for i, (mine, part) in enumerate(zip(split2(o), split2(whole))):
            near[pl.ds(2 * i + v, 16, stride=8), :] = mine
            picked = dot_nn(pick_rows, part.astype(BF16))
            for k in range(2):
                far[pl.ds(128 * k + 2 * i + v, 16, stride=8), :] = picked[16 * k : 16 * k + 16]
    for t in range(TILES):
        pair = jnp.concatenate([blocks[t, 0], blocks[t, 1]], axis=1)
        high = pair.astype(BF16)
        low = (pair - high.astype(F32)).astype(BF16)
        a = near[8 * t : 8 * t + 8, :].astype(BF16)
        b = jnp.concatenate(
            [far[128 * k + 8 * t : 128 * k + 8 * t + 8, :] for k in range(2)], axis=1
        ).astype(BF16)
        back = dot_nn(a, high) + dot_nn(a, low)
        for k in range(2):
            got_b[128 * k + 8 * t : 128 * k + 8 * t + 8, :] = back[:, LANES * k : LANES * (k + 1)]
        got_f[8 * t : 8 * t + 8, :] = dot_nt(b, high) + dot_nt(b, low)
    for v in range(vectors):
        def take(ref, at):
            if v == 2:
                return ref[pl.ds(at + 4, 16, stride=8), :]
            return ref[pl.ds(at + v, 16, stride=8), :] + ref[pl.ds(at + v + 2, 16, stride=8), :]

        forward = take(got_f, 0)
        backward = jnp.concatenate([take(got_b, 128 * k) for k in range(2)], axis=0)
        spread = sum(dot_nn(spread_rows, part.astype(BF16)) for part in split3(backward))
        lower, higher = spread[:16], spread[16:]
        local_ref[16 * v : 16 * v + 16, :] = forward + jnp.where(upper, higher, lower)
        back_ref[16 * v : 16 * v + 16, :] = jnp.where(upper, lower, higher)
        if v < 2:
            forward_ref[16 * v : 16 * v + 16, :] = forward


def owner_kernel(first, *refs):
    if first:
        (place, sent, got, cut_weight, star, forward_ref, state, parts, local_ref, back_ref,
         out_ref, sums_ref, degree_ref, rows) = refs
        degree = parts[...] + local_ref[32:48, :] + back_ref[32:48, :]
        degree_ref[...] = degree
    else:
        (place, sent, got, cut_weight, star, forward_ref, state, degree_in,
         out_ref, sums_ref, rows) = refs
        degree = degree_in[...]
    pin_rows = [got[pl.ds(4 * q + 2, 32, stride=16), :] for q in range(4)]
    sums = sum(jnp.sum(row, axis=0, keepdims=True) for row in pin_rows)
    sums_ref[...] = jnp.broadcast_to(sums, (8, LANES))
    nets = dense(pin_rows, 64).astype(I32)
    rows[...] = jnp.zeros(rows.shape, F32)
    for v in range(2):
        for i, part in enumerate(split3(dense(pin_rows, 32 * v))):
            rows[pl.ds(2 * i + v, 32, stride=8), :] = part
    acc = None
    for j in range(0, 32, 2):
        hot = jnp.concatenate([one_hot(nets[i : i + 1], LANES) for i in (j, j + 1)], axis=1)
        left = jnp.concatenate([rows[8 * i : 8 * i + 8, :] for i in (j, j + 1)], axis=1)
        part = dot_nt(left.astype(BF16), hot)
        acc = part if acc is None else acc + part
    weight = star[pl.ds(place[1], 1), :] * (1.0 / FANOUT)
    totals = [acc[v : v + 1] + acc[v + 2 : v + 3] + acc[v + 4 : v + 5] for v in range(2)]
    centres = [weight * t for t in totals]
    tail = jnp.zeros((1, LANES), F32)
    for v in range(2):
        r = state[16 * v : 16 * v + 16, :]
        share = r * (degree * r - 2.0 * forward_ref[16 * v : 16 * v + 16, :])
        line = jnp.sum(share, axis=0, keepdims=True) - centres[v] * totals[v]
        cut = cut_weight[...] * (sent[pl.ds(v, 128, stride=4), :] * got[pl.ds(v, 128, stride=4), :])
        line = line - jnp.sum(cut, axis=0, keepdims=True)
        tail = jnp.where(
            iota((1, LANES), 1) == SUM_LANE + v, jnp.sum(line, axis=1, keepdims=True), tail
        )
    lane = iota((8, LANES), 1)
    tables = [jnp.broadcast_to(c, (8, LANES)) for c in centres]
    for g in range(16):
        row = got[pl.ds(32 * g + 2, 8, stride=4), :]
        index = jnp.where(lane < 32, roll(row, -64), roll(row, -32)).astype(I32) & (LANES - 1)
        gx, gy = (
            jnp.take_along_axis(t, index, axis=1, mode="promise_in_bounds") for t in tables
        )
        out_ref[pl.ds(8 * g, 8), :] = jnp.where(
            lane < 32, gx, jnp.where(lane < 64, gy, jnp.where(lane < 96, 0.0, tail))
        )


def cut_kernel(cut_cells, cut_weight, got, local_ref, back_ref, sums_ref, out_ref):
    del sums_ref

    def values(j):
        weight = cut_weight[j : j + 1, :]
        parts = [split2(weight * got[4 * j + v : 4 * j + v + 1, :]) for v in range(2)]
        return [parts[0][0], parts[1][0], parts[0][1], parts[1][1]]

    acc = add_rows(128, lambda j: cut_cells[j : j + 1, :], values)
    out_ref[...] = fold(acc, 2, 2) + local_ref[0:32, :] + back_ref[0:32, :]


def step_kernel(first, last, pin_cell, got, degree_ref, others, sums_ref, *refs):
    refs = list(refs)
    state = refs.pop(0)
    old = None if first else refs.pop(0)
    if last:
        positions_ref, residual_ref, pins = refs
    else:
        cut_cells, pin_net, send_ref, state_ref, old_ref, pins = refs
    pin_rows = [got[pl.ds(q, 32, stride=4), :] for q in range(4)]
    energy = sum(jnp.sum(row, axis=0, keepdims=True) for row in pin_rows)
    for v in range(2):
        for i, part in enumerate(split2(dense(pin_rows, 32 * v))):
            pins[pl.ds(32 * (2 * i + v), 32), :] = part
    acc = add_rows(
        32,
        lambda j: pin_cell[j : j + 1, :],
        lambda j: [pins[32 * i + j : 32 * i + j + 1, :] for i in range(4)],
    )
    removed = fold(acc, 2, 2) + others[...]
    degree = degree_ref[...]
    news, line = [], jnp.zeros((1, LANES), F32)
    lanes = iota((1, LANES), 1)
    sent_sums = [None] * 4
    for v in range(2):
        part = slice(16 * v, 16 * v + 16)
        r = state[part, :]
        z = degree * r - removed[part]
        norm = lane_value(sums_ref[0:1, :], SUM_LANE + v)
        product = lane_value(energy, SUM_LANE + v)
        if first:
            p, q = r, z
        else:
            cross = lane_value(sums_ref[0:1, :], SUM_LANE + 2 + v)
            beta = norm / lane_value(old[0:1, :], v)
            product = product + beta * (2.0 * cross + beta * lane_value(old[0:1, :], 2 + v))
            p = r + beta * state[32 + 16 * v : 48 + 16 * v, :]
            q = z + beta * state[64 + 16 * v : 80 + 16 * v, :]
        step = norm / product
        x = step * p
        if not first:
            x = x + state[96 + 16 * v : 112 + 16 * v, :]
        r = r - step * q
        if last:
            for t in range(TILES):
                positions_ref[v : v + 1, LANES * t : LANES * (t + 1)] = x[t : t + 1]
                residual_ref[v : v + 1, LANES * t : LANES * (t + 1)] = r[t : t + 1]
            continue
        for i, new in enumerate((r, p, q, x)):
            state_ref[32 * i + 16 * v : 32 * i + 16 * v + 16, :] = new
        news.append([r[t : t + 1] for t in range(TILES)])
        sent_sums[v], sent_sums[2 + v] = total(r * r), total(r * q)
        line = jnp.where(lanes == v, norm, jnp.where(lanes == 2 + v, product, line))
    if last:
        return
    old_ref[...] = jnp.broadcast_to(line, (8, LANES))
    put_gathered(news, sent_sums, cut_cells, pin_cell, pin_net, send_ref)


def call(kernel, shapes, scratch, cost, args, smem=0):
    vmem = pl.BlockSpec(memory_space=pltpu.VMEM)
    return pl.pallas_call(
        kernel,
        out_shape=[jax.ShapeDtypeStruct(s, F32) for s in shapes],
        in_specs=[pl.BlockSpec(memory_space=pltpu.SMEM)] * smem + [vmem] * (len(args) - smem),
        out_specs=[vmem] * len(shapes),
        scratch_shapes=[pltpu.VMEM(s, F32) for s in scratch],
        compiler_params=pltpu.CompilerParams(vmem_limit_bytes=32 << 20),
        cost_estimate=pl.CostEstimate(flops=cost, bytes_accessed=1 << 20, transcendentals=0),
    )(*args)


def exchange(rows, height):
    return lax.all_to_all(
        rows.reshape(LANES, height, LANES), AXES, split_axis=0, concat_axis=0, tiled=True
    ).reshape(LANES * height, LANES)


def swap(x):
    return lax.ppermute(x, "coord", [(0, 1), (1, 0)])


def per_device(
    right_side, anchor, blocks, tile_nbr, cut_cells, cut_weight, pin_cell, pin_net, star_weight
):
    cut_cells, cut_weight = cut_cells[0], cut_weight[0]
    pin_cell, pin_net = pin_cell.reshape(32, LANES), pin_net.reshape(32, LANES)
    star, anchor = star_weight.reshape(LANES, LANES), anchor.reshape(TILES, LANES)
    coord = lax.axis_index("coord")
    place = jnp.stack([coord, lax.axis_index("region") * 2 + coord]).astype(I32)
    by_block = tile_nbr.T.reshape(1, 32)
    nbr_row, nbr_col = by_block, by_block.reshape(32, 1)

    send, state = call(
        first_kernel, [(512, LANES), (32, LANES)], [], 1 << 24, (right_side, cut_cells, pin_cell, pin_net)
    )
    parts = call(
        degree_kernel,
        [(16, LANES)],
        [(128, LANES), (96, LANES)],
        1 << 31,
        (cut_cells, cut_weight, pin_cell, pin_net, star, anchor),
    )[0]
    degree = old = None
    for iteration in range(ITERS):
        first, last = iteration == 0, iteration == ITERS - 1
        residual = state[0:32]
        got = exchange(send, 4)
        peer = swap(residual)
        rows = 48 if first else 32
        local_sum, forward, back = call(
            functools.partial(block_kernel, first),
            [(rows, LANES), (32, LANES), (rows, LANES)],
            [(128, LANES), (256, LANES), (128, LANES), (256, LANES)],
            1 << 31,
            (place, nbr_row, nbr_col, blocks, residual, peer),
            smem=1,
        )
        back = swap(back)
        args = (place, send, got, cut_weight, star, forward, state)
        if first:
            out, sums, degree = call(
                functools.partial(owner_kernel, True),
                [(128, LANES), (8, LANES), (16, LANES)],
                [(256, LANES)],
                1 << 26,
                args + (parts, local_sum, back),
                smem=1,
            )
        else:
            out, sums = call(
                functools.partial(owner_kernel, False),
                [(128, LANES), (8, LANES)],
                [(256, LANES)],
                1 << 26,
                args + (degree,),
                smem=1,
            )
        returned = exchange(out, 1)
        others = call(
            cut_kernel, [(32, LANES)], [], 1 << 31, (cut_cells, cut_weight, got, local_sum, back, sums)
        )[0]
        args = (pin_cell, returned, degree, others, sums, state)
        if not first:
            args = args + (old,)
        if last:
            shapes = [(2, TILES * LANES), (2, TILES * LANES)]
        else:
            args = args + (cut_cells, pin_net)
            shapes = [(512, LANES), (128, LANES), (8, LANES)]
        results = call(
            functools.partial(step_kernel, first, last), shapes, [(128, LANES)], 1 << 26, args
        )
        if last:
            return tuple(results)
        send, state, old = results


def solution(mesh):
    return jax.shard_map(
        per_device,
        mesh=mesh,
        in_specs=(
            P(None, AXES),
            P(AXES),
            P(AXES, None, None, None),
            P(AXES, None),
            P(AXES, None, None),
            P(AXES, None, None),
            P(AXES),
            P(AXES),
            P(),
        ),
        out_specs=(P(None, AXES), P(None, AXES)),
        check_vma=False,
    )
```

time: 1670 us -> 124 us (0.07)
  other arithmetic: 635 us -> 0.07 us
  waiting for transfers between devices: 402 us -> 44.6 us
  blocking collectives: 331 us -> 0 us
  local copies, waits for them, and re-layouts: 242 us -> 6.14 us
  Pallas kernels: 0 us -> 26.4 us
  starting transfers between devices: 21.3 us -> 45.3 us
    scatter-add x11 -> x0, other arithmetic: 632 us -> none  [the longest x3 264 us: per_device(): cut_part = jnp.zeros((2, cell_count), jnp.float32).at[:, send_cells.resha...]
    psum x3 -> x0, waiting for transfers between devices: 401 us -> none  [per_device(): lax.psum(jnp.zeros((2, net_count), jnp.float32).at[:, pin_net].add(direct...]
    psum x5 -> x0, blocking collectives: 320 us -> none  [the longest x3 192 us: squares(): lax.psum(jnp.sum(vectors * vectors, axis=1, keepdims=True), ('region', 'c...]
    gather x10 -> x0, local copies, waits for them, and re-layouts: 206 us -> none  [the longest x6 181 us: per_device(): outgoing = direction[:, send_cells]]
    all_to_all x3 -> x6, waiting for transfers between devices: 0.01 us -> 36 us  [exchange(): lax.all_to_all(rows.reshape(LANES, height, LANES), AXES, split_axis=0, co...]
    pallas_call x0 -> x14, Pallas kernels: none -> 26.4 us  [call(): pl.pallas_call(kernel, out_shape=[jax.ShapeDtypeStruct(s, F32) for s in s...]
    all_to_all x3 -> x6, starting transfers between devices: 21 us -> 40.7 us  [exchange(): lax.all_to_all(rows.reshape(LANES, height, LANES), AXES, split_axis=0, co...]
  transfers between devices with their start and end apart: 10 -> 12, of which waited for: 3 -> 10; matrix products, arithmetic and copies ran while one was open for 24% -> 1% of each run, Pallas kernels for 0% -> 13%
where the time goes in v1:
time: 124 us; the launch traced here: 123 us
  starting transfers between devices  45.3 us (37%)
  waiting for transfers between devices  44.6 us (36%)
  Pallas kernels  26.4 us (21%)
  local copies, waits for them, and re-layouts  6.14 us (5%)
    all_to_all x6, starting transfers between devices, exchange(): lax.all_to_all(rows.reshape(LANES, height, LANES), AXES, split_axis=0, co...  40.7 us
    all_to_all x6, waiting for transfers between devices, exchange(): lax.all_to_all(rows.reshape(LANES, height, LANES), AXES, split_axis=0, co...  36 us
    pallas_call x14, Pallas kernels, call(): pl.pallas_call(kernel, out_shape=[jax.ShapeDtypeStruct(s, F32) for s in s...  26.4 us
    ppermute x6, waiting for transfers between devices, swap(): return lax.ppermute(x, 'coord', [(0, 1), (1, 0)])  8.62 us
    unnamed x24, local copies, waits for them, and re-layouts  4.62 us
    ppermute x6, starting transfers between devices, swap(): return lax.ppermute(x, 'coord', [(0, 1), (1, 0)])  4.56 us
  transfers between devices with their start and end apart: 12, of which 10 were waited for; matrix products, arithmetic and copies ran while one was open for 1% of the time, Pallas kernels for 13%

profile of v1, /device:TPU:1, one launch (start us, length us, event | category | flops | bytes accessed | tf_op | source)
XLA Modules:
  0.0 123.4 jit_solution(2387977614870023190)
XLA Ops:
  0.6 0.0 copy-start.2
  0.6 0.8 copy-done.2
  1.5 0.0 copy-start.4
  1.5 0.7 copy-done.4
  2.2 0.0 copy-start.6
  2.2 0.7 copy-done.6
  2.9 0.0 copy-start.8
  2.9 0.7 copy-done.8
  3.6 1.9 %shard_map.104 = (f32[512,128]{1,0:T(8,128)}, f32[32,128]{1,0:T(8,128)S(1)}) custom-call(f32[2,2048]{1,0:T(2,128)S(1)} %copy-done.8, s32[128,128]{1,0:T(8,128)S(1)} %bitcast.44, s32[32,128]{1,0:T(8,128)S(1)} %bitcast.56, s32[32,128]{1,0:T(8,128)S(1)} %bitcast.52), custom_call_target="tpu_custom_call" | custom-call | flops 16777216 | bytes 1048576 | tf_op jit(solution)/shard_map/pallas_call | solution.py:330
  5.5 11.5 %all-to-all-start = ((f32[128,4,128]{2,1,0:T(4,128)}), f32[128,4,128]{2,1,0:T(4,128)S(1)}, u32[]{:S(2)}, u32[]{:S(2)}) async-start(f32[128,4,128]{2,1,0:T(4,128)} %bitcast.5), calls=%async_computation | async-start | bytes 524288 | tf_op jit(solution)/shard_map/all_to_all | solution.py:342
  17.0 1.5 %collective-permute-start = (f32[32,128]{1,0:T(8,128)S(1)}, f32[32,128]{1,0:T(8,128)S(1)}, u32[]{:S(2)}, u32[]{:S(2)}) collective-permute-start(f32[32,128]{1,0:T(8,128)S(1)} %get-tuple-element.27.own_ref.refs_6_.refs_0_), channel_id=1, source_target_pairs={{0,1},{1,0},{2,3},{3,2},{4,5},{5,4},{6,7},{7,6},{8,9},{9,8},{10,11... | collective-permute-start | bytes 49160 | tf_op jit(solution)/shard_map/ppermute | solution.py:348
  18.5 0.1 pad_add_fusion.place.refs_0_
  18.5 0.8 reshape.60.nbr_row
  19.3 0.8 reshape_reshape.4.nbr_col
  20.1 0.0 copy-start
  20.1 0.0 copy-start.1
  20.1 0.0 copy-start.3
  20.1 0.0 copy-start.5
  20.1 0.0 copy-start.7
  20.1 1.5 %collective-permute-done.peer_ref = f32[32,128]{1,0:T(8,128)S(1)} collective-permute-done((f32[32,128]{1,0:T(8,128)S(1)}, f32[32,128]{1,0:T(8,128)S(1)}, u32[]{:S(2)}, u32[]{:S(2)}) %collective-permute-start) | collective-permute-done | bytes 16416 | tf_op jit(solution)/shard_map/ppermute | solution.py:348
  21.6 0.0 copy-start.9
  21.6 1.6 %copy-done.9 = f32[16,2,128,128]{3,2,1,0:T(8,128)S(1)} copy-done((f32[16,2,128,128]{3,2,1,0:T(8,128)S(1)}, f32[16,2,128,128]{3,2,1,0:T(8,128)}, u32[]{:S(2)}) %copy-start.9) | copy-done | bytes 2097176
  23.2 1.7 %shard_map.105 = (f32[48,128]{1,0:T(8,128)S(1)}, f32[32,128]{1,0:T(8,128)S(1)}, f32[48,128]{1,0:T(8,128)S(1)}) custom-call(s32[2]{0:T(128)S(1)} %pad_add_fusion.place.refs_0_, s32[1,32]{1,0:T(1,128)S(1)} %reshape.60.nbr_row, s32[32,1]{1,0:T(8,128)S(1)} %reshape_reshape.4.nbr_col, f32[16,2,128,128]{3,2,1,0:T(8,128)S(1)} %copy-done.9, ...), custom_call_target="tpu_custom_call" | custom-call | flops 2147483648 | bytes 1048576 | tf_op jit(solution)/shard_map/pallas_call | solution.py:330
  25.0 0.1 collective-permute-start.1
  25.0 0.0 copy-done
  25.1 0.0 copy-done.1
  25.1 0.0 copy-done.3
  25.1 0.0 copy-done.5
  25.1 0.0 copy-done.7
  25.1 0.0 copy-done.11
  25.1 2.1 %shard_map.106.refs_7_ = f32[16,128]{1,0:T(8,128)S(1)} custom-call(s32[128,128]{1,0:T(8,128)S(1)} %bitcast.45, f32[128,128]{1,0:T(8,128)S(1)} %bitcast.37, s32[32,128]{1,0:T(8,128)S(1)} %bitcast.57, s32[32,128]{1,0:T(8,128)S(1)} %bitcast.53, f32[128,128]{1,0:T(8,128)S(1)} %bitcast.33, f32[16,128]{1,0:T(8,128)S(1)} %bitcast.63), custom_call_target="tpu_custom_call" | custom-call | flops 2147483648 | bytes 1048576 | tf_op jit(solution)/shard_map/pallas_call | solution.py:330
  27.3 0.8 collective-permute-done.1.refs_9_.back_ref
  28.0 0.6 all-to-all-done
  28.6 2.2 %shard_map.107 = (f32[128,128]{1,0:T(8,128)}, f32[8,128]{1,0:T(8,128)S(1)}, f32[16,128]{1,0:T(8,128)S(1)}) custom-call(s32[2]{0:T(128)S(1)} %pad_add_fusion.place.refs_0_, f32[512,128]{1,0:T(8,128)} %get-tuple-element.26.refs_1_, f32[512,128]{1,0:T(8,128)S(1)} %bitcast.27, f32[128,128]{1,0:T(8,128)S(1)} %bitcast.38, f32[128,128]{1,0:T(8,128)S(1)} %bitcast.34, ...), custom_call_target="tpu_custom_call" | custom-call | flops 67108864 | bytes 1048576 | tf_op jit(solution)/shard_map/pallas_call | solution.py:330
  30.8 10.1 %all-to-all-start.1 = ((f32[128,1,128]{2,1,0:T(1,128)}), f32[128,1,128]{2,1,0:T(1,128)S(1)}, u32[]{:S(2)}, u32[]{:S(2)}) async-start(f32[128,1,128]{2,1,0:T(1,128)} %bitcast.12), calls=%async_computation.1 | async-start | bytes 131072 | tf_op jit(solution)/shard_map/all_to_all | solution.py:342
  40.9 0.0 copy-start.10
  40.9 1.6 %shard_map.108.others = f32[32,128]{1,0:T(8,128)S(1)} custom-call(s32[128,128]{1,0:T(8,128)S(1)} %bitcast.46, f32[128,128]{1,0:T(8,128)S(1)} %bitcast.39, f32[512,128]{1,0:T(8,128)S(1)} %bitcast.28, f32[48,128]{1,0:T(8,128)S(1)} %get-tuple-element.29.refs_8_.local_ref, f32[48,128]{1,0:T(8,128)S(1)} %collective-permute-done.1.refs_9_.back_ref, ...), custom_call_target="tpu_custom_call" | custom-call | flops 2147483648 | bytes 1048576 | tf_op jit(solution)/shard_map/pallas_call | solution.py:330
  42.5 8.3 %all-to-all-done.1 = f32[128,1,128]{2,1,0:T(1,128)S(1)} async-done(((f32[128,1,128]{2,1,0:T(1,128)}), f32[128,1,128]{2,1,0:T(1,128)S(1)}, u32[]{:S(2)}, u32[]{:S(2)}) %all-to-all-start.1) | async-done | bytes 65568 | tf_op jit(solution)/shard_map/all_to_all | solution.py:342
  50.8 2.3 %shard_map.109 = (f32[512,128]{1,0:T(8,128)}, f32[128,128]{1,0:T(8,128)S(1)}, f32[8,128]{1,0:T(8,128)S(1)}) custom-call(s32[32,128]{1,0:T(8,128)S(1)} %bitcast.58, f32[128,128]{1,0:T(8,128)S(1)} %bitcast.62, f32[16,128]{1,0:T(8,128)S(1)} %get-tuple-element.32.degree_ref.refs_7_, f32[32,128]{1,0:T(8,128)S(1)} %shard_map.108.others, ...), custom_call_target="tpu_custom_call" | custom-call | flops 67108864 | bytes 1048576 | tf_op jit(solution)/shard_map/pallas_call | solution.py:330
  53.2 4.1 %all-to-all-start.2 = ((f32[128,4,128]{2,1,0:T(4,128)}), f32[128,4,128]{2,1,0:T(4,128)S(1)}, u32[]{:S(2)}, u32[]{:S(2)}) async-start(f32[128,4,128]{2,1,0:T(4,128)} %bitcast.14), calls=%async_computation.2 | async-start | bytes 524288 | tf_op jit(solution)/shard_map/all_to_all | solution.py:342
  57.3 1.5 %collective-permute-start.2 = (f32[32,128]{1,0:T(8,128)S(1)}, f32[32,128]{1,0:T(8,128)S(1)}, u32[]{:S(2)}, u32[]{:S(2)}) collective-permute-start(f32[32,128]{1,0:T(8,128)S(1)} %slice.6.own_ref), channel_id=1, source_target_pairs={{0,1},{1,0},{2,3},{3,2},{4,5},{5,4},{6,7},{7,6},{8,9},{9,8},{10,11... | collective-permute-start | bytes 49160 | tf_op jit(solution)/shard_map/ppermute | solution.py:348
  58.8 3.2 %collective-permute-done.2.peer_ref = f32[32,128]{1,0:T(8,128)S(1)} collective-permute-done((f32[32,128]{1,0:T(8,128)S(1)}, f32[32,128]{1,0:T(8,128)S(1)}, u32[]{:S(2)}, u32[]{:S(2)}) %collective-permute-start.2) | collective-permute-done | bytes 16416 | tf_op jit(solution)/shard_map/ppermute | solution.py:348
  62.0 0.0 copy-done.10
  62.0 1.7 %shard_map.110 = (f32[32,128]{1,0:T(8,128)S(1)}, f32[32,128]{1,0:T(8,128)S(1)}, f32[32,128]{1,0:T(8,128)S(1)}) custom-call(s32[2]{0:T(128)S(1)} %pad_add_fusion.place.refs_0_, s32[1,32]{1,0:T(1,128)S(1)} %reshape.60.nbr_row, s32[32,1]{1,0:T(8,128)S(1)} %reshape_reshape.4.nbr_col, f32[16,2,128,128]{3,2,1,0:T(8,128)S(1)} %copy-done.10, ...), custom_call_target="tpu_custom_call" | custom-call | flops 2147483648 | bytes 1048576 | tf_op jit(solution)/shard_map/pallas_call | solution.py:330
  63.7 0.0 collective-permute-start.3
  63.7 5.2 %all-to-all-done.2 = f32[128,4,128]{2,1,0:T(4,128)S(1)} async-done(((f32[128,4,128]{2,1,0:T(4,128)}), f32[128,4,128]{2,1,0:T(4,128)S(1)}, u32[]{:S(2)}, u32[]{:S(2)}) %all-to-all-start.2) | async-done | bytes 262176 | tf_op jit(solution)/shard_map/all_to_all | solution.py:342
  68.9 2.2 %shard_map.111 = (f32[128,128]{1,0:T(8,128)}, f32[8,128]{1,0:T(8,128)S(1)}) custom-call(s32[2]{0:T(128)S(1)} %pad_add_fusion.place.refs_0_, f32[512,128]{1,0:T(8,128)} %get-tuple-element.34.refs_1_, f32[512,128]{1,0:T(8,128)S(1)} %bitcast.31, f32[128,128]{1,0:T(8,128)S(1)} %bitcast.40, f32[128,128]{1,0:T(8,128)S(1)} %bitcast.35, ...), custom_call_target="tpu_custom_call" | custom-call | flops 67108864 | bytes 1048576 | tf_op jit(solution)/shard_map/pallas_call | solution.py:330
  71.2 5.4 %all-to-all-start.3 = ((f32[128,1,128]{2,1,0:T(1,128)}), f32[128,1,128]{2,1,0:T(1,128)S(1)}, u32[]{:S(2)}, u32[]{:S(2)}) async-start(f32[128,1,128]{2,1,0:T(1,128)} %bitcast.17), calls=%async_computation.3 | async-start | bytes 131072 | tf_op jit(solution)/shard_map/all_to_all | solution.py:342
  76.6 0.0 collective-permute-done.3.back_ref
  76.6 1.6 %shard_map.112.others = f32[32,128]{1,0:T(8,128)S(1)} custom-call(s32[128,128]{1,0:T(8,128)S(1)} %bitcast.48, f32[128,128]{1,0:T(8,128)S(1)} %bitcast.41, f32[512,128]{1,0:T(8,128)S(1)} %bitcast.32, f32[32,128]{1,0:T(8,128)S(1)} %get-tuple-element.38.local_ref, f32[32,128]{1,0:T(8,128)S(1)} %collective-permute-done.3.back_ref, ...), custom_call_target="tpu_custom_call" | custom-call | flops 2147483648 | bytes 1048576 | tf_op jit(solution)/shard_map/pallas_call | solution.py:330
  78.2 8.3 %all-to-all-done.3 = f32[128,1,128]{2,1,0:T(1,128)S(1)} async-done(((f32[128,1,128]{2,1,0:T(1,128)}), f32[128,1,128]{2,1,0:T(1,128)S(1)}, u32[]{:S(2)}, u32[]{:S(2)}) %all-to-all-start.3) | async-done | bytes 65568 | tf_op jit(solution)/shard_map/all_to_all | solution.py:342
  86.5 2.3 %shard_map.113 = (f32[512,128]{1,0:T(8,128)}, f32[128,128]{1,0:T(8,128)S(1)}, f32[8,128]{1,0:T(8,128)S(1)}) custom-call(s32[32,128]{1,0:T(8,128)S(1)} %bitcast.59, f32[128,128]{1,0:T(8,128)S(1)} %bitcast.51, f32[16,128]{1,0:T(8,128)S(1)} %get-tuple-element.32.degree_ref.refs_7_, f32[32,128]{1,0:T(8,128)S(1)} %shard_map.112.others, ...), custom_call_target="tpu_custom_call" | custom-call | flops 67108864 | bytes 1048576 | tf_op jit(solution)/shard_map/pallas_call | solution.py:330
  88.9 4.1 %all-to-all-start.4 = ((f32[128,4,128]{2,1,0:T(4,128)}), f32[128,4,128]{2,1,0:T(4,128)S(1)}, u32[]{:S(2)}, u32[]{:S(2)}) async-start(f32[128,4,128]{2,1,0:T(4,128)} %bitcast.19), calls=%async_computation.4 | async-start | bytes 524288 | tf_op jit(solution)/shard_map/all_to_all | solution.py:342
  93.0 1.5 %collective-permute-start.4 = (f32[32,128]{1,0:T(8,128)S(1)}, f32[32,128]{1,0:T(8,128)S(1)}, u32[]{:S(2)}, u32[]{:S(2)}) collective-permute-start(f32[32,128]{1,0:T(8,128)S(1)} %slice.7.own_ref), channel_id=1, source_target_pairs={{0,1},{1,0},{2,3},{3,2},{4,5},{5,4},{6,7},{7,6},{8,9},{9,8},{10,11... | collective-permute-start | bytes 49160 | tf_op jit(solution)/shard_map/ppermute | solution.py:348
  94.5 3.2 %collective-permute-done.4.peer_ref = f32[32,128]{1,0:T(8,128)S(1)} collective-permute-done((f32[32,128]{1,0:T(8,128)S(1)}, f32[32,128]{1,0:T(8,128)S(1)}, u32[]{:S(2)}, u32[]{:S(2)}) %collective-permute-start.4) | collective-permute-done | bytes 16416 | tf_op jit(solution)/shard_map/ppermute | solution.py:348
  97.7 1.7 %shard_map.114 = (f32[32,128]{1,0:T(8,128)S(1)}, f32[32,128]{1,0:T(8,128)S(1)}, f32[32,128]{1,0:T(8,128)S(1)}) custom-call(s32[2]{0:T(128)S(1)} %pad_add_fusion.place.refs_0_, s32[1,32]{1,0:T(1,128)S(1)} %reshape.60.nbr_row, s32[32,1]{1,0:T(8,128)S(1)} %reshape_reshape.4.nbr_col, f32[16,2,128,128]{3,2,1,0:T(8,128)S(1)} %copy-done.10, ...), custom_call_target="tpu_custom_call" | custom-call | flops 2147483648 | bytes 1048576 | tf_op jit(solution)/shard_map/pallas_call | solution.py:330
  99.4 0.0 collective-permute-start.5
  99.4 5.2 %all-to-all-done.4 = f32[128,4,128]{2,1,0:T(4,128)S(1)} async-done(((f32[128,4,128]{2,1,0:T(4,128)}), f32[128,4,128]{2,1,0:T(4,128)S(1)}, u32[]{:S(2)}, u32[]{:S(2)}) %all-to-all-start.4) | async-done | bytes 262176 | tf_op jit(solution)/shard_map/all_to_all | solution.py:342
  104.6 2.2 %shard_map.115 = (f32[128,128]{1,0:T(8,128)}, f32[8,128]{1,0:T(8,128)S(1)}) custom-call(s32[2]{0:T(128)S(1)} %pad_add_fusion.place.refs_0_, f32[512,128]{1,0:T(8,128)} %get-tuple-element.42.refs_1_, f32[512,128]{1,0:T(8,128)S(1)} %bitcast.29, f32[128,128]{1,0:T(8,128)S(1)} %bitcast.42, f32[128,128]{1,0:T(8,128)S(1)} %bitcast.36, ...), custom_call_target="tpu_custom_call" | custom-call | flops 67108864 | bytes 1048576 | tf_op jit(solution)/shard_map/pallas_call | solution.py:330
  106.9 5.4 %all-to-all-start.5 = ((f32[128,1,128]{2,1,0:T(1,128)}), f32[128,1,128]{2,1,0:T(1,128)S(1)}, u32[]{:S(2)}, u32[]{:S(2)}) async-start(f32[128,1,128]{2,1,0:T(1,128)} %bitcast.22), calls=%async_computation.5 | async-start | bytes 131072 | tf_op jit(solution)/shard_map/all_to_all | solution.py:342
  112.3 0.0 collective-permute-done.5.back_ref
  112.3 1.6 %shard_map.116.others = f32[32,128]{1,0:T(8,128)S(1)} custom-call(s32[128,128]{1,0:T(8,128)S(1)} %bitcast.50, f32[128,128]{1,0:T(8,128)S(1)} %bitcast.43, f32[512,128]{1,0:T(8,128)S(1)} %bitcast.30, f32[32,128]{1,0:T(8,128)S(1)} %get-tuple-element.46.local_ref, f32[32,128]{1,0:T(8,128)S(1)} %collective-permute-done.5.back_ref, ...), custom_call_target="tpu_custom_call" | custom-call | flops 2147483648 | bytes 1048576 | tf_op jit(solution)/shard_map/pallas_call | solution.py:330
  113.9 8.3 %all-to-all-done.5 = f32[128,1,128]{2,1,0:T(1,128)S(1)} async-done(((f32[128,1,128]{2,1,0:T(1,128)}), f32[128,1,128]{2,1,0:T(1,128)S(1)}, u32[]{:S(2)}, u32[]{:S(2)}) %all-to-all-start.5) | async-done | bytes 65568 | tf_op jit(solution)/shard_map/all_to_all | solution.py:342
  122.2 1.1 shard_map.117
  (3 shorter events, 0.0 us)
Async XLA Ops:
  0.6 0.8 copy-start.2
  1.5 0.7 copy-start.4
  2.2 0.7 copy-start.6
  2.9 0.7 copy-start.8
  5.5 23.1 %all-to-all-start = ((f32[128,4,128]{2,1,0:T(4,128)}), f32[128,4,128]{2,1,0:T(4,128)S(1)}, u32[]{:S(2)}, u32[]{:S(2)}) async-start(f32[128,4,128]{2,1,0:T(4,128)} %bitcast.5), calls=%async_computation | async-start | bytes 524288 | tf_op jit(solution)/shard_map/all_to_all | solution.py:342
  17.0 4.6 %collective-permute-start = (f32[32,128]{1,0:T(8,128)S(1)}, f32[32,128]{1,0:T(8,128)S(1)}, u32[]{:S(2)}, u32[]{:S(2)}) collective-permute-start(f32[32,128]{1,0:T(8,128)S(1)} %get-tuple-element.27.own_ref.refs_6_.refs_0_), channel_id=1, source_target_pairs={{0,1},{1,0},{2,3},{3,2},{4,5},{5,4},{6,7},{7,6},{8,9},{9,8},{10,11... | collective-permute-start | bytes 49160 | tf_op jit(solution)/shard_map/ppermute | solution.py:348
  20.1 5.0 %copy-start = (f32[16384]{0:T(1024)S(1)}, f32[16384]{0:T(1024)}, u32[]{:S(2)}) copy-start(f32[16384]{0:T(1024)} %param.17) | copy-start | bytes 196612
  20.1 5.0 %copy-start.1 = (f32[1,128,128]{2,1,0:T(8,128)S(1)}, f32[1,128,128]{2,1,0:T(8,128)}, u32[]{:S(2)}) copy-start(f32[1,128,128]{2,1,0:T(8,128)} %param.14) | copy-start | bytes 196612
  20.1 5.0 %copy-start.3 = (s32[1,128,128]{2,1,0:T(8,128)S(1)}, s32[1,128,128]{2,1,0:T(8,128)}, u32[]{:S(2)}) copy-start(s32[1,128,128]{2,1,0:T(8,128)} %param.13) | copy-start | bytes 196612
  20.1 5.0 %copy-start.5 = (s32[4096]{0:T(1024)S(1)}, s32[4096]{0:T(1024)}, u32[]{:S(2)}) copy-start(s32[4096]{0:T(1024)} %param.16) | copy-start | bytes 49156
  20.1 5.0 %copy-start.7 = (s32[4096]{0:T(1024)S(1)}, s32[4096]{0:T(1024)}, u32[]{:S(2)}) copy-start(s32[4096]{0:T(1024)} %param.15) | copy-start | bytes 49156
  21.6 1.6 %copy-start.9 = (f32[16,2,128,128]{3,2,1,0:T(8,128)S(1)}, f32[16,2,128,128]{3,2,1,0:T(8,128)}, u32[]{:S(2)}) copy-start(f32[16,2,128,128]{3,2,1,0:T(8,128)} %blocks.5) | copy-start | bytes 6291460
  23.2 1.9 %copy-start.11 = (f32[2048]{0:T(1024)S(1)}, f32[2048]{0:T(1024)}, u32[]{:S(2)}) copy-start(f32[2048]{0:T(1024)} %param.10) | copy-start | bytes 24580
  25.0 3.0 %collective-permute-start.1 = (f32[48,128]{1,0:T(8,128)S(1)}, f32[48,128]{1,0:T(8,128)S(1)}, u32[]{:S(2)}, u32[]{:S(2)}) collective-permute-start(f32[48,128]{1,0:T(8,128)S(1)} %get-tuple-element.30), channel_id=1, source_target_pairs={{0,1},{1,0},{2,3},{3,2},{4,5},{5,4},{6,7},{7,6},{8,9},{9,8},{10,11... | collective-permute-start | bytes 73736 | tf_op jit(solution)/shard_map/ppermute | solution.py:348
  30.8 20.0 %all-to-all-start.1 = ((f32[128,1,128]{2,1,0:T(1,128)}), f32[128,1,128]{2,1,0:T(1,128)S(1)}, u32[]{:S(2)}, u32[]{:S(2)}) async-start(f32[128,1,128]{2,1,0:T(1,128)} %bitcast.12), calls=%async_computation.1 | async-start | bytes 131072 | tf_op jit(solution)/shard_map/all_to_all | solution.py:342
  40.9 21.1 %copy-start.10 = (f32[16,2,128,128]{3,2,1,0:T(8,128)S(1)}, f32[16,2,128,128]{3,2,1,0:T(8,128)}, u32[]{:S(2)}) copy-start(f32[16,2,128,128]{3,2,1,0:T(8,128)} %blocks.5) | copy-start | bytes 6291460
  53.2 15.8 %all-to-all-start.2 = ((f32[128,4,128]{2,1,0:T(4,128)}), f32[128,4,128]{2,1,0:T(4,128)S(1)}, u32[]{:S(2)}, u32[]{:S(2)}) async-start(f32[128,4,128]{2,1,0:T(4,128)} %bitcast.14), calls=%async_computation.2 | async-start | bytes 524288 | tf_op jit(solution)/shard_map/all_to_all | solution.py:342
  57.3 4.6 %collective-permute-start.2 = (f32[32,128]{1,0:T(8,128)S(1)}, f32[32,128]{1,0:T(8,128)S(1)}, u32[]{:S(2)}, u32[]{:S(2)}) collective-permute-start(f32[32,128]{1,0:T(8,128)S(1)} %slice.6.own_ref), channel_id=1, source_target_pairs={{0,1},{1,0},{2,3},{3,2},{4,5},{5,4},{6,7},{7,6},{8,9},{9,8},{10,11... | collective-permute-start | bytes 49160 | tf_op jit(solution)/shard_map/ppermute | solution.py:348
  63.7 12.9 %collective-permute-start.3 = (f32[32,128]{1,0:T(8,128)S(1)}, f32[32,128]{1,0:T(8,128)S(1)}, u32[]{:S(2)}, u32[]{:S(2)}) collective-permute-start(f32[32,128]{1,0:T(8,128)S(1)} %get-tuple-element.39), channel_id=1, source_target_pairs={{0,1},{1,0},{2,3},{3,2},{4,5},{5,4},{6,7},{7,6},{8,9},{9,8},{10,11... | collective-permute-start | bytes 49160 | tf_op jit(solution)/shard_map/ppermute | solution.py:348
  71.2 15.4 %all-to-all-start.3 = ((f32[128,1,128]{2,1,0:T(1,128)}), f32[128,1,128]{2,1,0:T(1,128)S(1)}, u32[]{:S(2)}, u32[]{:S(2)}) async-start(f32[128,1,128]{2,1,0:T(1,128)} %bitcast.17), calls=%async_computation.3 | async-start | bytes 131072 | tf_op jit(solution)/shard_map/all_to_all | solution.py:342
  88.9 15.8 %all-to-all-start.4 = ((f32[128,4,128]{2,1,0:T(4,128)}), f32[128,4,128]{2,1,0:T(4,128)S(1)}, u32[]{:S(2)}, u32[]{:S(2)}) async-start(f32[128,4,128]{2,1,0:T(4,128)} %bitcast.19), calls=%async_computation.4 | async-start | bytes 524288 | tf_op jit(solution)/shard_map/all_to_all | solution.py:342
  93.0 4.6 %collective-permute-start.4 = (f32[32,128]{1,0:T(8,128)S(1)}, f32[32,128]{1,0:T(8,128)S(1)}, u32[]{:S(2)}, u32[]{:S(2)}) collective-permute-start(f32[32,128]{1,0:T(8,128)S(1)} %slice.7.own_ref), channel_id=1, source_target_pairs={{0,1},{1,0},{2,3},{3,2},{4,5},{5,4},{6,7},{7,6},{8,9},{9,8},{10,11... | collective-permute-start | bytes 49160 | tf_op jit(solution)/shard_map/ppermute | solution.py:348
  99.4 12.9 %collective-permute-start.5 = (f32[32,128]{1,0:T(8,128)S(1)}, f32[32,128]{1,0:T(8,128)S(1)}, u32[]{:S(2)}, u32[]{:S(2)}) collective-permute-start(f32[32,128]{1,0:T(8,128)S(1)} %get-tuple-element.47), channel_id=1, source_target_pairs={{0,1},{1,0},{2,3},{3,2},{4,5},{5,4},{6,7},{7,6},{8,9},{9,8},{10,11... | collective-permute-start | bytes 49160 | tf_op jit(solution)/shard_map/ppermute | solution.py:348
  106.9 15.4 %all-to-all-start.5 = ((f32[128,1,128]{2,1,0:T(1,128)}), f32[128,1,128]{2,1,0:T(1,128)S(1)}, u32[]{:S(2)}, u32[]{:S(2)}) async-start(f32[128,1,128]{2,1,0:T(1,128)} %bitcast.22), calls=%async_computation.5 | async-start | bytes 131072 | tf_op jit(solution)/shard_map/all_to_all | solution.py:342

commit v2 on v1

v2 whole, which is shorter than its diff:
```python
import functools

import jax
import jax.numpy as jnp
from jax import lax
from jax.experimental import pallas as pl
from jax.experimental.pallas import tpu as pltpu
from jax.sharding import PartitionSpec as P

FANOUT = 32
ITERS = 3
AXES = ("region", "coord")
LANES = 128
TILES = 16
F32 = jnp.float32
BF16 = jnp.bfloat16
I32 = jnp.int32
SUM_LANE = 96


def iota(shape, axis):
    return lax.broadcasted_iota(I32, shape, axis)


def split2(x):
    high = x.astype(BF16).astype(F32)
    return [high, (x - high).astype(BF16).astype(F32)]


def split3(x):
    high = x.astype(BF16).astype(F32)
    return [high] + split2(x - high)


def dot_nt(a, b):
    return lax.dot_general(a, b, (((1,), (1,)), ((), ())), preferred_element_type=F32)


def dot_nn(a, b):
    return lax.dot_general(a, b, (((1,), (0,)), ((), ())), preferred_element_type=F32)


def roll(x, shift):
    shift = shift % LANES
    return x if shift == 0 else pltpu.roll(x, shift, 1)


def total(x):
    return jnp.sum(jnp.sum(x, axis=0, keepdims=True), axis=1, keepdims=True)


def lane_value(row, lane):
    return jnp.sum(jnp.where(iota(row.shape, 1) == lane, row, 0.0), axis=1, keepdims=True)


def pick(tables, cells):
    low = cells & (LANES - 1)
    high = cells >> 7
    rows = [jnp.zeros(cells.shape, F32) for _ in tables]
    for tile in range(TILES):
        here = high == tile
        for v, table in enumerate(tables):
            wide = jnp.broadcast_to(table[tile], cells.shape)
            got = jnp.take_along_axis(wide, low, axis=1, mode="promise_in_bounds")
            rows[v] = jnp.where(here, got, rows[v])
    return rows


def one_hot(row, count):
    return jnp.where(iota((count, LANES), 0) == row, 1.0, 0.0).astype(BF16)


def add_rows(row_count, cell_row, value_rows):
    acc = None
    for j in range(0, row_count, 2):
        hots, masked = [], []
        for i in (j, j + 1):
            cells = cell_row(i)
            hots.append(one_hot(cells & (LANES - 1), LANES))
            here = iota((TILES, LANES), 0) == (cells >> 7)
            masked.append(
                jnp.concatenate([jnp.where(here, v, 0.0) for v in value_rows(i)], axis=0).astype(BF16)
            )
        part = dot_nt(jnp.concatenate(masked, axis=1), jnp.concatenate(hots, axis=1))
        acc = part if acc is None else acc + part
    return acc


def fold(acc, vectors, parts):
    size = vectors * TILES
    return sum(acc[i * size : (i + 1) * size] for i in range(parts))


def put_gathered(vectors, sums, cut_cells, pin_cell, pin_net, out_ref, kept_ref):
    lane = iota((32, LANES), 1)
    tail = jnp.zeros((1, LANES), F32)
    for i, s in enumerate(sums):
        tail = jnp.where(iota((1, LANES), 1) == SUM_LANE + i, s, tail)
    gx, gy = pick(vectors, pin_cell[...])
    net = (pin_net[...] & (LANES - 1)).astype(F32)
    for q in range(4):
        row = jnp.where(
            lane < 32,
            roll(gx, -32 * q),
            jnp.where(
                lane < 64,
                roll(gy, 32 - 32 * q),
                jnp.where(lane < 96, roll(net, 64 - 32 * q), tail),
            ),
        )
        out_ref[pl.ds(4 * q + 2, 32, stride=16), :] = row
        out_ref[pl.ds(4 * q + 3, 32, stride=16), :] = jnp.zeros((32, LANES), F32)
    for g in range(16):
        gx, gy = pick(vectors, cut_cells[pl.ds(8 * g, 8), :])
        out_ref[pl.ds(32 * g, 8, stride=4), :] = gx
        out_ref[pl.ds(32 * g + 1, 8, stride=4), :] = gy
        kept_ref[pl.ds(8 * g, 8), :] = gx
        kept_ref[pl.ds(128 + 8 * g, 8), :] = gy


def dense(rows, offset):
    lane = iota((32, LANES), 1)
    out = roll(rows[0], -offset)
    for q in range(1, 4):
        out = jnp.where(lane >= 32 * q, roll(rows[q], 32 * q - offset), out)
    return out


def first_kernel(right_hbm, cells_hbm, pin_cell_hbm, pin_net_hbm, send_ref, start_ref, kept_ref, right_ref, cut_cells, pin_cell, pin_net, sems):
    copies = [
        pltpu.make_async_copy(source, target, sems.at[i])
        for i, (source, target) in enumerate(
            (
                (right_hbm, right_ref),
                (pin_cell_hbm, pin_cell),
                (pin_net_hbm, pin_net),
                (cells_hbm, cut_cells),
            )
        )
    ]
    for copy in copies:
        copy.start()
    for copy in copies:
        copy.wait()
    tables = [
        [right_ref[v : v + 1, LANES * t : LANES * (t + 1)] for t in range(TILES)] for v in range(2)
    ]
    for v in range(2):
        for t in range(TILES):
            start_ref[TILES * v + t : TILES * v + t + 1, :] = tables[v][t]
    r = start_ref[...]
    sums = [total(r[16 * v : 16 * v + 16] * r[16 * v : 16 * v + 16]) for v in range(2)]
    put_gathered(tables, sums, cut_cells, pin_cell, pin_net, send_ref, kept_ref)


def block_kernel(first, place, own_ref, peer_ref, nbr, blocks, *refs):
    if first:
        (anchor, cut_weight, kept, local_ref, back_ref, share_ref, near, far, got_f, got_b, names, peers,
         *inner, sems) = refs
        copies = [
            pltpu.make_async_copy(source, target, sems.at[TILES + i])
            for i, (source, target) in enumerate(zip((nbr, anchor, cut_weight), inner))
        ]
        tiles = [
            pltpu.make_async_copy(blocks.at[t], inner[3].at[t], sems.at[t]) for t in range(TILES)
        ]
        for copy in copies + tiles:
            copy.start()
        nbr, anchor, cut_weight, blocks = inner
        for v in range(2):
            for t in range(TILES):
                peers[TILES * v + t : TILES * v + t + 1, :] = peer_ref[v : v + 1, LANES * t : LANES * (t + 1)]
        peer = peers[...]
    else:
        degree, local_ref, back_ref, share_ref, near, far, got_f, got_b, names = refs
        peer = peer_ref[...]
    own = own_ref[...]
    upper = place[0] == 1
    if first:
        for copy in copies:
            copy.wait()
    names[...] = jnp.zeros(names.shape, I32)
    for k in range(2):
        names[k : k + 1, 0:TILES] = nbr[k : k + 1, :]
    hot = [jnp.where(iota((128, LANES), 0) == names[k : k + 1, :], 1.0, 0.0) for k in range(2)]
    pick_rows = jnp.concatenate([h.T[:16] for h in hot], axis=0).astype(BF16)
    spread_rows = [h[:32].astype(BF16) for h in hot]
    near[...] = jnp.ones(near.shape, F32)
    far[...] = jnp.ones(far.shape, F32)
    zeros = jnp.zeros((96, LANES), F32)
    wholes = []
    for v in range(2):
        o, p = own[16 * v : 16 * v + 16], peer[16 * v : 16 * v + 16]
        whole = jnp.concatenate([jnp.where(upper, p, o), jnp.where(upper, o, p)], axis=0)
        wholes.append(whole)
        for i, (mine, part) in enumerate(zip(split2(o), split2(whole))):
            near[pl.ds(2 * i + v, 16, stride=8), :] = mine
            picked = dot_nn(pick_rows, jnp.concatenate([part, zeros], axis=0).astype(BF16))
            for k in range(2):
                far[pl.ds(128 * k + 2 * i + v, 16, stride=8), :] = picked[16 * k : 16 * k + 16]
    for t in range(TILES):
        if first:
            tiles[t].wait()
        pair = jnp.concatenate([blocks[t, 0], blocks[t, 1]], axis=1)
        high = pair.astype(BF16)
        low = (pair - high.astype(F32)).astype(BF16)
        a = near[8 * t : 8 * t + 8, :].astype(BF16)
        b = jnp.concatenate(
            [far[128 * k + 8 * t : 128 * k + 8 * t + 8, :] for k in range(2)], axis=1
        ).astype(BF16)
        back = dot_nn(a, high) + dot_nn(a, low)
        for k in range(2):
            got_b[128 * k + 8 * t : 128 * k + 8 * t + 8, :] = back[:, LANES * k : LANES * (k + 1)]
        got_f[8 * t : 8 * t + 8, :] = dot_nt(b, high) + dot_nt(b, low)
    filler = jnp.zeros((112, LANES), F32)
    ahead, whole_spread = [], []
    for v in range(3 if first else 2):
        def take(ref, at):
            if v == 2:
                return ref[pl.ds(at + 4, 16, stride=8), :]
            return ref[pl.ds(at + v, 16, stride=8), :] + ref[pl.ds(at + v + 2, 16, stride=8), :]

        forward = take(got_f, 0)
        spread = sum(
            dot_nn(spread_rows[k], jnp.concatenate([part, filler], axis=0).astype(BF16))
            for k in range(2)
            for part in split3(take(got_b, 128 * k))
        )
        ahead.append(forward)
        whole_spread.append(spread)
        lower, higher = spread[:16], spread[16:]
        local_ref[16 * v : 16 * v + 16, :] = forward + jnp.where(upper, higher, lower)
        back_ref[16 * v : 16 * v + 16, :] = jnp.where(upper, lower, higher)
    for v in range(2):
        r = own[16 * v : 16 * v + 16]
        if first:
            square = r * (r * (anchor[...] + ahead[2]) - 2.0 * ahead[v])
            line = jnp.sum(square, axis=0, keepdims=True)
            line = line + jnp.sum(wholes[v] * wholes[v] * whole_spread[2], axis=0, keepdims=True)
            cut = kept[128 * v : 128 * v + 128, :]
            line = line + jnp.sum(cut_weight[...] * cut * cut, axis=0, keepdims=True)
        else:
            line = jnp.sum(r * (r * degree[...] - 2.0 * ahead[v]), axis=0, keepdims=True)
        share_ref[v : v + 1, :] = line
    share_ref[2:8, :] = jnp.zeros((6, LANES), F32)


def owner_kernel(first, place, got, kept, cut_weight, star, share_ref, out_ref, sums_ref, rows):
    height = 16 if first else 8
    pin_rows = [got[pl.ds(4 * q + 2, 32, stride=16), :] for q in range(4)]
    sums = sum(jnp.sum(row, axis=0, keepdims=True) for row in pin_rows)
    sums_ref[...] = jnp.broadcast_to(sums, (8, LANES))
    nets = dense(pin_rows, 64).astype(I32)
    rows[...] = jnp.zeros(rows.shape, F32)
    for v in range(2):
        pins = dense(pin_rows, 32 * v)
        for i, part in enumerate(split3(pins)):
            rows[pl.ds(2 * i + v, 32, stride=height), :] = part
        if first:
            for i, part in enumerate(split3(pins * pins)):
                rows[pl.ds(8 + 2 * i + v, 32, stride=height), :] = part
    acc = None
    for j in range(0, 32, 2):
        hot = jnp.concatenate([one_hot(nets[i : i + 1], LANES) for i in (j, j + 1)], axis=1)
        left = jnp.concatenate(
            [rows[height * i : height * i + height, :] for i in (j, j + 1)], axis=1
        )
        part = dot_nt(left.astype(BF16), hot)
        acc = part if acc is None else acc + part
    weight = star[pl.ds(place[1], 1), :]
    totals = [acc[v : v + 1] + acc[v + 2 : v + 3] + acc[v + 4 : v + 5] for v in range(2)]
    centres = [weight * (1.0 / FANOUT) * t for t in totals]
    tail = jnp.zeros((1, LANES), F32)
    for v in range(2):
        line = share_ref[v : v + 1, :] - centres[v] * totals[v]
        if first:
            squares = acc[8 + v : 9 + v] + acc[10 + v : 11 + v] + acc[12 + v : 13 + v]
            line = line + weight * squares
        cut = cut_weight[...] * (kept[128 * v : 128 * v + 128, :] * got[pl.ds(v, 128, stride=4), :])
        line = line - jnp.sum(cut, axis=0, keepdims=True)
        tail = jnp.where(
            iota((1, LANES), 1) == SUM_LANE + v, jnp.sum(line, axis=1, keepdims=True), tail
        )
    lane = iota((8, LANES), 1)
    tables = [jnp.broadcast_to(c, (8, LANES)) for c in centres]
    for g in range(16):
        row = got[pl.ds(32 * g + 2, 8, stride=4), :]
        index = jnp.where(lane < 32, roll(row, -64), roll(row, -32)).astype(I32) & (LANES - 1)
        gx, gy = (
            jnp.take_along_axis(t, index, axis=1, mode="promise_in_bounds") for t in tables
        )
        out_ref[pl.ds(8 * g, 8), :] = jnp.where(
            lane < 32, gx, jnp.where(lane < 64, gy, jnp.where(lane < 96, 0.0, tail))
        )


def cut_kernel(first, cut_cells, cut_weight, got, local_ref, back_ref, sums_ref, *refs):
    del sums_ref

    def values(j):
        weight = cut_weight[j : j + 1, :]
        parts = [split2(weight * got[4 * j + v : 4 * j + v + 1, :]) for v in range(2)]
        moved = [parts[0][0], parts[1][0], parts[0][1], parts[1][1]]
        return moved + split3(weight) if first else moved

    acc = add_rows(128, lambda j: cut_cells[j : j + 1, :], values)
    if not first:
        (out_ref,) = refs
        out_ref[...] = fold(acc, 2, 2) + local_ref[...] + back_ref[...]
        return
    pin_cell, pin_net, star, anchor, out_ref, degree_ref, rows_ref, pins_ref = refs
    out_ref[...] = fold(acc[:64], 2, 2) + local_ref[0:32, :] + back_ref[0:32, :]
    net = pin_net[...] & (LANES - 1)
    for q in range(4):
        rows_ref[pl.ds(32 * q, 32), :] = jnp.take_along_axis(
            star[pl.ds(q, 32, stride=4), :], roll(net, -32 * q), axis=1, mode="promise_in_bounds"
        )
    weight = dense([rows_ref[pl.ds(32 * q, 32), :] for q in range(4)], 0)
    for i, part in enumerate(split3(weight)):
        pins_ref[pl.ds(32 * i, 32), :] = part
    pinned = add_rows(
        32,
        lambda j: pin_cell[j : j + 1, :],
        lambda j: [pins_ref[32 * i + j : 32 * i + j + 1, :] for i in range(3)],
    )
    degree_ref[...] = (
        anchor[...] + fold(acc[64:], 1, 3) + fold(pinned, 1, 3) + local_ref[32:48, :] + back_ref[32:48, :]
    )


def step_kernel(first, last, pin_cell, got, degree_ref, others, sums_ref, start_ref, *refs):
    refs = list(refs)
    state, old = (None, None) if first else (refs.pop(0), refs.pop(0))
    if last:
        positions_ref, residual_ref, pins = refs
    else:
        cut_cells, pin_net, send_ref, residual_ref, state_ref, old_ref, kept_ref, pins = refs
    pin_rows = [got[pl.ds(q, 32, stride=4), :] for q in range(4)]
    energy = sum(jnp.sum(row, axis=0, keepdims=True) for row in pin_rows)
    for v in range(2):
        for i, part in enumerate(split2(dense(pin_rows, 32 * v))):
            pins[pl.ds(32 * (2 * i + v), 32), :] = part
    acc = add_rows(
        32,
        lambda j: pin_cell[j : j + 1, :],
        lambda j: [pins[32 * i + j : 32 * i + j + 1, :] for i in range(4)],
    )
    removed = fold(acc, 2, 2) + others[...]
    degree = degree_ref[...]
    news, line = [], jnp.zeros((1, LANES), F32)
    lanes = iota((1, LANES), 1)
    sent_sums = [None] * 4
    for v in range(2):
        part = slice(16 * v, 16 * v + 16)
        r = start_ref[part, :]
        z = degree * r - removed[part]
        norm = lane_value(sums_ref[0:1, :], SUM_LANE + v)
        product = lane_value(energy, SUM_LANE + v)
        if first:
            p, q = r, z
        else:
            cross = lane_value(sums_ref[0:1, :], SUM_LANE + 2 + v)
            beta = norm / lane_value(old[0:1, :], v)
            product = product + beta * (2.0 * cross + beta * lane_value(old[0:1, :], 2 + v))
            p = r + beta * state[part, :]
            q = z + beta * state[32 + 16 * v : 48 + 16 * v, :]
        step = norm / product
        x = step * p
        if not first:
            x = x + state[64 + 16 * v : 80 + 16 * v, :]
        r = r - step * q
        if last:
            for t in range(TILES):
                positions_ref[v : v + 1, LANES * t : LANES * (t + 1)] = x[t : t + 1]
                residual_ref[v : v + 1, LANES * t : LANES * (t + 1)] = r[t : t + 1]
            continue
        residual_ref[part, :] = r
        for i, new in enumerate((p, q, x)):
            state_ref[32 * i + 16 * v : 32 * i + 16 * v + 16, :] = new
        news.append([r[t : t + 1] for t in range(TILES)])
        sent_sums[v], sent_sums[2 + v] = total(r * r), total(r * q)
        line = jnp.where(lanes == v, norm, jnp.where(lanes == 2 + v, product, line))
    if last:
        return
    old_ref[...] = jnp.broadcast_to(line, (8, LANES))
    put_gathered(news, sent_sums, cut_cells, pin_cell, pin_net, send_ref, kept_ref)


VMEM, SMEM, HBM = (pl.BlockSpec(memory_space=m) for m in (pltpu.VMEM, pltpu.SMEM, pltpu.HBM))


def call(kernel, shapes, scratch, cost, args, spaces=()):
    return pl.pallas_call(
        kernel,
        out_shape=[jax.ShapeDtypeStruct(s, F32) for s in shapes],
        in_specs=list(spaces) + [VMEM] * (len(args) - len(spaces)),
        out_specs=[VMEM] * len(shapes),
        scratch_shapes=[pltpu.VMEM(s, F32) if isinstance(s, tuple) else s for s in scratch],
        compiler_params=pltpu.CompilerParams(vmem_limit_bytes=32 << 20),
        cost_estimate=pl.CostEstimate(flops=cost, bytes_accessed=1 << 20, transcendentals=0),
    )(*args)


def stay(x):
    return pltpu.with_memory_space_constraint(x, pltpu.HBM)


def exchange(rows, height):
    return lax.all_to_all(
        rows.reshape(LANES, height, LANES), AXES, split_axis=0, concat_axis=0, tiled=True
    ).reshape(LANES * height, LANES)


def swap(x):
    return lax.ppermute(x, "coord", [(0, 1), (1, 0)])


def per_device(
    right_side, anchor, blocks, tile_nbr, cut_cells, cut_weight, pin_cell, pin_net, star_weight
):
    cut_cells, cut_weight = cut_cells[0], cut_weight[0]
    pin_cell, pin_net = pin_cell.reshape(32, LANES), pin_net.reshape(32, LANES)
    star, anchor = star_weight.reshape(LANES, LANES), anchor.reshape(TILES, LANES)
    coord = lax.axis_index("coord")
    place = jnp.stack([coord, lax.axis_index("region") * 2 + coord]).astype(I32)
    nbr = tile_nbr.T
    peer = swap(right_side)
    send, residual, kept = call(
        first_kernel,
        [(512, LANES), (32, LANES), (256, LANES)],
        [
            (2, TILES * LANES),
            pltpu.VMEM((128, LANES), I32),
            pltpu.VMEM((32, LANES), I32),
            pltpu.VMEM((32, LANES), I32),
            pltpu.SemaphoreType.DMA((4,)),
        ],
        1 << 24,
        tuple(stay(x) for x in (right_side, cut_cells, pin_cell, pin_net)),
        [HBM] * 4,
    )
    own_scratch = [
        (32, LANES),
        pltpu.VMEM((2, TILES), I32),
        (TILES, LANES),
        (LANES, LANES),
        (TILES, 2, LANES, LANES),
        pltpu.SemaphoreType.DMA((TILES + 3,)),
    ]
    for iteration in range(ITERS):
        first, last = iteration == 0, iteration == ITERS - 1
        got = exchange(send, 4)
        if not first:
            peer = swap(residual)
        rows = 48 if first else 32
        scratch = [(128, LANES), (256, LANES), (128, LANES), (256, LANES), pltpu.VMEM((8, LANES), I32)]
        local_sum, back, share = call(
            functools.partial(block_kernel, first),
            [(rows, LANES), (rows, LANES), (8, LANES)],
            scratch + own_scratch if first else scratch,
            1 << 31,
            (place, residual, peer)
            + (tuple(stay(x) for x in (nbr, blocks, anchor, cut_weight)) + (kept,) if first else (nbr, blocks, degree)),
            [SMEM, VMEM, VMEM] + [HBM] * 4 if first else [SMEM],
        )
        back = swap(back)
        out, sums = call(
            functools.partial(owner_kernel, first),
            [(128, LANES), (8, LANES)],
            [(512 if first else 256, LANES)],
            1 << 26,
            (place, got, kept, cut_weight, star, share),
            [SMEM],
        )
        returned = exchange(out, 1)
        args = (cut_cells, cut_weight, got, local_sum, back, sums)
        if first:
            others, degree = call(
                functools.partial(cut_kernel, True),
                [(32, LANES), (16, LANES)],
                [(128, LANES), (96, LANES)],
                1 << 31,
                args + (pin_cell, pin_net, star, anchor),
            )
        else:
            others = call(functools.partial(cut_kernel, False), [(32, LANES)], [], 1 << 31, args)[0]
        args = (pin_cell, returned, degree, others, sums, residual)
        if not first:
            args = args + (state, old)
        if last:
            shapes = [(2, TILES * LANES), (2, TILES * LANES)]
        else:
            args = args + (cut_cells, pin_net)
            shapes = [(512, LANES), (32, LANES), (96, LANES), (8, LANES), (256, LANES)]
        results = call(
            functools.partial(step_kernel, first, last), shapes, [(128, LANES)], 1 << 26, args
        )
        if last:
            return tuple(results)
        send, residual, state, old, kept = results


def solution(mesh):
    return jax.shard_map(
        per_device,
        mesh=mesh,
        in_specs=(
            P(None, AXES),
            P(AXES),
            P(AXES, None, None, None),
            P(AXES, None),
            P(AXES, None, None),
            P(AXES, None, None),
            P(AXES),
            P(AXES),
            P(),
        ),
        out_specs=(P(None, AXES), P(None, AXES)),
        check_vma=False,
    )
```

time: 124 us -> 117 us (0.944)
  local copies, waits for them, and re-layouts: 6.14 us -> 0.04 us
  starting transfers between devices: 45.3 us -> 41.7 us
  Pallas kernels: 26.4 us -> 28.3 us
    all_to_all x6, starting transfers between devices: 40.7 us -> 35.2 us  [exchange(): lax.all_to_all(rows.reshape(LANES, height, LANES), AXES, split_axis=0, co...]
    unnamed x24 -> x16, local copies, waits for them, and re-layouts: 4.62 us -> 0.04 us
    all_to_all x6, waiting for transfers between devices: 36 us -> 39.1 us  [exchange(): lax.all_to_all(rows.reshape(LANES, height, LANES), AXES, split_axis=0, co...]
    ppermute x6, waiting for transfers between devices: 8.62 us -> 6.37 us  [swap(): return lax.ppermute(x, 'coord', [(0, 1), (1, 0)])]
    ppermute x6, starting transfers between devices: 4.56 us -> 6.52 us  [swap(): return lax.ppermute(x, 'coord', [(0, 1), (1, 0)])]
    pallas_call x14 -> x13, Pallas kernels: 26.4 us -> 28.3 us  [call(): pl.pallas_call(kernel, out_shape=[jax.ShapeDtypeStruct(s, F32) for s in s...]
  transfers between devices with their start and end apart: 12 -> 12, of which waited for: 10 -> 8; matrix products, arithmetic and copies ran while one was open for 1% -> 0% of each run, Pallas kernels for 13% -> 19%
where the time goes in v2:
time: 117 us; the launch traced here: 116 us
  waiting for transfers between devices  45.5 us (39%)
  starting transfers between devices  41.7 us (36%)
  Pallas kernels  28.3 us (24%)
    all_to_all x6, waiting for transfers between devices, exchange(): lax.all_to_all(rows.reshape(LANES, height, LANES), AXES, split_axis=0, co...  39.1 us
    all_to_all x6, starting transfers between devices, exchange(): lax.all_to_all(rows.reshape(LANES, height, LANES), AXES, split_axis=0, co...  35.2 us
    pallas_call x13, Pallas kernels, call(): pl.pallas_call(kernel, out_shape=[jax.ShapeDtypeStruct(s, F32) for s in s...  28.3 us
    ppermute x6, starting transfers between devices, swap(): return lax.ppermute(x, 'coord', [(0, 1), (1, 0)])  6.52 us
    ppermute x6, waiting for transfers between devices, swap(): return lax.ppermute(x, 'coord', [(0, 1), (1, 0)])  6.37 us
  transfers between devices with their start and end apart: 12, of which 8 were waited for; matrix products, arithmetic and copies ran while one was open for 0% of the time, Pallas kernels for 19%

profile of v2, /device:TPU:1, one launch (start us, length us, event | category | flops | bytes accessed | tf_op | source)
XLA Modules:
  0.0 116.4 jit_solution(2066089128263721715)
XLA Ops:
  0.6 2.1 %collective-permute-start = (f32[2,2048]{1,0:T(2,128)}, f32[2,2048]{1,0:T(2,128)S(1)}, u32[]{:S(2)}, u32[]{:S(2)}) collective-permute-start(f32[2,2048]{1,0:T(2,128)} %right_hbm.1), channel_id=1, source_target_pairs={{0,1},{1,0},{2,3},{3,2},{4,5},{5,4},{6,7},{7,6},{8,9},{9,8},{10,11... | collective-permute-start | bytes 49160 | tf_op jit(solution)/shard_map/ppermute | solution.py:415
  2.7 2.8 %shard_map.104 = (f32[512,128]{1,0:T(8,128)}, f32[32,128]{1,0:T(8,128)S(1)}, f32[256,128]{1,0:T(8,128)S(1)}) custom-call(f32[2,2048]{1,0:T(2,128)} %right_hbm.1, s32[128,128]{1,0:T(8,128)} %bitcast.44, s32[32,128]{1,0:T(8,128)} %bitcast.55, s32[32,128]{1,0:T(8,128)} %bitcast.51), custom_call_target="tpu_custom_call" | custom-call | flops 16777216 | bytes 1048576 | tf_op jit(solution)/shard_map/pallas_call | solution.py:393
  5.5 10.7 %all-to-all-start = ((f32[128,4,128]{2,1,0:T(4,128)}), f32[128,4,128]{2,1,0:T(4,128)S(1)}, u32[]{:S(2)}, u32[]{:S(2)}) async-start(f32[128,4,128]{2,1,0:T(4,128)} %bitcast.5), calls=%async_computation | async-start | bytes 524288 | tf_op jit(solution)/shard_map/all_to_all | solution.py:409
  16.2 0.1 pad_add_fusion.place
  16.3 0.0 collective-permute-done.peer_ref
  16.3 0.0 copy-start
  16.3 0.0 copy-start.1
  16.3 0.0 copy-start.2
  16.3 0.0 copy-start.3
  16.3 0.0 copy-start.4
  16.3 0.0 copy-start.6
  16.3 5.5 %shard_map.105 = (f32[48,128]{1,0:T(8,128)S(1)}, f32[48,128]{1,0:T(8,128)S(1)}, f32[8,128]{1,0:T(8,128)S(1)}) custom-call(s32[2]{0:T(128)S(1)} %pad_add_fusion.place, f32[32,128]{1,0:T(8,128)S(1)} %get-tuple-element.34.own_ref.start_ref, f32[2,2048]{1,0:T(2,128)S(1)} %collective-permute-done.peer_ref, s32[2,16]{1,0:T(2,128)} %bitcast.64, ...), custom_call_target="tpu_custom_call" | custom-call | flops 2147483648 | bytes 1048576 | tf_op jit(solution)/shard_map/pallas_call | solution.py:393
  21.9 1.5 %collective-permute-start.1 = (f32[48,128]{1,0:T(8,128)S(1)}, f32[48,128]{1,0:T(8,128)S(1)}, u32[]{:S(2)}, u32[]{:S(2)}) collective-permute-start(f32[48,128]{1,0:T(8,128)S(1)} %get-tuple-element.38), channel_id=1, source_target_pairs={{0,1},{1,0},{2,3},{3,2},{4,5},{5,4},{6,7},{7,6},{8,9},{9,8},{10,11... | collective-permute-start | bytes 73736 | tf_op jit(solution)/shard_map/ppermute | solution.py:415
  23.3 4.3 %all-to-all-done = f32[128,4,128]{2,1,0:T(4,128)S(1)} async-done(((f32[128,4,128]{2,1,0:T(4,128)}), f32[128,4,128]{2,1,0:T(4,128)S(1)}, u32[]{:S(2)}, u32[]{:S(2)}) %all-to-all-start) | async-done | bytes 262176 | tf_op jit(solution)/shard_map/all_to_all | solution.py:409
  27.6 0.0 copy-done
  27.6 0.0 copy-done.1
  27.6 1.9 %shard_map.106 = (f32[128,128]{1,0:T(8,128)}, f32[8,128]{1,0:T(8,128)S(1)}) custom-call(s32[2]{0:T(128)S(1)} %pad_add_fusion.place, f32[512,128]{1,0:T(8,128)S(1)} %bitcast.27, f32[256,128]{1,0:T(8,128)S(1)} %get-tuple-element.33.refs_2_.kept, f32[128,128]{1,0:T(8,128)S(1)} %bitcast.38, f32[128,128]{1,0:T(8,128)S(1)} %bitcast.33, ...), custom_call_target="tpu_custom_call" | custom-call | flops 67108864 | bytes 1048576 | tf_op jit(solution)/shard_map/pallas_call | solution.py:393
  29.5 5.3 %all-to-all-start.1 = ((f32[128,1,128]{2,1,0:T(1,128)}), f32[128,1,128]{2,1,0:T(1,128)S(1)}, u32[]{:S(2)}, u32[]{:S(2)}) async-start(f32[128,1,128]{2,1,0:T(1,128)} %bitcast.12), calls=%async_computation.1 | async-start | bytes 131072 | tf_op jit(solution)/shard_map/all_to_all | solution.py:409
  34.8 0.0 collective-permute-done.1.back_ref
  34.8 0.0 copy-done.2
  34.8 0.0 copy-done.3
  34.8 0.0 copy-done.4
  34.8 0.0 copy-done.6
  34.8 0.0 copy-start.5
  34.8 0.0 copy-start.7
  34.9 2.0 %shard_map.107 = (f32[32,128]{1,0:T(8,128)S(1)}, f32[16,128]{1,0:T(8,128)S(1)}) custom-call(s32[128,128]{1,0:T(8,128)S(1)} %bitcast.45, f32[128,128]{1,0:T(8,128)S(1)} %bitcast.39, f32[512,128]{1,0:T(8,128)S(1)} %bitcast.28, f32[48,128]{1,0:T(8,128)S(1)} %get-tuple-element.37.local_ref, f32[48,128]{1,0:T(8,128)S(1)} %collective-permute-done.1.back_ref, ...), custom_call_target="tpu_custom_call" | custom-call | flops 2147483648 | bytes 1048576 | tf_op jit(solution)/shard_map/pallas_call | solution.py:393
  36.9 7.8 %all-to-all-done.1 = f32[128,1,128]{2,1,0:T(1,128)S(1)} async-done(((f32[128,1,128]{2,1,0:T(1,128)}), f32[128,1,128]{2,1,0:T(1,128)S(1)}, u32[]{:S(2)}, u32[]{:S(2)}) %all-to-all-start.1) | async-done | bytes 65568 | tf_op jit(solution)/shard_map/all_to_all | solution.py:409
  44.7 2.3 %shard_map.108 = (f32[512,128]{1,0:T(8,128)}, f32[32,128]{1,0:T(8,128)S(1)}, f32[96,128]{1,0:T(8,128)S(1)}, f32[8,128]{1,0:T(8,128)S(1)}, f32[256,128]{1,0:T(8,128)S(1)}) custom-call(s32[32,128]{1,0:T(8,128)S(1)} %bitcast.57, f32[128,128]{1,0:T(8,128)S(1)} %bitcast.60, f32[16,128]{1,0:T(8,128)S(1)} %get-tuple-element.40.degree_ref.refs_0_, ...), custom_call_target="tpu_custom_call" | custom-call | flops 67108864 | bytes 1048576 | tf_op jit(solution)/shard_map/pallas_call | solution.py:393
  47.0 4.1 %all-to-all-start.2 = ((f32[128,4,128]{2,1,0:T(4,128)}), f32[128,4,128]{2,1,0:T(4,128)S(1)}, u32[]{:S(2)}, u32[]{:S(2)}) async-start(f32[128,4,128]{2,1,0:T(4,128)} %bitcast.14), calls=%async_computation.2 | async-start | bytes 524288 | tf_op jit(solution)/shard_map/all_to_all | solution.py:409
  51.2 1.5 %collective-permute-start.2 = (f32[32,128]{1,0:T(8,128)S(1)}, f32[32,128]{1,0:T(8,128)S(1)}, u32[]{:S(2)}, u32[]{:S(2)}) collective-permute-start(f32[32,128]{1,0:T(8,128)S(1)} %get-tuple-element.44.own_ref.start_ref), channel_id=1, source_target_pairs={{0,1},{1,0},{2,3},{3,2},{4,5},{5,4},{6,7},{7,6},{8,9},{9,8},{10,11... | collective-permute-start | bytes 49160 | tf_op jit(solution)/shard_map/ppermute | solution.py:415
  52.6 3.2 %collective-permute-done.2.peer_ref = f32[32,128]{1,0:T(8,128)S(1)} collective-permute-done((f32[32,128]{1,0:T(8,128)S(1)}, f32[32,128]{1,0:T(8,128)S(1)}, u32[]{:S(2)}, u32[]{:S(2)}) %collective-permute-start.2) | collective-permute-done | bytes 16416 | tf_op jit(solution)/shard_map/ppermute | solution.py:415
  55.8 0.0 copy-done.5
  55.8 0.0 copy-done.7
  55.8 1.8 %shard_map.109 = (f32[32,128]{1,0:T(8,128)S(1)}, f32[32,128]{1,0:T(8,128)S(1)}, f32[8,128]{1,0:T(8,128)S(1)}) custom-call(s32[2]{0:T(128)S(1)} %pad_add_fusion.place, f32[32,128]{1,0:T(8,128)S(1)} %get-tuple-element.44.own_ref.start_ref, f32[32,128]{1,0:T(8,128)S(1)} %collective-permute-done.2.peer_ref, s32[2,16]{1,0:T(2,128)S(1)} %bitcast.65, ...), custom_call_target="tpu_custom_call" | custom-call | flops 2147483648 | bytes 1048576 | tf_op jit(solution)/shard_map/pallas_call | solution.py:393
  57.6 0.0 collective-permute-start.3
  57.6 5.2 %all-to-all-done.2 = f32[128,4,128]{2,1,0:T(4,128)S(1)} async-done(((f32[128,4,128]{2,1,0:T(4,128)}), f32[128,4,128]{2,1,0:T(4,128)S(1)}, u32[]{:S(2)}, u32[]{:S(2)}) %all-to-all-start.2) | async-done | bytes 262176 | tf_op jit(solution)/shard_map/all_to_all | solution.py:409
  62.8 1.8 %shard_map.110 = (f32[128,128]{1,0:T(8,128)}, f32[8,128]{1,0:T(8,128)S(1)}) custom-call(s32[2]{0:T(128)S(1)} %pad_add_fusion.place, f32[512,128]{1,0:T(8,128)S(1)} %bitcast.31, f32[256,128]{1,0:T(8,128)S(1)} %get-tuple-element.43.kept, f32[128,128]{1,0:T(8,128)S(1)} %bitcast.40, f32[128,128]{1,0:T(8,128)S(1)} %bitcast.35, ...), custom_call_target="tpu_custom_call" | custom-call | flops 67108864 | bytes 1048576 | tf_op jit(solution)/shard_map/pallas_call | solution.py:393
  64.6 5.5 %all-to-all-start.3 = ((f32[128,1,128]{2,1,0:T(1,128)}), f32[128,1,128]{2,1,0:T(1,128)S(1)}, u32[]{:S(2)}, u32[]{:S(2)}) async-start(f32[128,1,128]{2,1,0:T(1,128)} %bitcast.17), calls=%async_computation.3 | async-start | bytes 131072 | tf_op jit(solution)/shard_map/all_to_all | solution.py:409
  70.1 0.0 collective-permute-done.3.back_ref
  70.1 1.6 %shard_map.111.others = f32[32,128]{1,0:T(8,128)S(1)} custom-call(s32[128,128]{1,0:T(8,128)S(1)} %bitcast.47, f32[128,128]{1,0:T(8,128)S(1)} %bitcast.41, f32[512,128]{1,0:T(8,128)S(1)} %bitcast.32, f32[32,128]{1,0:T(8,128)S(1)} %get-tuple-element.47.local_ref, f32[32,128]{1,0:T(8,128)S(1)} %collective-permute-done.3.back_ref, ...), custom_call_target="tpu_custom_call" | custom-call | flops 2147483648 | bytes 1048576 | tf_op jit(solution)/shard_map/pallas_call | solution.py:393
  71.7 8.3 %all-to-all-done.3 = f32[128,1,128]{2,1,0:T(1,128)S(1)} async-done(((f32[128,1,128]{2,1,0:T(1,128)}), f32[128,1,128]{2,1,0:T(1,128)S(1)}, u32[]{:S(2)}, u32[]{:S(2)}) %all-to-all-start.3) | async-done | bytes 65568 | tf_op jit(solution)/shard_map/all_to_all | solution.py:409
  80.0 2.3 %shard_map.112 = (f32[512,128]{1,0:T(8,128)}, f32[32,128]{1,0:T(8,128)S(1)}, f32[96,128]{1,0:T(8,128)S(1)}, f32[8,128]{1,0:T(8,128)S(1)}, f32[256,128]{1,0:T(8,128)S(1)}) custom-call(s32[32,128]{1,0:T(8,128)S(1)} %bitcast.58, f32[128,128]{1,0:T(8,128)S(1)} %bitcast.50, f32[16,128]{1,0:T(8,128)S(1)} %get-tuple-element.40.degree_ref.refs_0_, ...), custom_call_target="tpu_custom_call" | custom-call | flops 67108864 | bytes 1048576 | tf_op jit(solution)/shard_map/pallas_call | solution.py:393
  82.3 4.1 %all-to-all-start.4 = ((f32[128,4,128]{2,1,0:T(4,128)}), f32[128,4,128]{2,1,0:T(4,128)S(1)}, u32[]{:S(2)}, u32[]{:S(2)}) async-start(f32[128,4,128]{2,1,0:T(4,128)} %bitcast.19), calls=%async_computation.4 | async-start | bytes 524288 | tf_op jit(solution)/shard_map/all_to_all | solution.py:409
  86.5 1.5 %collective-permute-start.4 = (f32[32,128]{1,0:T(8,128)S(1)}, f32[32,128]{1,0:T(8,128)S(1)}, u32[]{:S(2)}, u32[]{:S(2)}) collective-permute-start(f32[32,128]{1,0:T(8,128)S(1)} %get-tuple-element.54.own_ref.start_ref), channel_id=1, source_target_pairs={{0,1},{1,0},{2,3},{3,2},{4,5},{5,4},{6,7},{7,6},{8,9},{9,8},{10,11... | collective-permute-start | bytes 49160 | tf_op jit(solution)/shard_map/ppermute | solution.py:415
  87.9 3.2 %collective-permute-done.4.peer_ref = f32[32,128]{1,0:T(8,128)S(1)} collective-permute-done((f32[32,128]{1,0:T(8,128)S(1)}, f32[32,128]{1,0:T(8,128)S(1)}, u32[]{:S(2)}, u32[]{:S(2)}) %collective-permute-start.4) | collective-permute-done | bytes 16416 | tf_op jit(solution)/shard_map/ppermute | solution.py:415
  91.1 1.8 %shard_map.113 = (f32[32,128]{1,0:T(8,128)S(1)}, f32[32,128]{1,0:T(8,128)S(1)}, f32[8,128]{1,0:T(8,128)S(1)}) custom-call(s32[2]{0:T(128)S(1)} %pad_add_fusion.place, f32[32,128]{1,0:T(8,128)S(1)} %get-tuple-element.54.own_ref.start_ref, f32[32,128]{1,0:T(8,128)S(1)} %collective-permute-done.4.peer_ref, s32[2,16]{1,0:T(2,128)S(1)} %bitcast.66, ...), custom_call_target="tpu_custom_call" | custom-call | flops 2147483648 | bytes 1048576 | tf_op jit(solution)/shard_map/pallas_call | solution.py:393
  92.9 0.0 collective-permute-start.5
  92.9 5.2 %all-to-all-done.4 = f32[128,4,128]{2,1,0:T(4,128)S(1)} async-done(((f32[128,4,128]{2,1,0:T(4,128)}), f32[128,4,128]{2,1,0:T(4,128)S(1)}, u32[]{:S(2)}, u32[]{:S(2)}) %all-to-all-start.4) | async-done | bytes 262176 | tf_op jit(solution)/shard_map/all_to_all | solution.py:409
  98.1 1.8 %shard_map.114 = (f32[128,128]{1,0:T(8,128)}, f32[8,128]{1,0:T(8,128)S(1)}) custom-call(s32[2]{0:T(128)S(1)} %pad_add_fusion.place, f32[512,128]{1,0:T(8,128)S(1)} %bitcast.29, f32[256,128]{1,0:T(8,128)S(1)} %get-tuple-element.53.kept, f32[128,128]{1,0:T(8,128)S(1)} %bitcast.42, f32[128,128]{1,0:T(8,128)S(1)} %bitcast.36, ...), custom_call_target="tpu_custom_call" | custom-call | flops 67108864 | bytes 1048576 | tf_op jit(solution)/shard_map/pallas_call | solution.py:393
  99.9 5.5 %all-to-all-start.5 = ((f32[128,1,128]{2,1,0:T(1,128)}), f32[128,1,128]{2,1,0:T(1,128)S(1)}, u32[]{:S(2)}, u32[]{:S(2)}) async-start(f32[128,1,128]{2,1,0:T(1,128)} %bitcast.22), calls=%async_computation.5 | async-start | bytes 131072 | tf_op jit(solution)/shard_map/all_to_all | solution.py:409
  105.4 0.0 collective-permute-done.5.back_ref
  105.4 1.6 %shard_map.115.others = f32[32,128]{1,0:T(8,128)S(1)} custom-call(s32[128,128]{1,0:T(8,128)S(1)} %bitcast.49, f32[128,128]{1,0:T(8,128)S(1)} %bitcast.43, f32[512,128]{1,0:T(8,128)S(1)} %bitcast.30, f32[32,128]{1,0:T(8,128)S(1)} %get-tuple-element.57.local_ref, f32[32,128]{1,0:T(8,128)S(1)} %collective-permute-done.5.back_ref, ...), custom_call_target="tpu_custom_call" | custom-call | flops 2147483648 | bytes 1048576 | tf_op jit(solution)/shard_map/pallas_call | solution.py:393
  107.0 8.3 %all-to-all-done.5 = f32[128,1,128]{2,1,0:T(1,128)S(1)} async-done(((f32[128,1,128]{2,1,0:T(1,128)}), f32[128,1,128]{2,1,0:T(1,128)S(1)}, u32[]{:S(2)}, u32[]{:S(2)}) %all-to-all-start.5) | async-done | bytes 65568 | tf_op jit(solution)/shard_map/all_to_all | solution.py:409
  115.3 1.2 shard_map.116
Async XLA Ops:
  0.6 15.7 %collective-permute-start = (f32[2,2048]{1,0:T(2,128)}, f32[2,2048]{1,0:T(2,128)S(1)}, u32[]{:S(2)}, u32[]{:S(2)}) collective-permute-start(f32[2,2048]{1,0:T(2,128)} %right_hbm.1), channel_id=1, source_target_pairs={{0,1},{1,0},{2,3},{3,2},{4,5},{5,4},{6,7},{7,6},{8,9},{9,8},{10,11... | collective-permute-start | bytes 49160 | tf_op jit(solution)/shard_map/ppermute | solution.py:415
  5.5 22.1 %all-to-all-start = ((f32[128,4,128]{2,1,0:T(4,128)}), f32[128,4,128]{2,1,0:T(4,128)S(1)}, u32[]{:S(2)}, u32[]{:S(2)}) async-start(f32[128,4,128]{2,1,0:T(4,128)} %bitcast.5), calls=%async_computation | async-start | bytes 524288 | tf_op jit(solution)/shard_map/all_to_all | solution.py:409
  16.3 11.3 %copy-start = (f32[16384]{0:T(1024)S(1)}, f32[16384]{0:T(1024)}, u32[]{:S(2)}) copy-start(f32[16384]{0:T(1024)} %param.17) | copy-start | bytes 196612
  16.3 11.3 %copy-start.1 = (f32[1,128,128]{2,1,0:T(8,128)S(1)}, f32[1,128,128]{2,1,0:T(8,128)}, u32[]{:S(2)}) copy-start(f32[1,128,128]{2,1,0:T(8,128)} %param.14) | copy-start | bytes 196612
  16.3 18.5 %copy-start.2 = (s32[1,128,128]{2,1,0:T(8,128)S(1)}, s32[1,128,128]{2,1,0:T(8,128)}, u32[]{:S(2)}) copy-start(s32[1,128,128]{2,1,0:T(8,128)} %param.13) | copy-start | bytes 196612
  16.3 18.5 %copy-start.3 = (s32[4096]{0:T(1024)S(1)}, s32[4096]{0:T(1024)}, u32[]{:S(2)}) copy-start(s32[4096]{0:T(1024)} %param.16) | copy-start | bytes 49156
  16.3 18.5 %copy-start.4 = (s32[4096]{0:T(1024)S(1)}, s32[4096]{0:T(1024)}, u32[]{:S(2)}) copy-start(s32[4096]{0:T(1024)} %param.15) | copy-start | bytes 49156
  16.3 18.5 %copy-start.6 = (f32[2048]{0:T(1024)S(1)}, f32[2048]{0:T(1024)}, u32[]{:S(2)}) copy-start(f32[2048]{0:T(1024)} %param.10) | copy-start | bytes 24580
  21.9 12.9 %collective-permute-start.1 = (f32[48,128]{1,0:T(8,128)S(1)}, f32[48,128]{1,0:T(8,128)S(1)}, u32[]{:S(2)}, u32[]{:S(2)}) collective-permute-start(f32[48,128]{1,0:T(8,128)S(1)} %get-tuple-element.38), channel_id=1, source_target_pairs={{0,1},{1,0},{2,3},{3,2},{4,5},{5,4},{6,7},{7,6},{8,9},{9,8},{10,11... | collective-permute-start | bytes 73736 | tf_op jit(solution)/shard_map/ppermute | solution.py:415
  29.5 15.2 %all-to-all-start.1 = ((f32[128,1,128]{2,1,0:T(1,128)}), f32[128,1,128]{2,1,0:T(1,128)S(1)}, u32[]{:S(2)}, u32[]{:S(2)}) async-start(f32[128,1,128]{2,1,0:T(1,128)} %bitcast.12), calls=%async_computation.1 | async-start | bytes 131072 | tf_op jit(solution)/shard_map/all_to_all | solution.py:409
  34.8 21.0 %copy-start.5 = (f32[16,2,128,128]{3,2,1,0:T(8,128)S(1)}, f32[16,2,128,128]{3,2,1,0:T(8,128)}, u32[]{:S(2)}) copy-start(f32[16,2,128,128]{3,2,1,0:T(8,128)} %blocks.5) | copy-start | bytes 6291460
  34.8 21.0 %copy-start.7 = (s32[16,2]{0,1:T(2,128)S(1)}, s32[16,2]{0,1:T(2,128)}, u32[]{:S(2)}) copy-start(s32[16,2]{0,1:T(2,128)} %param.12) | copy-start | bytes 388
  47.0 15.7 %all-to-all-start.2 = ((f32[128,4,128]{2,1,0:T(4,128)}), f32[128,4,128]{2,1,0:T(4,128)S(1)}, u32[]{:S(2)}, u32[]{:S(2)}) async-start(f32[128,4,128]{2,1,0:T(4,128)} %bitcast.14), calls=%async_computation.2 | async-start | bytes 524288 | tf_op jit(solution)/shard_map/all_to_all | solution.py:409
  51.2 4.6 %collective-permute-start.2 = (f32[32,128]{1,0:T(8,128)S(1)}, f32[32,128]{1,0:T(8,128)S(1)}, u32[]{:S(2)}, u32[]{:S(2)}) collective-permute-start(f32[32,128]{1,0:T(8,128)S(1)} %get-tuple-element.44.own_ref.start_ref), channel_id=1, source_target_pairs={{0,1},{1,0},{2,3},{3,2},{4,5},{5,4},{6,7},{7,6},{8,9},{9,8},{10,11... | collective-permute-start | bytes 49160 | tf_op jit(solution)/shard_map/ppermute | solution.py:415
  57.6 12.5 %collective-permute-start.3 = (f32[32,128]{1,0:T(8,128)S(1)}, f32[32,128]{1,0:T(8,128)S(1)}, u32[]{:S(2)}, u32[]{:S(2)}) collective-permute-start(f32[32,128]{1,0:T(8,128)S(1)} %get-tuple-element.48), channel_id=1, source_target_pairs={{0,1},{1,0},{2,3},{3,2},{4,5},{5,4},{6,7},{7,6},{8,9},{9,8},{10,11... | collective-permute-start | bytes 49160 | tf_op jit(solution)/shard_map/ppermute | solution.py:415
  64.6 15.4 %all-to-all-start.3 = ((f32[128,1,128]{2,1,0:T(1,128)}), f32[128,1,128]{2,1,0:T(1,128)S(1)}, u32[]{:S(2)}, u32[]{:S(2)}) async-start(f32[128,1,128]{2,1,0:T(1,128)} %bitcast.17), calls=%async_computation.3 | async-start | bytes 131072 | tf_op jit(solution)/shard_map/all_to_all | solution.py:409
  82.3 15.7 %all-to-all-start.4 = ((f32[128,4,128]{2,1,0:T(4,128)}), f32[128,4,128]{2,1,0:T(4,128)S(1)}, u32[]{:S(2)}, u32[]{:S(2)}) async-start(f32[128,4,128]{2,1,0:T(4,128)} %bitcast.19), calls=%async_computation.4 | async-start | bytes 524288 | tf_op jit(solution)/shard_map/all_to_all | solution.py:409
  86.5 4.6 %collective-permute-start.4 = (f32[32,128]{1,0:T(8,128)S(1)}, f32[32,128]{1,0:T(8,128)S(1)}, u32[]{:S(2)}, u32[]{:S(2)}) collective-permute-start(f32[32,128]{1,0:T(8,128)S(1)} %get-tuple-element.54.own_ref.start_ref), channel_id=1, source_target_pairs={{0,1},{1,0},{2,3},{3,2},{4,5},{5,4},{6,7},{7,6},{8,9},{9,8},{10,11... | collective-permute-start | bytes 49160 | tf_op jit(solution)/shard_map/ppermute | solution.py:415
  92.9 12.5 %collective-permute-start.5 = (f32[32,128]{1,0:T(8,128)S(1)}, f32[32,128]{1,0:T(8,128)S(1)}, u32[]{:S(2)}, u32[]{:S(2)}) collective-permute-start(f32[32,128]{1,0:T(8,128)S(1)} %get-tuple-element.58), channel_id=1, source_target_pairs={{0,1},{1,0},{2,3},{3,2},{4,5},{5,4},{6,7},{7,6},{8,9},{9,8},{10,11... | collective-permute-start | bytes 49160 | tf_op jit(solution)/shard_map/ppermute | solution.py:415
  99.9 15.4 %all-to-all-start.5 = ((f32[128,1,128]{2,1,0:T(1,128)}), f32[128,1,128]{2,1,0:T(1,128)S(1)}, u32[]{:S(2)}, u32[]{:S(2)}) async-start(f32[128,1,128]{2,1,0:T(1,128)} %bitcast.22), calls=%async_computation.5 | async-start | bytes 131072 | tf_op jit(solution)/shard_map/all_to_all | solution.py:409

commit v3 on v2

--- a/solution.py
+++ b/solution.py
@@ -126,7 +126,9 @@
     return out
 
 
-def first_kernel(right_hbm, cells_hbm, pin_cell_hbm, pin_net_hbm, send_ref, start_ref, kept_ref, right_ref, cut_cells, pin_cell, pin_net, sems):
+def first_kernel(right_hbm, cells_hbm, pin_cell_hbm, pin_net_hbm, blocks_hbm, weight_hbm, anchor_hbm,
+                 send_ref, start_ref, kept_ref, blocks_ref, weight_ref, anchor_ref,
+                 right_ref, cut_cells, pin_cell, pin_net, sems):
     copies = [
         pltpu.make_async_copy(source, target, sems.at[i])
         for i, (source, target) in enumerate(
@@ -135,12 +137,15 @@
                 (pin_cell_hbm, pin_cell),
                 (pin_net_hbm, pin_net),
                 (cells_hbm, cut_cells),
+                (weight_hbm, weight_ref),
+                (anchor_hbm, anchor_ref),
+                (blocks_hbm, blocks_ref),
             )
         )
     ]
     for copy in copies:
         copy.start()
-    for copy in copies:
+    for copy in copies[:4]:
         copy.wait()
     tables = [
         [right_ref[v : v + 1, LANES * t : LANES * (t + 1)] for t in range(TILES)] for v in range(2)
@@ -151,22 +156,13 @@
     r = start_ref[...]
     sums = [total(r[16 * v : 16 * v + 16] * r[16 * v : 16 * v + 16]) for v in range(2)]
     put_gathered(tables, sums, cut_cells, pin_cell, pin_net, send_ref, kept_ref)
+    for copy in copies[4:]:
+        copy.wait()
 
 
 def block_kernel(first, place, own_ref, peer_ref, nbr, blocks, *refs):
     if first:
-        (anchor, cut_weight, kept, local_ref, back_ref, share_ref, near, far, got_f, got_b, names, peers,
-         *inner, sems) = refs
-        copies = [
-            pltpu.make_async_copy(source, target, sems.at[TILES + i])
-            for i, (source, target) in enumerate(zip((nbr, anchor, cut_weight), inner))
-        ]
-        tiles = [
-            pltpu.make_async_copy(blocks.at[t], inner[3].at[t], sems.at[t]) for t in range(TILES)
-        ]
-        for copy in copies + tiles:
-            copy.start()
-        nbr, anchor, cut_weight, blocks = inner
+        anchor, cut_weight, kept, local_ref, back_ref, share_ref, near, far, got_f, got_b, names, peers = refs
         for v in range(2):
             for t in range(TILES):
                 peers[TILES * v + t : TILES * v + t + 1, :] = peer_ref[v : v + 1, LANES * t : LANES * (t + 1)]
@@ -176,9 +172,6 @@
         peer = peer_ref[...]
     own = own_ref[...]
     upper = place[0] == 1
-    if first:
-        for copy in copies:
-            copy.wait()
     names[...] = jnp.zeros(names.shape, I32)
     for k in range(2):
         names[k : k + 1, 0:TILES] = nbr[k : k + 1, :]
@@ -199,8 +192,6 @@
             for k in range(2):
                 far[pl.ds(128 * k + 2 * i + v, 16, stride=8), :] = picked[16 * k : 16 * k + 16]
     for t in range(TILES):
-        if first:
-            tiles[t].wait()
         pair = jnp.concatenate([blocks[t, 0], blocks[t, 1]], axis=1)
         high = pair.astype(BF16)
         low = (pair - high.astype(F32)).astype(BF16)
@@ -425,28 +416,20 @@
     place = jnp.stack([coord, lax.axis_index("region") * 2 + coord]).astype(I32)
     nbr = tile_nbr.T
     peer = swap(right_side)
-    send, residual, kept = call(
+    send, residual, kept, blocks, cut_weight, anchor = call(
         first_kernel,
-        [(512, LANES), (32, LANES), (256, LANES)],
+        [(512, LANES), (32, LANES), (256, LANES), blocks.shape, (LANES, LANES), (TILES, LANES)],
         [
             (2, TILES * LANES),
             pltpu.VMEM((128, LANES), I32),
             pltpu.VMEM((32, LANES), I32),
             pltpu.VMEM((32, LANES), I32),
-            pltpu.SemaphoreType.DMA((4,)),
+            pltpu.SemaphoreType.DMA((7,)),
         ],
         1 << 24,
-        tuple(stay(x) for x in (right_side, cut_cells, pin_cell, pin_net)),
-        [HBM] * 4,
+        tuple(stay(x) for x in (right_side, cut_cells, pin_cell, pin_net, blocks, cut_weight, anchor)),
+        [HBM] * 7,
     )
-    own_scratch = [
-        (32, LANES),
-        pltpu.VMEM((2, TILES), I32),
-        (TILES, LANES),
-        (LANES, LANES),
-        (TILES, 2, LANES, LANES),
-        pltpu.SemaphoreType.DMA((TILES + 3,)),
-    ]
     for iteration in range(ITERS):
         first, last = iteration == 0, iteration == ITERS - 1
         got = exchange(send, 4)
@@ -457,11 +440,10 @@
         local_sum, back, share = call(
             functools.partial(block_kernel, first),
             [(rows, LANES), (rows, LANES), (8, LANES)],
-            scratch + own_scratch if first else scratch,
-            1 << 31,
-            (place, residual, peer)
-            + (tuple(stay(x) for x in (nbr, blocks, anchor, cut_weight)) + (kept,) if first else (nbr, blocks, degree)),
-            [SMEM, VMEM, VMEM] + [HBM] * 4 if first else [SMEM],
+            scratch + [(32, LANES)] if first else scratch,
+            1 << 32,
+            (place, residual, peer, nbr, blocks) + ((anchor, cut_weight, kept) if first else (degree,)),
+            [SMEM],
         )
         back = swap(back)
         out, sums = call(

time: 117 us -> 115 us (0.983)
  Pallas kernels: 28.3 us -> 24.7 us
  waiting for transfers between devices: 45.5 us -> 49 us
  starting transfers between devices: 41.7 us -> 39.7 us
    all_to_all x6, waiting for transfers between devices: 39.1 us -> 49 us  [exchange(): lax.all_to_all(rows.reshape(LANES, height, LANES), AXES, split_axis=0, co...]
    ppermute x6, waiting for transfers between devices: 6.37 us -> 0.02 us  [swap(): return lax.ppermute(x, 'coord', [(0, 1), (1, 0)])]
    pallas_call x13, Pallas kernels: 28.3 us -> 24.7 us  [call(): pl.pallas_call(kernel, out_shape=[jax.ShapeDtypeStruct(s, F32) for s in s...]
    all_to_all x6, starting transfers between devices: 35.2 us -> 32.7 us  [exchange(): lax.all_to_all(rows.reshape(LANES, height, LANES), AXES, split_axis=0, co...]
  transfers between devices with their start and end apart: 12 -> 12, of which waited for: 8 -> 6; matrix products, arithmetic and copies ran while one was open for 0% -> 0% of each run, Pallas kernels for 19% -> 17%
where the time goes in v3:
time: 115 us; the launch traced here: 114 us
  waiting for transfers between devices  49 us (43%)
  starting transfers between devices  39.7 us (35%)
  Pallas kernels  24.7 us (21%)
    all_to_all x6, waiting for transfers between devices, exchange(): lax.all_to_all(rows.reshape(LANES, height, LANES), AXES, split_axis=0, co...  49 us
    all_to_all x6, starting transfers between devices, exchange(): lax.all_to_all(rows.reshape(LANES, height, LANES), AXES, split_axis=0, co...  32.7 us
    pallas_call x13, Pallas kernels, call(): pl.pallas_call(kernel, out_shape=[jax.ShapeDtypeStruct(s, F32) for s in s...  24.7 us
    ppermute x6, starting transfers between devices, swap(): return lax.ppermute(x, 'coord', [(0, 1), (1, 0)])  6.98 us
  transfers between devices with their start and end apart: 12, of which 6 were waited for; matrix products, arithmetic and copies ran while one was open for 0% of the time, Pallas kernels for 17%

profile of v3, /device:TPU:1, one launch (start us, length us, event | category | flops | bytes accessed | tf_op | source)
XLA Modules:
  0.0 114.3 jit_solution(18277776876481954776)
XLA Ops:
  0.6 0.0 copy-start.4
  0.6 2.1 %collective-permute-start = (f32[2,2048]{1,0:T(2,128)}, f32[2,2048]{1,0:T(2,128)S(1)}, u32[]{:S(2)}, u32[]{:S(2)}) collective-permute-start(f32[2,2048]{1,0:T(2,128)} %right_hbm.1), channel_id=1, source_target_pairs={{0,1},{1,0},{2,3},{3,2},{4,5},{5,4},{6,7},{7,6},{8,9},{9,8},{10,11... | collective-permute-start | bytes 49160 | tf_op jit(solution)/shard_map/ppermute | solution.py:406
  2.8 2.8 %shard_map.104 = (f32[512,128]{1,0:T(8,128)}, f32[32,128]{1,0:T(8,128)S(1)}, f32[256,128]{1,0:T(8,128)S(1)}, f32[16,2,128,128]{3,2,1,0:T(8,128)S(1)}, f32[128,128]{1,0:T(8,128)S(1)}, /*index=5*/f32[16,128]{1,0:T(8,128)S(1)}) custom-call(f32[2,2048]{1,0:T(2,128)} %right_hbm.1, s32[128,128]{1,0:T(8,128)} %bitcast.37, s32[32,128]{1,0:T(8,128)} %bitcast.48, ...), custom_call_target="tpu_custom_call" | custom-call | flops 16777216 | bytes 1048576 | tf_op jit(solution)/shard_map/pallas_call | solution.py:384
  5.6 10.7 %all-to-all-start = ((f32[128,4,128]{2,1,0:T(4,128)}), f32[128,4,128]{2,1,0:T(4,128)S(1)}, u32[]{:S(2)}, u32[]{:S(2)}) async-start(f32[128,4,128]{2,1,0:T(4,128)} %bitcast.7), calls=%async_computation | async-start | bytes 524288 | tf_op jit(solution)/shard_map/all_to_all | solution.py:400
  16.3 0.1 pad_add_fusion.place
  16.3 0.0 collective-permute-done.peer_ref
  16.3 0.0 copy-done.4
  16.3 0.0 copy-start
  16.3 0.0 copy-start.1
  16.4 0.0 copy-start.2
  16.4 0.0 copy-start.3
  16.4 1.8 %shard_map.105 = (f32[48,128]{1,0:T(8,128)S(1)}, f32[48,128]{1,0:T(8,128)S(1)}, f32[8,128]{1,0:T(8,128)S(1)}) custom-call(s32[2]{0:T(128)S(1)} %pad_add_fusion.place, f32[32,128]{1,0:T(8,128)S(1)} %get-tuple-element.38.own_ref.start_ref, f32[2,2048]{1,0:T(2,128)S(1)} %collective-permute-done.peer_ref, s32[2,16]{1,0:T(2,128)S(1)} %bitcast.55, ...), custom_call_target="tpu_custom_call" | custom-call | flops 4294967296 | bytes 1048576 | tf_op jit(solution)/shard_map/pallas_call | solution.py:384
  18.2 1.5 %collective-permute-start.1 = (f32[48,128]{1,0:T(8,128)S(1)}, f32[48,128]{1,0:T(8,128)S(1)}, u32[]{:S(2)}, u32[]{:S(2)}) collective-permute-start(f32[48,128]{1,0:T(8,128)S(1)} %get-tuple-element.44), channel_id=1, source_target_pairs={{0,1},{1,0},{2,3},{3,2},{4,5},{5,4},{6,7},{7,6},{8,9},{9,8},{10,11... | collective-permute-start | bytes 73736 | tf_op jit(solution)/shard_map/ppermute | solution.py:406
  19.7 8.0 %all-to-all-done = f32[128,4,128]{2,1,0:T(4,128)S(1)} async-done(((f32[128,4,128]{2,1,0:T(4,128)}), f32[128,4,128]{2,1,0:T(4,128)S(1)}, u32[]{:S(2)}, u32[]{:S(2)}) %all-to-all-start) | async-done | bytes 262176 | tf_op jit(solution)/shard_map/all_to_all | solution.py:400
  27.7 0.0 copy-done
  27.7 1.9 %shard_map.106 = (f32[128,128]{1,0:T(8,128)}, f32[8,128]{1,0:T(8,128)S(1)}) custom-call(s32[2]{0:T(128)S(1)} %pad_add_fusion.place, f32[512,128]{1,0:T(8,128)S(1)} %bitcast.27, f32[256,128]{1,0:T(8,128)S(1)} %get-tuple-element.36.refs_2_.kept, f32[128,128]{1,0:T(8,128)S(1)} %get-tuple-element.37.refs_1_.cut_weight, f32[128,128]{1,0:T(8,128)S(1)} %bitcast.33, ...), custom_call_target="tpu_custom_call" | custom-call | flops 67108864 | bytes 1048576 | tf_op jit(solution)/shard_map/pallas_call | solution.py:384
  29.6 4.0 %all-to-all-start.1 = ((f32[128,1,128]{2,1,0:T(1,128)}), f32[128,1,128]{2,1,0:T(1,128)S(1)}, u32[]{:S(2)}, u32[]{:S(2)}) async-start(f32[128,1,128]{2,1,0:T(1,128)} %bitcast.12), calls=%async_computation.1 | async-start | bytes 131072 | tf_op jit(solution)/shard_map/all_to_all | solution.py:400
  33.6 0.0 collective-permute-done.1.back_ref
  33.6 0.0 copy-done.1
  33.6 0.0 copy-done.2
  33.6 0.0 copy-done.3
  33.6 2.0 %shard_map.107 = (f32[32,128]{1,0:T(8,128)S(1)}, f32[16,128]{1,0:T(8,128)S(1)}) custom-call(s32[128,128]{1,0:T(8,128)S(1)} %bitcast.38, f32[128,128]{1,0:T(8,128)S(1)} %get-tuple-element.37.refs_1_.cut_weight, f32[512,128]{1,0:T(8,128)S(1)} %bitcast.28, f32[48,128]{1,0:T(8,128)S(1)} %get-tuple-element.43.local_ref, ...), custom_call_target="tpu_custom_call" | custom-call | flops 2147483648 | bytes 1048576 | tf_op jit(solution)/shard_map/pallas_call | solution.py:384
  35.6 7.9 %all-to-all-done.1 = f32[128,1,128]{2,1,0:T(1,128)S(1)} async-done(((f32[128,1,128]{2,1,0:T(1,128)}), f32[128,1,128]{2,1,0:T(1,128)S(1)}, u32[]{:S(2)}, u32[]{:S(2)}) %all-to-all-start.1) | async-done | bytes 65568 | tf_op jit(solution)/shard_map/all_to_all | solution.py:400
  43.5 2.3 %shard_map.108 = (f32[512,128]{1,0:T(8,128)}, f32[32,128]{1,0:T(8,128)S(1)}, f32[96,128]{1,0:T(8,128)S(1)}, f32[8,128]{1,0:T(8,128)S(1)}, f32[256,128]{1,0:T(8,128)S(1)}) custom-call(s32[32,128]{1,0:T(8,128)S(1)} %bitcast.50, f32[128,128]{1,0:T(8,128)S(1)} %bitcast.53, f32[16,128]{1,0:T(8,128)S(1)} %get-tuple-element.46.degree_ref.refs_0_, ...), custom_call_target="tpu_custom_call" | custom-call | flops 67108864 | bytes 1048576 | tf_op jit(solution)/shard_map/pallas_call | solution.py:384
  45.9 0.3 collective-permute-start.2
  46.2 4.9 %all-to-all-start.2 = ((f32[128,4,128]{2,1,0:T(4,128)}), f32[128,4,128]{2,1,0:T(4,128)S(1)}, u32[]{:S(2)}, u32[]{:S(2)}) async-start(f32[128,4,128]{2,1,0:T(4,128)} %bitcast.14), calls=%async_computation.2 | async-start | bytes 524288 | tf_op jit(solution)/shard_map/all_to_all | solution.py:400
  51.1 0.0 collective-permute-done.2.peer_ref
  51.1 1.8 %shard_map.109 = (f32[32,128]{1,0:T(8,128)S(1)}, f32[32,128]{1,0:T(8,128)S(1)}, f32[8,128]{1,0:T(8,128)S(1)}) custom-call(s32[2]{0:T(128)S(1)} %pad_add_fusion.place, f32[32,128]{1,0:T(8,128)S(1)} %get-tuple-element.50.own_ref.start_ref, f32[32,128]{1,0:T(8,128)S(1)} %collective-permute-done.2.peer_ref, s32[2,16]{1,0:T(2,128)S(1)} %bitcast.56, ...), custom_call_target="tpu_custom_call" | custom-call | flops 4294967296 | bytes 1048576 | tf_op jit(solution)/shard_map/pallas_call | solution.py:384
  52.9 1.4 %collective-permute-start.3 = (f32[32,128]{1,0:T(8,128)S(1)}, f32[32,128]{1,0:T(8,128)S(1)}, u32[]{:S(2)}, u32[]{:S(2)}) collective-permute-start(f32[32,128]{1,0:T(8,128)S(1)} %get-tuple-element.54), channel_id=1, source_target_pairs={{0,1},{1,0},{2,3},{3,2},{4,5},{5,4},{6,7},{7,6},{8,9},{9,8},{10,11... | collective-permute-start | bytes 49160 | tf_op jit(solution)/shard_map/ppermute | solution.py:406
  54.3 8.2 %all-to-all-done.2 = f32[128,4,128]{2,1,0:T(4,128)S(1)} async-done(((f32[128,4,128]{2,1,0:T(4,128)}), f32[128,4,128]{2,1,0:T(4,128)S(1)}, u32[]{:S(2)}, u32[]{:S(2)}) %all-to-all-start.2) | async-done | bytes 262176 | tf_op jit(solution)/shard_map/all_to_all | solution.py:400
  62.5 1.8 %shard_map.110 = (f32[128,128]{1,0:T(8,128)}, f32[8,128]{1,0:T(8,128)S(1)}) custom-call(s32[2]{0:T(128)S(1)} %pad_add_fusion.place, f32[512,128]{1,0:T(8,128)S(1)} %bitcast.31, f32[256,128]{1,0:T(8,128)S(1)} %get-tuple-element.49.kept, f32[128,128]{1,0:T(8,128)S(1)} %get-tuple-element.37.refs_1_.cut_weight, f32[128,128]{1,0:T(8,128)S(1)} %bitcast.35, ...), custom_call_target="tpu_custom_call" | custom-call | flops 67108864 | bytes 1048576 | tf_op jit(solution)/shard_map/pallas_call | solution.py:384
  64.4 4.0 %all-to-all-start.3 = ((f32[128,1,128]{2,1,0:T(1,128)}), f32[128,1,128]{2,1,0:T(1,128)S(1)}, u32[]{:S(2)}, u32[]{:S(2)}) async-start(f32[128,1,128]{2,1,0:T(1,128)} %bitcast.17), calls=%async_computation.3 | async-start | bytes 131072 | tf_op jit(solution)/shard_map/all_to_all | solution.py:400
  68.4 0.0 collective-permute-done.3.back_ref
  68.4 1.6 %shard_map.111.others = f32[32,128]{1,0:T(8,128)S(1)} custom-call(s32[128,128]{1,0:T(8,128)S(1)} %bitcast.40, f32[128,128]{1,0:T(8,128)S(1)} %get-tuple-element.37.refs_1_.cut_weight, f32[512,128]{1,0:T(8,128)S(1)} %bitcast.32, f32[32,128]{1,0:T(8,128)S(1)} %get-tuple-element.53.local_ref, f32[32,128]{1,0:T(8,128)S(1)} %collective-permute-done.3.back_ref, ...), custom_call_target="tpu_custom_call" | custom-call | flops 2147483648 | bytes 1048576 | tf_op jit(solution)/shard_map/pallas_call | solution.py:384
  70.0 8.3 %all-to-all-done.3 = f32[128,1,128]{2,1,0:T(1,128)S(1)} async-done(((f32[128,1,128]{2,1,0:T(1,128)}), f32[128,1,128]{2,1,0:T(1,128)S(1)}, u32[]{:S(2)}, u32[]{:S(2)}) %all-to-all-start.3) | async-done | bytes 65568 | tf_op jit(solution)/shard_map/all_to_all | solution.py:400
  78.3 2.3 %shard_map.112 = (f32[512,128]{1,0:T(8,128)}, f32[32,128]{1,0:T(8,128)S(1)}, f32[96,128]{1,0:T(8,128)S(1)}, f32[8,128]{1,0:T(8,128)S(1)}, f32[256,128]{1,0:T(8,128)S(1)}) custom-call(s32[32,128]{1,0:T(8,128)S(1)} %bitcast.51, f32[128,128]{1,0:T(8,128)S(1)} %bitcast.43, f32[16,128]{1,0:T(8,128)S(1)} %get-tuple-element.46.degree_ref.refs_0_, ...), custom_call_target="tpu_custom_call" | custom-call | flops 67108864 | bytes 1048576 | tf_op jit(solution)/shard_map/pallas_call | solution.py:384
  80.7 0.3 collective-permute-start.4
  81.0 4.9 %all-to-all-start.4 = ((f32[128,4,128]{2,1,0:T(4,128)}), f32[128,4,128]{2,1,0:T(4,128)S(1)}, u32[]{:S(2)}, u32[]{:S(2)}) async-start(f32[128,4,128]{2,1,0:T(4,128)} %bitcast.19), calls=%async_computation.4 | async-start | bytes 524288 | tf_op jit(solution)/shard_map/all_to_all | solution.py:400
  85.9 0.0 collective-permute-done.4.peer_ref
  86.0 1.8 %shard_map.113 = (f32[32,128]{1,0:T(8,128)S(1)}, f32[32,128]{1,0:T(8,128)S(1)}, f32[8,128]{1,0:T(8,128)S(1)}) custom-call(s32[2]{0:T(128)S(1)} %pad_add_fusion.place, f32[32,128]{1,0:T(8,128)S(1)} %get-tuple-element.60.own_ref.start_ref, f32[32,128]{1,0:T(8,128)S(1)} %collective-permute-done.4.peer_ref, s32[2,16]{1,0:T(2,128)S(1)} %bitcast.57, ...), custom_call_target="tpu_custom_call" | custom-call | flops 4294967296 | bytes 1048576 | tf_op jit(solution)/shard_map/pallas_call | solution.py:384
  87.7 1.4 %collective-permute-start.5 = (f32[32,128]{1,0:T(8,128)S(1)}, f32[32,128]{1,0:T(8,128)S(1)}, u32[]{:S(2)}, u32[]{:S(2)}) collective-permute-start(f32[32,128]{1,0:T(8,128)S(1)} %get-tuple-element.64), channel_id=1, source_target_pairs={{0,1},{1,0},{2,3},{3,2},{4,5},{5,4},{6,7},{7,6},{8,9},{9,8},{10,11... | collective-permute-start | bytes 49160 | tf_op jit(solution)/shard_map/ppermute | solution.py:406
  89.1 8.2 %all-to-all-done.4 = f32[128,4,128]{2,1,0:T(4,128)S(1)} async-done(((f32[128,4,128]{2,1,0:T(4,128)}), f32[128,4,128]{2,1,0:T(4,128)S(1)}, u32[]{:S(2)}, u32[]{:S(2)}) %all-to-all-start.4) | async-done | bytes 262176 | tf_op jit(solution)/shard_map/all_to_all | solution.py:400
  97.4 1.8 %shard_map.114 = (f32[128,128]{1,0:T(8,128)}, f32[8,128]{1,0:T(8,128)S(1)}) custom-call(s32[2]{0:T(128)S(1)} %pad_add_fusion.place, f32[512,128]{1,0:T(8,128)S(1)} %bitcast.29, f32[256,128]{1,0:T(8,128)S(1)} %get-tuple-element.59.kept, f32[128,128]{1,0:T(8,128)S(1)} %get-tuple-element.37.refs_1_.cut_weight, f32[128,128]{1,0:T(8,128)S(1)} %bitcast.36, ...), custom_call_target="tpu_custom_call" | custom-call | flops 67108864 | bytes 1048576 | tf_op jit(solution)/shard_map/pallas_call | solution.py:384
  99.2 4.0 %all-to-all-start.5 = ((f32[128,1,128]{2,1,0:T(1,128)}), f32[128,1,128]{2,1,0:T(1,128)S(1)}, u32[]{:S(2)}, u32[]{:S(2)}) async-start(f32[128,1,128]{2,1,0:T(1,128)} %bitcast.22), calls=%async_computation.5 | async-start | bytes 131072 | tf_op jit(solution)/shard_map/all_to_all | solution.py:400
  103.3 0.0 collective-permute-done.5.back_ref
  103.3 1.6 %shard_map.115.others = f32[32,128]{1,0:T(8,128)S(1)} custom-call(s32[128,128]{1,0:T(8,128)S(1)} %bitcast.42, f32[128,128]{1,0:T(8,128)S(1)} %get-tuple-element.37.refs_1_.cut_weight, f32[512,128]{1,0:T(8,128)S(1)} %bitcast.30, f32[32,128]{1,0:T(8,128)S(1)} %get-tuple-element.63.local_ref, f32[32,128]{1,0:T(8,128)S(1)} %collective-permute-done.5.back_ref, ...), custom_call_target="tpu_custom_call" | custom-call | flops 2147483648 | bytes 1048576 | tf_op jit(solution)/shard_map/pallas_call | solution.py:384
  104.8 8.3 %all-to-all-done.5 = f32[128,1,128]{2,1,0:T(1,128)S(1)} async-done(((f32[128,1,128]{2,1,0:T(1,128)}), f32[128,1,128]{2,1,0:T(1,128)S(1)}, u32[]{:S(2)}, u32[]{:S(2)}) %all-to-all-start.5) | async-done | bytes 65568 | tf_op jit(solution)/shard_map/all_to_all | solution.py:400
  113.2 1.2 %shard_map.116 = (f32[2,2048]{1,0:T(2,128)}, f32[2,2048]{1,0:T(2,128)}) custom-call(s32[32,128]{1,0:T(8,128)S(1)} %bitcast.52, f32[128,128]{1,0:T(8,128)S(1)} %bitcast.54, f32[16,128]{1,0:T(8,128)S(1)} %get-tuple-element.46.degree_ref.refs_0_, f32[32,128]{1,0:T(8,128)S(1)} %shard_map.115.others, f32[8,128]{1,0:T(8,128)S(1)} %get-tuple-element.65.sums_ref, ...), custom_call_target="tpu_custom_call" | custom-call | flops 67108864 | bytes 1048576 | tf_op jit(solution)/shard_map/pallas_call | solution.py:384
Async XLA Ops:
  0.6 15.7 %copy-start.4 = (s32[16,2]{0,1:T(2,128)S(1)}, s32[16,2]{0,1:T(2,128)}, u32[]{:S(2)}) copy-start(s32[16,2]{0,1:T(2,128)} %param.12) | copy-start | bytes 388
  0.6 15.7 %collective-permute-start = (f32[2,2048]{1,0:T(2,128)}, f32[2,2048]{1,0:T(2,128)S(1)}, u32[]{:S(2)}, u32[]{:S(2)}) collective-permute-start(f32[2,2048]{1,0:T(2,128)} %right_hbm.1), channel_id=1, source_target_pairs={{0,1},{1,0},{2,3},{3,2},{4,5},{5,4},{6,7},{7,6},{8,9},{9,8},{10,11... | collective-permute-start | bytes 49160 | tf_op jit(solution)/shard_map/ppermute | solution.py:406
  5.6 22.1 %all-to-all-start = ((f32[128,4,128]{2,1,0:T(4,128)}), f32[128,4,128]{2,1,0:T(4,128)S(1)}, u32[]{:S(2)}, u32[]{:S(2)}) async-start(f32[128,4,128]{2,1,0:T(4,128)} %bitcast.7), calls=%async_computation | async-start | bytes 524288 | tf_op jit(solution)/shard_map/all_to_all | solution.py:400
  16.3 11.3 %copy-start = (f32[16384]{0:T(1024)S(1)}, f32[16384]{0:T(1024)}, u32[]{:S(2)}) copy-start(f32[16384]{0:T(1024)} %param.17) | copy-start | bytes 196612
  16.3 17.3 %copy-start.1 = (s32[1,128,128]{2,1,0:T(8,128)S(1)}, s32[1,128,128]{2,1,0:T(8,128)}, u32[]{:S(2)}) copy-start(s32[1,128,128]{2,1,0:T(8,128)} %param.13) | copy-start | bytes 196612
  16.4 17.3 %copy-start.2 = (s32[4096]{0:T(1024)S(1)}, s32[4096]{0:T(1024)}, u32[]{:S(2)}) copy-start(s32[4096]{0:T(1024)} %param.16) | copy-start | bytes 49156
  16.4 17.3 %copy-start.3 = (s32[4096]{0:T(1024)S(1)}, s32[4096]{0:T(1024)}, u32[]{:S(2)}) copy-start(s32[4096]{0:T(1024)} %param.15) | copy-start | bytes 49156
  18.2 15.4 %collective-permute-start.1 = (f32[48,128]{1,0:T(8,128)S(1)}, f32[48,128]{1,0:T(8,128)S(1)}, u32[]{:S(2)}, u32[]{:S(2)}) collective-permute-start(f32[48,128]{1,0:T(8,128)S(1)} %get-tuple-element.44), channel_id=1, source_target_pairs={{0,1},{1,0},{2,3},{3,2},{4,5},{5,4},{6,7},{7,6},{8,9},{9,8},{10,11... | collective-permute-start | bytes 73736 | tf_op jit(solution)/shard_map/ppermute | solution.py:406
  29.6 14.0 %all-to-all-start.1 = ((f32[128,1,128]{2,1,0:T(1,128)}), f32[128,1,128]{2,1,0:T(1,128)S(1)}, u32[]{:S(2)}, u32[]{:S(2)}) async-start(f32[128,1,128]{2,1,0:T(1,128)} %bitcast.12), calls=%async_computation.1 | async-start | bytes 131072 | tf_op jit(solution)/shard_map/all_to_all | solution.py:400
  45.9 5.3 %collective-permute-start.2 = (f32[32,128]{1,0:T(8,128)S(1)}, f32[32,128]{1,0:T(8,128)S(1)}, u32[]{:S(2)}, u32[]{:S(2)}) collective-permute-start(f32[32,128]{1,0:T(8,128)S(1)} %get-tuple-element.50.own_ref.start_ref), channel_id=1, source_target_pairs={{0,1},{1,0},{2,3},{3,2},{4,5},{5,4},{6,7},{7,6},{8,9},{9,8},{10,11... | collective-permute-start | bytes 49160 | tf_op jit(solution)/shard_map/ppermute | solution.py:406
  46.2 16.4 %all-to-all-start.2 = ((f32[128,4,128]{2,1,0:T(4,128)}), f32[128,4,128]{2,1,0:T(4,128)S(1)}, u32[]{:S(2)}, u32[]{:S(2)}) async-start(f32[128,4,128]{2,1,0:T(4,128)} %bitcast.14), calls=%async_computation.2 | async-start | bytes 524288 | tf_op jit(solution)/shard_map/all_to_all | solution.py:400
  52.9 15.5 %collective-permute-start.3 = (f32[32,128]{1,0:T(8,128)S(1)}, f32[32,128]{1,0:T(8,128)S(1)}, u32[]{:S(2)}, u32[]{:S(2)}) collective-permute-start(f32[32,128]{1,0:T(8,128)S(1)} %get-tuple-element.54), channel_id=1, source_target_pairs={{0,1},{1,0},{2,3},{3,2},{4,5},{5,4},{6,7},{7,6},{8,9},{9,8},{10,11... | collective-permute-start | bytes 49160 | tf_op jit(solution)/shard_map/ppermute | solution.py:406
  64.4 14.0 %all-to-all-start.3 = ((f32[128,1,128]{2,1,0:T(1,128)}), f32[128,1,128]{2,1,0:T(1,128)S(1)}, u32[]{:S(2)}, u32[]{:S(2)}) async-start(f32[128,1,128]{2,1,0:T(1,128)} %bitcast.17), calls=%async_computation.3 | async-start | bytes 131072 | tf_op jit(solution)/shard_map/all_to_all | solution.py:400
  80.7 5.3 %collective-permute-start.4 = (f32[32,128]{1,0:T(8,128)S(1)}, f32[32,128]{1,0:T(8,128)S(1)}, u32[]{:S(2)}, u32[]{:S(2)}) collective-permute-start(f32[32,128]{1,0:T(8,128)S(1)} %get-tuple-element.60.own_ref.start_ref), channel_id=1, source_target_pairs={{0,1},{1,0},{2,3},{3,2},{4,5},{5,4},{6,7},{7,6},{8,9},{9,8},{10,11... | collective-permute-start | bytes 49160 | tf_op jit(solution)/shard_map/ppermute | solution.py:406
  81.0 16.4 %all-to-all-start.4 = ((f32[128,4,128]{2,1,0:T(4,128)}), f32[128,4,128]{2,1,0:T(4,128)S(1)}, u32[]{:S(2)}, u32[]{:S(2)}) async-start(f32[128,4,128]{2,1,0:T(4,128)} %bitcast.19), calls=%async_computation.4 | async-start | bytes 524288 | tf_op jit(solution)/shard_map/all_to_all | solution.py:400
  87.7 15.5 %collective-permute-start.5 = (f32[32,128]{1,0:T(8,128)S(1)}, f32[32,128]{1,0:T(8,128)S(1)}, u32[]{:S(2)}, u32[]{:S(2)}) collective-permute-start(f32[32,128]{1,0:T(8,128)S(1)} %get-tuple-element.64), channel_id=1, source_target_pairs={{0,1},{1,0},{2,3},{3,2},{4,5},{5,4},{6,7},{7,6},{8,9},{9,8},{10,11... | collective-permute-start | bytes 49160 | tf_op jit(solution)/shard_map/ppermute | solution.py:406
  99.2 14.0 %all-to-all-start.5 = ((f32[128,1,128]{2,1,0:T(1,128)}), f32[128,1,128]{2,1,0:T(1,128)S(1)}, u32[]{:S(2)}, u32[]{:S(2)}) async-start(f32[128,1,128]{2,1,0:T(1,128)} %bitcast.22), calls=%async_computation.5 | async-start | bytes 131072 | tf_op jit(solution)/shard_map/all_to_all | solution.py:400

commit v4 on v3

--- a/solution.py
+++ b/solution.py
@@ -96,7 +96,8 @@
     tail = jnp.zeros((1, LANES), F32)
     for i, s in enumerate(sums):
         tail = jnp.where(iota((1, LANES), 1) == SUM_LANE + i, s, tail)
-    gx, gy = pick(vectors, pin_cell[...])
+    groups = [pick(vectors, pin_cell[8 * h : 8 * h + 8, :]) for h in range(4)]
+    gx, gy = (jnp.concatenate([g[v] for g in groups], axis=0) for v in range(2))
     net = (pin_net[...] & (LANES - 1)).astype(F32)
     for q in range(4):
         row = jnp.where(
@@ -108,12 +109,11 @@
                 jnp.where(lane < 96, roll(net, 64 - 32 * q), tail),
             ),
         )
-        out_ref[pl.ds(4 * q + 2, 32, stride=16), :] = row
-        out_ref[pl.ds(4 * q + 3, 32, stride=16), :] = jnp.zeros((32, LANES), F32)
+        out_ref[pl.ds(3 * q + 2, 32, stride=12), :] = row
     for g in range(16):
         gx, gy = pick(vectors, cut_cells[pl.ds(8 * g, 8), :])
-        out_ref[pl.ds(32 * g, 8, stride=4), :] = gx
-        out_ref[pl.ds(32 * g + 1, 8, stride=4), :] = gy
+        out_ref[pl.ds(24 * g, 8, stride=3), :] = gx
+        out_ref[pl.ds(24 * g + 1, 8, stride=3), :] = gy
         kept_ref[pl.ds(8 * g, 8), :] = gx
         kept_ref[pl.ds(128 + 8 * g, 8), :] = gy
 
@@ -162,7 +162,9 @@
 
 def block_kernel(first, place, own_ref, peer_ref, nbr, blocks, *refs):
     if first:
-        anchor, cut_weight, kept, local_ref, back_ref, share_ref, near, far, got_f, got_b, names, peers = refs
+        (anchor, cut_weight, kept, star, local_ref, back_ref, share_ref, net_weight_ref,
+         near, far, got_f, got_b, names, peers) = refs
+        net_weight_ref[...] = jnp.broadcast_to(star[pl.ds(place[1], 1), :], (8, LANES))
         for v in range(2):
             for t in range(TILES):
                 peers[TILES * v + t : TILES * v + t + 1, :] = peer_ref[v : v + 1, LANES * t : LANES * (t + 1)]
@@ -236,9 +238,9 @@
     share_ref[2:8, :] = jnp.zeros((6, LANES), F32)
 
 
-def owner_kernel(first, place, got, kept, cut_weight, star, share_ref, out_ref, sums_ref, rows):
+def owner_kernel(first, got, kept, cut_weight, net_weight, share_ref, out_ref, sums_ref, rows):
     height = 16 if first else 8
-    pin_rows = [got[pl.ds(4 * q + 2, 32, stride=16), :] for q in range(4)]
+    pin_rows = [got[pl.ds(3 * q + 2, 32, stride=12), :] for q in range(4)]
     sums = sum(jnp.sum(row, axis=0, keepdims=True) for row in pin_rows)
     sums_ref[...] = jnp.broadcast_to(sums, (8, LANES))
     nets = dense(pin_rows, 64).astype(I32)
@@ -258,7 +260,7 @@
         )
         part = dot_nt(left.astype(BF16), hot)
         acc = part if acc is None else acc + part
-    weight = star[pl.ds(place[1], 1), :]
+    weight = net_weight[0:1, :]
     totals = [acc[v : v + 1] + acc[v + 2 : v + 3] + acc[v + 4 : v + 5] for v in range(2)]
     centres = [weight * (1.0 / FANOUT) * t for t in totals]
     tail = jnp.zeros((1, LANES), F32)
@@ -267,7 +269,7 @@
         if first:
             squares = acc[8 + v : 9 + v] + acc[10 + v : 11 + v] + acc[12 + v : 13 + v]
             line = line + weight * squares
-        cut = cut_weight[...] * (kept[128 * v : 128 * v + 128, :] * got[pl.ds(v, 128, stride=4), :])
+        cut = cut_weight[...] * (kept[128 * v : 128 * v + 128, :] * got[pl.ds(v, 128, stride=3), :])
         line = line - jnp.sum(cut, axis=0, keepdims=True)
         tail = jnp.where(
             iota((1, LANES), 1) == SUM_LANE + v, jnp.sum(line, axis=1, keepdims=True), tail
@@ -275,7 +277,7 @@
     lane = iota((8, LANES), 1)
     tables = [jnp.broadcast_to(c, (8, LANES)) for c in centres]
     for g in range(16):
-        row = got[pl.ds(32 * g + 2, 8, stride=4), :]
+        row = got[pl.ds(24 * g + 2, 8, stride=3), :]
         index = jnp.where(lane < 32, roll(row, -64), roll(row, -32)).astype(I32) & (LANES - 1)
         gx, gy = (
             jnp.take_along_axis(t, index, axis=1, mode="promise_in_bounds") for t in tables
@@ -290,7 +292,7 @@
 
     def values(j):
         weight = cut_weight[j : j + 1, :]
-        parts = [split2(weight * got[4 * j + v : 4 * j + v + 1, :]) for v in range(2)]
+        parts = [split2(weight * got[3 * j + v : 3 * j + v + 1, :]) for v in range(2)]
         moved = [parts[0][0], parts[1][0], parts[0][1], parts[1][1]]
         return moved + split3(weight) if first else moved
 
@@ -398,7 +400,7 @@
 
 def exchange(rows, height):
     return lax.all_to_all(
-        rows.reshape(LANES, height, LANES), AXES, split_axis=0, concat_axis=0, tiled=True
+        rows.reshape(LANES, 1, height * LANES), AXES, split_axis=0, concat_axis=0, tiled=True
     ).reshape(LANES * height, LANES)
 
 
@@ -418,7 +420,7 @@
     peer = swap(right_side)
     send, residual, kept, blocks, cut_weight, anchor = call(
         first_kernel,
-        [(512, LANES), (32, LANES), (256, LANES), blocks.shape, (LANES, LANES), (TILES, LANES)],
+        [(384, LANES), (32, LANES), (256, LANES), blocks.shape, (LANES, LANES), (TILES, LANES)],
         [
             (2, TILES * LANES),
             pltpu.VMEM((128, LANES), I32),
@@ -432,27 +434,28 @@
     )
     for iteration in range(ITERS):
         first, last = iteration == 0, iteration == ITERS - 1
-        got = exchange(send, 4)
+        got = exchange(send, 3)
         if not first:
             peer = swap(residual)
         rows = 48 if first else 32
         scratch = [(128, LANES), (256, LANES), (128, LANES), (256, LANES), pltpu.VMEM((8, LANES), I32)]
-        local_sum, back, share = call(
+        local_sum, back, share, *more = call(
             functools.partial(block_kernel, first),
-            [(rows, LANES), (rows, LANES), (8, LANES)],
+            [(rows, LANES), (rows, LANES), (8, LANES)] + [(8, LANES)] * first,
             scratch + [(32, LANES)] if first else scratch,
             1 << 32,
-            (place, residual, peer, nbr, blocks) + ((anchor, cut_weight, kept) if first else (degree,)),
+            (place, residual, peer, nbr, blocks) + ((anchor, cut_weight, kept, star) if first else (degree,)),
             [SMEM],
         )
         back = swap(back)
+        if first:
+            net_weight = more[0]
         out, sums = call(
             functools.partial(owner_kernel, first),
             [(128, LANES), (8, LANES)],
             [(512 if first else 256, LANES)],
             1 << 26,
-            (place, got, kept, cut_weight, star, share),
-            [SMEM],
+            (got, kept, cut_weight, net_weight, share),
         )
         returned = exchange(out, 1)
         args = (cut_cells, cut_weight, got, local_sum, back, sums)
@@ -473,7 +476,7 @@
             shapes = [(2, TILES * LANES), (2, TILES * LANES)]
         else:
             args = args + (cut_cells, pin_net)
-            shapes = [(512, LANES), (32, LANES), (96, LANES), (8, LANES), (256, LANES)]
+            shapes = [(384, LANES), (32, LANES), (96, LANES), (8, LANES), (256, LANES)]
         results = call(
             functools.partial(step_kernel, first, last), shapes, [(128, LANES)], 1 << 26, args
         )

time: 115 us -> 110 us (0.957)
  Pallas kernels: 24.7 us -> 22.4 us
  waiting for transfers between devices: 49 us -> 47.1 us
    pallas_call x13, Pallas kernels: 24.7 us -> 22.4 us  [call(): pl.pallas_call(kernel, out_shape=[jax.ShapeDtypeStruct(s, F32) for s in s...]
    all_to_all x6, waiting for transfers between devices: 49 us -> 47.1 us  [exchange(): lax.all_to_all(rows.reshape(LANES, 1, height * LANES), AXES, split_axis=0...]
  transfers between devices with their start and end apart: 12 -> 12, of which waited for: 6 -> 6; matrix products, arithmetic and copies ran while one was open for 0% -> 0% of each run, Pallas kernels for 17% -> 15%
where the time goes in v4:
time: 110 us
  waiting for transfers between devices  47.1 us (43%)
  starting transfers between devices  39.6 us (36%)
  Pallas kernels  22.4 us (20%)
    all_to_all x6, waiting for transfers between devices, exchange(): lax.all_to_all(rows.reshape(LANES, 1, height * LANES), AXES, split_axis=0...  47.1 us
    all_to_all x6, starting transfers between devices, exchange(): lax.all_to_all(rows.reshape(LANES, 1, height * LANES), AXES, split_axis=0...  32.6 us
    pallas_call x13, Pallas kernels, call(): pl.pallas_call(kernel, out_shape=[jax.ShapeDtypeStruct(s, F32) for s in s...  22.4 us
    ppermute x6, starting transfers between devices, swap(): return lax.ppermute(x, 'coord', [(0, 1), (1, 0)])  6.98 us
  transfers between devices with their start and end apart: 12, of which 6 were waited for; matrix products, arithmetic and copies ran while one was open for 0% of the time, Pallas kernels for 15%

profile of v4, /device:TPU:1, one launch (start us, length us, event | category | flops | bytes accessed | tf_op | source)
XLA Modules:
  0.0 110.0 jit_solution(7269638438924635546)
XLA Ops:
  0.6 0.0 copy-start.3
  0.6 0.0 copy-start.4
  0.7 2.1 %collective-permute-start = (f32[2,2048]{1,0:T(2,128)}, f32[2,2048]{1,0:T(2,128)S(1)}, u32[]{:S(2)}, u32[]{:S(2)}) collective-permute-start(f32[2,2048]{1,0:T(2,128)} %right_hbm.1), channel_id=1, source_target_pairs={{0,1},{1,0},{2,3},{3,2},{4,5},{5,4},{6,7},{7,6},{8,9},{9,8},{10,11... | collective-permute-start | bytes 49160 | tf_op jit(solution)/shard_map/ppermute | solution.py:408
  2.8 2.5 %shard_map.104 = (f32[384,128]{1,0:T(8,128)}, f32[32,128]{1,0:T(8,128)S(1)}, f32[256,128]{1,0:T(8,128)S(1)}, f32[16,2,128,128]{3,2,1,0:T(8,128)S(1)}, f32[128,128]{1,0:T(8,128)S(1)}, /*index=5*/f32[16,128]{1,0:T(8,128)S(1)}) custom-call(f32[2,2048]{1,0:T(2,128)} %right_hbm.1, s32[128,128]{1,0:T(8,128)} %bitcast.33, s32[32,128]{1,0:T(8,128)} %bitcast.44, ...), custom_call_target="tpu_custom_call" | custom-call | flops 16777216 | bytes 1048576 | tf_op jit(solution)/shard_map/pallas_call | solution.py:386
  5.3 10.7 %all-to-all-start = ((f32[128,1,384]{2,1,0:T(1,128)}), f32[128,1,384]{2,1,0:T(1,128)S(1)}, u32[]{:S(2)}, u32[]{:S(2)}) async-start(f32[128,1,384]{2,1,0:T(1,128)} %bitcast.5), calls=%async_computation | async-start | bytes 393216 | tf_op jit(solution)/shard_map/all_to_all | solution.py:402
  16.0 0.1 pad_add_fusion.place
  16.1 0.0 collective-permute-done.peer_ref
  16.1 0.0 copy-done.3
  16.1 0.0 copy-done.4
  16.1 0.0 copy-start
  16.1 0.0 copy-start.1
  16.1 0.0 copy-start.2
  16.1 1.8 %shard_map.105 = (f32[48,128]{1,0:T(8,128)S(1)}, f32[48,128]{1,0:T(8,128)S(1)}, f32[8,128]{1,0:T(8,128)S(1)}, f32[8,128]{1,0:T(8,128)S(1)}) custom-call(s32[2]{0:T(128)S(1)} %pad_add_fusion.place, f32[32,128]{1,0:T(8,128)S(1)} %get-tuple-element.39.own_ref.start_ref, f32[2,2048]{1,0:T(2,128)S(1)} %collective-permute-done.peer_ref, s32[2,16]{1,0:T(2,128)S(1)} %bitcast.53, ...), custom_call_target="tpu_custom_call" | custom-call | flops 4294967296 | bytes 1048576 | tf_op jit(solution)/shard_map/pallas_call | solution.py:386
  17.9 1.5 %collective-permute-start.1 = (f32[48,128]{1,0:T(8,128)S(1)}, f32[48,128]{1,0:T(8,128)S(1)}, u32[]{:S(2)}, u32[]{:S(2)}) collective-permute-start(f32[48,128]{1,0:T(8,128)S(1)} %get-tuple-element.46), channel_id=1, source_target_pairs={{0,1},{1,0},{2,3},{3,2},{4,5},{5,4},{6,7},{7,6},{8,9},{9,8},{10,11... | collective-permute-start | bytes 73736 | tf_op jit(solution)/shard_map/ppermute | solution.py:408
  19.4 7.4 %all-to-all-done = f32[128,1,384]{2,1,0:T(1,128)S(1)} async-done(((f32[128,1,384]{2,1,0:T(1,128)}), f32[128,1,384]{2,1,0:T(1,128)S(1)}, u32[]{:S(2)}, u32[]{:S(2)}) %all-to-all-start) | async-done | bytes 196640 | tf_op jit(solution)/shard_map/all_to_all | solution.py:402
  26.7 1.3 %shard_map.106 = (f32[128,128]{1,0:T(8,128)}, f32[8,128]{1,0:T(8,128)S(1)}) custom-call(f32[384,128]{1,0:T(8,128)S(1)} %bitcast.27, f32[256,128]{1,0:T(8,128)S(1)} %get-tuple-element.37.refs_2_.kept, f32[128,128]{1,0:T(8,128)S(1)} %get-tuple-element.38.refs_1_.cut_weight, f32[8,128]{1,0:T(8,128)S(1)} %get-tuple-element.42.net_weight, ...), custom_call_target="tpu_custom_call" | custom-call | flops 67108864 | bytes 1048576 | tf_op jit(solution)/shard_map/pallas_call | solution.py:386
  28.1 4.0 %all-to-all-start.1 = ((f32[128,1,128]{2,1,0:T(1,128)}), f32[128,1,128]{2,1,0:T(1,128)S(1)}, u32[]{:S(2)}, u32[]{:S(2)}) async-start(f32[128,1,128]{2,1,0:T(1,128)} %bitcast.12), calls=%async_computation.1 | async-start | bytes 131072 | tf_op jit(solution)/shard_map/all_to_all | solution.py:402
  32.1 0.0 collective-permute-done.1.back_ref
  32.1 0.0 copy-done
  32.1 0.0 copy-done.1
  32.1 0.0 copy-done.2
  32.2 2.0 %shard_map.107 = (f32[32,128]{1,0:T(8,128)S(1)}, f32[16,128]{1,0:T(8,128)S(1)}) custom-call(s32[128,128]{1,0:T(8,128)S(1)} %bitcast.34, f32[128,128]{1,0:T(8,128)S(1)} %get-tuple-element.38.refs_1_.cut_weight, f32[384,128]{1,0:T(8,128)S(1)} %bitcast.28, f32[48,128]{1,0:T(8,128)S(1)} %get-tuple-element.45.local_ref, ...), custom_call_target="tpu_custom_call" | custom-call | flops 2147483648 | bytes 1048576 | tf_op jit(solution)/shard_map/pallas_call | solution.py:386
  34.2 7.9 %all-to-all-done.1 = f32[128,1,128]{2,1,0:T(1,128)S(1)} async-done(((f32[128,1,128]{2,1,0:T(1,128)}), f32[128,1,128]{2,1,0:T(1,128)S(1)}, u32[]{:S(2)}, u32[]{:S(2)}) %all-to-all-start.1) | async-done | bytes 65568 | tf_op jit(solution)/shard_map/all_to_all | solution.py:402
  42.0 2.1 %shard_map.108 = (f32[384,128]{1,0:T(8,128)}, f32[32,128]{1,0:T(8,128)S(1)}, f32[96,128]{1,0:T(8,128)S(1)}, f32[8,128]{1,0:T(8,128)S(1)}, f32[256,128]{1,0:T(8,128)S(1)}) custom-call(s32[32,128]{1,0:T(8,128)S(1)} %bitcast.46, f32[128,128]{1,0:T(8,128)S(1)} %bitcast.49, f32[16,128]{1,0:T(8,128)S(1)} %get-tuple-element.48.degree_ref.refs_0_, ...), custom_call_target="tpu_custom_call" | custom-call | flops 67108864 | bytes 1048576 | tf_op jit(solution)/shard_map/pallas_call | solution.py:386
  44.1 0.3 collective-permute-start.2
  44.4 4.9 %all-to-all-start.2 = ((f32[128,1,384]{2,1,0:T(1,128)}), f32[128,1,384]{2,1,0:T(1,128)S(1)}, u32[]{:S(2)}, u32[]{:S(2)}) async-start(f32[128,1,384]{2,1,0:T(1,128)} %bitcast.14), calls=%async_computation.2 | async-start | bytes 393216 | tf_op jit(solution)/shard_map/all_to_all | solution.py:402
  49.4 0.0 collective-permute-done.2.peer_ref
  49.4 1.8 %shard_map.109 = (f32[32,128]{1,0:T(8,128)S(1)}, f32[32,128]{1,0:T(8,128)S(1)}, f32[8,128]{1,0:T(8,128)S(1)}) custom-call(s32[2]{0:T(128)S(1)} %pad_add_fusion.place, f32[32,128]{1,0:T(8,128)S(1)} %get-tuple-element.52.own_ref.start_ref, f32[32,128]{1,0:T(8,128)S(1)} %collective-permute-done.2.peer_ref, s32[2,16]{1,0:T(2,128)S(1)} %bitcast.54, ...), custom_call_target="tpu_custom_call" | custom-call | flops 4294967296 | bytes 1048576 | tf_op jit(solution)/shard_map/pallas_call | solution.py:386
  51.2 1.4 %collective-permute-start.3 = (f32[32,128]{1,0:T(8,128)S(1)}, f32[32,128]{1,0:T(8,128)S(1)}, u32[]{:S(2)}, u32[]{:S(2)}) collective-permute-start(f32[32,128]{1,0:T(8,128)S(1)} %get-tuple-element.56), channel_id=1, source_target_pairs={{0,1},{1,0},{2,3},{3,2},{4,5},{5,4},{6,7},{7,6},{8,9},{9,8},{10,11... | collective-permute-start | bytes 49160 | tf_op jit(solution)/shard_map/ppermute | solution.py:408
  52.6 7.6 %all-to-all-done.2 = f32[128,1,384]{2,1,0:T(1,128)S(1)} async-done(((f32[128,1,384]{2,1,0:T(1,128)}), f32[128,1,384]{2,1,0:T(1,128)S(1)}, u32[]{:S(2)}, u32[]{:S(2)}) %all-to-all-start.2) | async-done | bytes 196640 | tf_op jit(solution)/shard_map/all_to_all | solution.py:402
  60.2 1.3 %shard_map.110 = (f32[128,128]{1,0:T(8,128)}, f32[8,128]{1,0:T(8,128)S(1)}) custom-call(f32[384,128]{1,0:T(8,128)S(1)} %bitcast.31, f32[256,128]{1,0:T(8,128)S(1)} %get-tuple-element.51.kept, f32[128,128]{1,0:T(8,128)S(1)} %get-tuple-element.38.refs_1_.cut_weight, f32[8,128]{1,0:T(8,128)S(1)} %get-tuple-element.42.net_weight, ...), custom_call_target="tpu_custom_call" | custom-call | flops 67108864 | bytes 1048576 | tf_op jit(solution)/shard_map/pallas_call | solution.py:386
  61.5 4.0 %all-to-all-start.3 = ((f32[128,1,128]{2,1,0:T(1,128)}), f32[128,1,128]{2,1,0:T(1,128)S(1)}, u32[]{:S(2)}, u32[]{:S(2)}) async-start(f32[128,1,128]{2,1,0:T(1,128)} %bitcast.17), calls=%async_computation.3 | async-start | bytes 131072 | tf_op jit(solution)/shard_map/all_to_all | solution.py:402
  65.5 0.0 collective-permute-done.3.back_ref
  65.5 1.6 %shard_map.111.others = f32[32,128]{1,0:T(8,128)S(1)} custom-call(s32[128,128]{1,0:T(8,128)S(1)} %bitcast.36, f32[128,128]{1,0:T(8,128)S(1)} %get-tuple-element.38.refs_1_.cut_weight, f32[384,128]{1,0:T(8,128)S(1)} %bitcast.32, f32[32,128]{1,0:T(8,128)S(1)} %get-tuple-element.55.local_ref, f32[32,128]{1,0:T(8,128)S(1)} %collective-permute-done.3.back_ref, ...), custom_call_target="tpu_custom_call" | custom-call | flops 2147483648 | bytes 1048576 | tf_op jit(solution)/shard_map/pallas_call | solution.py:386
  67.1 8.3 %all-to-all-done.3 = f32[128,1,128]{2,1,0:T(1,128)S(1)} async-done(((f32[128,1,128]{2,1,0:T(1,128)}), f32[128,1,128]{2,1,0:T(1,128)S(1)}, u32[]{:S(2)}, u32[]{:S(2)}) %all-to-all-start.3) | async-done | bytes 65568 | tf_op jit(solution)/shard_map/all_to_all | solution.py:402
  75.4 2.1 %shard_map.112 = (f32[384,128]{1,0:T(8,128)}, f32[32,128]{1,0:T(8,128)S(1)}, f32[96,128]{1,0:T(8,128)S(1)}, f32[8,128]{1,0:T(8,128)S(1)}, f32[256,128]{1,0:T(8,128)S(1)}) custom-call(s32[32,128]{1,0:T(8,128)S(1)} %bitcast.47, f32[128,128]{1,0:T(8,128)S(1)} %bitcast.39, f32[16,128]{1,0:T(8,128)S(1)} %get-tuple-element.48.degree_ref.refs_0_, ...), custom_call_target="tpu_custom_call" | custom-call | flops 67108864 | bytes 1048576 | tf_op jit(solution)/shard_map/pallas_call | solution.py:386
  77.6 0.3 collective-permute-start.4
  77.9 5.0 %all-to-all-start.4 = ((f32[128,1,384]{2,1,0:T(1,128)}), f32[128,1,384]{2,1,0:T(1,128)S(1)}, u32[]{:S(2)}, u32[]{:S(2)}) async-start(f32[128,1,384]{2,1,0:T(1,128)} %bitcast.19), calls=%async_computation.4 | async-start | bytes 393216 | tf_op jit(solution)/shard_map/all_to_all | solution.py:402
  82.8 0.0 collective-permute-done.4.peer_ref
  82.8 1.8 %shard_map.113 = (f32[32,128]{1,0:T(8,128)S(1)}, f32[32,128]{1,0:T(8,128)S(1)}, f32[8,128]{1,0:T(8,128)S(1)}) custom-call(s32[2]{0:T(128)S(1)} %pad_add_fusion.place, f32[32,128]{1,0:T(8,128)S(1)} %get-tuple-element.62.own_ref.start_ref, f32[32,128]{1,0:T(8,128)S(1)} %collective-permute-done.4.peer_ref, s32[2,16]{1,0:T(2,128)S(1)} %bitcast.55, ...), custom_call_target="tpu_custom_call" | custom-call | flops 4294967296 | bytes 1048576 | tf_op jit(solution)/shard_map/pallas_call | solution.py:386
  84.6 1.4 %collective-permute-start.5 = (f32[32,128]{1,0:T(8,128)S(1)}, f32[32,128]{1,0:T(8,128)S(1)}, u32[]{:S(2)}, u32[]{:S(2)}) collective-permute-start(f32[32,128]{1,0:T(8,128)S(1)} %get-tuple-element.66), channel_id=1, source_target_pairs={{0,1},{1,0},{2,3},{3,2},{4,5},{5,4},{6,7},{7,6},{8,9},{9,8},{10,11... | collective-permute-start | bytes 49160 | tf_op jit(solution)/shard_map/ppermute | solution.py:408
  86.0 7.6 %all-to-all-done.4 = f32[128,1,384]{2,1,0:T(1,128)S(1)} async-done(((f32[128,1,384]{2,1,0:T(1,128)}), f32[128,1,384]{2,1,0:T(1,128)S(1)}, u32[]{:S(2)}, u32[]{:S(2)}) %all-to-all-start.4) | async-done | bytes 196640 | tf_op jit(solution)/shard_map/all_to_all | solution.py:402
  93.6 1.3 %shard_map.114 = (f32[128,128]{1,0:T(8,128)}, f32[8,128]{1,0:T(8,128)S(1)}) custom-call(f32[384,128]{1,0:T(8,128)S(1)} %bitcast.29, f32[256,128]{1,0:T(8,128)S(1)} %get-tuple-element.61.kept, f32[128,128]{1,0:T(8,128)S(1)} %get-tuple-element.38.refs_1_.cut_weight, f32[8,128]{1,0:T(8,128)S(1)} %get-tuple-element.42.net_weight, ...), custom_call_target="tpu_custom_call" | custom-call | flops 67108864 | bytes 1048576 | tf_op jit(solution)/shard_map/pallas_call | solution.py:386
  94.9 4.0 %all-to-all-start.5 = ((f32[128,1,128]{2,1,0:T(1,128)}), f32[128,1,128]{2,1,0:T(1,128)S(1)}, u32[]{:S(2)}, u32[]{:S(2)}) async-start(f32[128,1,128]{2,1,0:T(1,128)} %bitcast.22), calls=%async_computation.5 | async-start | bytes 131072 | tf_op jit(solution)/shard_map/all_to_all | solution.py:402
  98.9 0.0 collective-permute-done.5.back_ref
  98.9 1.6 %shard_map.115.others = f32[32,128]{1,0:T(8,128)S(1)} custom-call(s32[128,128]{1,0:T(8,128)S(1)} %bitcast.38, f32[128,128]{1,0:T(8,128)S(1)} %get-tuple-element.38.refs_1_.cut_weight, f32[384,128]{1,0:T(8,128)S(1)} %bitcast.30, f32[32,128]{1,0:T(8,128)S(1)} %get-tuple-element.65.local_ref, f32[32,128]{1,0:T(8,128)S(1)} %collective-permute-done.5.back_ref, ...), custom_call_target="tpu_custom_call" | custom-call | flops 2147483648 | bytes 1048576 | tf_op jit(solution)/shard_map/pallas_call | solution.py:386
  100.5 8.3 %all-to-all-done.5 = f32[128,1,128]{2,1,0:T(1,128)S(1)} async-done(((f32[128,1,128]{2,1,0:T(1,128)}), f32[128,1,128]{2,1,0:T(1,128)S(1)}, u32[]{:S(2)}, u32[]{:S(2)}) %all-to-all-start.5) | async-done | bytes 65568 | tf_op jit(solution)/shard_map/all_to_all | solution.py:402
  108.8 1.2 %shard_map.116 = (f32[2,2048]{1,0:T(2,128)}, f32[2,2048]{1,0:T(2,128)}) custom-call(s32[32,128]{1,0:T(8,128)S(1)} %bitcast.48, f32[128,128]{1,0:T(8,128)S(1)} %bitcast.50, f32[16,128]{1,0:T(8,128)S(1)} %get-tuple-element.48.degree_ref.refs_0_, f32[32,128]{1,0:T(8,128)S(1)} %shard_map.115.others, f32[8,128]{1,0:T(8,128)S(1)} %get-tuple-element.67.sums_ref, ...), custom_call_target="tpu_custom_call" | custom-call | flops 67108864 | bytes 1048576 | tf_op jit(solution)/shard_map/pallas_call | solution.py:386
Async XLA Ops:
  0.6 15.4 %copy-start.3 = (f32[16384]{0:T(1024)S(1)}, f32[16384]{0:T(1024)}, u32[]{:S(2)}) copy-start(f32[16384]{0:T(1024)} %param.17) | copy-start | bytes 196612
  0.6 15.4 %copy-start.4 = (s32[16,2]{0,1:T(2,128)S(1)}, s32[16,2]{0,1:T(2,128)}, u32[]{:S(2)}) copy-start(s32[16,2]{0,1:T(2,128)} %param.12) | copy-start | bytes 388
  0.7 15.4 %collective-permute-start = (f32[2,2048]{1,0:T(2,128)}, f32[2,2048]{1,0:T(2,128)S(1)}, u32[]{:S(2)}, u32[]{:S(2)}) collective-permute-start(f32[2,2048]{1,0:T(2,128)} %right_hbm.1), channel_id=1, source_target_pairs={{0,1},{1,0},{2,3},{3,2},{4,5},{5,4},{6,7},{7,6},{8,9},{9,8},{10,11... | collective-permute-start | bytes 49160 | tf_op jit(solution)/shard_map/ppermute | solution.py:408
  5.3 21.4 %all-to-all-start = ((f32[128,1,384]{2,1,0:T(1,128)}), f32[128,1,384]{2,1,0:T(1,128)S(1)}, u32[]{:S(2)}, u32[]{:S(2)}) async-start(f32[128,1,384]{2,1,0:T(1,128)} %bitcast.5), calls=%async_computation | async-start | bytes 393216 | tf_op jit(solution)/shard_map/all_to_all | solution.py:402
  16.1 16.1 %copy-start = (s32[1,128,128]{2,1,0:T(8,128)S(1)}, s32[1,128,128]{2,1,0:T(8,128)}, u32[]{:S(2)}) copy-start(s32[1,128,128]{2,1,0:T(8,128)} %param.13) | copy-start | bytes 196612
  16.1 16.1 %copy-start.1 = (s32[4096]{0:T(1024)S(1)}, s32[4096]{0:T(1024)}, u32[]{:S(2)}) copy-start(s32[4096]{0:T(1024)} %param.16) | copy-start | bytes 49156
  16.1 16.1 %copy-start.2 = (s32[4096]{0:T(1024)S(1)}, s32[4096]{0:T(1024)}, u32[]{:S(2)}) copy-start(s32[4096]{0:T(1024)} %param.15) | copy-start | bytes 49156
  17.9 14.2 %collective-permute-start.1 = (f32[48,128]{1,0:T(8,128)S(1)}, f32[48,128]{1,0:T(8,128)S(1)}, u32[]{:S(2)}, u32[]{:S(2)}) collective-permute-start(f32[48,128]{1,0:T(8,128)S(1)} %get-tuple-element.46), channel_id=1, source_target_pairs={{0,1},{1,0},{2,3},{3,2},{4,5},{5,4},{6,7},{7,6},{8,9},{9,8},{10,11... | collective-permute-start | bytes 73736 | tf_op jit(solution)/shard_map/ppermute | solution.py:408
  28.1 13.9 %all-to-all-start.1 = ((f32[128,1,128]{2,1,0:T(1,128)}), f32[128,1,128]{2,1,0:T(1,128)S(1)}, u32[]{:S(2)}, u32[]{:S(2)}) async-start(f32[128,1,128]{2,1,0:T(1,128)} %bitcast.12), calls=%async_computation.1 | async-start | bytes 131072 | tf_op jit(solution)/shard_map/all_to_all | solution.py:402
  44.1 5.3 %collective-permute-start.2 = (f32[32,128]{1,0:T(8,128)S(1)}, f32[32,128]{1,0:T(8,128)S(1)}, u32[]{:S(2)}, u32[]{:S(2)}) collective-permute-start(f32[32,128]{1,0:T(8,128)S(1)} %get-tuple-element.52.own_ref.start_ref), channel_id=1, source_target_pairs={{0,1},{1,0},{2,3},{3,2},{4,5},{5,4},{6,7},{7,6},{8,9},{9,8},{10,11... | collective-permute-start | bytes 49160 | tf_op jit(solution)/shard_map/ppermute | solution.py:408
  44.4 15.7 %all-to-all-start.2 = ((f32[128,1,384]{2,1,0:T(1,128)}), f32[128,1,384]{2,1,0:T(1,128)S(1)}, u32[]{:S(2)}, u32[]{:S(2)}) async-start(f32[128,1,384]{2,1,0:T(1,128)} %bitcast.14), calls=%async_computation.2 | async-start | bytes 393216 | tf_op jit(solution)/shard_map/all_to_all | solution.py:402
  51.2 14.3 %collective-permute-start.3 = (f32[32,128]{1,0:T(8,128)S(1)}, f32[32,128]{1,0:T(8,128)S(1)}, u32[]{:S(2)}, u32[]{:S(2)}) collective-permute-start(f32[32,128]{1,0:T(8,128)S(1)} %get-tuple-element.56), channel_id=1, source_target_pairs={{0,1},{1,0},{2,3},{3,2},{4,5},{5,4},{6,7},{7,6},{8,9},{9,8},{10,11... | collective-permute-start | bytes 49160 | tf_op jit(solution)/shard_map/ppermute | solution.py:408
  61.5 14.0 %all-to-all-start.3 = ((f32[128,1,128]{2,1,0:T(1,128)}), f32[128,1,128]{2,1,0:T(1,128)S(1)}, u32[]{:S(2)}, u32[]{:S(2)}) async-start(f32[128,1,128]{2,1,0:T(1,128)} %bitcast.17), calls=%async_computation.3 | async-start | bytes 131072 | tf_op jit(solution)/shard_map/all_to_all | solution.py:402
  77.6 5.3 %collective-permute-start.4 = (f32[32,128]{1,0:T(8,128)S(1)}, f32[32,128]{1,0:T(8,128)S(1)}, u32[]{:S(2)}, u32[]{:S(2)}) collective-permute-start(f32[32,128]{1,0:T(8,128)S(1)} %get-tuple-element.62.own_ref.start_ref), channel_id=1, source_target_pairs={{0,1},{1,0},{2,3},{3,2},{4,5},{5,4},{6,7},{7,6},{8,9},{9,8},{10,11... | collective-permute-start | bytes 49160 | tf_op jit(solution)/shard_map/ppermute | solution.py:408
  77.9 15.7 %all-to-all-start.4 = ((f32[128,1,384]{2,1,0:T(1,128)}), f32[128,1,384]{2,1,0:T(1,128)S(1)}, u32[]{:S(2)}, u32[]{:S(2)}) async-start(f32[128,1,384]{2,1,0:T(1,128)} %bitcast.19), calls=%async_computation.4 | async-start | bytes 393216 | tf_op jit(solution)/shard_map/all_to_all | solution.py:402
  84.6 14.3 %collective-permute-start.5 = (f32[32,128]{1,0:T(8,128)S(1)}, f32[32,128]{1,0:T(8,128)S(1)}, u32[]{:S(2)}, u32[]{:S(2)}) collective-permute-start(f32[32,128]{1,0:T(8,128)S(1)} %get-tuple-element.66), channel_id=1, source_target_pairs={{0,1},{1,0},{2,3},{3,2},{4,5},{5,4},{6,7},{7,6},{8,9},{9,8},{10,11... | collective-permute-start | bytes 49160 | tf_op jit(solution)/shard_map/ppermute | solution.py:408
  94.9 13.9 %all-to-all-start.5 = ((f32[128,1,128]{2,1,0:T(1,128)}), f32[128,1,128]{2,1,0:T(1,128)S(1)}, u32[]{:S(2)}, u32[]{:S(2)}) async-start(f32[128,1,128]{2,1,0:T(1,128)} %bitcast.22), calls=%async_computation.5 | async-start | bytes 131072 | tf_op jit(solution)/shard_map/all_to_all | solution.py:402

commit v5 on v4

--- a/solution.py
+++ b/solution.py
@@ -8,6 +8,8 @@
 from jax.sharding import PartitionSpec as P
 
 FANOUT = 32
+BACKWARD_COST = 1 << 30
+FORWARD_COST = 1 << 30
 ITERS = 3
 AXES = ("region", "coord")
 LANES = 128
@@ -160,76 +162,94 @@
         copy.wait()
 
 
-def block_kernel(first, place, own_ref, peer_ref, nbr, blocks, *refs):
+def tile_names(nbr, names):
+    names[...] = jnp.zeros(names.shape, I32)
+    for k in range(2):
+        names[k : k + 1, 0:TILES] = nbr[k : k + 1, :]
+    return [jnp.where(iota((LANES, LANES), 0) == names[k : k + 1, :], 1.0, 0.0) for k in range(2)]
+
+
+def block_parts(blocks, t):
+    pair = jnp.concatenate([blocks[t, 0], blocks[t, 1]], axis=1)
+    high = pair.astype(BF16)
+    return high, (pair - high.astype(F32)).astype(BF16)
+
+
+def tile_rows(ref, at, v):
+    if v == 2:
+        return ref[pl.ds(at + 4, 16, stride=8), :]
+    return ref[pl.ds(at + v, 16, stride=8), :] + ref[pl.ds(at + v + 2, 16, stride=8), :]
+
+
+def backward_kernel(first, own_ref, side, nbr, blocks, *refs):
     if first:
-        (anchor, cut_weight, kept, star, local_ref, back_ref, share_ref, net_weight_ref,
-         near, far, got_f, got_b, names, peers) = refs
+        place, star, local_ref, back_ref, ones_ref, net_weight_ref, near, got, names = refs
         net_weight_ref[...] = jnp.broadcast_to(star[pl.ds(place[1], 1), :], (8, LANES))
+    else:
+        local_ref, back_ref, near, got, names = refs
+    spread_rows = [h[:32].astype(BF16) for h in tile_names(nbr, names)]
+    near[...] = jnp.ones(near.shape, F32)
+    for v in range(2):
+        for i, part in enumerate(split2(own_ref[16 * v : 16 * v + 16, :])):
+            near[pl.ds(2 * i + v, 16, stride=8), :] = part
+    for t in range(TILES):
+        a = near[8 * t : 8 * t + 8, :].astype(BF16)
+        high, low = block_parts(blocks, t)
+        back = dot_nn(a, high) + dot_nn(a, low)
+        for k in range(2):
+            got[128 * k + 8 * t : 128 * k + 8 * t + 8, :] = back[:, LANES * k : LANES * (k + 1)]
+    filler = jnp.zeros((112, LANES), F32)
+    upper = side[0:1, :] > 0.5
+    for v in range(3 if first else 2):
+        spread = sum(
+            dot_nn(spread_rows[k], jnp.concatenate([part, filler], axis=0).astype(BF16))
+            for k in range(2)
+            for part in split3(tile_rows(got, 128 * k, v))
+        )
+        lower, higher = spread[:16], spread[16:]
+        local_ref[16 * v : 16 * v + 16, :] = jnp.where(upper, higher, lower)
+        back_ref[16 * v : 16 * v + 16, :] = jnp.where(upper, lower, higher)
+        if v == 2:
+            ones_ref[...] = spread
+
+
+def forward_kernel(first, own_ref, peer_ref, side, nbr, blocks, before_ref, *refs):
+    if first:
+        ones_ref, anchor, cut_weight, kept, local_ref, share_ref, far, got, names, peers = refs
         for v in range(2):
             for t in range(TILES):
                 peers[TILES * v + t : TILES * v + t + 1, :] = peer_ref[v : v + 1, LANES * t : LANES * (t + 1)]
-        peer = peers[...]
+        peer_ref = peers
     else:
-        degree, local_ref, back_ref, share_ref, near, far, got_f, got_b, names = refs
-        peer = peer_ref[...]
-    own = own_ref[...]
-    upper = place[0] == 1
-    names[...] = jnp.zeros(names.shape, I32)
-    for k in range(2):
-        names[k : k + 1, 0:TILES] = nbr[k : k + 1, :]
-    hot = [jnp.where(iota((128, LANES), 0) == names[k : k + 1, :], 1.0, 0.0) for k in range(2)]
-    pick_rows = jnp.concatenate([h.T[:16] for h in hot], axis=0).astype(BF16)
-    spread_rows = [h[:32].astype(BF16) for h in hot]
-    near[...] = jnp.ones(near.shape, F32)
+        degree, local_ref, share_ref, far, got, names = refs
+    upper = side[0:1, :] > 0.5
+    pick_rows = jnp.concatenate([h.T[:16] for h in tile_names(nbr, names)], axis=0).astype(BF16)
     far[...] = jnp.ones(far.shape, F32)
     zeros = jnp.zeros((96, LANES), F32)
     wholes = []
     for v in range(2):
-        o, p = own[16 * v : 16 * v + 16], peer[16 * v : 16 * v + 16]
+        o, p = own_ref[16 * v : 16 * v + 16, :], peer_ref[16 * v : 16 * v + 16, :]
         whole = jnp.concatenate([jnp.where(upper, p, o), jnp.where(upper, o, p)], axis=0)
         wholes.append(whole)
-        for i, (mine, part) in enumerate(zip(split2(o), split2(whole))):
-            near[pl.ds(2 * i + v, 16, stride=8), :] = mine
+        for i, part in enumerate(split2(whole)):
             picked = dot_nn(pick_rows, jnp.concatenate([part, zeros], axis=0).astype(BF16))
             for k in range(2):
                 far[pl.ds(128 * k + 2 * i + v, 16, stride=8), :] = picked[16 * k : 16 * k + 16]
     for t in range(TILES):
-        pair = jnp.concatenate([blocks[t, 0], blocks[t, 1]], axis=1)
-        high = pair.astype(BF16)
-        low = (pair - high.astype(F32)).astype(BF16)
-        a = near[8 * t : 8 * t + 8, :].astype(BF16)
         b = jnp.concatenate(
             [far[128 * k + 8 * t : 128 * k + 8 * t + 8, :] for k in range(2)], axis=1
         ).astype(BF16)
-        back = dot_nn(a, high) + dot_nn(a, low)
-        for k in range(2):
-            got_b[128 * k + 8 * t : 128 * k + 8 * t + 8, :] = back[:, LANES * k : LANES * (k + 1)]
-        got_f[8 * t : 8 * t + 8, :] = dot_nt(b, high) + dot_nt(b, low)
-    filler = jnp.zeros((112, LANES), F32)
-    ahead, whole_spread = [], []
-    for v in range(3 if first else 2):
-        def take(ref, at):
-            if v == 2:
-                return ref[pl.ds(at + 4, 16, stride=8), :]
-            return ref[pl.ds(at + v, 16, stride=8), :] + ref[pl.ds(at + v + 2, 16, stride=8), :]
-
-        forward = take(got_f, 0)
-        spread = sum(
-            dot_nn(spread_rows[k], jnp.concatenate([part, filler], axis=0).astype(BF16))
-            for k in range(2)
-            for part in split3(take(got_b, 128 * k))
-        )
-        ahead.append(forward)
-        whole_spread.append(spread)
-        lower, higher = spread[:16], spread[16:]
-        local_ref[16 * v : 16 * v + 16, :] = forward + jnp.where(upper, higher, lower)
-        back_ref[16 * v : 16 * v + 16, :] = jnp.where(upper, lower, higher)
-    for v in range(2):
-        r = own[16 * v : 16 * v + 16]
+        high, low = block_parts(blocks, t)
+        got[8 * t : 8 * t + 8, :] = dot_nt(b, high) + dot_nt(b, low)
+    ahead = [tile_rows(got, 0, v) for v in range(3 if first else 2)]
+    for v, forward in enumerate(ahead):
+        local_ref[16 * v : 16 * v + 16, :] = before_ref[16 * v : 16 * v + 16, :] + forward
+    for v in range(2):
+        r = own_ref[16 * v : 16 * v + 16, :]
         if first:
             square = r * (r * (anchor[...] + ahead[2]) - 2.0 * ahead[v])
             line = jnp.sum(square, axis=0, keepdims=True)
-            line = line + jnp.sum(wholes[v] * wholes[v] * whole_spread[2], axis=0, keepdims=True)
+            line = line + jnp.sum(wholes[v] * wholes[v] * ones_ref[...], axis=0, keepdims=True)
             cut = kept[128 * v : 128 * v + 128, :]
             line = line + jnp.sum(cut_weight[...] * cut * cut, axis=0, keepdims=True)
         else:
@@ -287,7 +307,7 @@
         )
 
 
-def cut_kernel(first, cut_cells, cut_weight, got, local_ref, back_ref, sums_ref, *refs):
+def cut_kernel(first, cut_cells, cut_weight, got, local_ref, sums_ref, *refs):
     del sums_ref
 
     def values(j):
@@ -299,10 +319,10 @@
     acc = add_rows(128, lambda j: cut_cells[j : j + 1, :], values)
     if not first:
         (out_ref,) = refs
-        out_ref[...] = fold(acc, 2, 2) + local_ref[...] + back_ref[...]
+        out_ref[...] = fold(acc, 2, 2) + local_ref[...]
         return
     pin_cell, pin_net, star, anchor, out_ref, degree_ref, rows_ref, pins_ref = refs
-    out_ref[...] = fold(acc[:64], 2, 2) + local_ref[0:32, :] + back_ref[0:32, :]
+    out_ref[...] = fold(acc[:64], 2, 2) + local_ref[0:32, :]
     net = pin_net[...] & (LANES - 1)
     for q in range(4):
         rows_ref[pl.ds(32 * q, 32), :] = jnp.take_along_axis(
@@ -317,15 +337,17 @@
         lambda j: [pins_ref[32 * i + j : 32 * i + j + 1, :] for i in range(3)],
     )
     degree_ref[...] = (
-        anchor[...] + fold(acc[64:], 1, 3) + fold(pinned, 1, 3) + local_ref[32:48, :] + back_ref[32:48, :]
+        anchor[...] + fold(acc[64:], 1, 3) + fold(pinned, 1, 3) + local_ref[32:48, :]
     )
 
 
-def step_kernel(first, last, pin_cell, got, degree_ref, others, sums_ref, start_ref, *refs):
+def step_kernel(first, last, pin_cell, got, degree_in, others, back_ref, sums_ref, start_ref, *refs):
     refs = list(refs)
     state, old = (None, None) if first else (refs.pop(0), refs.pop(0))
     if last:
         positions_ref, residual_ref, pins = refs
+    elif first:
+        cut_cells, pin_net, send_ref, residual_ref, state_ref, old_ref, kept_ref, degree_ref, pins = refs
     else:
         cut_cells, pin_net, send_ref, residual_ref, state_ref, old_ref, kept_ref, pins = refs
     pin_rows = [got[pl.ds(q, 32, stride=4), :] for q in range(4)]
@@ -338,8 +360,11 @@
         lambda j: pin_cell[j : j + 1, :],
         lambda j: [pins[32 * i + j : 32 * i + j + 1, :] for i in range(4)],
     )
-    removed = fold(acc, 2, 2) + others[...]
-    degree = degree_ref[...]
+    removed = fold(acc, 2, 2) + others[...] + back_ref[0:32, :]
+    degree = degree_in[...]
+    if first:
+        degree = degree + back_ref[32:48, :]
+        degree_ref[...] = degree
     news, line = [], jnp.zeros((1, LANES), F32)
     lanes = iota((1, LANES), 1)
     sent_sums = [None] * 4
@@ -416,6 +441,7 @@
     star, anchor = star_weight.reshape(LANES, LANES), anchor.reshape(TILES, LANES)
     coord = lax.axis_index("coord")
     place = jnp.stack([coord, lax.axis_index("region") * 2 + coord]).astype(I32)
+    side = jnp.full((8, LANES), coord).astype(F32)
     nbr = tile_nbr.T
     peer = swap(right_side)
     send, residual, kept, blocks, cut_weight, anchor = call(
@@ -438,18 +464,25 @@
         if not first:
             peer = swap(residual)
         rows = 48 if first else 32
-        scratch = [(128, LANES), (256, LANES), (128, LANES), (256, LANES), pltpu.VMEM((8, LANES), I32)]
-        local_sum, back, share, *more = call(
-            functools.partial(block_kernel, first),
-            [(rows, LANES), (rows, LANES), (8, LANES)] + [(8, LANES)] * first,
-            scratch + [(32, LANES)] if first else scratch,
-            1 << 32,
-            (place, residual, peer, nbr, blocks) + ((anchor, cut_weight, kept, star) if first else (degree,)),
-            [SMEM],
-        )
-        back = swap(back)
-        if first:
-            net_weight = more[0]
+        scratch = [(256, LANES), (128, LANES), pltpu.VMEM((8, LANES), I32)]
+        local_sum, back, *more = call(
+            functools.partial(backward_kernel, first),
+            [(rows, LANES), (rows, LANES)] + [(32, LANES), (8, LANES)] * first,
+            [(128, LANES), (256, LANES), pltpu.VMEM((8, LANES), I32)],
+            BACKWARD_COST,
+            (residual, side, nbr, blocks) + ((place, star) if first else ()),
+            [VMEM] * 4 + [SMEM] * first,
+        )
+        if first:
+            ones, net_weight = more
+        local_sum, share = call(
+            functools.partial(forward_kernel, first),
+            [(rows, LANES), (8, LANES)],
+            scratch + [(32, LANES)] * first,
+            FORWARD_COST,
+            (residual, peer, side, nbr, blocks, local_sum)
+            + ((ones, anchor, cut_weight, kept) if first else (degree,)),
+        )
         out, sums = call(
             functools.partial(owner_kernel, first),
             [(128, LANES), (8, LANES)],
@@ -458,7 +491,9 @@
             (got, kept, cut_weight, net_weight, share),
         )
         returned = exchange(out, 1)
-        args = (cut_cells, cut_weight, got, local_sum, back, sums)
+        back, sums = lax.optimization_barrier((back, sums))
+        back = swap(back)
+        args = (cut_cells, cut_weight, got, local_sum, sums)
         if first:
             others, degree = call(
                 functools.partial(cut_kernel, True),
@@ -469,7 +504,7 @@
             )
         else:
             others = call(functools.partial(cut_kernel, False), [(32, LANES)], [], 1 << 31, args)[0]
-        args = (pin_cell, returned, degree, others, sums, residual)
+        args = (pin_cell, returned, degree, others, back, sums, residual)
         if not first:
             args = args + (state, old)
         if last:
@@ -477,12 +512,15 @@
         else:
             args = args + (cut_cells, pin_net)
             shapes = [(384, LANES), (32, LANES), (96, LANES), (8, LANES), (256, LANES)]
+            shapes = shapes + [(16, LANES)] * first
         results = call(
             functools.partial(step_kernel, first, last), shapes, [(128, LANES)], 1 << 26, args
         )
         if last:
             return tuple(results)
-        send, residual, state, old, kept = results
+        send, residual, state, old, kept, *more = results
+        if first:
+            degree = more[0]
 
 
 def solution(mesh):

time: 110 us -> 108 us (0.982)
  waiting for transfers between devices: 47.1 us -> 44.7 us
    all_to_all x6, waiting for transfers between devices: 47.1 us -> 40.8 us  [exchange(): lax.all_to_all(rows.reshape(LANES, 1, height * LANES), AXES, split_axis=0...]
    ppermute x6, waiting for transfers between devices: 0.02 us -> 3.91 us  [swap(): return lax.ppermute(x, 'coord', [(0, 1), (1, 0)])]
    ppermute x6, starting transfers between devices: 6.98 us -> 9.62 us  [swap(): return lax.ppermute(x, 'coord', [(0, 1), (1, 0)])]
    all_to_all x6, starting transfers between devices: 32.6 us -> 31 us  [exchange(): lax.all_to_all(rows.reshape(LANES, 1, height * LANES), AXES, split_axis=0...]
    pallas_call x13 -> x16, Pallas kernels: 22.4 us -> 21.7 us  [call(): pl.pallas_call(kernel, out_shape=[jax.ShapeDtypeStruct(s, F32) for s in s...]
  transfers between devices with their start and end apart: 12 -> 12, of which waited for: 6 -> 9; matrix products, arithmetic and copies ran while one was open for 0% -> 0% of each run, Pallas kernels for 15% -> 12%
where the time goes in v5:
time: 108 us
  waiting for transfers between devices  44.7 us (41%)
  starting transfers between devices  40.6 us (38%)
  Pallas kernels  21.7 us (20%)
    all_to_all x6, waiting for transfers between devices, exchange(): lax.all_to_all(rows.reshape(LANES, 1, height * LANES), AXES, split_axis=0...  40.8 us
    all_to_all x6, starting transfers between devices, exchange(): lax.all_to_all(rows.reshape(LANES, 1, height * LANES), AXES, split_axis=0...  31 us
    pallas_call x16, Pallas kernels, call(): pl.pallas_call(kernel, out_shape=[jax.ShapeDtypeStruct(s, F32) for s in s...  21.7 us
    ppermute x6, starting transfers between devices, swap(): return lax.ppermute(x, 'coord', [(0, 1), (1, 0)])  9.62 us
    ppermute x6, waiting for transfers between devices, swap(): return lax.ppermute(x, 'coord', [(0, 1), (1, 0)])  3.91 us
  transfers between devices with their start and end apart: 12, of which 9 were waited for; matrix products, arithmetic and copies ran while one was open for 0% of the time, Pallas kernels for 12%

profile of v5, /device:TPU:1, one launch (start us, length us, event | category | flops | bytes accessed | tf_op | source)
XLA Modules:
  0.0 108.0 jit_solution(709265128059150110)
XLA Ops:
  0.6 0.0 copy-start.3
  0.6 0.0 copy-start.4
  0.7 2.1 %collective-permute-start = (f32[2,2048]{1,0:T(2,128)}, f32[2,2048]{1,0:T(2,128)S(1)}, u32[]{:S(2)}, u32[]{:S(2)}) collective-permute-start(f32[2,2048]{1,0:T(2,128)} %right_hbm.1), channel_id=1, source_target_pairs={{0,1},{1,0},{2,3},{3,2},{4,5},{5,4},{6,7},{7,6},{8,9},{9,8},{10,11... | collective-permute-start | bytes 49160 | tf_op jit(solution)/shard_map/ppermute | solution.py:433
  2.8 2.5 %shard_map.104 = (f32[384,128]{1,0:T(8,128)}, f32[32,128]{1,0:T(8,128)S(1)}, f32[256,128]{1,0:T(8,128)S(1)}, f32[16,2,128,128]{3,2,1,0:T(8,128)S(1)}, f32[128,128]{1,0:T(8,128)S(1)}, /*index=5*/f32[16,128]{1,0:T(8,128)S(1)}) custom-call(f32[2,2048]{1,0:T(2,128)} %right_hbm.1, s32[128,128]{1,0:T(8,128)} %bitcast.33, s32[32,128]{1,0:T(8,128)} %bitcast.44, ...), custom_call_target="tpu_custom_call" | custom-call | flops 16777216 | bytes 1048576 | tf_op jit(solution)/shard_map/pallas_call | solution.py:411
  5.3 10.7 %all-to-all-start = ((f32[128,1,384]{2,1,0:T(1,128)}), f32[128,1,384]{2,1,0:T(1,128)S(1)}, u32[]{:S(2)}, u32[]{:S(2)}) async-start(f32[128,1,384]{2,1,0:T(1,128)} %bitcast.5), calls=%async_computation | async-start | bytes 393216 | tf_op jit(solution)/shard_map/all_to_all | solution.py:427
  16.0 0.1 pad_add_fusion.refs_0_
  16.0 0.0 copy-done.3
  16.1 0.0 copy-done.4
  16.1 1.1 %shard_map.105 = (f32[48,128]{1,0:T(8,128)S(1)}, f32[48,128]{1,0:T(8,128)S(1)}, f32[32,128]{1,0:T(8,128)S(1)}, f32[8,128]{1,0:T(8,128)S(1)}) custom-call(f32[32,128]{1,0:T(8,128)S(1)} %get-tuple-element.50.own_ref.start_ref, f32[8,128]{1,0:T(8,128)S(1)} %broadcast_in_dim.3.side, s32[2,16]{1,0:T(2,128)S(1)} %bitcast.53, ...), custom_call_target="tpu_custom_call" | custom-call | flops 1073741824 | bytes 1048576 | tf_op jit(solution)/shard_map/pallas_call | solution.py:411
  17.2 0.0 collective-permute-done.peer_ref
  17.2 0.0 copy-start
  17.2 0.0 copy-start.1
  17.3 0.0 copy-start.2
  17.3 0.9 shard_map.106
  18.1 8.6 %all-to-all-done = f32[128,1,384]{2,1,0:T(1,128)S(1)} async-done(((f32[128,1,384]{2,1,0:T(1,128)}), f32[128,1,384]{2,1,0:T(1,128)S(1)}, u32[]{:S(2)}, u32[]{:S(2)}) %all-to-all-start) | async-done | bytes 196640 | tf_op jit(solution)/shard_map/all_to_all | solution.py:427
  26.7 1.3 %shard_map.107 = (f32[128,128]{1,0:T(8,128)}, f32[8,128]{1,0:T(8,128)S(1)}) custom-call(f32[384,128]{1,0:T(8,128)S(1)} %bitcast.27, f32[256,128]{1,0:T(8,128)S(1)} %get-tuple-element.48.refs_3_.kept, f32[128,128]{1,0:T(8,128)S(1)} %get-tuple-element.49.refs_2_.cut_weight, f32[8,128]{1,0:T(8,128)S(1)} %get-tuple-element.52.net_weight, ...), custom_call_target="tpu_custom_call" | custom-call | flops 67108864 | bytes 1048576 | tf_op jit(solution)/shard_map/pallas_call | solution.py:411
  28.1 4.0 %all-to-all-start.1 = ((f32[128,1,128]{2,1,0:T(1,128)}), f32[128,1,128]{2,1,0:T(1,128)S(1)}, u32[]{:S(2)}, u32[]{:S(2)}) async-start(f32[128,1,128]{2,1,0:T(1,128)} %bitcast.12), calls=%async_computation.1 | async-start | bytes 131072 | tf_op jit(solution)/shard_map/all_to_all | solution.py:427
  32.1 1.5 %collective-permute-start.1 = (f32[48,128]{1,0:T(8,128)S(1)}, f32[48,128]{1,0:T(8,128)S(1)}, u32[]{:S(2)}, u32[]{:S(2)}) collective-permute-start(f32[48,128]{1,0:T(8,128)S(1)} %get-tuple-element.64), channel_id=1, source_target_pairs={{0,1},{1,0},{2,3},{3,2},{4,5},{5,4},{6,7},{7,6},{8,9},{9,8},{10,11... | collective-permute-start | bytes 73736 | tf_op jit(solution)/shard_map/ppermute | solution.py:433
  33.6 0.0 copy-done
  33.6 0.0 copy-done.1
  33.6 0.0 copy-done.2
  33.6 2.0 %shard_map.108 = (f32[32,128]{1,0:T(8,128)S(1)}, f32[16,128]{1,0:T(8,128)S(1)}) custom-call(s32[128,128]{1,0:T(8,128)S(1)} %bitcast.34, f32[128,128]{1,0:T(8,128)S(1)} %get-tuple-element.49.refs_2_.cut_weight, f32[384,128]{1,0:T(8,128)S(1)} %bitcast.28, f32[48,128]{1,0:T(8,128)S(1)} %get-tuple-element.58.local_ref, f32[8,128]{1,0:T(8,128)S(1)} %get-tuple-element.61.sums_ref, ...), custom_call_target="tpu_custom_call" | custom-call | flops 2147483648 | bytes 1048576 | tf_op jit(solution)/shard_map/pallas_call | solution.py:411
  35.6 0.0 collective-permute-done.1.back_ref
  35.6 6.4 %all-to-all-done.1 = f32[128,1,128]{2,1,0:T(1,128)S(1)} async-done(((f32[128,1,128]{2,1,0:T(1,128)}), f32[128,1,128]{2,1,0:T(1,128)S(1)}, u32[]{:S(2)}, u32[]{:S(2)}) %all-to-all-start.1) | async-done | bytes 65568 | tf_op jit(solution)/shard_map/all_to_all | solution.py:427
  42.0 2.1 %shard_map.109 = (f32[384,128]{1,0:T(8,128)}, f32[32,128]{1,0:T(8,128)S(1)}, f32[96,128]{1,0:T(8,128)S(1)}, f32[8,128]{1,0:T(8,128)S(1)}, f32[256,128]{1,0:T(8,128)S(1)}, /*index=5*/f32[16,128]{1,0:T(8,128)S(1)}) custom-call(s32[32,128]{1,0:T(8,128)S(1)} %bitcast.46, f32[128,128]{1,0:T(8,128)S(1)} %bitcast.49, f32[16,128]{1,0:T(8,128)S(1)} %get-tuple-element.62.degree_in, ...), custom_call_target="tpu_custom_call" | custom-call | flops 67108864 | bytes 1048576 | tf_op jit(solution)/shard_map/pallas_call | solution.py:411
  44.1 4.1 %all-to-all-start.2 = ((f32[128,1,384]{2,1,0:T(1,128)}), f32[128,1,384]{2,1,0:T(1,128)S(1)}, u32[]{:S(2)}, u32[]{:S(2)}) async-start(f32[128,1,384]{2,1,0:T(1,128)} %bitcast.14), calls=%async_computation.2 | async-start | bytes 393216 | tf_op jit(solution)/shard_map/all_to_all | solution.py:427
  48.3 1.5 %collective-permute-start.2 = (f32[32,128]{1,0:T(8,128)S(1)}, f32[32,128]{1,0:T(8,128)S(1)}, u32[]{:S(2)}, u32[]{:S(2)}) collective-permute-start(f32[32,128]{1,0:T(8,128)S(1)} %get-tuple-element.67.own_ref.start_ref), channel_id=1, source_target_pairs={{0,1},{1,0},{2,3},{3,2},{4,5},{5,4},{6,7},{7,6},{8,9},{9,8},{10,11... | collective-permute-start | bytes 49160 | tf_op jit(solution)/shard_map/ppermute | solution.py:433
  49.7 0.6 shard_map.110
  50.3 1.9 %collective-permute-done.2.peer_ref = f32[32,128]{1,0:T(8,128)S(1)} collective-permute-done((f32[32,128]{1,0:T(8,128)S(1)}, f32[32,128]{1,0:T(8,128)S(1)}, u32[]{:S(2)}, u32[]{:S(2)}) %collective-permute-start.2) | collective-permute-done | bytes 16416 | tf_op jit(solution)/shard_map/ppermute | solution.py:433
  52.2 0.8 shard_map.111
  53.1 6.2 %all-to-all-done.2 = f32[128,1,384]{2,1,0:T(1,128)S(1)} async-done(((f32[128,1,384]{2,1,0:T(1,128)}), f32[128,1,384]{2,1,0:T(1,128)S(1)}, u32[]{:S(2)}, u32[]{:S(2)}) %all-to-all-start.2) | async-done | bytes 196640 | tf_op jit(solution)/shard_map/all_to_all | solution.py:427
  59.2 1.3 %shard_map.112 = (f32[128,128]{1,0:T(8,128)}, f32[8,128]{1,0:T(8,128)S(1)}) custom-call(f32[384,128]{1,0:T(8,128)S(1)} %bitcast.31, f32[256,128]{1,0:T(8,128)S(1)} %get-tuple-element.66.kept, f32[128,128]{1,0:T(8,128)S(1)} %get-tuple-element.49.refs_2_.cut_weight, f32[8,128]{1,0:T(8,128)S(1)} %get-tuple-element.52.net_weight, ...), custom_call_target="tpu_custom_call" | custom-call | flops 67108864 | bytes 1048576 | tf_op jit(solution)/shard_map/pallas_call | solution.py:411
  60.5 4.0 %all-to-all-start.3 = ((f32[128,1,128]{2,1,0:T(1,128)}), f32[128,1,128]{2,1,0:T(1,128)S(1)}, u32[]{:S(2)}, u32[]{:S(2)}) async-start(f32[128,1,128]{2,1,0:T(1,128)} %bitcast.17), calls=%async_computation.3 | async-start | bytes 131072 | tf_op jit(solution)/shard_map/all_to_all | solution.py:427
  64.5 1.6 %collective-permute-start.3 = (f32[32,128]{1,0:T(8,128)S(1)}, f32[32,128]{1,0:T(8,128)S(1)}, u32[]{:S(2)}, u32[]{:S(2)}) collective-permute-start(f32[32,128]{1,0:T(8,128)S(1)} %get-tuple-element.76), channel_id=1, source_target_pairs={{0,1},{1,0},{2,3},{3,2},{4,5},{5,4},{6,7},{7,6},{8,9},{9,8},{10,11... | collective-permute-start | bytes 49160 | tf_op jit(solution)/shard_map/ppermute | solution.py:433
  66.2 1.6 %shard_map.113.others = f32[32,128]{1,0:T(8,128)S(1)} custom-call(s32[128,128]{1,0:T(8,128)S(1)} %bitcast.36, f32[128,128]{1,0:T(8,128)S(1)} %get-tuple-element.49.refs_2_.cut_weight, f32[384,128]{1,0:T(8,128)S(1)} %bitcast.32, f32[32,128]{1,0:T(8,128)S(1)} %get-tuple-element.72.local_ref, f32[8,128]{1,0:T(8,128)S(1)} %get-tuple-element.75.sums_ref), custom_call_target="tpu_custom_call" | custom-call | flops 2147483648 | bytes 1048576 | tf_op jit(solution)/shard_map/pallas_call | solution.py:411
  67.7 0.0 collective-permute-done.3.back_ref
  67.8 6.7 %all-to-all-done.3 = f32[128,1,128]{2,1,0:T(1,128)S(1)} async-done(((f32[128,1,128]{2,1,0:T(1,128)}), f32[128,1,128]{2,1,0:T(1,128)S(1)}, u32[]{:S(2)}, u32[]{:S(2)}) %all-to-all-start.3) | async-done | bytes 65568 | tf_op jit(solution)/shard_map/all_to_all | solution.py:427
  74.4 2.1 %shard_map.114 = (f32[384,128]{1,0:T(8,128)}, f32[32,128]{1,0:T(8,128)S(1)}, f32[96,128]{1,0:T(8,128)S(1)}, f32[8,128]{1,0:T(8,128)S(1)}, f32[256,128]{1,0:T(8,128)S(1)}) custom-call(s32[32,128]{1,0:T(8,128)S(1)} %bitcast.47, f32[128,128]{1,0:T(8,128)S(1)} %bitcast.39, f32[16,128]{1,0:T(8,128)S(1)} %get-tuple-element.69.refs_0_.degree_in, ...), custom_call_target="tpu_custom_call" | custom-call | flops 67108864 | bytes 1048576 | tf_op jit(solution)/shard_map/pallas_call | solution.py:411
  76.6 4.1 %all-to-all-start.4 = ((f32[128,1,384]{2,1,0:T(1,128)}), f32[128,1,384]{2,1,0:T(1,128)S(1)}, u32[]{:S(2)}, u32[]{:S(2)}) async-start(f32[128,1,384]{2,1,0:T(1,128)} %bitcast.19), calls=%async_computation.4 | async-start | bytes 393216 | tf_op jit(solution)/shard_map/all_to_all | solution.py:427
  80.7 1.5 %collective-permute-start.4 = (f32[32,128]{1,0:T(8,128)S(1)}, f32[32,128]{1,0:T(8,128)S(1)}, u32[]{:S(2)}, u32[]{:S(2)}) collective-permute-start(f32[32,128]{1,0:T(8,128)S(1)} %get-tuple-element.81.own_ref.start_ref), channel_id=1, source_target_pairs={{0,1},{1,0},{2,3},{3,2},{4,5},{5,4},{6,7},{7,6},{8,9},{9,8},{10,11... | collective-permute-start | bytes 49160 | tf_op jit(solution)/shard_map/ppermute | solution.py:433
  82.2 0.6 shard_map.115
  82.7 1.9 %collective-permute-done.4.peer_ref = f32[32,128]{1,0:T(8,128)S(1)} collective-permute-done((f32[32,128]{1,0:T(8,128)S(1)}, f32[32,128]{1,0:T(8,128)S(1)}, u32[]{:S(2)}, u32[]{:S(2)}) %collective-permute-start.4) | collective-permute-done | bytes 16416 | tf_op jit(solution)/shard_map/ppermute | solution.py:433
  84.7 0.8 shard_map.116
  85.5 6.2 %all-to-all-done.4 = f32[128,1,384]{2,1,0:T(1,128)S(1)} async-done(((f32[128,1,384]{2,1,0:T(1,128)}), f32[128,1,384]{2,1,0:T(1,128)S(1)}, u32[]{:S(2)}, u32[]{:S(2)}) %all-to-all-start.4) | async-done | bytes 196640 | tf_op jit(solution)/shard_map/all_to_all | solution.py:427
  91.7 1.3 %shard_map.117 = (f32[128,128]{1,0:T(8,128)}, f32[8,128]{1,0:T(8,128)S(1)}) custom-call(f32[384,128]{1,0:T(8,128)S(1)} %bitcast.29, f32[256,128]{1,0:T(8,128)S(1)} %get-tuple-element.80.kept, f32[128,128]{1,0:T(8,128)S(1)} %get-tuple-element.49.refs_2_.cut_weight, f32[8,128]{1,0:T(8,128)S(1)} %get-tuple-element.52.net_weight, ...), custom_call_target="tpu_custom_call" | custom-call | flops 67108864 | bytes 1048576 | tf_op jit(solution)/shard_map/pallas_call | solution.py:411
  92.9 4.0 %all-to-all-start.5 = ((f32[128,1,128]{2,1,0:T(1,128)}), f32[128,1,128]{2,1,0:T(1,128)S(1)}, u32[]{:S(2)}, u32[]{:S(2)}) async-start(f32[128,1,128]{2,1,0:T(1,128)} %bitcast.22), calls=%async_computation.5 | async-start | bytes 131072 | tf_op jit(solution)/shard_map/all_to_all | solution.py:427
  97.0 1.5 %collective-permute-start.5 = (f32[32,128]{1,0:T(8,128)S(1)}, f32[32,128]{1,0:T(8,128)S(1)}, u32[]{:S(2)}, u32[]{:S(2)}) collective-permute-start(f32[32,128]{1,0:T(8,128)S(1)} %get-tuple-element.89), channel_id=1, source_target_pairs={{0,1},{1,0},{2,3},{3,2},{4,5},{5,4},{6,7},{7,6},{8,9},{9,8},{10,11... | collective-permute-start | bytes 49160 | tf_op jit(solution)/shard_map/ppermute | solution.py:433
  98.4 1.6 %shard_map.118.others = f32[32,128]{1,0:T(8,128)S(1)} custom-call(s32[128,128]{1,0:T(8,128)S(1)} %bitcast.38, f32[128,128]{1,0:T(8,128)S(1)} %get-tuple-element.49.refs_2_.cut_weight, f32[384,128]{1,0:T(8,128)S(1)} %bitcast.30, f32[32,128]{1,0:T(8,128)S(1)} %get-tuple-element.85.local_ref, f32[8,128]{1,0:T(8,128)S(1)} %get-tuple-element.88.sums_ref), custom_call_target="tpu_custom_call" | custom-call | flops 2147483648 | bytes 1048576 | tf_op jit(solution)/shard_map/pallas_call | solution.py:411
  100.0 0.1 collective-permute-done.5.back_ref
  100.1 6.8 %all-to-all-done.5 = f32[128,1,128]{2,1,0:T(1,128)S(1)} async-done(((f32[128,1,128]{2,1,0:T(1,128)}), f32[128,1,128]{2,1,0:T(1,128)S(1)}, u32[]{:S(2)}, u32[]{:S(2)}) %all-to-all-start.5) | async-done | bytes 65568 | tf_op jit(solution)/shard_map/all_to_all | solution.py:427
  106.9 1.2 %shard_map.119 = (f32[2,2048]{1,0:T(2,128)}, f32[2,2048]{1,0:T(2,128)}) custom-call(s32[32,128]{1,0:T(8,128)S(1)} %bitcast.48, f32[128,128]{1,0:T(8,128)S(1)} %bitcast.50, f32[16,128]{1,0:T(8,128)S(1)} %get-tuple-element.69.refs_0_.degree_in, f32[32,128]{1,0:T(8,128)S(1)} %shard_map.118.others, f32[32,128]{1,0:T(8,128)S(1)} %collective-permute-done.5.back_ref, ...), custom_call_target="tpu_custom_call" | custom-call | flops 67108864 | bytes 1048576 | tf_op jit(solution)/shard_map/pallas_call | solution.py:411
  (1 shorter events, 0.0 us)
Async XLA Ops:
  0.6 15.4 %copy-start.3 = (f32[16384]{0:T(1024)S(1)}, f32[16384]{0:T(1024)}, u32[]{:S(2)}) copy-start(f32[16384]{0:T(1024)} %param.17) | copy-start | bytes 196612
  0.6 15.4 %copy-start.4 = (s32[16,2]{0,1:T(2,128)S(1)}, s32[16,2]{0,1:T(2,128)}, u32[]{:S(2)}) copy-start(s32[16,2]{0,1:T(2,128)} %param.12) | copy-start | bytes 388
  0.7 16.6 %collective-permute-start = (f32[2,2048]{1,0:T(2,128)}, f32[2,2048]{1,0:T(2,128)S(1)}, u32[]{:S(2)}, u32[]{:S(2)}) collective-permute-start(f32[2,2048]{1,0:T(2,128)} %right_hbm.1), channel_id=1, source_target_pairs={{0,1},{1,0},{2,3},{3,2},{4,5},{5,4},{6,7},{7,6},{8,9},{9,8},{10,11... | collective-permute-start | bytes 49160 | tf_op jit(solution)/shard_map/ppermute | solution.py:433
  5.3 21.4 %all-to-all-start = ((f32[128,1,384]{2,1,0:T(1,128)}), f32[128,1,384]{2,1,0:T(1,128)S(1)}, u32[]{:S(2)}, u32[]{:S(2)}) async-start(f32[128,1,384]{2,1,0:T(1,128)} %bitcast.5), calls=%async_computation | async-start | bytes 393216 | tf_op jit(solution)/shard_map/all_to_all | solution.py:427
  17.2 16.3 %copy-start = (s32[1,128,128]{2,1,0:T(8,128)S(1)}, s32[1,128,128]{2,1,0:T(8,128)}, u32[]{:S(2)}) copy-start(s32[1,128,128]{2,1,0:T(8,128)} %param.13) | copy-start | bytes 196612
  17.2 16.3 %copy-start.1 = (s32[4096]{0:T(1024)S(1)}, s32[4096]{0:T(1024)}, u32[]{:S(2)}) copy-start(s32[4096]{0:T(1024)} %param.16) | copy-start | bytes 49156
  17.3 16.3 %copy-start.2 = (s32[4096]{0:T(1024)S(1)}, s32[4096]{0:T(1024)}, u32[]{:S(2)}) copy-start(s32[4096]{0:T(1024)} %param.15) | copy-start | bytes 49156
  28.1 13.9 %all-to-all-start.1 = ((f32[128,1,128]{2,1,0:T(1,128)}), f32[128,1,128]{2,1,0:T(1,128)S(1)}, u32[]{:S(2)}, u32[]{:S(2)}) async-start(f32[128,1,128]{2,1,0:T(1,128)} %bitcast.12), calls=%async_computation.1 | async-start | bytes 131072 | tf_op jit(solution)/shard_map/all_to_all | solution.py:427
  32.1 3.5 %collective-permute-start.1 = (f32[48,128]{1,0:T(8,128)S(1)}, f32[48,128]{1,0:T(8,128)S(1)}, u32[]{:S(2)}, u32[]{:S(2)}) collective-permute-start(f32[48,128]{1,0:T(8,128)S(1)} %get-tuple-element.64), channel_id=1, source_target_pairs={{0,1},{1,0},{2,3},{3,2},{4,5},{5,4},{6,7},{7,6},{8,9},{9,8},{10,11... | collective-permute-start | bytes 73736 | tf_op jit(solution)/shard_map/ppermute | solution.py:433
  44.1 15.1 %all-to-all-start.2 = ((f32[128,1,384]{2,1,0:T(1,128)}), f32[128,1,384]{2,1,0:T(1,128)S(1)}, u32[]{:S(2)}, u32[]{:S(2)}) async-start(f32[128,1,384]{2,1,0:T(1,128)} %bitcast.14), calls=%async_computation.2 | async-start | bytes 393216 | tf_op jit(solution)/shard_map/all_to_all | solution.py:427
  48.3 3.9 %collective-permute-start.2 = (f32[32,128]{1,0:T(8,128)S(1)}, f32[32,128]{1,0:T(8,128)S(1)}, u32[]{:S(2)}, u32[]{:S(2)}) collective-permute-start(f32[32,128]{1,0:T(8,128)S(1)} %get-tuple-element.67.own_ref.start_ref), channel_id=1, source_target_pairs={{0,1},{1,0},{2,3},{3,2},{4,5},{5,4},{6,7},{7,6},{8,9},{9,8},{10,11... | collective-permute-start | bytes 49160 | tf_op jit(solution)/shard_map/ppermute | solution.py:433
  60.5 13.9 %all-to-all-start.3 = ((f32[128,1,128]{2,1,0:T(1,128)}), f32[128,1,128]{2,1,0:T(1,128)S(1)}, u32[]{:S(2)}, u32[]{:S(2)}) async-start(f32[128,1,128]{2,1,0:T(1,128)} %bitcast.17), calls=%async_computation.3 | async-start | bytes 131072 | tf_op jit(solution)/shard_map/all_to_all | solution.py:427
  64.5 3.3 %collective-permute-start.3 = (f32[32,128]{1,0:T(8,128)S(1)}, f32[32,128]{1,0:T(8,128)S(1)}, u32[]{:S(2)}, u32[]{:S(2)}) collective-permute-start(f32[32,128]{1,0:T(8,128)S(1)} %get-tuple-element.76), channel_id=1, source_target_pairs={{0,1},{1,0},{2,3},{3,2},{4,5},{5,4},{6,7},{7,6},{8,9},{9,8},{10,11... | collective-permute-start | bytes 49160 | tf_op jit(solution)/shard_map/ppermute | solution.py:433
  76.6 15.1 %all-to-all-start.4 = ((f32[128,1,384]{2,1,0:T(1,128)}), f32[128,1,384]{2,1,0:T(1,128)S(1)}, u32[]{:S(2)}, u32[]{:S(2)}) async-start(f32[128,1,384]{2,1,0:T(1,128)} %bitcast.19), calls=%async_computation.4 | async-start | bytes 393216 | tf_op jit(solution)/shard_map/all_to_all | solution.py:427
  80.7 3.9 %collective-permute-start.4 = (f32[32,128]{1,0:T(8,128)S(1)}, f32[32,128]{1,0:T(8,128)S(1)}, u32[]{:S(2)}, u32[]{:S(2)}) collective-permute-start(f32[32,128]{1,0:T(8,128)S(1)} %get-tuple-element.81.own_ref.start_ref), channel_id=1, source_target_pairs={{0,1},{1,0},{2,3},{3,2},{4,5},{5,4},{6,7},{7,6},{8,9},{9,8},{10,11... | collective-permute-start | bytes 49160 | tf_op jit(solution)/shard_map/ppermute | solution.py:433
  92.9 13.9 %all-to-all-start.5 = ((f32[128,1,128]{2,1,0:T(1,128)}), f32[128,1,128]{2,1,0:T(1,128)S(1)}, u32[]{:S(2)}, u32[]{:S(2)}) async-start(f32[128,1,128]{2,1,0:T(1,128)} %bitcast.22), calls=%async_computation.5 | async-start | bytes 131072 | tf_op jit(solution)/shard_map/all_to_all | solution.py:427
  97.0 3.1 %collective-permute-start.5 = (f32[32,128]{1,0:T(8,128)S(1)}, f32[32,128]{1,0:T(8,128)S(1)}, u32[]{:S(2)}, u32[]{:S(2)}) collective-permute-start(f32[32,128]{1,0:T(8,128)S(1)} %get-tuple-element.89), channel_id=1, source_target_pairs={{0,1},{1,0},{2,3},{3,2},{4,5},{5,4},{6,7},{7,6},{8,9},{9,8},{10,11... | collective-permute-start | bytes 49160 | tf_op jit(solution)/shard_map/ppermute | solution.py:433

commit v6 on v5

--- a/solution.py
+++ b/solution.py
@@ -215,11 +215,7 @@
 
 def forward_kernel(first, own_ref, peer_ref, side, nbr, blocks, before_ref, *refs):
     if first:
-        ones_ref, anchor, cut_weight, kept, local_ref, share_ref, far, got, names, peers = refs
-        for v in range(2):
-            for t in range(TILES):
-                peers[TILES * v + t : TILES * v + t + 1, :] = peer_ref[v : v + 1, LANES * t : LANES * (t + 1)]
-        peer_ref = peers
+        ones_ref, anchor, cut_weight, kept, local_ref, share_ref, far, got, names = refs
     else:
         degree, local_ref, share_ref, far, got, names = refs
     upper = side[0:1, :] > 0.5
@@ -443,7 +439,6 @@
     place = jnp.stack([coord, lax.axis_index("region") * 2 + coord]).astype(I32)
     side = jnp.full((8, LANES), coord).astype(F32)
     nbr = tile_nbr.T
-    peer = swap(right_side)
     send, residual, kept, blocks, cut_weight, anchor = call(
         first_kernel,
         [(384, LANES), (32, LANES), (256, LANES), blocks.shape, (LANES, LANES), (TILES, LANES)],
@@ -461,8 +456,7 @@
     for iteration in range(ITERS):
         first, last = iteration == 0, iteration == ITERS - 1
         got = exchange(send, 3)
-        if not first:
-            peer = swap(residual)
+        peer = swap(residual)
         rows = 48 if first else 32
         scratch = [(256, LANES), (128, LANES), pltpu.VMEM((8, LANES), I32)]
         local_sum, back, *more = call(
@@ -478,7 +472,7 @@
         local_sum, share = call(
             functools.partial(forward_kernel, first),
             [(rows, LANES), (8, LANES)],
-            scratch + [(32, LANES)] * first,
+            scratch,
             FORWARD_COST,
             (residual, peer, side, nbr, blocks, local_sum)
             + ((ones, anchor, cut_weight, kept) if first else (degree,)),

time: 108 us -> 107 us (level)
  waiting for transfers between devices: 44.7 us -> 43.5 us
    all_to_all x6, waiting for transfers between devices: 40.8 us -> 38.4 us  [exchange(): lax.all_to_all(rows.reshape(LANES, 1, height * LANES), AXES, split_axis=0...]
    ppermute x6, waiting for transfers between devices: 3.91 us -> 5.15 us  [swap(): return lax.ppermute(x, 'coord', [(0, 1), (1, 0)])]
  transfers between devices with their start and end apart: 12 -> 12, of which waited for: 9 -> 10; matrix products, arithmetic and copies ran while one was open for 0% -> 0% of each run, Pallas kernels for 12% -> 9%
where the time goes in v6:
time: 107 us
  waiting for transfers between devices  43.5 us (41%)
  starting transfers between devices  40.8 us (38%)
  Pallas kernels  21.8 us (20%)
    all_to_all x6, waiting for transfers between devices, exchange(): lax.all_to_all(rows.reshape(LANES, 1, height * LANES), AXES, split_axis=0...  38.4 us
    all_to_all x6, starting transfers between devices, exchange(): lax.all_to_all(rows.reshape(LANES, 1, height * LANES), AXES, split_axis=0...  31.8 us
    pallas_call x16, Pallas kernels, call(): pl.pallas_call(kernel, out_shape=[jax.ShapeDtypeStruct(s, F32) for s in s...  21.8 us
    ppermute x6, starting transfers between devices, swap(): return lax.ppermute(x, 'coord', [(0, 1), (1, 0)])  8.97 us
    ppermute x6, waiting for transfers between devices, swap(): return lax.ppermute(x, 'coord', [(0, 1), (1, 0)])  5.15 us
  transfers between devices with their start and end apart: 12, of which 10 were waited for; matrix products, arithmetic and copies ran while one was open for 0% of the time, Pallas kernels for 9%

profile of v6, /device:TPU:1, one launch (start us, length us, event | category | flops | bytes accessed | tf_op | source)
XLA Modules:
  0.0 107.0 jit_solution(622844610688733125)
XLA Ops:
  0.6 0.0 copy-start.3
  0.6 0.0 copy-start.4
  0.7 2.6 %shard_map.104 = (f32[384,128]{1,0:T(8,128)}, f32[32,128]{1,0:T(8,128)S(1)}, f32[256,128]{1,0:T(8,128)S(1)}, f32[16,2,128,128]{3,2,1,0:T(8,128)S(1)}, f32[128,128]{1,0:T(8,128)S(1)}, /*index=5*/f32[16,128]{1,0:T(8,128)S(1)}) custom-call(f32[2,2048]{1,0:T(2,128)} %right_hbm.1, s32[128,128]{1,0:T(8,128)} %bitcast.33, s32[32,128]{1,0:T(8,128)} %bitcast.44, ...), custom_call_target="tpu_custom_call" | custom-call | flops 16777216 | bytes 1048576 | tf_op jit(solution)/shard_map/pallas_call | solution.py:407
  3.2 11.5 %all-to-all-start = ((f32[128,1,384]{2,1,0:T(1,128)}), f32[128,1,384]{2,1,0:T(1,128)S(1)}, u32[]{:S(2)}, u32[]{:S(2)}) async-start(f32[128,1,384]{2,1,0:T(1,128)} %bitcast.5), calls=%async_computation | async-start | bytes 393216 | tf_op jit(solution)/shard_map/all_to_all | solution.py:423
  14.7 1.5 %collective-permute-start = (f32[32,128]{1,0:T(8,128)S(1)}, f32[32,128]{1,0:T(8,128)S(1)}, u32[]{:S(2)}, u32[]{:S(2)}) collective-permute-start(f32[32,128]{1,0:T(8,128)S(1)} %get-tuple-element.50.own_ref.start_ref), channel_id=1, source_target_pairs={{0,1},{1,0},{2,3},{3,2},{4,5},{5,4},{6,7},{7,6},{8,9},{9,8},{10,11... | collective-permute-start | bytes 49160 | tf_op jit(solution)/shard_map/ppermute | solution.py:429
  16.2 0.1 pad_add_fusion.refs_0_
  16.3 0.0 copy-done.3
  16.3 0.0 copy-done.4
  16.3 1.1 %shard_map.105 = (f32[48,128]{1,0:T(8,128)S(1)}, f32[48,128]{1,0:T(8,128)S(1)}, f32[32,128]{1,0:T(8,128)S(1)}, f32[8,128]{1,0:T(8,128)S(1)}) custom-call(f32[32,128]{1,0:T(8,128)S(1)} %get-tuple-element.50.own_ref.start_ref, f32[8,128]{1,0:T(8,128)S(1)} %broadcast_in_dim.3.side, s32[2,16]{1,0:T(2,128)S(1)} %bitcast.53, ...), custom_call_target="tpu_custom_call" | custom-call | flops 1073741824 | bytes 1048576 | tf_op jit(solution)/shard_map/pallas_call | solution.py:407
  17.4 1.2 %collective-permute-done.peer_ref = f32[32,128]{1,0:T(8,128)S(1)} collective-permute-done((f32[32,128]{1,0:T(8,128)S(1)}, f32[32,128]{1,0:T(8,128)S(1)}, u32[]{:S(2)}, u32[]{:S(2)}) %collective-permute-start) | collective-permute-done | bytes 16416 | tf_op jit(solution)/shard_map/ppermute | solution.py:429
  18.7 0.0 copy-start
  18.7 0.0 copy-start.1
  18.7 0.0 copy-start.2
  18.7 0.9 shard_map.106
  19.5 6.2 %all-to-all-done = f32[128,1,384]{2,1,0:T(1,128)S(1)} async-done(((f32[128,1,384]{2,1,0:T(1,128)}), f32[128,1,384]{2,1,0:T(1,128)S(1)}, u32[]{:S(2)}, u32[]{:S(2)}) %all-to-all-start) | async-done | bytes 196640 | tf_op jit(solution)/shard_map/all_to_all | solution.py:423
  25.7 1.3 %shard_map.107 = (f32[128,128]{1,0:T(8,128)}, f32[8,128]{1,0:T(8,128)S(1)}) custom-call(f32[384,128]{1,0:T(8,128)S(1)} %bitcast.27, f32[256,128]{1,0:T(8,128)S(1)} %get-tuple-element.48.refs_3_.kept, f32[128,128]{1,0:T(8,128)S(1)} %get-tuple-element.49.refs_2_.cut_weight, f32[8,128]{1,0:T(8,128)S(1)} %get-tuple-element.52.net_weight, ...), custom_call_target="tpu_custom_call" | custom-call | flops 67108864 | bytes 1048576 | tf_op jit(solution)/shard_map/pallas_call | solution.py:407
  27.0 4.0 %all-to-all-start.1 = ((f32[128,1,128]{2,1,0:T(1,128)}), f32[128,1,128]{2,1,0:T(1,128)S(1)}, u32[]{:S(2)}, u32[]{:S(2)}) async-start(f32[128,1,128]{2,1,0:T(1,128)} %bitcast.12), calls=%async_computation.1 | async-start | bytes 131072 | tf_op jit(solution)/shard_map/all_to_all | solution.py:423
  31.0 1.5 %collective-permute-start.1 = (f32[48,128]{1,0:T(8,128)S(1)}, f32[48,128]{1,0:T(8,128)S(1)}, u32[]{:S(2)}, u32[]{:S(2)}) collective-permute-start(f32[48,128]{1,0:T(8,128)S(1)} %get-tuple-element.64), channel_id=1, source_target_pairs={{0,1},{1,0},{2,3},{3,2},{4,5},{5,4},{6,7},{7,6},{8,9},{9,8},{10,11... | collective-permute-start | bytes 73736 | tf_op jit(solution)/shard_map/ppermute | solution.py:429
  32.5 0.0 copy-done
  32.5 0.0 copy-done.1
  32.5 0.0 copy-done.2
  32.5 2.0 %shard_map.108 = (f32[32,128]{1,0:T(8,128)S(1)}, f32[16,128]{1,0:T(8,128)S(1)}) custom-call(s32[128,128]{1,0:T(8,128)S(1)} %bitcast.34, f32[128,128]{1,0:T(8,128)S(1)} %get-tuple-element.49.refs_2_.cut_weight, f32[384,128]{1,0:T(8,128)S(1)} %bitcast.28, f32[48,128]{1,0:T(8,128)S(1)} %get-tuple-element.58.local_ref, f32[8,128]{1,0:T(8,128)S(1)} %get-tuple-element.61.sums_ref, ...), custom_call_target="tpu_custom_call" | custom-call | flops 2147483648 | bytes 1048576 | tf_op jit(solution)/shard_map/pallas_call | solution.py:407
  34.5 0.0 collective-permute-done.1.back_ref
  34.5 6.4 %all-to-all-done.1 = f32[128,1,128]{2,1,0:T(1,128)S(1)} async-done(((f32[128,1,128]{2,1,0:T(1,128)}), f32[128,1,128]{2,1,0:T(1,128)S(1)}, u32[]{:S(2)}, u32[]{:S(2)}) %all-to-all-start.1) | async-done | bytes 65568 | tf_op jit(solution)/shard_map/all_to_all | solution.py:423
  40.9 2.1 %shard_map.109 = (f32[384,128]{1,0:T(8,128)}, f32[32,128]{1,0:T(8,128)S(1)}, f32[96,128]{1,0:T(8,128)S(1)}, f32[8,128]{1,0:T(8,128)S(1)}, f32[256,128]{1,0:T(8,128)S(1)}, /*index=5*/f32[16,128]{1,0:T(8,128)S(1)}) custom-call(s32[32,128]{1,0:T(8,128)S(1)} %bitcast.46, f32[128,128]{1,0:T(8,128)S(1)} %bitcast.49, f32[16,128]{1,0:T(8,128)S(1)} %get-tuple-element.62.degree_in, ...), custom_call_target="tpu_custom_call" | custom-call | flops 67108864 | bytes 1048576 | tf_op jit(solution)/shard_map/pallas_call | solution.py:407
  43.0 4.1 %all-to-all-start.2 = ((f32[128,1,384]{2,1,0:T(1,128)}), f32[128,1,384]{2,1,0:T(1,128)S(1)}, u32[]{:S(2)}, u32[]{:S(2)}) async-start(f32[128,1,384]{2,1,0:T(1,128)} %bitcast.14), calls=%async_computation.2 | async-start | bytes 393216 | tf_op jit(solution)/shard_map/all_to_all | solution.py:423
  47.2 1.5 %collective-permute-start.2 = (f32[32,128]{1,0:T(8,128)S(1)}, f32[32,128]{1,0:T(8,128)S(1)}, u32[]{:S(2)}, u32[]{:S(2)}) collective-permute-start(f32[32,128]{1,0:T(8,128)S(1)} %get-tuple-element.67.own_ref.start_ref), channel_id=1, source_target_pairs={{0,1},{1,0},{2,3},{3,2},{4,5},{5,4},{6,7},{7,6},{8,9},{9,8},{10,11... | collective-permute-start | bytes 49160 | tf_op jit(solution)/shard_map/ppermute | solution.py:429
  48.7 0.6 shard_map.110
  49.2 1.9 %collective-permute-done.2.peer_ref = f32[32,128]{1,0:T(8,128)S(1)} collective-permute-done((f32[32,128]{1,0:T(8,128)S(1)}, f32[32,128]{1,0:T(8,128)S(1)}, u32[]{:S(2)}, u32[]{:S(2)}) %collective-permute-start.2) | collective-permute-done | bytes 16416 | tf_op jit(solution)/shard_map/ppermute | solution.py:429
  51.1 0.8 shard_map.111
  52.0 6.2 %all-to-all-done.2 = f32[128,1,384]{2,1,0:T(1,128)S(1)} async-done(((f32[128,1,384]{2,1,0:T(1,128)}), f32[128,1,384]{2,1,0:T(1,128)S(1)}, u32[]{:S(2)}, u32[]{:S(2)}) %all-to-all-start.2) | async-done | bytes 196640 | tf_op jit(solution)/shard_map/all_to_all | solution.py:423
  58.1 1.3 %shard_map.112 = (f32[128,128]{1,0:T(8,128)}, f32[8,128]{1,0:T(8,128)S(1)}) custom-call(f32[384,128]{1,0:T(8,128)S(1)} %bitcast.31, f32[256,128]{1,0:T(8,128)S(1)} %get-tuple-element.66.kept, f32[128,128]{1,0:T(8,128)S(1)} %get-tuple-element.49.refs_2_.cut_weight, f32[8,128]{1,0:T(8,128)S(1)} %get-tuple-element.52.net_weight, ...), custom_call_target="tpu_custom_call" | custom-call | flops 67108864 | bytes 1048576 | tf_op jit(solution)/shard_map/pallas_call | solution.py:407
  59.4 4.0 %all-to-all-start.3 = ((f32[128,1,128]{2,1,0:T(1,128)}), f32[128,1,128]{2,1,0:T(1,128)S(1)}, u32[]{:S(2)}, u32[]{:S(2)}) async-start(f32[128,1,128]{2,1,0:T(1,128)} %bitcast.17), calls=%async_computation.3 | async-start | bytes 131072 | tf_op jit(solution)/shard_map/all_to_all | solution.py:423
  63.4 1.6 %collective-permute-start.3 = (f32[32,128]{1,0:T(8,128)S(1)}, f32[32,128]{1,0:T(8,128)S(1)}, u32[]{:S(2)}, u32[]{:S(2)}) collective-permute-start(f32[32,128]{1,0:T(8,128)S(1)} %get-tuple-element.76), channel_id=1, source_target_pairs={{0,1},{1,0},{2,3},{3,2},{4,5},{5,4},{6,7},{7,6},{8,9},{9,8},{10,11... | collective-permute-start | bytes 49160 | tf_op jit(solution)/shard_map/ppermute | solution.py:429
  65.1 1.6 %shard_map.113.others = f32[32,128]{1,0:T(8,128)S(1)} custom-call(s32[128,128]{1,0:T(8,128)S(1)} %bitcast.36, f32[128,128]{1,0:T(8,128)S(1)} %get-tuple-element.49.refs_2_.cut_weight, f32[384,128]{1,0:T(8,128)S(1)} %bitcast.32, f32[32,128]{1,0:T(8,128)S(1)} %get-tuple-element.72.local_ref, f32[8,128]{1,0:T(8,128)S(1)} %get-tuple-element.75.sums_ref), custom_call_target="tpu_custom_call" | custom-call | flops 2147483648 | bytes 1048576 | tf_op jit(solution)/shard_map/pallas_call | solution.py:407
  66.7 0.0 collective-permute-done.3.back_ref
  66.7 6.7 %all-to-all-done.3 = f32[128,1,128]{2,1,0:T(1,128)S(1)} async-done(((f32[128,1,128]{2,1,0:T(1,128)}), f32[128,1,128]{2,1,0:T(1,128)S(1)}, u32[]{:S(2)}, u32[]{:S(2)}) %all-to-all-start.3) | async-done | bytes 65568 | tf_op jit(solution)/shard_map/all_to_all | solution.py:423
  73.4 2.1 %shard_map.114 = (f32[384,128]{1,0:T(8,128)}, f32[32,128]{1,0:T(8,128)S(1)}, f32[96,128]{1,0:T(8,128)S(1)}, f32[8,128]{1,0:T(8,128)S(1)}, f32[256,128]{1,0:T(8,128)S(1)}) custom-call(s32[32,128]{1,0:T(8,128)S(1)} %bitcast.47, f32[128,128]{1,0:T(8,128)S(1)} %bitcast.39, f32[16,128]{1,0:T(8,128)S(1)} %get-tuple-element.69.refs_0_.degree_in, ...), custom_call_target="tpu_custom_call" | custom-call | flops 67108864 | bytes 1048576 | tf_op jit(solution)/shard_map/pallas_call | solution.py:407
  75.5 4.1 %all-to-all-start.4 = ((f32[128,1,384]{2,1,0:T(1,128)}), f32[128,1,384]{2,1,0:T(1,128)S(1)}, u32[]{:S(2)}, u32[]{:S(2)}) async-start(f32[128,1,384]{2,1,0:T(1,128)} %bitcast.19), calls=%async_computation.4 | async-start | bytes 393216 | tf_op jit(solution)/shard_map/all_to_all | solution.py:423
  79.6 1.5 %collective-permute-start.4 = (f32[32,128]{1,0:T(8,128)S(1)}, f32[32,128]{1,0:T(8,128)S(1)}, u32[]{:S(2)}, u32[]{:S(2)}) collective-permute-start(f32[32,128]{1,0:T(8,128)S(1)} %get-tuple-element.81.own_ref.start_ref), channel_id=1, source_target_pairs={{0,1},{1,0},{2,3},{3,2},{4,5},{5,4},{6,7},{7,6},{8,9},{9,8},{10,11... | collective-permute-start | bytes 49160 | tf_op jit(solution)/shard_map/ppermute | solution.py:429
  81.1 0.6 shard_map.115
  81.7 1.9 %collective-permute-done.4.peer_ref = f32[32,128]{1,0:T(8,128)S(1)} collective-permute-done((f32[32,128]{1,0:T(8,128)S(1)}, f32[32,128]{1,0:T(8,128)S(1)}, u32[]{:S(2)}, u32[]{:S(2)}) %collective-permute-start.4) | collective-permute-done | bytes 16416 | tf_op jit(solution)/shard_map/ppermute | solution.py:429
  83.6 0.8 shard_map.116
  84.4 6.2 %all-to-all-done.4 = f32[128,1,384]{2,1,0:T(1,128)S(1)} async-done(((f32[128,1,384]{2,1,0:T(1,128)}), f32[128,1,384]{2,1,0:T(1,128)S(1)}, u32[]{:S(2)}, u32[]{:S(2)}) %all-to-all-start.4) | async-done | bytes 196640 | tf_op jit(solution)/shard_map/all_to_all | solution.py:423
  90.6 1.3 %shard_map.117 = (f32[128,128]{1,0:T(8,128)}, f32[8,128]{1,0:T(8,128)S(1)}) custom-call(f32[384,128]{1,0:T(8,128)S(1)} %bitcast.29, f32[256,128]{1,0:T(8,128)S(1)} %get-tuple-element.80.kept, f32[128,128]{1,0:T(8,128)S(1)} %get-tuple-element.49.refs_2_.cut_weight, f32[8,128]{1,0:T(8,128)S(1)} %get-tuple-element.52.net_weight, ...), custom_call_target="tpu_custom_call" | custom-call | flops 67108864 | bytes 1048576 | tf_op jit(solution)/shard_map/pallas_call | solution.py:407
  91.9 4.0 %all-to-all-start.5 = ((f32[128,1,128]{2,1,0:T(1,128)}), f32[128,1,128]{2,1,0:T(1,128)S(1)}, u32[]{:S(2)}, u32[]{:S(2)}) async-start(f32[128,1,128]{2,1,0:T(1,128)} %bitcast.22), calls=%async_computation.5 | async-start | bytes 131072 | tf_op jit(solution)/shard_map/all_to_all | solution.py:423
  95.9 1.5 %collective-permute-start.5 = (f32[32,128]{1,0:T(8,128)S(1)}, f32[32,128]{1,0:T(8,128)S(1)}, u32[]{:S(2)}, u32[]{:S(2)}) collective-permute-start(f32[32,128]{1,0:T(8,128)S(1)} %get-tuple-element.89), channel_id=1, source_target_pairs={{0,1},{1,0},{2,3},{3,2},{4,5},{5,4},{6,7},{7,6},{8,9},{9,8},{10,11... | collective-permute-start | bytes 49160 | tf_op jit(solution)/shard_map/ppermute | solution.py:429
  97.4 1.6 %shard_map.118.others = f32[32,128]{1,0:T(8,128)S(1)} custom-call(s32[128,128]{1,0:T(8,128)S(1)} %bitcast.38, f32[128,128]{1,0:T(8,128)S(1)} %get-tuple-element.49.refs_2_.cut_weight, f32[384,128]{1,0:T(8,128)S(1)} %bitcast.30, f32[32,128]{1,0:T(8,128)S(1)} %get-tuple-element.85.local_ref, f32[8,128]{1,0:T(8,128)S(1)} %get-tuple-element.88.sums_ref), custom_call_target="tpu_custom_call" | custom-call | flops 2147483648 | bytes 1048576 | tf_op jit(solution)/shard_map/pallas_call | solution.py:407
  98.9 0.1 collective-permute-done.5.back_ref
  99.0 6.8 %all-to-all-done.5 = f32[128,1,128]{2,1,0:T(1,128)S(1)} async-done(((f32[128,1,128]{2,1,0:T(1,128)}), f32[128,1,128]{2,1,0:T(1,128)S(1)}, u32[]{:S(2)}, u32[]{:S(2)}) %all-to-all-start.5) | async-done | bytes 65568 | tf_op jit(solution)/shard_map/all_to_all | solution.py:423
  105.8 1.2 %shard_map.119 = (f32[2,2048]{1,0:T(2,128)}, f32[2,2048]{1,0:T(2,128)}) custom-call(s32[32,128]{1,0:T(8,128)S(1)} %bitcast.48, f32[128,128]{1,0:T(8,128)S(1)} %bitcast.50, f32[16,128]{1,0:T(8,128)S(1)} %get-tuple-element.69.refs_0_.degree_in, f32[32,128]{1,0:T(8,128)S(1)} %shard_map.118.others, f32[32,128]{1,0:T(8,128)S(1)} %collective-permute-done.5.back_ref, ...), custom_call_target="tpu_custom_call" | custom-call | flops 67108864 | bytes 1048576 | tf_op jit(solution)/shard_map/pallas_call | solution.py:407
  (1 shorter events, 0.0 us)
Async XLA Ops:
  0.6 15.6 %copy-start.3 = (f32[16384]{0:T(1024)S(1)}, f32[16384]{0:T(1024)}, u32[]{:S(2)}) copy-start(f32[16384]{0:T(1024)} %param.17) | copy-start | bytes 196612
  0.6 15.6 %copy-start.4 = (s32[16,2]{0,1:T(2,128)S(1)}, s32[16,2]{0,1:T(2,128)}, u32[]{:S(2)}) copy-start(s32[16,2]{0,1:T(2,128)} %param.12) | copy-start | bytes 388
  3.2 22.5 %all-to-all-start = ((f32[128,1,384]{2,1,0:T(1,128)}), f32[128,1,384]{2,1,0:T(1,128)S(1)}, u32[]{:S(2)}, u32[]{:S(2)}) async-start(f32[128,1,384]{2,1,0:T(1,128)} %bitcast.5), calls=%async_computation | async-start | bytes 393216 | tf_op jit(solution)/shard_map/all_to_all | solution.py:423
  14.7 3.9 %collective-permute-start = (f32[32,128]{1,0:T(8,128)S(1)}, f32[32,128]{1,0:T(8,128)S(1)}, u32[]{:S(2)}, u32[]{:S(2)}) collective-permute-start(f32[32,128]{1,0:T(8,128)S(1)} %get-tuple-element.50.own_ref.start_ref), channel_id=1, source_target_pairs={{0,1},{1,0},{2,3},{3,2},{4,5},{5,4},{6,7},{7,6},{8,9},{9,8},{10,11... | collective-permute-start | bytes 49160 | tf_op jit(solution)/shard_map/ppermute | solution.py:429
  18.7 13.8 %copy-start = (s32[1,128,128]{2,1,0:T(8,128)S(1)}, s32[1,128,128]{2,1,0:T(8,128)}, u32[]{:S(2)}) copy-start(s32[1,128,128]{2,1,0:T(8,128)} %param.13) | copy-start | bytes 196612
  18.7 13.8 %copy-start.1 = (s32[4096]{0:T(1024)S(1)}, s32[4096]{0:T(1024)}, u32[]{:S(2)}) copy-start(s32[4096]{0:T(1024)} %param.16) | copy-start | bytes 49156
  18.7 13.8 %copy-start.2 = (s32[4096]{0:T(1024)S(1)}, s32[4096]{0:T(1024)}, u32[]{:S(2)}) copy-start(s32[4096]{0:T(1024)} %param.15) | copy-start | bytes 49156
  27.0 13.9 %all-to-all-start.1 = ((f32[128,1,128]{2,1,0:T(1,128)}), f32[128,1,128]{2,1,0:T(1,128)S(1)}, u32[]{:S(2)}, u32[]{:S(2)}) async-start(f32[128,1,128]{2,1,0:T(1,128)} %bitcast.12), calls=%async_computation.1 | async-start | bytes 131072 | tf_op jit(solution)/shard_map/all_to_all | solution.py:423
  31.0 3.5 %collective-permute-start.1 = (f32[48,128]{1,0:T(8,128)S(1)}, f32[48,128]{1,0:T(8,128)S(1)}, u32[]{:S(2)}, u32[]{:S(2)}) collective-permute-start(f32[48,128]{1,0:T(8,128)S(1)} %get-tuple-element.64), channel_id=1, source_target_pairs={{0,1},{1,0},{2,3},{3,2},{4,5},{5,4},{6,7},{7,6},{8,9},{9,8},{10,11... | collective-permute-start | bytes 73736 | tf_op jit(solution)/shard_map/ppermute | solution.py:429
  43.0 15.1 %all-to-all-start.2 = ((f32[128,1,384]{2,1,0:T(1,128)}), f32[128,1,384]{2,1,0:T(1,128)S(1)}, u32[]{:S(2)}, u32[]{:S(2)}) async-start(f32[128,1,384]{2,1,0:T(1,128)} %bitcast.14), calls=%async_computation.2 | async-start | bytes 393216 | tf_op jit(solution)/shard_map/all_to_all | solution.py:423
  47.2 3.9 %collective-permute-start.2 = (f32[32,128]{1,0:T(8,128)S(1)}, f32[32,128]{1,0:T(8,128)S(1)}, u32[]{:S(2)}, u32[]{:S(2)}) collective-permute-start(f32[32,128]{1,0:T(8,128)S(1)} %get-tuple-element.67.own_ref.start_ref), channel_id=1, source_target_pairs={{0,1},{1,0},{2,3},{3,2},{4,5},{5,4},{6,7},{7,6},{8,9},{9,8},{10,11... | collective-permute-start | bytes 49160 | tf_op jit(solution)/shard_map/ppermute | solution.py:429
  59.4 13.9 %all-to-all-start.3 = ((f32[128,1,128]{2,1,0:T(1,128)}), f32[128,1,128]{2,1,0:T(1,128)S(1)}, u32[]{:S(2)}, u32[]{:S(2)}) async-start(f32[128,1,128]{2,1,0:T(1,128)} %bitcast.17), calls=%async_computation.3 | async-start | bytes 131072 | tf_op jit(solution)/shard_map/all_to_all | solution.py:423
  63.4 3.3 %collective-permute-start.3 = (f32[32,128]{1,0:T(8,128)S(1)}, f32[32,128]{1,0:T(8,128)S(1)}, u32[]{:S(2)}, u32[]{:S(2)}) collective-permute-start(f32[32,128]{1,0:T(8,128)S(1)} %get-tuple-element.76), channel_id=1, source_target_pairs={{0,1},{1,0},{2,3},{3,2},{4,5},{5,4},{6,7},{7,6},{8,9},{9,8},{10,11... | collective-permute-start | bytes 49160 | tf_op jit(solution)/shard_map/ppermute | solution.py:429
  75.5 15.1 %all-to-all-start.4 = ((f32[128,1,384]{2,1,0:T(1,128)}), f32[128,1,384]{2,1,0:T(1,128)S(1)}, u32[]{:S(2)}, u32[]{:S(2)}) async-start(f32[128,1,384]{2,1,0:T(1,128)} %bitcast.19), calls=%async_computation.4 | async-start | bytes 393216 | tf_op jit(solution)/shard_map/all_to_all | solution.py:423
  79.6 3.9 %collective-permute-start.4 = (f32[32,128]{1,0:T(8,128)S(1)}, f32[32,128]{1,0:T(8,128)S(1)}, u32[]{:S(2)}, u32[]{:S(2)}) collective-permute-start(f32[32,128]{1,0:T(8,128)S(1)} %get-tuple-element.81.own_ref.start_ref), channel_id=1, source_target_pairs={{0,1},{1,0},{2,3},{3,2},{4,5},{5,4},{6,7},{7,6},{8,9},{9,8},{10,11... | collective-permute-start | bytes 49160 | tf_op jit(solution)/shard_map/ppermute | solution.py:429
  91.9 13.9 %all-to-all-start.5 = ((f32[128,1,128]{2,1,0:T(1,128)}), f32[128,1,128]{2,1,0:T(1,128)S(1)}, u32[]{:S(2)}, u32[]{:S(2)}) async-start(f32[128,1,128]{2,1,0:T(1,128)} %bitcast.22), calls=%async_computation.5 | async-start | bytes 131072 | tf_op jit(solution)/shard_map/all_to_all | solution.py:423
  95.9 3.1 %collective-permute-start.5 = (f32[32,128]{1,0:T(8,128)S(1)}, f32[32,128]{1,0:T(8,128)S(1)}, u32[]{:S(2)}, u32[]{:S(2)}) collective-permute-start(f32[32,128]{1,0:T(8,128)S(1)} %get-tuple-element.89), channel_id=1, source_target_pairs={{0,1},{1,0},{2,3},{3,2},{4,5},{5,4},{6,7},{7,6},{8,9},{9,8},{10,11... | collective-permute-start | bytes 49160 | tf_op jit(solution)/shard_map/ppermute | solution.py:429

commit v7 on v6

--- a/solution.py
+++ b/solution.py
@@ -128,8 +128,8 @@
     return out
 
 
-def first_kernel(right_hbm, cells_hbm, pin_cell_hbm, pin_net_hbm, blocks_hbm, weight_hbm, anchor_hbm,
-                 send_ref, start_ref, kept_ref, blocks_ref, weight_ref, anchor_ref,
+def first_kernel(right_hbm, cells_hbm, pin_cell_hbm, pin_net_hbm, weight_hbm, anchor_hbm, star_hbm, nbr_hbm,
+                 send_ref, start_ref, kept_ref, weight_ref, anchor_ref, star_ref, nbr_ref,
                  right_ref, cut_cells, pin_cell, pin_net, sems):
     copies = [
         pltpu.make_async_copy(source, target, sems.at[i])
@@ -141,7 +141,8 @@
                 (cells_hbm, cut_cells),
                 (weight_hbm, weight_ref),
                 (anchor_hbm, anchor_ref),
-                (blocks_hbm, blocks_ref),
+                (star_hbm, star_ref),
+                (nbr_hbm, nbr_ref),
             )
         )
     ]
@@ -303,7 +304,15 @@
         )
 
 
-def cut_kernel(first, cut_cells, cut_weight, got, local_ref, sums_ref, *refs):
+def put_hots(hot_ref, numbers):
+    columns = jnp.concatenate([numbers, numbers, numbers, numbers], axis=0).astype(F32).T
+    for j in range(32):
+        wide = jnp.broadcast_to(columns[:, j : j + 1], (LANES, LANES)).astype(I32)
+        hot = jnp.where(iota((LANES, LANES), 1) == wide, 1.0, 0.0)
+        hot_ref[LANES * j : LANES * (j + 1), :] = hot.astype(BF16)
+
+
+def cut_kernel(first, cut_cells, cut_weight, got, local_ref, sums_ref, pin_cell, *refs):
     del sums_ref
 
     def values(j):
@@ -314,10 +323,12 @@
 
     acc = add_rows(128, lambda j: cut_cells[j : j + 1, :], values)
     if not first:
-        (out_ref,) = refs
+        out_ref, cell_hot = refs
+        put_hots(cell_hot, pin_cell[...] & (LANES - 1))
         out_ref[...] = fold(acc, 2, 2) + local_ref[...]
         return
-    pin_cell, pin_net, star, anchor, out_ref, degree_ref, rows_ref, pins_ref = refs
+    pin_net, star, anchor, out_ref, cell_hot, degree_ref, rows_ref, pins_ref = refs
+    put_hots(cell_hot, pin_cell[...] & (LANES - 1))
     out_ref[...] = fold(acc[:64], 2, 2) + local_ref[0:32, :]
     net = pin_net[...] & (LANES - 1)
     for q in range(4):
@@ -337,7 +348,7 @@
     )
 
 
-def step_kernel(first, last, pin_cell, got, degree_in, others, back_ref, sums_ref, start_ref, *refs):
+def step_kernel(first, last, pin_cell, cell_hot, got, degree_in, others, back_ref, sums_ref, start_ref, *refs):
     refs = list(refs)
     state, old = (None, None) if first else (refs.pop(0), refs.pop(0))
     if last:
@@ -351,11 +362,15 @@
     for v in range(2):
         for i, part in enumerate(split2(dense(pin_rows, 32 * v))):
             pins[pl.ds(32 * (2 * i + v), 32), :] = part
-    acc = add_rows(
-        32,
-        lambda j: pin_cell[j : j + 1, :],
-        lambda j: [pins[32 * i + j : 32 * i + j + 1, :] for i in range(4)],
-    )
+    acc = None
+    for j in range(0, 32, 2):
+        masked = []
+        for k in (j, j + 1):
+            here = iota((TILES, LANES), 0) == (pin_cell[k : k + 1, :] >> 7)
+            values = [pins[32 * i + k : 32 * i + k + 1, :] for i in range(4)]
+            masked.append(jnp.concatenate([jnp.where(here, v, 0.0) for v in values], axis=0).astype(BF16))
+        part = dot_nn(jnp.concatenate(masked, axis=1), cell_hot[LANES * j : LANES * (j + 2), :])
+        acc = part if acc is None else acc + part
     removed = fold(acc, 2, 2) + others[...] + back_ref[0:32, :]
     degree = degree_in[...]
     if first:
@@ -406,7 +421,7 @@
 def call(kernel, shapes, scratch, cost, args, spaces=()):
     return pl.pallas_call(
         kernel,
-        out_shape=[jax.ShapeDtypeStruct(s, F32) for s in shapes],
+        out_shape=[jax.ShapeDtypeStruct(s, F32) if isinstance(s, tuple) else s for s in shapes],
         in_specs=list(spaces) + [VMEM] * (len(args) - len(spaces)),
         out_specs=[VMEM] * len(shapes),
         scratch_shapes=[pltpu.VMEM(s, F32) if isinstance(s, tuple) else s for s in scratch],
@@ -439,20 +454,22 @@
     place = jnp.stack([coord, lax.axis_index("region") * 2 + coord]).astype(I32)
     side = jnp.full((8, LANES), coord).astype(F32)
     nbr = tile_nbr.T
-    send, residual, kept, blocks, cut_weight, anchor = call(
+    send, residual, kept, cut_weight, anchor, star, nbr = call(
         first_kernel,
-        [(384, LANES), (32, LANES), (256, LANES), blocks.shape, (LANES, LANES), (TILES, LANES)],
+        [(384, LANES), (32, LANES), (256, LANES), (LANES, LANES), (TILES, LANES), (LANES, LANES),
+         jax.ShapeDtypeStruct(nbr.shape, I32)],
         [
             (2, TILES * LANES),
             pltpu.VMEM((128, LANES), I32),
             pltpu.VMEM((32, LANES), I32),
             pltpu.VMEM((32, LANES), I32),
-            pltpu.SemaphoreType.DMA((7,)),
+            pltpu.SemaphoreType.DMA((8,)),
         ],
         1 << 24,
-        tuple(stay(x) for x in (right_side, cut_cells, pin_cell, pin_net, blocks, cut_weight, anchor)),
-        [HBM] * 7,
+        tuple(stay(x) for x in (right_side, cut_cells, pin_cell, pin_net, cut_weight, anchor, star, nbr)),
+        [HBM] * 8,
     )
+    hots = jax.ShapeDtypeStruct((32 * LANES, LANES), BF16)
     for iteration in range(ITERS):
         first, last = iteration == 0, iteration == ITERS - 1
         got = exchange(send, 3)
@@ -487,18 +504,20 @@
         returned = exchange(out, 1)
         back, sums = lax.optimization_barrier((back, sums))
         back = swap(back)
-        args = (cut_cells, cut_weight, got, local_sum, sums)
-        if first:
-            others, degree = call(
+        args = (cut_cells, cut_weight, got, local_sum, sums, pin_cell)
+        if first:
+            others, cell_hot, degree = call(
                 functools.partial(cut_kernel, True),
-                [(32, LANES), (16, LANES)],
+                [(32, LANES), hots, (16, LANES)],
                 [(128, LANES), (96, LANES)],
                 1 << 31,
-                args + (pin_cell, pin_net, star, anchor),
+                args + (pin_net, star, anchor),
             )
         else:
-            others = call(functools.partial(cut_kernel, False), [(32, LANES)], [], 1 << 31, args)[0]
-        args = (pin_cell, returned, degree, others, back, sums, residual)
+            others, cell_hot = call(
+                functools.partial(cut_kernel, False), [(32, LANES), hots], [], 1 << 31, args
+            )
+        args = (pin_cell, cell_hot, returned, degree, others, back, sums, residual)
         if not first:
             args = args + (state, old)
         if last:

time: 107 us -> 107 us (level)
  waiting for transfers between devices: 43.5 us -> 37.6 us
  local copies, waits for them, and re-layouts: 0.02 us -> 5.21 us
    unnamed x10 -> x14, local copies, waits for them, and re-layouts: 0.02 us -> 5.21 us
    ppermute x6, waiting for transfers between devices: 5.15 us -> 0.64 us  [swap(): return lax.ppermute(x, 'coord', [(0, 1), (1, 0)])]
    all_to_all x6, waiting for transfers between devices: 38.4 us -> 37 us  [exchange(): lax.all_to_all(rows.reshape(LANES, 1, height * LANES), AXES, split_axis=0...]
  transfers between devices with their start and end apart: 12 -> 12, of which waited for: 10 -> 8; matrix products, arithmetic and copies ran while one was open for 0% -> 0% of each run, Pallas kernels for 9% -> 10%
where the time goes in v7:
time: 107 us
  starting transfers between devices  41 us (38%)
  waiting for transfers between devices  37.6 us (35%)
  Pallas kernels  21.9 us (20%)
  local copies, waits for them, and re-layouts  5.21 us (5%)
    all_to_all x6, waiting for transfers between devices, exchange(): lax.all_to_all(rows.reshape(LANES, 1, height * LANES), AXES, split_axis=0...  37 us
    all_to_all x6, starting transfers between devices, exchange(): lax.all_to_all(rows.reshape(LANES, 1, height * LANES), AXES, split_axis=0...  32 us
    pallas_call x16, Pallas kernels, call(): pl.pallas_call(kernel, out_shape=[jax.ShapeDtypeStruct(s, F32) if isinsta...  21.9 us
    ppermute x6, starting transfers between devices, swap(): return lax.ppermute(x, 'coord', [(0, 1), (1, 0)])  8.97 us
    unnamed x14, local copies, waits for them, and re-layouts  5.21 us
  transfers between devices with their start and end apart: 12, of which 8 were waited for; matrix products, arithmetic and copies ran while one was open for 0% of the time, Pallas kernels for 10%

profile of v7, /device:TPU:1, one launch (start us, length us, event | category | flops | bytes accessed | tf_op | source)
XLA Modules:
  0.0 106.6 jit_solution(3137117042019117375)
XLA Ops:
  0.6 2.5 %shard_map.104 = (f32[384,128]{1,0:T(8,128)}, f32[32,128]{1,0:T(8,128)S(1)}, f32[256,128]{1,0:T(8,128)S(1)}, f32[128,128]{1,0:T(8,128)S(1)}, f32[16,128]{1,0:T(8...) custom-call(f32[2,2048]{1,0:T(2,128)} %right_hbm.1, s32[128,128]{1,0:T(8,128)} %bitcast.33, s32[32,128]{1,0:T(8,128)} %bitcast.39, ...), custom_call_target="tpu_custom_call" | custom-call | flops 16777216 | bytes 1048576 | tf_op jit(solution)/shard_map/pallas_call | solution.py:422
  3.2 11.5 %all-to-all-start = ((f32[128,1,384]{2,1,0:T(1,128)}), f32[128,1,384]{2,1,0:T(1,128)S(1)}, u32[]{:S(2)}, u32[]{:S(2)}) async-start(f32[128,1,384]{2,1,0:T(1,128)} %bitcast.7), calls=%async_computation | async-start | bytes 393216 | tf_op jit(solution)/shard_map/all_to_all | solution.py:438
  14.7 1.5 %collective-permute-start = (f32[32,128]{1,0:T(8,128)S(1)}, f32[32,128]{1,0:T(8,128)S(1)}, u32[]{:S(2)}, u32[]{:S(2)}) collective-permute-start(f32[32,128]{1,0:T(8,128)S(1)} %get-tuple-element.55.own_ref.start_ref), channel_id=1, source_target_pairs={{0,1},{1,0},{2,3},{3,2},{4,5},{5,4},{6,7},{7,6},{8,9},{9,8},{10,11... | collective-permute-start | bytes 49160 | tf_op jit(solution)/shard_map/ppermute | solution.py:444
  16.1 0.1 pad_add_fusion.refs_0_
  16.2 0.0 copy-start.3
  16.2 1.6 %copy-done.3 = f32[16,2,128,128]{3,2,1,0:T(8,128)S(1)} copy-done((f32[16,2,128,128]{3,2,1,0:T(8,128)S(1)}, f32[16,2,128,128]{3,2,1,0:T(8,128)}, u32[]{:S(2)}) %copy-start.3) | copy-done | bytes 2097176
  17.8 0.0 copy-start.4
  17.8 1.1 %shard_map.105 = (f32[48,128]{1,0:T(8,128)S(1)}, f32[48,128]{1,0:T(8,128)S(1)}, f32[32,128]{1,0:T(8,128)S(1)}, f32[8,128]{1,0:T(8,128)S(1)}) custom-call(f32[32,128]{1,0:T(8,128)S(1)} %get-tuple-element.55.own_ref.start_ref, f32[8,128]{1,0:T(8,128)S(1)} %broadcast_in_dim.3.side, s32[2,16]{1,0:T(2,128)S(1)} %get-tuple-element.56.nbr, ...), custom_call_target="tpu_custom_call" | custom-call | flops 1073741824 | bytes 1048576 | tf_op jit(solution)/shard_map/pallas_call | solution.py:422
  19.0 0.0 collective-permute-done.peer_ref
  19.0 0.4 copy-done.4
  19.4 0.0 copy-start
  19.4 0.0 copy-start.1
  19.4 0.0 copy-start.2
  19.4 0.9 shard_map.106
  20.3 5.4 %all-to-all-done = f32[128,1,384]{2,1,0:T(1,128)S(1)} async-done(((f32[128,1,384]{2,1,0:T(1,128)}), f32[128,1,384]{2,1,0:T(1,128)S(1)}, u32[]{:S(2)}, u32[]{:S(2)}) %all-to-all-start) | async-done | bytes 196640 | tf_op jit(solution)/shard_map/all_to_all | solution.py:438
  25.6 1.3 %shard_map.107 = (f32[128,128]{1,0:T(8,128)}, f32[8,128]{1,0:T(8,128)S(1)}) custom-call(f32[384,128]{1,0:T(8,128)S(1)} %bitcast.27, f32[256,128]{1,0:T(8,128)S(1)} %get-tuple-element.61.refs_3_.kept, f32[128,128]{1,0:T(8,128)S(1)} %get-tuple-element.53.refs_2_.cut_weight, f32[8,128]{1,0:T(8,128)S(1)} %get-tuple-element.64.net_weight, ...), custom_call_target="tpu_custom_call" | custom-call | flops 67108864 | bytes 1048576 | tf_op jit(solution)/shard_map/pallas_call | solution.py:422
  26.9 4.2 %all-to-all-start.1 = ((f32[128,1,128]{2,1,0:T(1,128)}), f32[128,1,128]{2,1,0:T(1,128)S(1)}, u32[]{:S(2)}, u32[]{:S(2)}) async-start(f32[128,1,128]{2,1,0:T(1,128)} %bitcast.12), calls=%async_computation.1 | async-start | bytes 131072 | tf_op jit(solution)/shard_map/all_to_all | solution.py:438
  31.2 1.5 %collective-permute-start.1 = (f32[48,128]{1,0:T(8,128)S(1)}, f32[48,128]{1,0:T(8,128)S(1)}, u32[]{:S(2)}, u32[]{:S(2)}) collective-permute-start(f32[48,128]{1,0:T(8,128)S(1)} %get-tuple-element.72), channel_id=1, source_target_pairs={{0,1},{1,0},{2,3},{3,2},{4,5},{5,4},{6,7},{7,6},{8,9},{9,8},{10,11... | collective-permute-start | bytes 73736 | tf_op jit(solution)/shard_map/ppermute | solution.py:444
  32.6 0.0 copy-done
  32.6 0.0 copy-done.1
  32.6 0.0 copy-done.2
  32.6 2.2 %shard_map.108 = (f32[32,128]{1,0:T(8,128)S(1)}, bf16[4096,128]{1,0:T(8,128)(2,1)S(1)}, f32[16,128]{1,0:T(8,128)S(1)}) custom-call(s32[128,128]{1,0:T(8,128)S(1)} %bitcast.34, f32[128,128]{1,0:T(8,128)S(1)} %get-tuple-element.53.refs_2_.cut_weight, f32[384,128]{1,0:T(8,128)S(1)} %bitcast.28, f32[48,128]{1,0:T(8,128)S(1)} %get-tuple-element.62.local_ref, ...), custom_call_target="tpu_custom_call" | custom-call | flops 2147483648 | bytes 1048576 | tf_op jit(solution)/shard_map/pallas_call | solution.py:422
  34.8 0.0 collective-permute-done.1.back_ref
  34.9 6.2 %all-to-all-done.1 = f32[128,1,128]{2,1,0:T(1,128)S(1)} async-done(((f32[128,1,128]{2,1,0:T(1,128)}), f32[128,1,128]{2,1,0:T(1,128)S(1)}, u32[]{:S(2)}, u32[]{:S(2)}) %all-to-all-start.1) | async-done | bytes 65568 | tf_op jit(solution)/shard_map/all_to_all | solution.py:438
  41.1 1.9 %shard_map.109 = (f32[384,128]{1,0:T(8,128)}, f32[32,128]{1,0:T(8,128)S(1)}, f32[96,128]{1,0:T(8,128)S(1)}, f32[8,128]{1,0:T(8,128)S(1)}, f32[256,128]{1,0:T(8,128)S(1)}, /*index=5*/f32[16,128]{1,0:T(8,128)S(1)}) custom-call(s32[32,128]{1,0:T(8,128)S(1)} %bitcast.41, bf16[4096,128]{1,0:T(8,128)(2,1)S(1)} %get-tuple-element.68.cell_hot, ...), custom_call_target="tpu_custom_call" | custom-call | flops 67108864 | bytes 1048576 | tf_op jit(solution)/shard_map/pallas_call | solution.py:422
  43.0 4.1 %all-to-all-start.2 = ((f32[128,1,384]{2,1,0:T(1,128)}), f32[128,1,384]{2,1,0:T(1,128)S(1)}, u32[]{:S(2)}, u32[]{:S(2)}) async-start(f32[128,1,384]{2,1,0:T(1,128)} %bitcast.14), calls=%async_computation.2 | async-start | bytes 393216 | tf_op jit(solution)/shard_map/all_to_all | solution.py:438
  47.1 1.5 %collective-permute-start.2 = (f32[32,128]{1,0:T(8,128)S(1)}, f32[32,128]{1,0:T(8,128)S(1)}, u32[]{:S(2)}, u32[]{:S(2)}) collective-permute-start(f32[32,128]{1,0:T(8,128)S(1)} %get-tuple-element.74.own_ref.start_ref), channel_id=1, source_target_pairs={{0,1},{1,0},{2,3},{3,2},{4,5},{5,4},{6,7},{7,6},{8,9},{9,8},{10,11... | collective-permute-start | bytes 49160 | tf_op jit(solution)/shard_map/ppermute | solution.py:444
  48.6 0.0 copy-start.5
  48.6 1.6 %copy-done.5 = f32[16,2,128,128]{3,2,1,0:T(8,128)S(1)} copy-done((f32[16,2,128,128]{3,2,1,0:T(8,128)S(1)}, f32[16,2,128,128]{3,2,1,0:T(8,128)}, u32[]{:S(2)}) %copy-start.5) | copy-done | bytes 2097176
  50.2 0.6 shard_map.110
  50.8 0.3 collective-permute-done.2.peer_ref
  51.1 0.8 shard_map.111
  51.9 6.2 %all-to-all-done.2 = f32[128,1,384]{2,1,0:T(1,128)S(1)} async-done(((f32[128,1,384]{2,1,0:T(1,128)}), f32[128,1,384]{2,1,0:T(1,128)S(1)}, u32[]{:S(2)}, u32[]{:S(2)}) %all-to-all-start.2) | async-done | bytes 196640 | tf_op jit(solution)/shard_map/all_to_all | solution.py:438
  58.1 1.3 %shard_map.112 = (f32[128,128]{1,0:T(8,128)}, f32[8,128]{1,0:T(8,128)S(1)}) custom-call(f32[384,128]{1,0:T(8,128)S(1)} %bitcast.31, f32[256,128]{1,0:T(8,128)S(1)} %get-tuple-element.79.kept, f32[128,128]{1,0:T(8,128)S(1)} %get-tuple-element.53.refs_2_.cut_weight, f32[8,128]{1,0:T(8,128)S(1)} %get-tuple-element.64.net_weight, ...), custom_call_target="tpu_custom_call" | custom-call | flops 67108864 | bytes 1048576 | tf_op jit(solution)/shard_map/pallas_call | solution.py:422
  59.4 4.0 %all-to-all-start.3 = ((f32[128,1,128]{2,1,0:T(1,128)}), f32[128,1,128]{2,1,0:T(1,128)S(1)}, u32[]{:S(2)}, u32[]{:S(2)}) async-start(f32[128,1,128]{2,1,0:T(1,128)} %bitcast.17), calls=%async_computation.3 | async-start | bytes 131072 | tf_op jit(solution)/shard_map/all_to_all | solution.py:438
  63.4 1.6 %collective-permute-start.3 = (f32[32,128]{1,0:T(8,128)S(1)}, f32[32,128]{1,0:T(8,128)S(1)}, u32[]{:S(2)}, u32[]{:S(2)}) collective-permute-start(f32[32,128]{1,0:T(8,128)S(1)} %get-tuple-element.86), channel_id=1, source_target_pairs={{0,1},{1,0},{2,3},{3,2},{4,5},{5,4},{6,7},{7,6},{8,9},{9,8},{10,11... | collective-permute-start | bytes 49160 | tf_op jit(solution)/shard_map/ppermute | solution.py:444
  65.0 1.8 %shard_map.113 = (f32[32,128]{1,0:T(8,128)S(1)}, bf16[4096,128]{1,0:T(8,128)(2,1)S(1)}) custom-call(s32[128,128]{1,0:T(8,128)S(1)} %bitcast.36, f32[128,128]{1,0:T(8,128)S(1)} %get-tuple-element.53.refs_2_.cut_weight, f32[384,128]{1,0:T(8,128)S(1)} %bitcast.32, f32[32,128]{1,0:T(8,128)S(1)} %get-tuple-element.77.local_ref, ...), custom_call_target="tpu_custom_call" | custom-call | flops 2147483648 | bytes 1048576 | tf_op jit(solution)/shard_map/pallas_call | solution.py:422
  66.9 0.0 collective-permute-done.3.back_ref
  66.9 6.4 %all-to-all-done.3 = f32[128,1,128]{2,1,0:T(1,128)S(1)} async-done(((f32[128,1,128]{2,1,0:T(1,128)}), f32[128,1,128]{2,1,0:T(1,128)S(1)}, u32[]{:S(2)}, u32[]{:S(2)}) %all-to-all-start.3) | async-done | bytes 65568 | tf_op jit(solution)/shard_map/all_to_all | solution.py:438
  73.3 2.0 %shard_map.114 = (f32[384,128]{1,0:T(8,128)}, f32[32,128]{1,0:T(8,128)S(1)}, f32[96,128]{1,0:T(8,128)S(1)}, f32[8,128]{1,0:T(8,128)S(1)}, f32[256,128]{1,0:T(8,128)S(1)}) custom-call(s32[32,128]{1,0:T(8,128)S(1)} %bitcast.43, bf16[4096,128]{1,0:T(8,128)(2,1)S(1)} %get-tuple-element.83.cell_hot, f32[128,128]{1,0:T(8,128)S(1)} %bitcast.48, ...), custom_call_target="tpu_custom_call" | custom-call | flops 67108864 | bytes 1048576 | tf_op jit(solution)/shard_map/pallas_call | solution.py:422
  75.3 4.1 %all-to-all-start.4 = ((f32[128,1,384]{2,1,0:T(1,128)}), f32[128,1,384]{2,1,0:T(1,128)S(1)}, u32[]{:S(2)}, u32[]{:S(2)}) async-start(f32[128,1,384]{2,1,0:T(1,128)} %bitcast.19), calls=%async_computation.4 | async-start | bytes 393216 | tf_op jit(solution)/shard_map/all_to_all | solution.py:438
  79.4 1.5 %collective-permute-start.4 = (f32[32,128]{1,0:T(8,128)S(1)}, f32[32,128]{1,0:T(8,128)S(1)}, u32[]{:S(2)}, u32[]{:S(2)}) collective-permute-start(f32[32,128]{1,0:T(8,128)S(1)} %get-tuple-element.90.own_ref.start_ref), channel_id=1, source_target_pairs={{0,1},{1,0},{2,3},{3,2},{4,5},{5,4},{6,7},{7,6},{8,9},{9,8},{10,11... | collective-permute-start | bytes 49160 | tf_op jit(solution)/shard_map/ppermute | solution.py:444
  80.9 0.0 copy-start.6
  80.9 1.6 %copy-done.6 = f32[16,2,128,128]{3,2,1,0:T(8,128)S(1)} copy-done((f32[16,2,128,128]{3,2,1,0:T(8,128)S(1)}, f32[16,2,128,128]{3,2,1,0:T(8,128)}, u32[]{:S(2)}) %copy-start.6) | copy-done | bytes 2097176
  82.5 0.6 shard_map.115
  83.0 0.3 collective-permute-done.4.peer_ref
  83.4 0.8 shard_map.116
  84.2 6.2 %all-to-all-done.4 = f32[128,1,384]{2,1,0:T(1,128)S(1)} async-done(((f32[128,1,384]{2,1,0:T(1,128)}), f32[128,1,384]{2,1,0:T(1,128)S(1)}, u32[]{:S(2)}, u32[]{:S(2)}) %all-to-all-start.4) | async-done | bytes 196640 | tf_op jit(solution)/shard_map/all_to_all | solution.py:438
  90.4 1.3 %shard_map.117 = (f32[128,128]{1,0:T(8,128)}, f32[8,128]{1,0:T(8,128)S(1)}) custom-call(f32[384,128]{1,0:T(8,128)S(1)} %bitcast.29, f32[256,128]{1,0:T(8,128)S(1)} %get-tuple-element.94.kept, f32[128,128]{1,0:T(8,128)S(1)} %get-tuple-element.53.refs_2_.cut_weight, f32[8,128]{1,0:T(8,128)S(1)} %get-tuple-element.64.net_weight, ...), custom_call_target="tpu_custom_call" | custom-call | flops 67108864 | bytes 1048576 | tf_op jit(solution)/shard_map/pallas_call | solution.py:422
  91.6 4.0 %all-to-all-start.5 = ((f32[128,1,128]{2,1,0:T(1,128)}), f32[128,1,128]{2,1,0:T(1,128)S(1)}, u32[]{:S(2)}, u32[]{:S(2)}) async-start(f32[128,1,128]{2,1,0:T(1,128)} %bitcast.22), calls=%async_computation.5 | async-start | bytes 131072 | tf_op jit(solution)/shard_map/all_to_all | solution.py:438
  95.7 1.5 %collective-permute-start.5 = (f32[32,128]{1,0:T(8,128)S(1)}, f32[32,128]{1,0:T(8,128)S(1)}, u32[]{:S(2)}, u32[]{:S(2)}) collective-permute-start(f32[32,128]{1,0:T(8,128)S(1)} %get-tuple-element.101), channel_id=1, source_target_pairs={{0,1},{1,0},{2,3},{3,2},{4,5},{5,4},{6,7},{7,6},{8,9},{9,8},{10,11... | collective-permute-start | bytes 49160 | tf_op jit(solution)/shard_map/ppermute | solution.py:444
  97.1 1.8 %shard_map.118 = (f32[32,128]{1,0:T(8,128)S(1)}, bf16[4096,128]{1,0:T(8,128)(2,1)S(1)}) custom-call(s32[128,128]{1,0:T(8,128)S(1)} %bitcast.38, f32[128,128]{1,0:T(8,128)S(1)} %get-tuple-element.53.refs_2_.cut_weight, f32[384,128]{1,0:T(8,128)S(1)} %bitcast.30, f32[32,128]{1,0:T(8,128)S(1)} %get-tuple-element.92.local_ref, ...), custom_call_target="tpu_custom_call" | custom-call | flops 2147483648 | bytes 1048576 | tf_op jit(solution)/shard_map/pallas_call | solution.py:422
  99.0 0.0 collective-permute-done.5.back_ref
  99.0 6.6 %all-to-all-done.5 = f32[128,1,128]{2,1,0:T(1,128)S(1)} async-done(((f32[128,1,128]{2,1,0:T(1,128)}), f32[128,1,128]{2,1,0:T(1,128)S(1)}, u32[]{:S(2)}, u32[]{:S(2)}) %all-to-all-start.5) | async-done | bytes 65568 | tf_op jit(solution)/shard_map/all_to_all | solution.py:438
  105.6 1.0 shard_map.119
  (1 shorter events, 0.0 us)
Async XLA Ops:
  3.2 22.5 %all-to-all-start = ((f32[128,1,384]{2,1,0:T(1,128)}), f32[128,1,384]{2,1,0:T(1,128)S(1)}, u32[]{:S(2)}, u32[]{:S(2)}) async-start(f32[128,1,384]{2,1,0:T(1,128)} %bitcast.7), calls=%async_computation | async-start | bytes 393216 | tf_op jit(solution)/shard_map/all_to_all | solution.py:438
  14.7 4.3 %collective-permute-start = (f32[32,128]{1,0:T(8,128)S(1)}, f32[32,128]{1,0:T(8,128)S(1)}, u32[]{:S(2)}, u32[]{:S(2)}) collective-permute-start(f32[32,128]{1,0:T(8,128)S(1)} %get-tuple-element.55.own_ref.start_ref), channel_id=1, source_target_pairs={{0,1},{1,0},{2,3},{3,2},{4,5},{5,4},{6,7},{7,6},{8,9},{9,8},{10,11... | collective-permute-start | bytes 49160 | tf_op jit(solution)/shard_map/ppermute | solution.py:444
  16.2 1.6 %copy-start.3 = (f32[16,2,128,128]{3,2,1,0:T(8,128)S(1)}, f32[16,2,128,128]{3,2,1,0:T(8,128)}, u32[]{:S(2)}) copy-start(f32[16,2,128,128]{3,2,1,0:T(8,128)} %blocks.11) | copy-start | bytes 6291460
  17.8 1.6 %copy-start.4 = (f32[16,2,128,128]{3,2,1,0:T(8,128)S(1)}, f32[16,2,128,128]{3,2,1,0:T(8,128)}, u32[]{:S(2)}) copy-start(f32[16,2,128,128]{3,2,1,0:T(8,128)} %blocks.11) | copy-start | bytes 6291460
  19.4 13.2 %copy-start = (s32[1,128,128]{2,1,0:T(8,128)S(1)}, s32[1,128,128]{2,1,0:T(8,128)}, u32[]{:S(2)}) copy-start(s32[1,128,128]{2,1,0:T(8,128)} %param.13) | copy-start | bytes 196612
  19.4 13.2 %copy-start.1 = (s32[4096]{0:T(1024)S(1)}, s32[4096]{0:T(1024)}, u32[]{:S(2)}) copy-start(s32[4096]{0:T(1024)} %param.15) | copy-start | bytes 49156
  19.4 13.2 %copy-start.2 = (s32[4096]{0:T(1024)S(1)}, s32[4096]{0:T(1024)}, u32[]{:S(2)}) copy-start(s32[4096]{0:T(1024)} %param.16) | copy-start | bytes 49156
  26.9 14.1 %all-to-all-start.1 = ((f32[128,1,128]{2,1,0:T(1,128)}), f32[128,1,128]{2,1,0:T(1,128)S(1)}, u32[]{:S(2)}, u32[]{:S(2)}) async-start(f32[128,1,128]{2,1,0:T(1,128)} %bitcast.12), calls=%async_computation.1 | async-start | bytes 131072 | tf_op jit(solution)/shard_map/all_to_all | solution.py:438
  31.2 3.7 %collective-permute-start.1 = (f32[48,128]{1,0:T(8,128)S(1)}, f32[48,128]{1,0:T(8,128)S(1)}, u32[]{:S(2)}, u32[]{:S(2)}) collective-permute-start(f32[48,128]{1,0:T(8,128)S(1)} %get-tuple-element.72), channel_id=1, source_target_pairs={{0,1},{1,0},{2,3},{3,2},{4,5},{5,4},{6,7},{7,6},{8,9},{9,8},{10,11... | collective-permute-start | bytes 73736 | tf_op jit(solution)/shard_map/ppermute | solution.py:444
  43.0 15.1 %all-to-all-start.2 = ((f32[128,1,384]{2,1,0:T(1,128)}), f32[128,1,384]{2,1,0:T(1,128)S(1)}, u32[]{:S(2)}, u32[]{:S(2)}) async-start(f32[128,1,384]{2,1,0:T(1,128)} %bitcast.14), calls=%async_computation.2 | async-start | bytes 393216 | tf_op jit(solution)/shard_map/all_to_all | solution.py:438
  47.1 3.9 %collective-permute-start.2 = (f32[32,128]{1,0:T(8,128)S(1)}, f32[32,128]{1,0:T(8,128)S(1)}, u32[]{:S(2)}, u32[]{:S(2)}) collective-permute-start(f32[32,128]{1,0:T(8,128)S(1)} %get-tuple-element.74.own_ref.start_ref), channel_id=1, source_target_pairs={{0,1},{1,0},{2,3},{3,2},{4,5},{5,4},{6,7},{7,6},{8,9},{9,8},{10,11... | collective-permute-start | bytes 49160 | tf_op jit(solution)/shard_map/ppermute | solution.py:444
  48.6 1.6 %copy-start.5 = (f32[16,2,128,128]{3,2,1,0:T(8,128)S(1)}, f32[16,2,128,128]{3,2,1,0:T(8,128)}, u32[]{:S(2)}) copy-start(f32[16,2,128,128]{3,2,1,0:T(8,128)} %blocks.11) | copy-start | bytes 6291460
  59.4 13.9 %all-to-all-start.3 = ((f32[128,1,128]{2,1,0:T(1,128)}), f32[128,1,128]{2,1,0:T(1,128)S(1)}, u32[]{:S(2)}, u32[]{:S(2)}) async-start(f32[128,1,128]{2,1,0:T(1,128)} %bitcast.17), calls=%async_computation.3 | async-start | bytes 131072 | tf_op jit(solution)/shard_map/all_to_all | solution.py:438
  63.4 3.5 %collective-permute-start.3 = (f32[32,128]{1,0:T(8,128)S(1)}, f32[32,128]{1,0:T(8,128)S(1)}, u32[]{:S(2)}, u32[]{:S(2)}) collective-permute-start(f32[32,128]{1,0:T(8,128)S(1)} %get-tuple-element.86), channel_id=1, source_target_pairs={{0,1},{1,0},{2,3},{3,2},{4,5},{5,4},{6,7},{7,6},{8,9},{9,8},{10,11... | collective-permute-start | bytes 49160 | tf_op jit(solution)/shard_map/ppermute | solution.py:444
  75.3 15.1 %all-to-all-start.4 = ((f32[128,1,384]{2,1,0:T(1,128)}), f32[128,1,384]{2,1,0:T(1,128)S(1)}, u32[]{:S(2)}, u32[]{:S(2)}) async-start(f32[128,1,384]{2,1,0:T(1,128)} %bitcast.19), calls=%async_computation.4 | async-start | bytes 393216 | tf_op jit(solution)/shard_map/all_to_all | solution.py:438
  79.4 3.9 %collective-permute-start.4 = (f32[32,128]{1,0:T(8,128)S(1)}, f32[32,128]{1,0:T(8,128)S(1)}, u32[]{:S(2)}, u32[]{:S(2)}) collective-permute-start(f32[32,128]{1,0:T(8,128)S(1)} %get-tuple-element.90.own_ref.start_ref), channel_id=1, source_target_pairs={{0,1},{1,0},{2,3},{3,2},{4,5},{5,4},{6,7},{7,6},{8,9},{9,8},{10,11... | collective-permute-start | bytes 49160 | tf_op jit(solution)/shard_map/ppermute | solution.py:444
  80.9 1.6 %copy-start.6 = (f32[16,2,128,128]{3,2,1,0:T(8,128)S(1)}, f32[16,2,128,128]{3,2,1,0:T(8,128)}, u32[]{:S(2)}) copy-start(f32[16,2,128,128]{3,2,1,0:T(8,128)} %blocks.11) | copy-start | bytes 6291460
  91.6 13.9 %all-to-all-start.5 = ((f32[128,1,128]{2,1,0:T(1,128)}), f32[128,1,128]{2,1,0:T(1,128)S(1)}, u32[]{:S(2)}, u32[]{:S(2)}) async-start(f32[128,1,128]{2,1,0:T(1,128)} %bitcast.22), calls=%async_computation.5 | async-start | bytes 131072 | tf_op jit(solution)/shard_map/all_to_all | solution.py:438
  95.7 3.3 %collective-permute-start.5 = (f32[32,128]{1,0:T(8,128)S(1)}, f32[32,128]{1,0:T(8,128)S(1)}, u32[]{:S(2)}, u32[]{:S(2)}) collective-permute-start(f32[32,128]{1,0:T(8,128)S(1)} %get-tuple-element.101), channel_id=1, source_target_pairs={{0,1},{1,0},{2,3},{3,2},{4,5},{5,4},{6,7},{7,6},{8,9},{9,8},{10,11... | collective-permute-start | bytes 49160 | tf_op jit(solution)/shard_map/ppermute | solution.py:444

commit v8 on v7

--- a/solution.py
+++ b/solution.py
@@ -255,12 +255,18 @@
     share_ref[2:8, :] = jnp.zeros((6, LANES), F32)
 
 
-def owner_kernel(first, got, kept, cut_weight, net_weight, share_ref, out_ref, sums_ref, rows):
+def owner_kernel(first, got, kept, cut_weight, net_weight, share_ref, *refs):
+    if first:
+        out_ref, sums_ref, nets_ref, rows = refs
+    else:
+        net_hot, out_ref, sums_ref, rows = refs
     height = 16 if first else 8
     pin_rows = [got[pl.ds(3 * q + 2, 32, stride=12), :] for q in range(4)]
     sums = sum(jnp.sum(row, axis=0, keepdims=True) for row in pin_rows)
     sums_ref[...] = jnp.broadcast_to(sums, (8, LANES))
-    nets = dense(pin_rows, 64).astype(I32)
+    if first:
+        nets_ref[...] = dense(pin_rows, 64)
+        nets = nets_ref[...].astype(I32)
     rows[...] = jnp.zeros(rows.shape, F32)
     for v in range(2):
         pins = dense(pin_rows, 32 * v)
@@ -271,11 +277,14 @@
                 rows[pl.ds(8 + 2 * i + v, 32, stride=height), :] = part
     acc = None
     for j in range(0, 32, 2):
-        hot = jnp.concatenate([one_hot(nets[i : i + 1], LANES) for i in (j, j + 1)], axis=1)
         left = jnp.concatenate(
             [rows[height * i : height * i + height, :] for i in (j, j + 1)], axis=1
-        )
-        part = dot_nt(left.astype(BF16), hot)
+        ).astype(BF16)
+        if first:
+            hot = jnp.concatenate([one_hot(nets[i : i + 1], LANES) for i in (j, j + 1)], axis=1)
+            part = dot_nt(left, hot)
+        else:
+            part = dot_nn(left, net_hot[LANES * j : LANES * (j + 2), :])
         acc = part if acc is None else acc + part
     weight = net_weight[0:1, :]
     totals = [acc[v : v + 1] + acc[v + 2 : v + 3] + acc[v + 4 : v + 5] for v in range(2)]
@@ -310,6 +319,11 @@
         wide = jnp.broadcast_to(columns[:, j : j + 1], (LANES, LANES)).astype(I32)
         hot = jnp.where(iota((LANES, LANES), 1) == wide, 1.0, 0.0)
         hot_ref[LANES * j : LANES * (j + 1), :] = hot.astype(BF16)
+
+
+def net_kernel(nets, share_ref, hot_ref):
+    del share_ref
+    put_hots(hot_ref, nets[...].astype(I32))
 
 
 def cut_kernel(first, cut_cells, cut_weight, got, local_ref, sums_ref, pin_cell, *refs):
@@ -494,13 +508,17 @@
             (residual, peer, side, nbr, blocks, local_sum)
             + ((ones, anchor, cut_weight, kept) if first else (degree,)),
         )
-        out, sums = call(
+        if not first:
+            net_hot = call(net_kernel, [hots], [], 1 << 28, (nets, share))[0]
+        out, sums, *more = call(
             functools.partial(owner_kernel, first),
-            [(128, LANES), (8, LANES)],
+            [(128, LANES), (8, LANES)] + [(32, LANES)] * first,
             [(512 if first else 256, LANES)],
             1 << 26,
-            (got, kept, cut_weight, net_weight, share),
-        )
+            (got, kept, cut_weight, net_weight, share) + (() if first else (net_hot,)),
+        )
+        if first:
+            nets = more[0]
         returned = exchange(out, 1)
         back, sums = lax.optimization_barrier((back, sums))
         back = swap(back)

time: 107 us -> 108 us (level)
  waiting for transfers between devices: 37.6 us -> 36 us
  Pallas kernels: 21.9 us -> 23.2 us
    all_to_all x6, waiting for transfers between devices: 37 us -> 35.4 us  [exchange(): lax.all_to_all(rows.reshape(LANES, 1, height * LANES), AXES, split_axis=0...]
    pallas_call x16 -> x18, Pallas kernels: 21.9 us -> 23.2 us  [call(): pl.pallas_call(kernel, out_shape=[jax.ShapeDtypeStruct(s, F32) if isinsta...]
  transfers between devices with their start and end apart: 12 -> 12, of which waited for: 8 -> 8; matrix products, arithmetic and copies ran while one was open for 0% -> 0% of each run, Pallas kernels for 10% -> 11%
where the time goes in v8:
time: 108 us; the launch traced here: 107 us
  starting transfers between devices  41.8 us (39%)
  waiting for transfers between devices  36 us (33%)
  Pallas kernels  23.2 us (21%)
  local copies, waits for them, and re-layouts  5.21 us (5%)
    all_to_all x6, waiting for transfers between devices, exchange(): lax.all_to_all(rows.reshape(LANES, 1, height * LANES), AXES, split_axis=0...  35.4 us
    all_to_all x6, starting transfers between devices, exchange(): lax.all_to_all(rows.reshape(LANES, 1, height * LANES), AXES, split_axis=0...  32.8 us
    pallas_call x18, Pallas kernels, call(): pl.pallas_call(kernel, out_shape=[jax.ShapeDtypeStruct(s, F32) if isinsta...  23.2 us
    ppermute x6, starting transfers between devices, swap(): return lax.ppermute(x, 'coord', [(0, 1), (1, 0)])  8.97 us
    unnamed x14, local copies, waits for them, and re-layouts  5.21 us
  transfers between devices with their start and end apart: 12, of which 8 were waited for; matrix products, arithmetic and copies ran while one was open for 0% of the time, Pallas kernels for 11%

profile of v8, /device:TPU:1, one launch (start us, length us, event | category | flops | bytes accessed | tf_op | source)
XLA Modules:
  0.0 107.1 jit_solution(16698262783108946862)
XLA Ops:
  0.6 2.5 %shard_map.104 = (f32[384,128]{1,0:T(8,128)}, f32[32,128]{1,0:T(8,128)S(1)}, f32[256,128]{1,0:T(8,128)S(1)}, f32[128,128]{1,0:T(8,128)S(1)}, f32[16,128]{1,0:T(8...) custom-call(f32[2,2048]{1,0:T(2,128)} %right_hbm.1, s32[128,128]{1,0:T(8,128)} %bitcast.33, s32[32,128]{1,0:T(8,128)} %bitcast.39, ...), custom_call_target="tpu_custom_call" | custom-call | flops 16777216 | bytes 1048576 | tf_op jit(solution)/shard_map/pallas_call | solution.py:436
  3.2 11.5 %all-to-all-start = ((f32[128,1,384]{2,1,0:T(1,128)}), f32[128,1,384]{2,1,0:T(1,128)S(1)}, u32[]{:S(2)}, u32[]{:S(2)}) async-start(f32[128,1,384]{2,1,0:T(1,128)} %bitcast.7), calls=%async_computation | async-start | bytes 393216 | tf_op jit(solution)/shard_map/all_to_all | solution.py:452
  14.7 1.5 %collective-permute-start = (f32[32,128]{1,0:T(8,128)S(1)}, f32[32,128]{1,0:T(8,128)S(1)}, u32[]{:S(2)}, u32[]{:S(2)}) collective-permute-start(f32[32,128]{1,0:T(8,128)S(1)} %get-tuple-element.56.own_ref.start_ref), channel_id=1, source_target_pairs={{0,1},{1,0},{2,3},{3,2},{4,5},{5,4},{6,7},{7,6},{8,9},{9,8},{10,11... | collective-permute-start | bytes 49160 | tf_op jit(solution)/shard_map/ppermute | solution.py:458
  16.1 0.1 pad_add_fusion.refs_0_
  16.2 0.0 copy-start.3
  16.2 1.6 %copy-done.3 = f32[16,2,128,128]{3,2,1,0:T(8,128)S(1)} copy-done((f32[16,2,128,128]{3,2,1,0:T(8,128)S(1)}, f32[16,2,128,128]{3,2,1,0:T(8,128)}, u32[]{:S(2)}) %copy-start.3) | copy-done | bytes 2097176
  17.8 0.0 copy-start.4
  17.8 1.1 %shard_map.105 = (f32[48,128]{1,0:T(8,128)S(1)}, f32[48,128]{1,0:T(8,128)S(1)}, f32[32,128]{1,0:T(8,128)S(1)}, f32[8,128]{1,0:T(8,128)S(1)}) custom-call(f32[32,128]{1,0:T(8,128)S(1)} %get-tuple-element.56.own_ref.start_ref, f32[8,128]{1,0:T(8,128)S(1)} %broadcast_in_dim.3.side, s32[2,16]{1,0:T(2,128)S(1)} %get-tuple-element.57.nbr, ...), custom_call_target="tpu_custom_call" | custom-call | flops 1073741824 | bytes 1048576 | tf_op jit(solution)/shard_map/pallas_call | solution.py:436
  19.0 0.0 collective-permute-done.peer_ref
  19.0 0.4 copy-done.4
  19.4 0.0 copy-start
  19.4 0.0 copy-start.1
  19.4 0.0 copy-start.2
  19.4 0.9 shard_map.106
  20.3 5.4 %all-to-all-done = f32[128,1,384]{2,1,0:T(1,128)S(1)} async-done(((f32[128,1,384]{2,1,0:T(1,128)}), f32[128,1,384]{2,1,0:T(1,128)S(1)}, u32[]{:S(2)}, u32[]{:S(2)}) %all-to-all-start) | async-done | bytes 196640 | tf_op jit(solution)/shard_map/all_to_all | solution.py:452
  25.6 1.3 %shard_map.107 = (f32[128,128]{1,0:T(8,128)}, f32[8,128]{1,0:T(8,128)S(1)}, f32[32,128]{1,0:T(8,128)S(1)}) custom-call(f32[384,128]{1,0:T(8,128)S(1)} %bitcast.27, f32[256,128]{1,0:T(8,128)S(1)} %get-tuple-element.62.refs_3_.kept, f32[128,128]{1,0:T(8,128)S(1)} %get-tuple-element.54.refs_2_.cut_weight, f32[8,128]{1,0:T(8,128)S(1)} %get-tuple-element.65.net_weight, ...), custom_call_target="tpu_custom_call" | custom-call | flops 67108864 | bytes 1048576 | tf_op jit(solution)/shard_map/pallas_call | solution.py:436
  26.9 4.2 %all-to-all-start.1 = ((f32[128,1,128]{2,1,0:T(1,128)}), f32[128,1,128]{2,1,0:T(1,128)S(1)}, u32[]{:S(2)}, u32[]{:S(2)}) async-start(f32[128,1,128]{2,1,0:T(1,128)} %bitcast.12), calls=%async_computation.1 | async-start | bytes 131072 | tf_op jit(solution)/shard_map/all_to_all | solution.py:452
  31.2 1.5 %collective-permute-start.1 = (f32[48,128]{1,0:T(8,128)S(1)}, f32[48,128]{1,0:T(8,128)S(1)}, u32[]{:S(2)}, u32[]{:S(2)}) collective-permute-start(f32[48,128]{1,0:T(8,128)S(1)} %get-tuple-element.73), channel_id=1, source_target_pairs={{0,1},{1,0},{2,3},{3,2},{4,5},{5,4},{6,7},{7,6},{8,9},{9,8},{10,11... | collective-permute-start | bytes 73736 | tf_op jit(solution)/shard_map/ppermute | solution.py:458
  32.6 0.0 copy-done
  32.6 0.0 copy-done.1
  32.6 0.0 copy-done.2
  32.6 2.2 %shard_map.108 = (f32[32,128]{1,0:T(8,128)S(1)}, bf16[4096,128]{1,0:T(8,128)(2,1)S(1)}, f32[16,128]{1,0:T(8,128)S(1)}) custom-call(s32[128,128]{1,0:T(8,128)S(1)} %bitcast.34, f32[128,128]{1,0:T(8,128)S(1)} %get-tuple-element.54.refs_2_.cut_weight, f32[384,128]{1,0:T(8,128)S(1)} %bitcast.28, f32[48,128]{1,0:T(8,128)S(1)} %get-tuple-element.63.local_ref, ...), custom_call_target="tpu_custom_call" | custom-call | flops 2147483648 | bytes 1048576 | tf_op jit(solution)/shard_map/pallas_call | solution.py:436
  34.8 0.0 collective-permute-done.1.back_ref
  34.9 6.2 %all-to-all-done.1 = f32[128,1,128]{2,1,0:T(1,128)S(1)} async-done(((f32[128,1,128]{2,1,0:T(1,128)}), f32[128,1,128]{2,1,0:T(1,128)S(1)}, u32[]{:S(2)}, u32[]{:S(2)}) %all-to-all-start.1) | async-done | bytes 65568 | tf_op jit(solution)/shard_map/all_to_all | solution.py:452
  41.1 1.9 %shard_map.109 = (f32[384,128]{1,0:T(8,128)}, f32[32,128]{1,0:T(8,128)S(1)}, f32[96,128]{1,0:T(8,128)S(1)}, f32[8,128]{1,0:T(8,128)S(1)}, f32[256,128]{1,0:T(8,128)S(1)}, /*index=5*/f32[16,128]{1,0:T(8,128)S(1)}) custom-call(s32[32,128]{1,0:T(8,128)S(1)} %bitcast.41, bf16[4096,128]{1,0:T(8,128)(2,1)S(1)} %get-tuple-element.69.cell_hot, ...), custom_call_target="tpu_custom_call" | custom-call | flops 67108864 | bytes 1048576 | tf_op jit(solution)/shard_map/pallas_call | solution.py:436
  43.0 4.1 %all-to-all-start.2 = ((f32[128,1,384]{2,1,0:T(1,128)}), f32[128,1,384]{2,1,0:T(1,128)S(1)}, u32[]{:S(2)}, u32[]{:S(2)}) async-start(f32[128,1,384]{2,1,0:T(1,128)} %bitcast.14), calls=%async_computation.2 | async-start | bytes 393216 | tf_op jit(solution)/shard_map/all_to_all | solution.py:452
  47.1 1.5 %collective-permute-start.2 = (f32[32,128]{1,0:T(8,128)S(1)}, f32[32,128]{1,0:T(8,128)S(1)}, u32[]{:S(2)}, u32[]{:S(2)}) collective-permute-start(f32[32,128]{1,0:T(8,128)S(1)} %get-tuple-element.75.own_ref.start_ref), channel_id=1, source_target_pairs={{0,1},{1,0},{2,3},{3,2},{4,5},{5,4},{6,7},{7,6},{8,9},{9,8},{10,11... | collective-permute-start | bytes 49160 | tf_op jit(solution)/shard_map/ppermute | solution.py:458
  48.6 0.0 copy-start.5
  48.6 1.6 %copy-done.5 = f32[16,2,128,128]{3,2,1,0:T(8,128)S(1)} copy-done((f32[16,2,128,128]{3,2,1,0:T(8,128)S(1)}, f32[16,2,128,128]{3,2,1,0:T(8,128)}, u32[]{:S(2)}) %copy-start.5) | copy-done | bytes 2097176
  50.2 0.6 shard_map.110
  50.8 0.3 collective-permute-done.2.peer_ref
  51.1 0.8 shard_map.111
  51.9 0.8 shard_map.112.refs_0_
  52.7 5.4 %all-to-all-done.2 = f32[128,1,384]{2,1,0:T(1,128)S(1)} async-done(((f32[128,1,384]{2,1,0:T(1,128)}), f32[128,1,384]{2,1,0:T(1,128)S(1)}, u32[]{:S(2)}, u32[]{:S(2)}) %all-to-all-start.2) | async-done | bytes 196640 | tf_op jit(solution)/shard_map/all_to_all | solution.py:452
  58.1 1.1 %shard_map.113 = (f32[128,128]{1,0:T(8,128)}, f32[8,128]{1,0:T(8,128)S(1)}) custom-call(f32[384,128]{1,0:T(8,128)S(1)} %bitcast.31, f32[256,128]{1,0:T(8,128)S(1)} %get-tuple-element.80.kept, f32[128,128]{1,0:T(8,128)S(1)} %get-tuple-element.54.refs_2_.cut_weight, f32[8,128]{1,0:T(8,128)S(1)} %get-tuple-element.65.net_weight, ...), custom_call_target="tpu_custom_call" | custom-call | flops 67108864 | bytes 1048576 | tf_op jit(solution)/shard_map/pallas_call | solution.py:436
  59.2 4.4 %all-to-all-start.3 = ((f32[128,1,128]{2,1,0:T(1,128)}), f32[128,1,128]{2,1,0:T(1,128)S(1)}, u32[]{:S(2)}, u32[]{:S(2)}) async-start(f32[128,1,128]{2,1,0:T(1,128)} %bitcast.17), calls=%async_computation.3 | async-start | bytes 131072 | tf_op jit(solution)/shard_map/all_to_all | solution.py:452
  63.7 1.6 %collective-permute-start.3 = (f32[32,128]{1,0:T(8,128)S(1)}, f32[32,128]{1,0:T(8,128)S(1)}, u32[]{:S(2)}, u32[]{:S(2)}) collective-permute-start(f32[32,128]{1,0:T(8,128)S(1)} %get-tuple-element.88), channel_id=1, source_target_pairs={{0,1},{1,0},{2,3},{3,2},{4,5},{5,4},{6,7},{7,6},{8,9},{9,8},{10,11... | collective-permute-start | bytes 49160 | tf_op jit(solution)/shard_map/ppermute | solution.py:458
  65.3 1.8 %shard_map.114 = (f32[32,128]{1,0:T(8,128)S(1)}, bf16[4096,128]{1,0:T(8,128)(2,1)S(1)}) custom-call(s32[128,128]{1,0:T(8,128)S(1)} %bitcast.36, f32[128,128]{1,0:T(8,128)S(1)} %get-tuple-element.54.refs_2_.cut_weight, f32[384,128]{1,0:T(8,128)S(1)} %bitcast.32, f32[32,128]{1,0:T(8,128)S(1)} %get-tuple-element.78.local_ref, ...), custom_call_target="tpu_custom_call" | custom-call | flops 2147483648 | bytes 1048576 | tf_op jit(solution)/shard_map/pallas_call | solution.py:436
  67.1 0.0 collective-permute-done.3.back_ref
  67.1 6.4 %all-to-all-done.3 = f32[128,1,128]{2,1,0:T(1,128)S(1)} async-done(((f32[128,1,128]{2,1,0:T(1,128)}), f32[128,1,128]{2,1,0:T(1,128)S(1)}, u32[]{:S(2)}, u32[]{:S(2)}) %all-to-all-start.3) | async-done | bytes 65568 | tf_op jit(solution)/shard_map/all_to_all | solution.py:452
  73.6 2.0 %shard_map.115 = (f32[384,128]{1,0:T(8,128)}, f32[32,128]{1,0:T(8,128)S(1)}, f32[96,128]{1,0:T(8,128)S(1)}, f32[8,128]{1,0:T(8,128)S(1)}, f32[256,128]{1,0:T(8,128)S(1)}) custom-call(s32[32,128]{1,0:T(8,128)S(1)} %bitcast.43, bf16[4096,128]{1,0:T(8,128)(2,1)S(1)} %get-tuple-element.85.cell_hot, f32[128,128]{1,0:T(8,128)S(1)} %bitcast.48, ...), custom_call_target="tpu_custom_call" | custom-call | flops 67108864 | bytes 1048576 | tf_op jit(solution)/shard_map/pallas_call | solution.py:436
  75.5 4.1 %all-to-all-start.4 = ((f32[128,1,384]{2,1,0:T(1,128)}), f32[128,1,384]{2,1,0:T(1,128)S(1)}, u32[]{:S(2)}, u32[]{:S(2)}) async-start(f32[128,1,384]{2,1,0:T(1,128)} %bitcast.19), calls=%async_computation.4 | async-start | bytes 393216 | tf_op jit(solution)/shard_map/all_to_all | solution.py:452
  79.7 1.5 %collective-permute-start.4 = (f32[32,128]{1,0:T(8,128)S(1)}, f32[32,128]{1,0:T(8,128)S(1)}, u32[]{:S(2)}, u32[]{:S(2)}) collective-permute-start(f32[32,128]{1,0:T(8,128)S(1)} %get-tuple-element.92.own_ref.start_ref), channel_id=1, source_target_pairs={{0,1},{1,0},{2,3},{3,2},{4,5},{5,4},{6,7},{7,6},{8,9},{9,8},{10,11... | collective-permute-start | bytes 49160 | tf_op jit(solution)/shard_map/ppermute | solution.py:458
  81.1 0.0 copy-start.6
  81.1 1.6 %copy-done.6 = f32[16,2,128,128]{3,2,1,0:T(8,128)S(1)} copy-done((f32[16,2,128,128]{3,2,1,0:T(8,128)S(1)}, f32[16,2,128,128]{3,2,1,0:T(8,128)}, u32[]{:S(2)}) %copy-start.6) | copy-done | bytes 2097176
  82.7 0.6 shard_map.116
  83.3 0.3 collective-permute-done.4.peer_ref
  83.6 0.8 shard_map.117
  84.5 0.8 shard_map.118.refs_0_
  85.3 5.4 %all-to-all-done.4 = f32[128,1,384]{2,1,0:T(1,128)S(1)} async-done(((f32[128,1,384]{2,1,0:T(1,128)}), f32[128,1,384]{2,1,0:T(1,128)S(1)}, u32[]{:S(2)}, u32[]{:S(2)}) %all-to-all-start.4) | async-done | bytes 196640 | tf_op jit(solution)/shard_map/all_to_all | solution.py:452
  90.6 1.1 %shard_map.119 = (f32[128,128]{1,0:T(8,128)}, f32[8,128]{1,0:T(8,128)S(1)}) custom-call(f32[384,128]{1,0:T(8,128)S(1)} %bitcast.29, f32[256,128]{1,0:T(8,128)S(1)} %get-tuple-element.96.kept, f32[128,128]{1,0:T(8,128)S(1)} %get-tuple-element.54.refs_2_.cut_weight, f32[8,128]{1,0:T(8,128)S(1)} %get-tuple-element.65.net_weight, ...), custom_call_target="tpu_custom_call" | custom-call | flops 67108864 | bytes 1048576 | tf_op jit(solution)/shard_map/pallas_call | solution.py:436
  91.8 4.4 %all-to-all-start.5 = ((f32[128,1,128]{2,1,0:T(1,128)}), f32[128,1,128]{2,1,0:T(1,128)S(1)}, u32[]{:S(2)}, u32[]{:S(2)}) async-start(f32[128,1,128]{2,1,0:T(1,128)} %bitcast.22), calls=%async_computation.5 | async-start | bytes 131072 | tf_op jit(solution)/shard_map/all_to_all | solution.py:452
  96.2 1.5 %collective-permute-start.5 = (f32[32,128]{1,0:T(8,128)S(1)}, f32[32,128]{1,0:T(8,128)S(1)}, u32[]{:S(2)}, u32[]{:S(2)}) collective-permute-start(f32[32,128]{1,0:T(8,128)S(1)} %get-tuple-element.103), channel_id=1, source_target_pairs={{0,1},{1,0},{2,3},{3,2},{4,5},{5,4},{6,7},{7,6},{8,9},{9,8},{10,11... | collective-permute-start | bytes 49160 | tf_op jit(solution)/shard_map/ppermute | solution.py:458
  97.7 1.8 %shard_map.120 = (f32[32,128]{1,0:T(8,128)S(1)}, bf16[4096,128]{1,0:T(8,128)(2,1)S(1)}) custom-call(s32[128,128]{1,0:T(8,128)S(1)} %bitcast.38, f32[128,128]{1,0:T(8,128)S(1)} %get-tuple-element.54.refs_2_.cut_weight, f32[384,128]{1,0:T(8,128)S(1)} %bitcast.30, f32[32,128]{1,0:T(8,128)S(1)} %get-tuple-element.94.local_ref, ...), custom_call_target="tpu_custom_call" | custom-call | flops 2147483648 | bytes 1048576 | tf_op jit(solution)/shard_map/pallas_call | solution.py:436
  99.5 0.0 collective-permute-done.5.back_ref
  99.5 6.6 %all-to-all-done.5 = f32[128,1,128]{2,1,0:T(1,128)S(1)} async-done(((f32[128,1,128]{2,1,0:T(1,128)}), f32[128,1,128]{2,1,0:T(1,128)S(1)}, u32[]{:S(2)}, u32[]{:S(2)}) %all-to-all-start.5) | async-done | bytes 65568 | tf_op jit(solution)/shard_map/all_to_all | solution.py:452
  106.1 1.0 shard_map.121
  (1 shorter events, 0.0 us)
Async XLA Ops:
  3.2 22.5 %all-to-all-start = ((f32[128,1,384]{2,1,0:T(1,128)}), f32[128,1,384]{2,1,0:T(1,128)S(1)}, u32[]{:S(2)}, u32[]{:S(2)}) async-start(f32[128,1,384]{2,1,0:T(1,128)} %bitcast.7), calls=%async_computation | async-start | bytes 393216 | tf_op jit(solution)/shard_map/all_to_all | solution.py:452
  14.7 4.3 %collective-permute-start = (f32[32,128]{1,0:T(8,128)S(1)}, f32[32,128]{1,0:T(8,128)S(1)}, u32[]{:S(2)}, u32[]{:S(2)}) collective-permute-start(f32[32,128]{1,0:T(8,128)S(1)} %get-tuple-element.56.own_ref.start_ref), channel_id=1, source_target_pairs={{0,1},{1,0},{2,3},{3,2},{4,5},{5,4},{6,7},{7,6},{8,9},{9,8},{10,11... | collective-permute-start | bytes 49160 | tf_op jit(solution)/shard_map/ppermute | solution.py:458
  16.2 1.6 %copy-start.3 = (f32[16,2,128,128]{3,2,1,0:T(8,128)S(1)}, f32[16,2,128,128]{3,2,1,0:T(8,128)}, u32[]{:S(2)}) copy-start(f32[16,2,128,128]{3,2,1,0:T(8,128)} %blocks.11) | copy-start | bytes 6291460
  17.8 1.6 %copy-start.4 = (f32[16,2,128,128]{3,2,1,0:T(8,128)S(1)}, f32[16,2,128,128]{3,2,1,0:T(8,128)}, u32[]{:S(2)}) copy-start(f32[16,2,128,128]{3,2,1,0:T(8,128)} %blocks.11) | copy-start | bytes 6291460
  19.4 13.2 %copy-start = (s32[1,128,128]{2,1,0:T(8,128)S(1)}, s32[1,128,128]{2,1,0:T(8,128)}, u32[]{:S(2)}) copy-start(s32[1,128,128]{2,1,0:T(8,128)} %param.13) | copy-start | bytes 196612
  19.4 13.2 %copy-start.1 = (s32[4096]{0:T(1024)S(1)}, s32[4096]{0:T(1024)}, u32[]{:S(2)}) copy-start(s32[4096]{0:T(1024)} %param.15) | copy-start | bytes 49156
  19.4 13.2 %copy-start.2 = (s32[4096]{0:T(1024)S(1)}, s32[4096]{0:T(1024)}, u32[]{:S(2)}) copy-start(s32[4096]{0:T(1024)} %param.16) | copy-start | bytes 49156
  26.9 14.1 %all-to-all-start.1 = ((f32[128,1,128]{2,1,0:T(1,128)}), f32[128,1,128]{2,1,0:T(1,128)S(1)}, u32[]{:S(2)}, u32[]{:S(2)}) async-start(f32[128,1,128]{2,1,0:T(1,128)} %bitcast.12), calls=%async_computation.1 | async-start | bytes 131072 | tf_op jit(solution)/shard_map/all_to_all | solution.py:452
  31.2 3.7 %collective-permute-start.1 = (f32[48,128]{1,0:T(8,128)S(1)}, f32[48,128]{1,0:T(8,128)S(1)}, u32[]{:S(2)}, u32[]{:S(2)}) collective-permute-start(f32[48,128]{1,0:T(8,128)S(1)} %get-tuple-element.73), channel_id=1, source_target_pairs={{0,1},{1,0},{2,3},{3,2},{4,5},{5,4},{6,7},{7,6},{8,9},{9,8},{10,11... | collective-permute-start | bytes 73736 | tf_op jit(solution)/shard_map/ppermute | solution.py:458
  43.0 15.1 %all-to-all-start.2 = ((f32[128,1,384]{2,1,0:T(1,128)}), f32[128,1,384]{2,1,0:T(1,128)S(1)}, u32[]{:S(2)}, u32[]{:S(2)}) async-start(f32[128,1,384]{2,1,0:T(1,128)} %bitcast.14), calls=%async_computation.2 | async-start | bytes 393216 | tf_op jit(solution)/shard_map/all_to_all | solution.py:452
  47.1 3.9 %collective-permute-start.2 = (f32[32,128]{1,0:T(8,128)S(1)}, f32[32,128]{1,0:T(8,128)S(1)}, u32[]{:S(2)}, u32[]{:S(2)}) collective-permute-start(f32[32,128]{1,0:T(8,128)S(1)} %get-tuple-element.75.own_ref.start_ref), channel_id=1, source_target_pairs={{0,1},{1,0},{2,3},{3,2},{4,5},{5,4},{6,7},{7,6},{8,9},{9,8},{10,11... | collective-permute-start | bytes 49160 | tf_op jit(solution)/shard_map/ppermute | solution.py:458
  48.6 1.6 %copy-start.5 = (f32[16,2,128,128]{3,2,1,0:T(8,128)S(1)}, f32[16,2,128,128]{3,2,1,0:T(8,128)}, u32[]{:S(2)}) copy-start(f32[16,2,128,128]{3,2,1,0:T(8,128)} %blocks.11) | copy-start | bytes 6291460
  59.2 14.3 %all-to-all-start.3 = ((f32[128,1,128]{2,1,0:T(1,128)}), f32[128,1,128]{2,1,0:T(1,128)S(1)}, u32[]{:S(2)}, u32[]{:S(2)}) async-start(f32[128,1,128]{2,1,0:T(1,128)} %bitcast.17), calls=%async_computation.3 | async-start | bytes 131072 | tf_op jit(solution)/shard_map/all_to_all | solution.py:452
  63.7 3.5 %collective-permute-start.3 = (f32[32,128]{1,0:T(8,128)S(1)}, f32[32,128]{1,0:T(8,128)S(1)}, u32[]{:S(2)}, u32[]{:S(2)}) collective-permute-start(f32[32,128]{1,0:T(8,128)S(1)} %get-tuple-element.88), channel_id=1, source_target_pairs={{0,1},{1,0},{2,3},{3,2},{4,5},{5,4},{6,7},{7,6},{8,9},{9,8},{10,11... | collective-permute-start | bytes 49160 | tf_op jit(solution)/shard_map/ppermute | solution.py:458
  75.5 15.1 %all-to-all-start.4 = ((f32[128,1,384]{2,1,0:T(1,128)}), f32[128,1,384]{2,1,0:T(1,128)S(1)}, u32[]{:S(2)}, u32[]{:S(2)}) async-start(f32[128,1,384]{2,1,0:T(1,128)} %bitcast.19), calls=%async_computation.4 | async-start | bytes 393216 | tf_op jit(solution)/shard_map/all_to_all | solution.py:452
  79.7 3.9 %collective-permute-start.4 = (f32[32,128]{1,0:T(8,128)S(1)}, f32[32,128]{1,0:T(8,128)S(1)}, u32[]{:S(2)}, u32[]{:S(2)}) collective-permute-start(f32[32,128]{1,0:T(8,128)S(1)} %get-tuple-element.92.own_ref.start_ref), channel_id=1, source_target_pairs={{0,1},{1,0},{2,3},{3,2},{4,5},{5,4},{6,7},{7,6},{8,9},{9,8},{10,11... | collective-permute-start | bytes 49160 | tf_op jit(solution)/shard_map/ppermute | solution.py:458
  81.1 1.6 %copy-start.6 = (f32[16,2,128,128]{3,2,1,0:T(8,128)S(1)}, f32[16,2,128,128]{3,2,1,0:T(8,128)}, u32[]{:S(2)}) copy-start(f32[16,2,128,128]{3,2,1,0:T(8,128)} %blocks.11) | copy-start | bytes 6291460
  91.8 14.3 %all-to-all-start.5 = ((f32[128,1,128]{2,1,0:T(1,128)}), f32[128,1,128]{2,1,0:T(1,128)S(1)}, u32[]{:S(2)}, u32[]{:S(2)}) async-start(f32[128,1,128]{2,1,0:T(1,128)} %bitcast.22), calls=%async_computation.5 | async-start | bytes 131072 | tf_op jit(solution)/shard_map/all_to_all | solution.py:452
  96.2 3.3 %collective-permute-start.5 = (f32[32,128]{1,0:T(8,128)S(1)}, f32[32,128]{1,0:T(8,128)S(1)}, u32[]{:S(2)}, u32[]{:S(2)}) collective-permute-start(f32[32,128]{1,0:T(8,128)S(1)} %get-tuple-element.103), channel_id=1, source_target_pairs={{0,1},{1,0},{2,3},{3,2},{4,5},{5,4},{6,7},{7,6},{8,9},{9,8},{10,11... | collective-permute-start | bytes 49160 | tf_op jit(solution)/shard_map/ppermute | solution.py:458

commit v9 on v7

--- a/solution.py
+++ b/solution.py
@@ -184,8 +184,10 @@
 
 def backward_kernel(first, own_ref, side, nbr, blocks, *refs):
     if first:
-        place, star, local_ref, back_ref, ones_ref, net_weight_ref, near, got, names = refs
-        net_weight_ref[...] = jnp.broadcast_to(star[pl.ds(place[1], 1), :], (8, LANES))
+        star, local_ref, back_ref, ones_ref, net_weight_ref, near, got, names = refs
+        mine = iota((LANES, LANES), 0) == side[0:1, :]
+        weight = jnp.sum(jnp.where(mine, star[...], 0.0), axis=0, keepdims=True)
+        net_weight_ref[...] = jnp.broadcast_to(weight, (8, LANES))
     else:
         local_ref, back_ref, near, got, names = refs
     spread_rows = [h[:32].astype(BF16) for h in tile_names(nbr, names)]
@@ -200,7 +202,7 @@
         for k in range(2):
             got[128 * k + 8 * t : 128 * k + 8 * t + 8, :] = back[:, LANES * k : LANES * (k + 1)]
     filler = jnp.zeros((112, LANES), F32)
-    upper = side[0:1, :] > 0.5
+    upper = (side[0:1, :] & 1) == 1
     for v in range(3 if first else 2):
         spread = sum(
             dot_nn(spread_rows[k], jnp.concatenate([part, filler], axis=0).astype(BF16))
@@ -219,7 +221,7 @@
         ones_ref, anchor, cut_weight, kept, local_ref, share_ref, far, got, names = refs
     else:
         degree, local_ref, share_ref, far, got, names = refs
-    upper = side[0:1, :] > 0.5
+    upper = (side[0:1, :] & 1) == 1
     pick_rows = jnp.concatenate([h.T[:16] for h in tile_names(nbr, names)], axis=0).astype(BF16)
     far[...] = jnp.ones(far.shape, F32)
     zeros = jnp.zeros((96, LANES), F32)
@@ -415,7 +417,7 @@
     put_gathered(news, sent_sums, cut_cells, pin_cell, pin_net, send_ref, kept_ref)
 
 
-VMEM, SMEM, HBM = (pl.BlockSpec(memory_space=m) for m in (pltpu.VMEM, pltpu.SMEM, pltpu.HBM))
+VMEM, HBM = (pl.BlockSpec(memory_space=m) for m in (pltpu.VMEM, pltpu.HBM))
 
 
 def call(kernel, shapes, scratch, cost, args, spaces=()):
@@ -450,9 +452,8 @@
     cut_cells, cut_weight = cut_cells[0], cut_weight[0]
     pin_cell, pin_net = pin_cell.reshape(32, LANES), pin_net.reshape(32, LANES)
     star, anchor = star_weight.reshape(LANES, LANES), anchor.reshape(TILES, LANES)
-    coord = lax.axis_index("coord")
-    place = jnp.stack([coord, lax.axis_index("region") * 2 + coord]).astype(I32)
-    side = jnp.full((8, LANES), coord).astype(F32)
+    number = lax.axis_index("region") * 2 + lax.axis_index("coord")
+    side = jnp.full((8, LANES), number, I32)
     nbr = tile_nbr.T
     send, residual, kept, cut_weight, anchor, star, nbr = call(
         first_kernel,
@@ -481,8 +482,7 @@
             [(rows, LANES), (rows, LANES)] + [(32, LANES), (8, LANES)] * first,
             [(128, LANES), (256, LANES), pltpu.VMEM((8, LANES), I32)],
             BACKWARD_COST,
-            (residual, side, nbr, blocks) + ((place, star) if first else ()),
-            [VMEM] * 4 + [SMEM] * first,
+            (residual, side, nbr, blocks) + ((star,) if first else ()),
         )
         if first:
             ones, net_weight = more

time: 107 us -> 107 us (level)
  transfers between devices with their start and end apart: 12 -> 12, of which waited for: 8 -> 9; matrix products, arithmetic and copies ran while one was open for 0% -> 0% of each run, Pallas kernels for 10% -> 9%
where the time goes in v9:
time: 107 us; the launch traced here: 106 us
  starting transfers between devices  40.9 us (38%)
  waiting for transfers between devices  37.9 us (35%)
  Pallas kernels  21.3 us (20%)
  local copies, waits for them, and re-layouts  5.49 us (5%)
    all_to_all x6, waiting for transfers between devices, exchange(): lax.all_to_all(rows.reshape(LANES, 1, height * LANES), AXES, split_axis=0...  37 us
    all_to_all x6, starting transfers between devices, exchange(): lax.all_to_all(rows.reshape(LANES, 1, height * LANES), AXES, split_axis=0...  31.9 us
    pallas_call x16, Pallas kernels, call(): pl.pallas_call(kernel, out_shape=[jax.ShapeDtypeStruct(s, F32) if isinsta...  21.3 us
    ppermute x6, starting transfers between devices, swap(): return lax.ppermute(x, 'coord', [(0, 1), (1, 0)])  8.97 us
    unnamed x14, local copies, waits for them, and re-layouts  5.49 us
  transfers between devices with their start and end apart: 12, of which 9 were waited for; matrix products, arithmetic and copies ran while one was open for 0% of the time, Pallas kernels for 9%

profile of v9, /device:TPU:1, one launch (start us, length us, event | category | flops | bytes accessed | tf_op | source)
XLA Modules:
  0.0 106.5 jit_solution(7164796293856965308)
XLA Ops:
  0.6 2.5 %shard_map.104 = (f32[384,128]{1,0:T(8,128)}, f32[32,128]{1,0:T(8,128)S(1)}, f32[256,128]{1,0:T(8,128)S(1)}, f32[128,128]{1,0:T(8,128)S(1)}, f32[16,128]{1,0:T(8...) custom-call(f32[2,2048]{1,0:T(2,128)} %right_hbm.1, s32[128,128]{1,0:T(8,128)} %bitcast.31, s32[32,128]{1,0:T(8,128)} %bitcast.37, ...), custom_call_target="tpu_custom_call" | custom-call | flops 16777216 | bytes 1048576 | tf_op jit(solution)/shard_map/pallas_call | solution.py:424
  3.2 11.5 %all-to-all-start = ((f32[128,1,384]{2,1,0:T(1,128)}), f32[128,1,384]{2,1,0:T(1,128)S(1)}, u32[]{:S(2)}, u32[]{:S(2)}) async-start(f32[128,1,384]{2,1,0:T(1,128)} %bitcast.7), calls=%async_computation | async-start | bytes 393216 | tf_op jit(solution)/shard_map/all_to_all | solution.py:440
  14.7 1.5 %collective-permute-start = (f32[32,128]{1,0:T(8,128)S(1)}, f32[32,128]{1,0:T(8,128)S(1)}, u32[]{:S(2)}, u32[]{:S(2)}) collective-permute-start(f32[32,128]{1,0:T(8,128)S(1)} %get-tuple-element.55.own_ref.start_ref), channel_id=1, source_target_pairs={{0,1},{1,0},{2,3},{3,2},{4,5},{5,4},{6,7},{7,6},{8,9},{9,8},{10,11... | collective-permute-start | bytes 49160 | tf_op jit(solution)/shard_map/ppermute | solution.py:446
  16.1 0.0 copy-start.3
  16.1 1.6 %copy-done.3 = f32[16,2,128,128]{3,2,1,0:T(8,128)S(1)} copy-done((f32[16,2,128,128]{3,2,1,0:T(8,128)S(1)}, f32[16,2,128,128]{3,2,1,0:T(8,128)}, u32[]{:S(2)}) %copy-start.3) | copy-done | bytes 2097176
  17.7 0.0 copy-start.4
  17.7 0.6 shard_map.105
  18.3 0.3 collective-permute-done.peer_ref
  18.6 0.7 copy-done.4
  19.3 0.0 copy-start
  19.3 0.0 copy-start.1
  19.3 0.0 copy-start.2
  19.3 0.9 shard_map.106
  20.2 5.4 %all-to-all-done = f32[128,1,384]{2,1,0:T(1,128)S(1)} async-done(((f32[128,1,384]{2,1,0:T(1,128)}), f32[128,1,384]{2,1,0:T(1,128)S(1)}, u32[]{:S(2)}, u32[]{:S(2)}) %all-to-all-start) | async-done | bytes 196640 | tf_op jit(solution)/shard_map/all_to_all | solution.py:440
  25.6 1.3 %shard_map.107 = (f32[128,128]{1,0:T(8,128)}, f32[8,128]{1,0:T(8,128)S(1)}) custom-call(f32[384,128]{1,0:T(8,128)S(1)} %bitcast.25, f32[256,128]{1,0:T(8,128)S(1)} %get-tuple-element.61.refs_3_.kept, f32[128,128]{1,0:T(8,128)S(1)} %get-tuple-element.53.refs_2_.cut_weight, f32[8,128]{1,0:T(8,128)S(1)} %get-tuple-element.64.net_weight, ...), custom_call_target="tpu_custom_call" | custom-call | flops 67108864 | bytes 1048576 | tf_op jit(solution)/shard_map/pallas_call | solution.py:424
  26.9 4.1 %all-to-all-start.1 = ((f32[128,1,128]{2,1,0:T(1,128)}), f32[128,1,128]{2,1,0:T(1,128)S(1)}, u32[]{:S(2)}, u32[]{:S(2)}) async-start(f32[128,1,128]{2,1,0:T(1,128)} %bitcast.10), calls=%async_computation.1 | async-start | bytes 131072 | tf_op jit(solution)/shard_map/all_to_all | solution.py:440
  31.1 1.5 %collective-permute-start.1 = (f32[48,128]{1,0:T(8,128)S(1)}, f32[48,128]{1,0:T(8,128)S(1)}, u32[]{:S(2)}, u32[]{:S(2)}) collective-permute-start(f32[48,128]{1,0:T(8,128)S(1)} %get-tuple-element.72), channel_id=1, source_target_pairs={{0,1},{1,0},{2,3},{3,2},{4,5},{5,4},{6,7},{7,6},{8,9},{9,8},{10,11... | collective-permute-start | bytes 73736 | tf_op jit(solution)/shard_map/ppermute | solution.py:446
  32.6 0.0 copy-done
  32.6 0.0 copy-done.1
  32.6 0.0 copy-done.2
  32.6 2.2 %shard_map.108 = (f32[32,128]{1,0:T(8,128)S(1)}, bf16[4096,128]{1,0:T(8,128)(2,1)S(1)}, f32[16,128]{1,0:T(8,128)S(1)}) custom-call(s32[128,128]{1,0:T(8,128)S(1)} %bitcast.32, f32[128,128]{1,0:T(8,128)S(1)} %get-tuple-element.53.refs_2_.cut_weight, f32[384,128]{1,0:T(8,128)S(1)} %bitcast.26, f32[48,128]{1,0:T(8,128)S(1)} %get-tuple-element.62.local_ref, ...), custom_call_target="tpu_custom_call" | custom-call | flops 2147483648 | bytes 1048576 | tf_op jit(solution)/shard_map/pallas_call | solution.py:424
  34.8 0.0 collective-permute-done.1.back_ref
  34.8 6.2 %all-to-all-done.1 = f32[128,1,128]{2,1,0:T(1,128)S(1)} async-done(((f32[128,1,128]{2,1,0:T(1,128)}), f32[128,1,128]{2,1,0:T(1,128)S(1)}, u32[]{:S(2)}, u32[]{:S(2)}) %all-to-all-start.1) | async-done | bytes 65568 | tf_op jit(solution)/shard_map/all_to_all | solution.py:440
  41.0 1.9 %shard_map.109 = (f32[384,128]{1,0:T(8,128)}, f32[32,128]{1,0:T(8,128)S(1)}, f32[96,128]{1,0:T(8,128)S(1)}, f32[8,128]{1,0:T(8,128)S(1)}, f32[256,128]{1,0:T(8,128)S(1)}, /*index=5*/f32[16,128]{1,0:T(8,128)S(1)}) custom-call(s32[32,128]{1,0:T(8,128)S(1)} %bitcast.39, bf16[4096,128]{1,0:T(8,128)(2,1)S(1)} %get-tuple-element.68.cell_hot, ...), custom_call_target="tpu_custom_call" | custom-call | flops 67108864 | bytes 1048576 | tf_op jit(solution)/shard_map/pallas_call | solution.py:424
  42.9 4.1 %all-to-all-start.2 = ((f32[128,1,384]{2,1,0:T(1,128)}), f32[128,1,384]{2,1,0:T(1,128)S(1)}, u32[]{:S(2)}, u32[]{:S(2)}) async-start(f32[128,1,384]{2,1,0:T(1,128)} %bitcast.12), calls=%async_computation.2 | async-start | bytes 393216 | tf_op jit(solution)/shard_map/all_to_all | solution.py:440
  47.1 1.5 %collective-permute-start.2 = (f32[32,128]{1,0:T(8,128)S(1)}, f32[32,128]{1,0:T(8,128)S(1)}, u32[]{:S(2)}, u32[]{:S(2)}) collective-permute-start(f32[32,128]{1,0:T(8,128)S(1)} %get-tuple-element.74.own_ref.start_ref), channel_id=1, source_target_pairs={{0,1},{1,0},{2,3},{3,2},{4,5},{5,4},{6,7},{7,6},{8,9},{9,8},{10,11... | collective-permute-start | bytes 49160 | tf_op jit(solution)/shard_map/ppermute | solution.py:446
  48.5 0.0 copy-start.5
  48.5 1.6 %copy-done.5 = f32[16,2,128,128]{3,2,1,0:T(8,128)S(1)} copy-done((f32[16,2,128,128]{3,2,1,0:T(8,128)S(1)}, f32[16,2,128,128]{3,2,1,0:T(8,128)}, u32[]{:S(2)}) %copy-start.5) | copy-done | bytes 2097176
  50.1 0.6 shard_map.110
  50.7 0.3 collective-permute-done.2.peer_ref
  51.0 0.8 shard_map.111
  51.9 6.2 %all-to-all-done.2 = f32[128,1,384]{2,1,0:T(1,128)S(1)} async-done(((f32[128,1,384]{2,1,0:T(1,128)}), f32[128,1,384]{2,1,0:T(1,128)S(1)}, u32[]{:S(2)}, u32[]{:S(2)}) %all-to-all-start.2) | async-done | bytes 196640 | tf_op jit(solution)/shard_map/all_to_all | solution.py:440
  58.0 1.3 %shard_map.112 = (f32[128,128]{1,0:T(8,128)}, f32[8,128]{1,0:T(8,128)S(1)}) custom-call(f32[384,128]{1,0:T(8,128)S(1)} %bitcast.29, f32[256,128]{1,0:T(8,128)S(1)} %get-tuple-element.79.kept, f32[128,128]{1,0:T(8,128)S(1)} %get-tuple-element.53.refs_2_.cut_weight, f32[8,128]{1,0:T(8,128)S(1)} %get-tuple-element.64.net_weight, ...), custom_call_target="tpu_custom_call" | custom-call | flops 67108864 | bytes 1048576 | tf_op jit(solution)/shard_map/pallas_call | solution.py:424
  59.3 4.0 %all-to-all-start.3 = ((f32[128,1,128]{2,1,0:T(1,128)}), f32[128,1,128]{2,1,0:T(1,128)S(1)}, u32[]{:S(2)}, u32[]{:S(2)}) async-start(f32[128,1,128]{2,1,0:T(1,128)} %bitcast.15), calls=%async_computation.3 | async-start | bytes 131072 | tf_op jit(solution)/shard_map/all_to_all | solution.py:440
  63.3 1.6 %collective-permute-start.3 = (f32[32,128]{1,0:T(8,128)S(1)}, f32[32,128]{1,0:T(8,128)S(1)}, u32[]{:S(2)}, u32[]{:S(2)}) collective-permute-start(f32[32,128]{1,0:T(8,128)S(1)} %get-tuple-element.86), channel_id=1, source_target_pairs={{0,1},{1,0},{2,3},{3,2},{4,5},{5,4},{6,7},{7,6},{8,9},{9,8},{10,11... | collective-permute-start | bytes 49160 | tf_op jit(solution)/shard_map/ppermute | solution.py:446
  65.0 1.8 %shard_map.113 = (f32[32,128]{1,0:T(8,128)S(1)}, bf16[4096,128]{1,0:T(8,128)(2,1)S(1)}) custom-call(s32[128,128]{1,0:T(8,128)S(1)} %bitcast.34, f32[128,128]{1,0:T(8,128)S(1)} %get-tuple-element.53.refs_2_.cut_weight, f32[384,128]{1,0:T(8,128)S(1)} %bitcast.30, f32[32,128]{1,0:T(8,128)S(1)} %get-tuple-element.77.local_ref, ...), custom_call_target="tpu_custom_call" | custom-call | flops 2147483648 | bytes 1048576 | tf_op jit(solution)/shard_map/pallas_call | solution.py:424
  66.8 0.0 collective-permute-done.3.back_ref
  66.8 6.4 %all-to-all-done.3 = f32[128,1,128]{2,1,0:T(1,128)S(1)} async-done(((f32[128,1,128]{2,1,0:T(1,128)}), f32[128,1,128]{2,1,0:T(1,128)S(1)}, u32[]{:S(2)}, u32[]{:S(2)}) %all-to-all-start.3) | async-done | bytes 65568 | tf_op jit(solution)/shard_map/all_to_all | solution.py:440
  73.2 2.0 %shard_map.114 = (f32[384,128]{1,0:T(8,128)}, f32[32,128]{1,0:T(8,128)S(1)}, f32[96,128]{1,0:T(8,128)S(1)}, f32[8,128]{1,0:T(8,128)S(1)}, f32[256,128]{1,0:T(8,128)S(1)}) custom-call(s32[32,128]{1,0:T(8,128)S(1)} %bitcast.41, bf16[4096,128]{1,0:T(8,128)(2,1)S(1)} %get-tuple-element.83.cell_hot, f32[128,128]{1,0:T(8,128)S(1)} %bitcast.46, ...), custom_call_target="tpu_custom_call" | custom-call | flops 67108864 | bytes 1048576 | tf_op jit(solution)/shard_map/pallas_call | solution.py:424
  75.2 4.1 %all-to-all-start.4 = ((f32[128,1,384]{2,1,0:T(1,128)}), f32[128,1,384]{2,1,0:T(1,128)S(1)}, u32[]{:S(2)}, u32[]{:S(2)}) async-start(f32[128,1,384]{2,1,0:T(1,128)} %bitcast.17), calls=%async_computation.4 | async-start | bytes 393216 | tf_op jit(solution)/shard_map/all_to_all | solution.py:440
  79.3 1.5 %collective-permute-start.4 = (f32[32,128]{1,0:T(8,128)S(1)}, f32[32,128]{1,0:T(8,128)S(1)}, u32[]{:S(2)}, u32[]{:S(2)}) collective-permute-start(f32[32,128]{1,0:T(8,128)S(1)} %get-tuple-element.90.own_ref.start_ref), channel_id=1, source_target_pairs={{0,1},{1,0},{2,3},{3,2},{4,5},{5,4},{6,7},{7,6},{8,9},{9,8},{10,11... | collective-permute-start | bytes 49160 | tf_op jit(solution)/shard_map/ppermute | solution.py:446
  80.8 0.0 copy-start.6
  80.8 1.6 %copy-done.6 = f32[16,2,128,128]{3,2,1,0:T(8,128)S(1)} copy-done((f32[16,2,128,128]{3,2,1,0:T(8,128)S(1)}, f32[16,2,128,128]{3,2,1,0:T(8,128)}, u32[]{:S(2)}) %copy-start.6) | copy-done | bytes 2097176
  82.4 0.6 shard_map.115
  83.0 0.3 collective-permute-done.4.peer_ref
  83.3 0.8 shard_map.116
  84.1 6.2 %all-to-all-done.4 = f32[128,1,384]{2,1,0:T(1,128)S(1)} async-done(((f32[128,1,384]{2,1,0:T(1,128)}), f32[128,1,384]{2,1,0:T(1,128)S(1)}, u32[]{:S(2)}, u32[]{:S(2)}) %all-to-all-start.4) | async-done | bytes 196640 | tf_op jit(solution)/shard_map/all_to_all | solution.py:440
  90.3 1.3 %shard_map.117 = (f32[128,128]{1,0:T(8,128)}, f32[8,128]{1,0:T(8,128)S(1)}) custom-call(f32[384,128]{1,0:T(8,128)S(1)} %bitcast.27, f32[256,128]{1,0:T(8,128)S(1)} %get-tuple-element.94.kept, f32[128,128]{1,0:T(8,128)S(1)} %get-tuple-element.53.refs_2_.cut_weight, f32[8,128]{1,0:T(8,128)S(1)} %get-tuple-element.64.net_weight, ...), custom_call_target="tpu_custom_call" | custom-call | flops 67108864 | bytes 1048576 | tf_op jit(solution)/shard_map/pallas_call | solution.py:424
  91.6 4.0 %all-to-all-start.5 = ((f32[128,1,128]{2,1,0:T(1,128)}), f32[128,1,128]{2,1,0:T(1,128)S(1)}, u32[]{:S(2)}, u32[]{:S(2)}) async-start(f32[128,1,128]{2,1,0:T(1,128)} %bitcast.20), calls=%async_computation.5 | async-start | bytes 131072 | tf_op jit(solution)/shard_map/all_to_all | solution.py:440
  95.6 1.5 %collective-permute-start.5 = (f32[32,128]{1,0:T(8,128)S(1)}, f32[32,128]{1,0:T(8,128)S(1)}, u32[]{:S(2)}, u32[]{:S(2)}) collective-permute-start(f32[32,128]{1,0:T(8,128)S(1)} %get-tuple-element.101), channel_id=1, source_target_pairs={{0,1},{1,0},{2,3},{3,2},{4,5},{5,4},{6,7},{7,6},{8,9},{9,8},{10,11... | collective-permute-start | bytes 49160 | tf_op jit(solution)/shard_map/ppermute | solution.py:446
  97.1 1.8 %shard_map.118 = (f32[32,128]{1,0:T(8,128)S(1)}, bf16[4096,128]{1,0:T(8,128)(2,1)S(1)}) custom-call(s32[128,128]{1,0:T(8,128)S(1)} %bitcast.36, f32[128,128]{1,0:T(8,128)S(1)} %get-tuple-element.53.refs_2_.cut_weight, f32[384,128]{1,0:T(8,128)S(1)} %bitcast.28, f32[32,128]{1,0:T(8,128)S(1)} %get-tuple-element.92.local_ref, ...), custom_call_target="tpu_custom_call" | custom-call | flops 2147483648 | bytes 1048576 | tf_op jit(solution)/shard_map/pallas_call | solution.py:424
  98.9 0.0 collective-permute-done.5.back_ref
  98.9 6.6 %all-to-all-done.5 = f32[128,1,128]{2,1,0:T(1,128)S(1)} async-done(((f32[128,1,128]{2,1,0:T(1,128)}), f32[128,1,128]{2,1,0:T(1,128)S(1)}, u32[]{:S(2)}, u32[]{:S(2)}) %all-to-all-start.5) | async-done | bytes 65568 | tf_op jit(solution)/shard_map/all_to_all | solution.py:440
  105.5 1.0 shard_map.119
  (1 shorter events, 0.0 us)
Async XLA Ops:
  3.2 22.5 %all-to-all-start = ((f32[128,1,384]{2,1,0:T(1,128)}), f32[128,1,384]{2,1,0:T(1,128)S(1)}, u32[]{:S(2)}, u32[]{:S(2)}) async-start(f32[128,1,384]{2,1,0:T(1,128)} %bitcast.7), calls=%async_computation | async-start | bytes 393216 | tf_op jit(solution)/shard_map/all_to_all | solution.py:440
  14.7 3.9 %collective-permute-start = (f32[32,128]{1,0:T(8,128)S(1)}, f32[32,128]{1,0:T(8,128)S(1)}, u32[]{:S(2)}, u32[]{:S(2)}) collective-permute-start(f32[32,128]{1,0:T(8,128)S(1)} %get-tuple-element.55.own_ref.start_ref), channel_id=1, source_target_pairs={{0,1},{1,0},{2,3},{3,2},{4,5},{5,4},{6,7},{7,6},{8,9},{9,8},{10,11... | collective-permute-start | bytes 49160 | tf_op jit(solution)/shard_map/ppermute | solution.py:446
  16.1 1.6 %copy-start.3 = (f32[16,2,128,128]{3,2,1,0:T(8,128)S(1)}, f32[16,2,128,128]{3,2,1,0:T(8,128)}, u32[]{:S(2)}) copy-start(f32[16,2,128,128]{3,2,1,0:T(8,128)} %blocks.11) | copy-start | bytes 6291460
  17.7 1.6 %copy-start.4 = (f32[16,2,128,128]{3,2,1,0:T(8,128)S(1)}, f32[16,2,128,128]{3,2,1,0:T(8,128)}, u32[]{:S(2)}) copy-start(f32[16,2,128,128]{3,2,1,0:T(8,128)} %blocks.11) | copy-start | bytes 6291460
  19.3 13.2 %copy-start = (s32[1,128,128]{2,1,0:T(8,128)S(1)}, s32[1,128,128]{2,1,0:T(8,128)}, u32[]{:S(2)}) copy-start(s32[1,128,128]{2,1,0:T(8,128)} %param.13) | copy-start | bytes 196612
  19.3 13.2 %copy-start.1 = (s32[4096]{0:T(1024)S(1)}, s32[4096]{0:T(1024)}, u32[]{:S(2)}) copy-start(s32[4096]{0:T(1024)} %param.15) | copy-start | bytes 49156
  19.3 13.2 %copy-start.2 = (s32[4096]{0:T(1024)S(1)}, s32[4096]{0:T(1024)}, u32[]{:S(2)}) copy-start(s32[4096]{0:T(1024)} %param.16) | copy-start | bytes 49156
  26.9 14.1 %all-to-all-start.1 = ((f32[128,1,128]{2,1,0:T(1,128)}), f32[128,1,128]{2,1,0:T(1,128)S(1)}, u32[]{:S(2)}, u32[]{:S(2)}) async-start(f32[128,1,128]{2,1,0:T(1,128)} %bitcast.10), calls=%async_computation.1 | async-start | bytes 131072 | tf_op jit(solution)/shard_map/all_to_all | solution.py:440
  31.1 3.7 %collective-permute-start.1 = (f32[48,128]{1,0:T(8,128)S(1)}, f32[48,128]{1,0:T(8,128)S(1)}, u32[]{:S(2)}, u32[]{:S(2)}) collective-permute-start(f32[48,128]{1,0:T(8,128)S(1)} %get-tuple-element.72), channel_id=1, source_target_pairs={{0,1},{1,0},{2,3},{3,2},{4,5},{5,4},{6,7},{7,6},{8,9},{9,8},{10,11... | collective-permute-start | bytes 73736 | tf_op jit(solution)/shard_map/ppermute | solution.py:446
  42.9 15.1 %all-to-all-start.2 = ((f32[128,1,384]{2,1,0:T(1,128)}), f32[128,1,384]{2,1,0:T(1,128)S(1)}, u32[]{:S(2)}, u32[]{:S(2)}) async-start(f32[128,1,384]{2,1,0:T(1,128)} %bitcast.12), calls=%async_computation.2 | async-start | bytes 393216 | tf_op jit(solution)/shard_map/all_to_all | solution.py:440
  47.1 3.9 %collective-permute-start.2 = (f32[32,128]{1,0:T(8,128)S(1)}, f32[32,128]{1,0:T(8,128)S(1)}, u32[]{:S(2)}, u32[]{:S(2)}) collective-permute-start(f32[32,128]{1,0:T(8,128)S(1)} %get-tuple-element.74.own_ref.start_ref), channel_id=1, source_target_pairs={{0,1},{1,0},{2,3},{3,2},{4,5},{5,4},{6,7},{7,6},{8,9},{9,8},{10,11... | collective-permute-start | bytes 49160 | tf_op jit(solution)/shard_map/ppermute | solution.py:446
  48.5 1.6 %copy-start.5 = (f32[16,2,128,128]{3,2,1,0:T(8,128)S(1)}, f32[16,2,128,128]{3,2,1,0:T(8,128)}, u32[]{:S(2)}) copy-start(f32[16,2,128,128]{3,2,1,0:T(8,128)} %blocks.11) | copy-start | bytes 6291460
  59.3 13.9 %all-to-all-start.3 = ((f32[128,1,128]{2,1,0:T(1,128)}), f32[128,1,128]{2,1,0:T(1,128)S(1)}, u32[]{:S(2)}, u32[]{:S(2)}) async-start(f32[128,1,128]{2,1,0:T(1,128)} %bitcast.15), calls=%async_computation.3 | async-start | bytes 131072 | tf_op jit(solution)/shard_map/all_to_all | solution.py:440
  63.3 3.5 %collective-permute-start.3 = (f32[32,128]{1,0:T(8,128)S(1)}, f32[32,128]{1,0:T(8,128)S(1)}, u32[]{:S(2)}, u32[]{:S(2)}) collective-permute-start(f32[32,128]{1,0:T(8,128)S(1)} %get-tuple-element.86), channel_id=1, source_target_pairs={{0,1},{1,0},{2,3},{3,2},{4,5},{5,4},{6,7},{7,6},{8,9},{9,8},{10,11... | collective-permute-start | bytes 49160 | tf_op jit(solution)/shard_map/ppermute | solution.py:446
  75.2 15.1 %all-to-all-start.4 = ((f32[128,1,384]{2,1,0:T(1,128)}), f32[128,1,384]{2,1,0:T(1,128)S(1)}, u32[]{:S(2)}, u32[]{:S(2)}) async-start(f32[128,1,384]{2,1,0:T(1,128)} %bitcast.17), calls=%async_computation.4 | async-start | bytes 393216 | tf_op jit(solution)/shard_map/all_to_all | solution.py:440
  79.3 3.9 %collective-permute-start.4 = (f32[32,128]{1,0:T(8,128)S(1)}, f32[32,128]{1,0:T(8,128)S(1)}, u32[]{:S(2)}, u32[]{:S(2)}) collective-permute-start(f32[32,128]{1,0:T(8,128)S(1)} %get-tuple-element.90.own_ref.start_ref), channel_id=1, source_target_pairs={{0,1},{1,0},{2,3},{3,2},{4,5},{5,4},{6,7},{7,6},{8,9},{9,8},{10,11... | collective-permute-start | bytes 49160 | tf_op jit(solution)/shard_map/ppermute | solution.py:446
  80.8 1.6 %copy-start.6 = (f32[16,2,128,128]{3,2,1,0:T(8,128)S(1)}, f32[16,2,128,128]{3,2,1,0:T(8,128)}, u32[]{:S(2)}) copy-start(f32[16,2,128,128]{3,2,1,0:T(8,128)} %blocks.11) | copy-start | bytes 6291460
  91.6 13.9 %all-to-all-start.5 = ((f32[128,1,128]{2,1,0:T(1,128)}), f32[128,1,128]{2,1,0:T(1,128)S(1)}, u32[]{:S(2)}, u32[]{:S(2)}) async-start(f32[128,1,128]{2,1,0:T(1,128)} %bitcast.20), calls=%async_computation.5 | async-start | bytes 131072 | tf_op jit(solution)/shard_map/all_to_all | solution.py:440
  95.6 3.3 %collective-permute-start.5 = (f32[32,128]{1,0:T(8,128)S(1)}, f32[32,128]{1,0:T(8,128)S(1)}, u32[]{:S(2)}, u32[]{:S(2)}) collective-permute-start(f32[32,128]{1,0:T(8,128)S(1)} %get-tuple-element.101), channel_id=1, source_target_pairs={{0,1},{1,0},{2,3},{3,2},{4,5},{5,4},{6,7},{7,6},{8,9},{9,8},{10,11... | collective-permute-start | bytes 49160 | tf_op jit(solution)/shard_map/ppermute | solution.py:446

commit v10 on v9

--- a/solution.py
+++ b/solution.py
@@ -100,15 +100,17 @@
         tail = jnp.where(iota((1, LANES), 1) == SUM_LANE + i, s, tail)
     groups = [pick(vectors, pin_cell[8 * h : 8 * h + 8, :]) for h in range(4)]
     gx, gy = (jnp.concatenate([g[v] for g in groups], axis=0) for v in range(2))
-    net = (pin_net[...] & (LANES - 1)).astype(F32)
+    if pin_net is not None:
+        net = (pin_net[...] & (LANES - 1)).astype(F32)
     for q in range(4):
+        more = 0.0 if pin_net is None else roll(net, 64 - 32 * q)
         row = jnp.where(
             lane < 32,
             roll(gx, -32 * q),
             jnp.where(
                 lane < 64,
                 roll(gy, 32 - 32 * q),
-                jnp.where(lane < 96, roll(net, 64 - 32 * q), tail),
+                jnp.where(lane < 96, more, tail),
             ),
         )
         out_ref[pl.ds(3 * q + 2, 32, stride=12), :] = row
@@ -257,12 +259,18 @@
     share_ref[2:8, :] = jnp.zeros((6, LANES), F32)
 
 
-def owner_kernel(first, got, kept, cut_weight, net_weight, share_ref, out_ref, sums_ref, rows):
+def owner_kernel(first, got, kept, cut_weight, net_weight, share_ref, *refs):
+    if first:
+        out_ref, sums_ref, nets_ref, index_ref, rows = refs
+    else:
+        nets_ref, index_ref, out_ref, sums_ref, rows = refs
     height = 16 if first else 8
     pin_rows = [got[pl.ds(3 * q + 2, 32, stride=12), :] for q in range(4)]
     sums = sum(jnp.sum(row, axis=0, keepdims=True) for row in pin_rows)
     sums_ref[...] = jnp.broadcast_to(sums, (8, LANES))
-    nets = dense(pin_rows, 64).astype(I32)
+    if first:
+        nets_ref[...] = dense(pin_rows, 64).astype(I32)
+    nets = nets_ref[...]
     rows[...] = jnp.zeros(rows.shape, F32)
     for v in range(2):
         pins = dense(pin_rows, 32 * v)
@@ -296,8 +304,12 @@
     lane = iota((8, LANES), 1)
     tables = [jnp.broadcast_to(c, (8, LANES)) for c in centres]
     for g in range(16):
-        row = got[pl.ds(24 * g + 2, 8, stride=3), :]
-        index = jnp.where(lane < 32, roll(row, -64), roll(row, -32)).astype(I32) & (LANES - 1)
+        if first:
+            row = got[pl.ds(24 * g + 2, 8, stride=3), :]
+            index = jnp.where(lane < 32, roll(row, -64), roll(row, -32)).astype(I32) & (LANES - 1)
+            index_ref[pl.ds(8 * g, 8), :] = index
+        else:
+            index = index_ref[pl.ds(8 * g, 8), :]
         gx, gy = (
             jnp.take_along_axis(t, index, axis=1, mode="promise_in_bounds") for t in tables
         )
@@ -356,9 +368,9 @@
     if last:
         positions_ref, residual_ref, pins = refs
     elif first:
-        cut_cells, pin_net, send_ref, residual_ref, state_ref, old_ref, kept_ref, degree_ref, pins = refs
+        cut_cells, send_ref, residual_ref, state_ref, old_ref, kept_ref, degree_ref, pins = refs
     else:
-        cut_cells, pin_net, send_ref, residual_ref, state_ref, old_ref, kept_ref, pins = refs
+        cut_cells, send_ref, residual_ref, state_ref, old_ref, kept_ref, pins = refs
     pin_rows = [got[pl.ds(q, 32, stride=4), :] for q in range(4)]
     energy = sum(jnp.sum(row, axis=0, keepdims=True) for row in pin_rows)
     for v in range(2):
@@ -414,7 +426,7 @@
     if last:
         return
     old_ref[...] = jnp.broadcast_to(line, (8, LANES))
-    put_gathered(news, sent_sums, cut_cells, pin_cell, pin_net, send_ref, kept_ref)
+    put_gathered(news, sent_sums, cut_cells, pin_cell, None, send_ref, kept_ref)
 
 
 VMEM, HBM = (pl.BlockSpec(memory_space=m) for m in (pltpu.VMEM, pltpu.HBM))
@@ -471,6 +483,7 @@
         [HBM] * 8,
     )
     hots = jax.ShapeDtypeStruct((32 * LANES, LANES), BF16)
+    numbers = [jax.ShapeDtypeStruct((n, LANES), I32) for n in (32, LANES)]
     for iteration in range(ITERS):
         first, last = iteration == 0, iteration == ITERS - 1
         got = exchange(send, 3)
@@ -494,13 +507,15 @@
             (residual, peer, side, nbr, blocks, local_sum)
             + ((ones, anchor, cut_weight, kept) if first else (degree,)),
         )
-        out, sums = call(
+        out, sums, *more = call(
             functools.partial(owner_kernel, first),
-            [(128, LANES), (8, LANES)],
+            [(128, LANES), (8, LANES)] + numbers * first,
             [(512 if first else 256, LANES)],
             1 << 26,
-            (got, kept, cut_weight, net_weight, share),
-        )
+            (got, kept, cut_weight, net_weight, share) + (() if first else (nets, index)),
+        )
+        if first:
+            nets, index = more
         returned = exchange(out, 1)
         back, sums = lax.optimization_barrier((back, sums))
         back = swap(back)
@@ -523,7 +538,7 @@
         if last:
             shapes = [(2, TILES * LANES), (2, TILES * LANES)]
         else:
-            args = args + (cut_cells, pin_net)
+            args = args + (cut_cells,)
             shapes = [(384, LANES), (32, LANES), (96, LANES), (8, LANES), (256, LANES)]
             shapes = shapes + [(16, LANES)] * first
         results = call(

time: 107 us -> 107 us (level)
  no operation moved by 1% of the time
where the time goes in v10:
time: 107 us
  starting transfers between devices  40.9 us (38%)
  waiting for transfers between devices  37.9 us (35%)
  Pallas kernels  21.4 us (20%)
  local copies, waits for them, and re-layouts  5.49 us (5%)
    all_to_all x6, waiting for transfers between devices, exchange(): lax.all_to_all(rows.reshape(LANES, 1, height * LANES), AXES, split_axis=0...  37 us
    all_to_all x6, starting transfers between devices, exchange(): lax.all_to_all(rows.reshape(LANES, 1, height * LANES), AXES, split_axis=0...  32 us
    pallas_call x16, Pallas kernels, call(): pl.pallas_call(kernel, out_shape=[jax.ShapeDtypeStruct(s, F32) if isinsta...  21.4 us
    ppermute x6, starting transfers between devices, swap(): return lax.ppermute(x, 'coord', [(0, 1), (1, 0)])  8.97 us
    unnamed x14, local copies, waits for them, and re-layouts  5.49 us
  transfers between devices with their start and end apart: 12, of which 9 were waited for; matrix products, arithmetic and copies ran while one was open for 0% of the time, Pallas kernels for 9%

profile of v10, /device:TPU:1, one launch (start us, length us, event | category | flops | bytes accessed | tf_op | source)
XLA Modules:
  0.0 106.5 jit_solution(4342654836342669410)
XLA Ops:
  0.6 2.5 %shard_map.104 = (f32[384,128]{1,0:T(8,128)}, f32[32,128]{1,0:T(8,128)S(1)}, f32[256,128]{1,0:T(8,128)S(1)}, f32[128,128]{1,0:T(8,128)S(1)}, f32[16,128]{1,0:T(8...) custom-call(f32[2,2048]{1,0:T(2,128)} %right_hbm.1, s32[128,128]{1,0:T(8,128)} %bitcast.31, s32[32,128]{1,0:T(8,128)} %bitcast.37, ...), custom_call_target="tpu_custom_call" | custom-call | flops 16777216 | bytes 1048576 | tf_op jit(solution)/shard_map/pallas_call | solution.py:436
  3.2 11.5 %all-to-all-start = ((f32[128,1,384]{2,1,0:T(1,128)}), f32[128,1,384]{2,1,0:T(1,128)S(1)}, u32[]{:S(2)}, u32[]{:S(2)}) async-start(f32[128,1,384]{2,1,0:T(1,128)} %bitcast.7), calls=%async_computation | async-start | bytes 393216 | tf_op jit(solution)/shard_map/all_to_all | solution.py:452
  14.7 1.5 %collective-permute-start = (f32[32,128]{1,0:T(8,128)S(1)}, f32[32,128]{1,0:T(8,128)S(1)}, u32[]{:S(2)}, u32[]{:S(2)}) collective-permute-start(f32[32,128]{1,0:T(8,128)S(1)} %get-tuple-element.57.own_ref.start_ref), channel_id=1, source_target_pairs={{0,1},{1,0},{2,3},{3,2},{4,5},{5,4},{6,7},{7,6},{8,9},{9,8},{10,11... | collective-permute-start | bytes 49160 | tf_op jit(solution)/shard_map/ppermute | solution.py:458
  16.1 0.0 copy-start.3
  16.1 1.6 %copy-done.3 = f32[16,2,128,128]{3,2,1,0:T(8,128)S(1)} copy-done((f32[16,2,128,128]{3,2,1,0:T(8,128)S(1)}, f32[16,2,128,128]{3,2,1,0:T(8,128)}, u32[]{:S(2)}) %copy-start.3) | copy-done | bytes 2097176
  17.7 0.0 copy-start.4
  17.7 0.6 shard_map.105
  18.3 0.3 collective-permute-done.peer_ref
  18.6 0.7 copy-done.4
  19.3 0.0 copy-start
  19.3 0.0 copy-start.1
  19.3 0.0 copy-start.2
  19.3 0.9 shard_map.106
  20.2 5.4 %all-to-all-done = f32[128,1,384]{2,1,0:T(1,128)S(1)} async-done(((f32[128,1,384]{2,1,0:T(1,128)}), f32[128,1,384]{2,1,0:T(1,128)S(1)}, u32[]{:S(2)}, u32[]{:S(2)}) %all-to-all-start) | async-done | bytes 196640 | tf_op jit(solution)/shard_map/all_to_all | solution.py:452
  25.6 1.3 %shard_map.107 = (f32[128,128]{1,0:T(8,128)}, f32[8,128]{1,0:T(8,128)S(1)}, s32[32,128]{1,0:T(8,128)S(1)}, s32[128,128]{1,0:T(8,128)S(1)}) custom-call(f32[384,128]{1,0:T(8,128)S(1)} %bitcast.25, f32[256,128]{1,0:T(8,128)S(1)} %get-tuple-element.63.refs_3_.kept, f32[128,128]{1,0:T(8,128)S(1)} %get-tuple-element.55.refs_2_.cut_weight, ...), custom_call_target="tpu_custom_call" | custom-call | flops 67108864 | bytes 1048576 | tf_op jit(solution)/shard_map/pallas_call | solution.py:436
  26.9 4.1 %all-to-all-start.1 = ((f32[128,1,128]{2,1,0:T(1,128)}), f32[128,1,128]{2,1,0:T(1,128)S(1)}, u32[]{:S(2)}, u32[]{:S(2)}) async-start(f32[128,1,128]{2,1,0:T(1,128)} %bitcast.10), calls=%async_computation.1 | async-start | bytes 131072 | tf_op jit(solution)/shard_map/all_to_all | solution.py:452
  31.1 1.5 %collective-permute-start.1 = (f32[48,128]{1,0:T(8,128)S(1)}, f32[48,128]{1,0:T(8,128)S(1)}, u32[]{:S(2)}, u32[]{:S(2)}) collective-permute-start(f32[48,128]{1,0:T(8,128)S(1)} %get-tuple-element.74), channel_id=1, source_target_pairs={{0,1},{1,0},{2,3},{3,2},{4,5},{5,4},{6,7},{7,6},{8,9},{9,8},{10,11... | collective-permute-start | bytes 73736 | tf_op jit(solution)/shard_map/ppermute | solution.py:458
  32.5 0.0 copy-done
  32.6 0.0 copy-done.1
  32.6 0.0 copy-done.2
  32.6 2.2 %shard_map.108 = (f32[32,128]{1,0:T(8,128)S(1)}, bf16[4096,128]{1,0:T(8,128)(2,1)S(1)}, f32[16,128]{1,0:T(8,128)S(1)}) custom-call(s32[128,128]{1,0:T(8,128)S(1)} %bitcast.32, f32[128,128]{1,0:T(8,128)S(1)} %get-tuple-element.55.refs_2_.cut_weight, f32[384,128]{1,0:T(8,128)S(1)} %bitcast.26, f32[48,128]{1,0:T(8,128)S(1)} %get-tuple-element.64.local_ref, ...), custom_call_target="tpu_custom_call" | custom-call | flops 2147483648 | bytes 1048576 | tf_op jit(solution)/shard_map/pallas_call | solution.py:436
  34.8 0.0 collective-permute-done.1.back_ref
  34.8 6.2 %all-to-all-done.1 = f32[128,1,128]{2,1,0:T(1,128)S(1)} async-done(((f32[128,1,128]{2,1,0:T(1,128)}), f32[128,1,128]{2,1,0:T(1,128)S(1)}, u32[]{:S(2)}, u32[]{:S(2)}) %all-to-all-start.1) | async-done | bytes 65568 | tf_op jit(solution)/shard_map/all_to_all | solution.py:452
  41.0 1.9 %shard_map.109 = (f32[384,128]{1,0:T(8,128)}, f32[32,128]{1,0:T(8,128)S(1)}, f32[96,128]{1,0:T(8,128)S(1)}, f32[8,128]{1,0:T(8,128)S(1)}, f32[256,128]{1,0:T(8,128)S(1)}, /*index=5*/f32[16,128]{1,0:T(8,128)S(1)}) custom-call(s32[32,128]{1,0:T(8,128)S(1)} %bitcast.39, bf16[4096,128]{1,0:T(8,128)(2,1)S(1)} %get-tuple-element.70.cell_hot, ...), custom_call_target="tpu_custom_call" | custom-call | flops 67108864 | bytes 1048576 | tf_op jit(solution)/shard_map/pallas_call | solution.py:436
  42.9 4.1 %all-to-all-start.2 = ((f32[128,1,384]{2,1,0:T(1,128)}), f32[128,1,384]{2,1,0:T(1,128)S(1)}, u32[]{:S(2)}, u32[]{:S(2)}) async-start(f32[128,1,384]{2,1,0:T(1,128)} %bitcast.12), calls=%async_computation.2 | async-start | bytes 393216 | tf_op jit(solution)/shard_map/all_to_all | solution.py:452
  47.1 1.5 %collective-permute-start.2 = (f32[32,128]{1,0:T(8,128)S(1)}, f32[32,128]{1,0:T(8,128)S(1)}, u32[]{:S(2)}, u32[]{:S(2)}) collective-permute-start(f32[32,128]{1,0:T(8,128)S(1)} %get-tuple-element.76.own_ref.start_ref), channel_id=1, source_target_pairs={{0,1},{1,0},{2,3},{3,2},{4,5},{5,4},{6,7},{7,6},{8,9},{9,8},{10,11... | collective-permute-start | bytes 49160 | tf_op jit(solution)/shard_map/ppermute | solution.py:458
  48.5 0.0 copy-start.5
  48.5 1.6 %copy-done.5 = f32[16,2,128,128]{3,2,1,0:T(8,128)S(1)} copy-done((f32[16,2,128,128]{3,2,1,0:T(8,128)S(1)}, f32[16,2,128,128]{3,2,1,0:T(8,128)}, u32[]{:S(2)}) %copy-start.5) | copy-done | bytes 2097176
  50.1 0.6 shard_map.110
  50.7 0.3 collective-permute-done.2.peer_ref
  51.0 0.8 shard_map.111
  51.9 6.2 %all-to-all-done.2 = f32[128,1,384]{2,1,0:T(1,128)S(1)} async-done(((f32[128,1,384]{2,1,0:T(1,128)}), f32[128,1,384]{2,1,0:T(1,128)S(1)}, u32[]{:S(2)}, u32[]{:S(2)}) %all-to-all-start.2) | async-done | bytes 196640 | tf_op jit(solution)/shard_map/all_to_all | solution.py:452
  58.0 1.3 %shard_map.112 = (f32[128,128]{1,0:T(8,128)}, f32[8,128]{1,0:T(8,128)S(1)}) custom-call(f32[384,128]{1,0:T(8,128)S(1)} %bitcast.29, f32[256,128]{1,0:T(8,128)S(1)} %get-tuple-element.81.kept, f32[128,128]{1,0:T(8,128)S(1)} %get-tuple-element.55.refs_2_.cut_weight, f32[8,128]{1,0:T(8,128)S(1)} %get-tuple-element.66.net_weight, ...), custom_call_target="tpu_custom_call" | custom-call | flops 67108864 | bytes 1048576 | tf_op jit(solution)/shard_map/pallas_call | solution.py:436
  59.3 4.0 %all-to-all-start.3 = ((f32[128,1,128]{2,1,0:T(1,128)}), f32[128,1,128]{2,1,0:T(1,128)S(1)}, u32[]{:S(2)}, u32[]{:S(2)}) async-start(f32[128,1,128]{2,1,0:T(1,128)} %bitcast.15), calls=%async_computation.3 | async-start | bytes 131072 | tf_op jit(solution)/shard_map/all_to_all | solution.py:452
  63.3 1.6 %collective-permute-start.3 = (f32[32,128]{1,0:T(8,128)S(1)}, f32[32,128]{1,0:T(8,128)S(1)}, u32[]{:S(2)}, u32[]{:S(2)}) collective-permute-start(f32[32,128]{1,0:T(8,128)S(1)} %get-tuple-element.90), channel_id=1, source_target_pairs={{0,1},{1,0},{2,3},{3,2},{4,5},{5,4},{6,7},{7,6},{8,9},{9,8},{10,11... | collective-permute-start | bytes 49160 | tf_op jit(solution)/shard_map/ppermute | solution.py:458
  65.0 1.8 %shard_map.113 = (f32[32,128]{1,0:T(8,128)S(1)}, bf16[4096,128]{1,0:T(8,128)(2,1)S(1)}) custom-call(s32[128,128]{1,0:T(8,128)S(1)} %bitcast.34, f32[128,128]{1,0:T(8,128)S(1)} %get-tuple-element.55.refs_2_.cut_weight, f32[384,128]{1,0:T(8,128)S(1)} %bitcast.30, f32[32,128]{1,0:T(8,128)S(1)} %get-tuple-element.79.local_ref, ...), custom_call_target="tpu_custom_call" | custom-call | flops 2147483648 | bytes 1048576 | tf_op jit(solution)/shard_map/pallas_call | solution.py:436
  66.8 0.0 collective-permute-done.3.back_ref
  66.8 6.4 %all-to-all-done.3 = f32[128,1,128]{2,1,0:T(1,128)S(1)} async-done(((f32[128,1,128]{2,1,0:T(1,128)}), f32[128,1,128]{2,1,0:T(1,128)S(1)}, u32[]{:S(2)}, u32[]{:S(2)}) %all-to-all-start.3) | async-done | bytes 65568 | tf_op jit(solution)/shard_map/all_to_all | solution.py:452
  73.3 2.0 %shard_map.114 = (f32[384,128]{1,0:T(8,128)}, f32[32,128]{1,0:T(8,128)S(1)}, f32[96,128]{1,0:T(8,128)S(1)}, f32[8,128]{1,0:T(8,128)S(1)}, f32[256,128]{1,0:T(8,128)S(1)}) custom-call(s32[32,128]{1,0:T(8,128)S(1)} %bitcast.41, bf16[4096,128]{1,0:T(8,128)(2,1)S(1)} %get-tuple-element.87.cell_hot, f32[128,128]{1,0:T(8,128)S(1)} %bitcast.45, ...), custom_call_target="tpu_custom_call" | custom-call | flops 67108864 | bytes 1048576 | tf_op jit(solution)/shard_map/pallas_call | solution.py:436
  75.2 4.1 %all-to-all-start.4 = ((f32[128,1,384]{2,1,0:T(1,128)}), f32[128,1,384]{2,1,0:T(1,128)S(1)}, u32[]{:S(2)}, u32[]{:S(2)}) async-start(f32[128,1,384]{2,1,0:T(1,128)} %bitcast.17), calls=%async_computation.4 | async-start | bytes 393216 | tf_op jit(solution)/shard_map/all_to_all | solution.py:452
  79.4 1.5 %collective-permute-start.4 = (f32[32,128]{1,0:T(8,128)S(1)}, f32[32,128]{1,0:T(8,128)S(1)}, u32[]{:S(2)}, u32[]{:S(2)}) collective-permute-start(f32[32,128]{1,0:T(8,128)S(1)} %get-tuple-element.94.own_ref.start_ref), channel_id=1, source_target_pairs={{0,1},{1,0},{2,3},{3,2},{4,5},{5,4},{6,7},{7,6},{8,9},{9,8},{10,11... | collective-permute-start | bytes 49160 | tf_op jit(solution)/shard_map/ppermute | solution.py:458
  80.8 0.0 copy-start.6
  80.8 1.6 %copy-done.6 = f32[16,2,128,128]{3,2,1,0:T(8,128)S(1)} copy-done((f32[16,2,128,128]{3,2,1,0:T(8,128)S(1)}, f32[16,2,128,128]{3,2,1,0:T(8,128)}, u32[]{:S(2)}) %copy-start.6) | copy-done | bytes 2097176
  82.4 0.6 shard_map.115
  83.0 0.3 collective-permute-done.4.peer_ref
  83.3 0.8 shard_map.116
  84.1 6.2 %all-to-all-done.4 = f32[128,1,384]{2,1,0:T(1,128)S(1)} async-done(((f32[128,1,384]{2,1,0:T(1,128)}), f32[128,1,384]{2,1,0:T(1,128)S(1)}, u32[]{:S(2)}, u32[]{:S(2)}) %all-to-all-start.4) | async-done | bytes 196640 | tf_op jit(solution)/shard_map/all_to_all | solution.py:452
  90.3 1.3 %shard_map.117 = (f32[128,128]{1,0:T(8,128)}, f32[8,128]{1,0:T(8,128)S(1)}) custom-call(f32[384,128]{1,0:T(8,128)S(1)} %bitcast.27, f32[256,128]{1,0:T(8,128)S(1)} %get-tuple-element.98.kept, f32[128,128]{1,0:T(8,128)S(1)} %get-tuple-element.55.refs_2_.cut_weight, f32[8,128]{1,0:T(8,128)S(1)} %get-tuple-element.66.net_weight, ...), custom_call_target="tpu_custom_call" | custom-call | flops 67108864 | bytes 1048576 | tf_op jit(solution)/shard_map/pallas_call | solution.py:436
  91.6 4.0 %all-to-all-start.5 = ((f32[128,1,128]{2,1,0:T(1,128)}), f32[128,1,128]{2,1,0:T(1,128)S(1)}, u32[]{:S(2)}, u32[]{:S(2)}) async-start(f32[128,1,128]{2,1,0:T(1,128)} %bitcast.20), calls=%async_computation.5 | async-start | bytes 131072 | tf_op jit(solution)/shard_map/all_to_all | solution.py:452
  95.6 1.5 %collective-permute-start.5 = (f32[32,128]{1,0:T(8,128)S(1)}, f32[32,128]{1,0:T(8,128)S(1)}, u32[]{:S(2)}, u32[]{:S(2)}) collective-permute-start(f32[32,128]{1,0:T(8,128)S(1)} %get-tuple-element.105), channel_id=1, source_target_pairs={{0,1},{1,0},{2,3},{3,2},{4,5},{5,4},{6,7},{7,6},{8,9},{9,8},{10,11... | collective-permute-start | bytes 49160 | tf_op jit(solution)/shard_map/ppermute | solution.py:458
  97.1 1.8 %shard_map.118 = (f32[32,128]{1,0:T(8,128)S(1)}, bf16[4096,128]{1,0:T(8,128)(2,1)S(1)}) custom-call(s32[128,128]{1,0:T(8,128)S(1)} %bitcast.36, f32[128,128]{1,0:T(8,128)S(1)} %get-tuple-element.55.refs_2_.cut_weight, f32[384,128]{1,0:T(8,128)S(1)} %bitcast.28, f32[32,128]{1,0:T(8,128)S(1)} %get-tuple-element.96.local_ref, ...), custom_call_target="tpu_custom_call" | custom-call | flops 2147483648 | bytes 1048576 | tf_op jit(solution)/shard_map/pallas_call | solution.py:436
  98.9 0.0 collective-permute-done.5.back_ref
  98.9 6.6 %all-to-all-done.5 = f32[128,1,128]{2,1,0:T(1,128)S(1)} async-done(((f32[128,1,128]{2,1,0:T(1,128)}), f32[128,1,128]{2,1,0:T(1,128)S(1)}, u32[]{:S(2)}, u32[]{:S(2)}) %all-to-all-start.5) | async-done | bytes 65568 | tf_op jit(solution)/shard_map/all_to_all | solution.py:452
  105.5 1.0 shard_map.119
  (1 shorter events, 0.0 us)
Async XLA Ops:
  3.2 22.5 %all-to-all-start = ((f32[128,1,384]{2,1,0:T(1,128)}), f32[128,1,384]{2,1,0:T(1,128)S(1)}, u32[]{:S(2)}, u32[]{:S(2)}) async-start(f32[128,1,384]{2,1,0:T(1,128)} %bitcast.7), calls=%async_computation | async-start | bytes 393216 | tf_op jit(solution)/shard_map/all_to_all | solution.py:452
  14.7 3.9 %collective-permute-start = (f32[32,128]{1,0:T(8,128)S(1)}, f32[32,128]{1,0:T(8,128)S(1)}, u32[]{:S(2)}, u32[]{:S(2)}) collective-permute-start(f32[32,128]{1,0:T(8,128)S(1)} %get-tuple-element.57.own_ref.start_ref), channel_id=1, source_target_pairs={{0,1},{1,0},{2,3},{3,2},{4,5},{5,4},{6,7},{7,6},{8,9},{9,8},{10,11... | collective-permute-start | bytes 49160 | tf_op jit(solution)/shard_map/ppermute | solution.py:458
  16.1 1.6 %copy-start.3 = (f32[16,2,128,128]{3,2,1,0:T(8,128)S(1)}, f32[16,2,128,128]{3,2,1,0:T(8,128)}, u32[]{:S(2)}) copy-start(f32[16,2,128,128]{3,2,1,0:T(8,128)} %blocks.11) | copy-start | bytes 6291460
  17.7 1.6 %copy-start.4 = (f32[16,2,128,128]{3,2,1,0:T(8,128)S(1)}, f32[16,2,128,128]{3,2,1,0:T(8,128)}, u32[]{:S(2)}) copy-start(f32[16,2,128,128]{3,2,1,0:T(8,128)} %blocks.11) | copy-start | bytes 6291460
  19.3 13.2 %copy-start = (s32[1,128,128]{2,1,0:T(8,128)S(1)}, s32[1,128,128]{2,1,0:T(8,128)}, u32[]{:S(2)}) copy-start(s32[1,128,128]{2,1,0:T(8,128)} %param.13) | copy-start | bytes 196612
  19.3 13.2 %copy-start.1 = (s32[4096]{0:T(1024)S(1)}, s32[4096]{0:T(1024)}, u32[]{:S(2)}) copy-start(s32[4096]{0:T(1024)} %param.15) | copy-start | bytes 49156
  19.3 13.2 %copy-start.2 = (s32[4096]{0:T(1024)S(1)}, s32[4096]{0:T(1024)}, u32[]{:S(2)}) copy-start(s32[4096]{0:T(1024)} %param.16) | copy-start | bytes 49156
  26.9 14.1 %all-to-all-start.1 = ((f32[128,1,128]{2,1,0:T(1,128)}), f32[128,1,128]{2,1,0:T(1,128)S(1)}, u32[]{:S(2)}, u32[]{:S(2)}) async-start(f32[128,1,128]{2,1,0:T(1,128)} %bitcast.10), calls=%async_computation.1 | async-start | bytes 131072 | tf_op jit(solution)/shard_map/all_to_all | solution.py:452
  31.1 3.7 %collective-permute-start.1 = (f32[48,128]{1,0:T(8,128)S(1)}, f32[48,128]{1,0:T(8,128)S(1)}, u32[]{:S(2)}, u32[]{:S(2)}) collective-permute-start(f32[48,128]{1,0:T(8,128)S(1)} %get-tuple-element.74), channel_id=1, source_target_pairs={{0,1},{1,0},{2,3},{3,2},{4,5},{5,4},{6,7},{7,6},{8,9},{9,8},{10,11... | collective-permute-start | bytes 73736 | tf_op jit(solution)/shard_map/ppermute | solution.py:458
  42.9 15.1 %all-to-all-start.2 = ((f32[128,1,384]{2,1,0:T(1,128)}), f32[128,1,384]{2,1,0:T(1,128)S(1)}, u32[]{:S(2)}, u32[]{:S(2)}) async-start(f32[128,1,384]{2,1,0:T(1,128)} %bitcast.12), calls=%async_computation.2 | async-start | bytes 393216 | tf_op jit(solution)/shard_map/all_to_all | solution.py:452
  47.1 3.9 %collective-permute-start.2 = (f32[32,128]{1,0:T(8,128)S(1)}, f32[32,128]{1,0:T(8,128)S(1)}, u32[]{:S(2)}, u32[]{:S(2)}) collective-permute-start(f32[32,128]{1,0:T(8,128)S(1)} %get-tuple-element.76.own_ref.start_ref), channel_id=1, source_target_pairs={{0,1},{1,0},{2,3},{3,2},{4,5},{5,4},{6,7},{7,6},{8,9},{9,8},{10,11... | collective-permute-start | bytes 49160 | tf_op jit(solution)/shard_map/ppermute | solution.py:458
  48.5 1.6 %copy-start.5 = (f32[16,2,128,128]{3,2,1,0:T(8,128)S(1)}, f32[16,2,128,128]{3,2,1,0:T(8,128)}, u32[]{:S(2)}) copy-start(f32[16,2,128,128]{3,2,1,0:T(8,128)} %blocks.11) | copy-start | bytes 6291460
  59.3 13.9 %all-to-all-start.3 = ((f32[128,1,128]{2,1,0:T(1,128)}), f32[128,1,128]{2,1,0:T(1,128)S(1)}, u32[]{:S(2)}, u32[]{:S(2)}) async-start(f32[128,1,128]{2,1,0:T(1,128)} %bitcast.15), calls=%async_computation.3 | async-start | bytes 131072 | tf_op jit(solution)/shard_map/all_to_all | solution.py:452
  63.3 3.5 %collective-permute-start.3 = (f32[32,128]{1,0:T(8,128)S(1)}, f32[32,128]{1,0:T(8,128)S(1)}, u32[]{:S(2)}, u32[]{:S(2)}) collective-permute-start(f32[32,128]{1,0:T(8,128)S(1)} %get-tuple-element.90), channel_id=1, source_target_pairs={{0,1},{1,0},{2,3},{3,2},{4,5},{5,4},{6,7},{7,6},{8,9},{9,8},{10,11... | collective-permute-start | bytes 49160 | tf_op jit(solution)/shard_map/ppermute | solution.py:458
  75.2 15.1 %all-to-all-start.4 = ((f32[128,1,384]{2,1,0:T(1,128)}), f32[128,1,384]{2,1,0:T(1,128)S(1)}, u32[]{:S(2)}, u32[]{:S(2)}) async-start(f32[128,1,384]{2,1,0:T(1,128)} %bitcast.17), calls=%async_computation.4 | async-start | bytes 393216 | tf_op jit(solution)/shard_map/all_to_all | solution.py:452
  79.4 3.9 %collective-permute-start.4 = (f32[32,128]{1,0:T(8,128)S(1)}, f32[32,128]{1,0:T(8,128)S(1)}, u32[]{:S(2)}, u32[]{:S(2)}) collective-permute-start(f32[32,128]{1,0:T(8,128)S(1)} %get-tuple-element.94.own_ref.start_ref), channel_id=1, source_target_pairs={{0,1},{1,0},{2,3},{3,2},{4,5},{5,4},{6,7},{7,6},{8,9},{9,8},{10,11... | collective-permute-start | bytes 49160 | tf_op jit(solution)/shard_map/ppermute | solution.py:458
  80.8 1.6 %copy-start.6 = (f32[16,2,128,128]{3,2,1,0:T(8,128)S(1)}, f32[16,2,128,128]{3,2,1,0:T(8,128)}, u32[]{:S(2)}) copy-start(f32[16,2,128,128]{3,2,1,0:T(8,128)} %blocks.11) | copy-start | bytes 6291460
  91.6 13.9 %all-to-all-start.5 = ((f32[128,1,128]{2,1,0:T(1,128)}), f32[128,1,128]{2,1,0:T(1,128)S(1)}, u32[]{:S(2)}, u32[]{:S(2)}) async-start(f32[128,1,128]{2,1,0:T(1,128)} %bitcast.20), calls=%async_computation.5 | async-start | bytes 131072 | tf_op jit(solution)/shard_map/all_to_all | solution.py:452
  95.6 3.3 %collective-permute-start.5 = (f32[32,128]{1,0:T(8,128)S(1)}, f32[32,128]{1,0:T(8,128)S(1)}, u32[]{:S(2)}, u32[]{:S(2)}) collective-permute-start(f32[32,128]{1,0:T(8,128)S(1)} %get-tuple-element.105), channel_id=1, source_target_pairs={{0,1},{1,0},{2,3},{3,2},{4,5},{5,4},{6,7},{7,6},{8,9},{9,8},{10,11... | collective-permute-start | bytes 49160 | tf_op jit(solution)/shard_map/ppermute | solution.py:458
